TPU v7x, 32 devices: a whole 2x2x4 slice. The times are simulated.
32 devices in a mesh: seq: 8 (over z, y), state: 4 (over x, core).
Axes of the slice: x: 2, y: 2, z: 4, core: 2. Of those that a mesh axis runs over, the one named last changes fastest.
Arguments:
- tokens: bfloat16 [2048, 16, 512], P('state', 'seq'), may hold values from -6 to 6
- norm_gain: float32 [512], replicated, may hold values from 0.5 to 1.5
- norm_bias: float32 [512], replicated, may hold values from -2 to 2
- input_weight: bfloat16 [512, 256, 2], P(None, 'state'), may hold values from -0.25 to 0.25
- output_weight: bfloat16 [256, 2, 512], P('state'), may hold values from -0.25 to 0.25
- log_rate: float32 [256], P('state'), may hold values from -9.91 to -2.99
- log_angle: float32 [256], P('state'), may hold values from -4.5 to 1
- log_gain: float32 [256], P('state'), may hold values from -4.91 to -0.87
- skip_gain: float32 [512], replicated, may hold values from -4 to 4
- glu_weight: bfloat16 [512, 1024], replicated, may hold values from -0.25 to 0.25
- lengths: int32 [16], P('seq'), may hold values from 1024 to 2048, as said below
- cotangent: bfloat16 [2048, 16, 512], P('state', 'seq'), may hold values from -6 to 6
Outputs:
- output: bfloat16 [2048, 16, 512], P('state', 'seq')
- grad_tokens: float32 [2048, 16, 512], P('state', 'seq')
- grad_norm_gain: float32 [512], replicated
- grad_norm_bias: float32 [512], replicated
- grad_input_weight: float32 [512, 256, 2], P(None, 'state')
- grad_output_weight: float32 [256, 2, 512], P('state')
- grad_log_rate: float32 [256], P('state')
- grad_log_angle: float32 [256], P('state')
- grad_log_gain: float32 [256], P('state')
- grad_skip_gain: float32 [512], replicated
- grad_glu_weight: float32 [512, 1024], replicated
Inputs may be any that keep to these rules, and one draw needn't show every extreme that they name: `lengths`: valid positions of each sequence counted from its start; of the 2 sequences on each index of seq, one is valid over all 2048 positions.
All inputs are finite; a program needn't handle non-finite values.
Results may differ from a plain program's by a relative error of at most 0.008.
Values may be sent and summed in bfloat16 or wider, within the bound.
No kernel may reach another device: no remote copies, remote signals or barrier semaphores. Data moves between devices by JAX's collectives and lax.ppermute only.
A program may use at most 128 MiB of HBM per device.

v0:
```python
import functools

import jax
import jax.numpy as jnp
from jax import lax
from jax.experimental import pallas as pl
from jax.experimental.pallas import tpu as pltpu
from jax.sharding import PartitionSpec as P

F32, BF16 = jnp.float32, jnp.bfloat16
EPSILON = 1e-05
SUB = 8
CHUNK = 256
PARAM_ROWS = 16
GELU_A = 0.7978845608028654
GELU_B = 0.044715
MIB = 1 << 20


def cmul(ar, ai, br, bi):
    return ar * br - ai * bi, ar * bi + ai * br


def nn(a, b):
    return lax.dot_general(a, b, (((1,), (0,)), ((), ())), preferred_element_type=F32)


def nt(a, b):
    return lax.dot_general(a, b, (((1,), (1,)), ((), ())), preferred_element_type=F32)


def tn(a, b):
    return lax.dot_general(a, b, (((0,), (0,)), ((), ())), preferred_element_type=F32)


def to_rows(x):
    span, group, feats = x.shape
    segs = SUB // group
    steps = span // segs
    return x.reshape(segs, steps, group, feats).transpose(1, 0, 2, 3).reshape(steps * SUB, feats)


def from_rows(y, group):
    rows, feats = y.shape
    segs, steps = SUB // group, rows // SUB
    return y.reshape(steps, segs, group, feats).transpose(1, 0, 2, 3).reshape(segs * steps, group, feats)


def row_mask(base, rows, group, steps, me, lens_ref):
    segs = SUB // group
    row = lax.broadcasted_iota(jnp.int32, (rows, 128), 0) + base
    place = row & (SUB - 1)
    seq = place & (group - 1)
    position = me * (segs * steps) + (place // group) * steps + (row // SUB)
    length = jnp.full((rows, 128), lens_ref[0], jnp.int32)
    for k in range(1, group):
        length = jnp.where(seq == k, lens_ref[k], length)
    return (position < length).astype(F32)


def wide(column, lanes):
    return jnp.concatenate([column] * (lanes // column.shape[1]), axis=1)


def call(body, outs, ins, smem, scratch, limit_mib, flops, name):
    n_smem = len(smem)
    return pl.pallas_call(
        body,
        out_shape=[jax.ShapeDtypeStruct(s, d) for s, d in outs],
        in_specs=[pl.BlockSpec(memory_space=pltpu.SMEM)] * n_smem
        + [pl.BlockSpec(memory_space=pltpu.VMEM)] * len(ins),
        out_specs=[pl.BlockSpec(memory_space=pltpu.VMEM)] * len(outs),
        scratch_shapes=scratch,
        compiler_params=pltpu.CompilerParams(vmem_limit_bytes=limit_mib * MIB),
        cost_estimate=pl.CostEstimate(flops=flops, bytes_accessed=4 * MIB, transcendentals=0),
        name=name,
    )(*smem, *ins)


def norm_kernel(x_ref, gain_ref, bias_ref, low_ref, unit_ref, inv_ref):
    rows, feats = x_ref.shape

    def chunk(c, carry):
        at = pl.ds(pl.multiple_of(c * CHUNK, CHUNK), CHUNK)
        x = x_ref[at, :].astype(F32)
        centred = x - jnp.mean(x, axis=1, keepdims=True)
        inv = lax.rsqrt(jnp.mean(centred * centred, axis=1, keepdims=True) + EPSILON)
        unit = centred * inv
        unit_ref[at, :] = unit
        low_ref[at, :] = (unit * gain_ref[...] + bias_ref[...]).astype(BF16)
        inv_ref[at, :] = jnp.broadcast_to(inv, (CHUNK, 128))
        return carry

    lax.fori_loop(0, rows // CHUNK, chunk, 0)


def gather_rows(me, blocks, own, channels, dst_ref):
    for m, block in enumerate(blocks):
        off = pl.multiple_of((me ^ m) * own, own)
        dst_ref[pl.ds(off, own), :] = block[0:own, :]
        dst_ref[pl.ds(pl.multiple_of(channels + off, own), own), :] = block[own : 2 * own, :]


def seg_of(group):
    row = lax.broadcasted_iota(jnp.int32, (SUB, 128), 0)
    return row // group


def shift_rows(x, by, keep):
    return jnp.where(wide(keep, x.shape[1]), pltpu.roll(x, by % SUB, 0), 0.0)


def seg_prefix(xr, xi, qr, qi, group, forward):
    seg = seg_of(group)
    segs = SUB // group
    dist = 1
    while dist < segs:
        by = group * dist if forward else SUB - group * dist
        keep = seg >= dist if forward else seg < segs - dist
        sr, si = shift_rows(xr, by, keep), shift_rows(xi, by, keep)
        ar, ai = cmul(qr, qi, sr, si)
        xr, xi = xr + ar, xi + ai
        qr, qi = cmul(qr, qi, qr, qi)
        dist *= 2
    return xr, xi


def seg_enter(xr, xi, qr, qi, dr, di, group, forward):
    seg = seg_of(group)
    segs = SUB // group
    by = group if forward else SUB - group
    keep = seg >= 1 if forward else seg < segs - 1
    er, ei = shift_rows(xr, by, keep), shift_rows(xi, by, keep)
    gap = seg if forward else segs - 1 - seg
    pr, pi = jnp.ones_like(er), jnp.zeros_like(ei)
    bit = 1
    while bit < segs:
        nr, ni = cmul(pr, pi, qr, qi)
        take = wide((gap & bit) != 0, er.shape[1])
        pr, pi = jnp.where(take, nr, pr), jnp.where(take, ni, pi)
        qr, qi = cmul(qr, qi, qr, qi)
        bit *= 2
    ar, ai = cmul(pr, pi, dr, di)
    return er + ar, ei + ai


def device_entry(recvs, channels, qr, qi, group, forward):
    seg = seg_of(group)
    segs = SUB // group
    keep = seg == (segs - 1 if forward else 0)
    total_r = total_i = None
    for recv in reversed(recvs):
        if total_r is not None:
            total_r, total_i = cmul(total_r, total_i, qr, qi)
            total_r, total_i = total_r + recv[:, :channels], total_i + recv[:, channels:]
        else:
            total_r, total_i = recv[:, :channels], recv[:, channels:]
    out = []
    for x in (total_r, total_i):
        x = jnp.where(wide(keep, channels), x, 0.0)
        y = x
        for k in range(1, segs):
            y = y + pltpu.roll(x, group * k, 0)
        out.append(y)
    return out


def project_kernel(parts, own, group, me_ref, lens_ref, low_ref, *refs):
    blocks = refs[:parts]
    drive_ref, end_ref, win_ref, cst_ref = refs[parts:]
    rows = low_ref.shape[0]
    channels = own * parts
    steps = rows // SUB
    me = me_ref[0]
    gather_rows(me, blocks, own, channels, win_ref)
    rows_of = []
    for k in range(3):
        total = None
        for block in blocks:
            tile = block[2 * own : 2 * own + PARAM_ROWS, :].astype(F32)
            for part in range(3):
                piece = tile[3 * k + part : 3 * k + part + 1, :channels]
                total = piece if total is None else total + piece
        rows_of.append(total)
    pr, pi, gain = rows_of
    powers = [(pr, pi)]
    span = steps * (SUB // group)
    ar, ai = pr, pi
    count = 1
    while count < span:
        ar, ai = cmul(ar, ai, ar, ai)
        count *= 2
        if count in (steps, span):
            powers.append((ar, ai))
    while len(powers) < 3:
        powers.append(powers[-1])
    for k, (r, i) in enumerate(powers):
        cst_ref[k : k + 1, :] = jnp.concatenate([r, i], axis=1)
    gains = jnp.concatenate([gain, gain], axis=1)
    cst_ref[3:4, :] = gains
    cst_ref[4:8, :] = jnp.zeros((4, 2 * channels), F32)

    def chunk(c, carry):
        base = pl.multiple_of(c * CHUNK, CHUNK)
        at = pl.ds(base, CHUNK)
        mask = row_mask(base, CHUNK, group, steps, me, lens_ref)
        drive_ref[at, :] = nt(low_ref[at, :], win_ref[...]) * (gains * wide(mask, 2 * channels))
        return carry

    lax.fori_loop(0, rows // CHUNK, chunk, 0)
    br = jnp.broadcast_to(pr, (SUB, channels))
    bi = jnp.broadcast_to(pi, (SUB, channels))

    def step(j, h):
        u = drive_ref[pl.ds(pl.multiple_of(j * SUB, SUB), SUB), :]
        nr, ni = cmul(br, bi, h[0], h[1])
        return nr + u[:, :channels], ni + u[:, channels:]

    zero = jnp.zeros((SUB, channels), F32)
    er, ei = lax.fori_loop(0, steps, step, (zero, zero), unroll=8)
    er, ei = seg_prefix(er, ei, *powers[1], group, True)
    end_ref[...] = jnp.concatenate([er, ei], axis=1)


def mix_kernel(parts, n_recv, own, group, orders, me_ref, place_ref, lens_ref, *refs):
    it = iter(refs)
    take = lambda n: [next(it) for _ in range(n)]
    drive_ref, end_ref, cst_ref = take(3)
    recvs = take(n_recv)
    blocks = take(parts)
    x_ref, unit_ref, cot_ref, gain_ref, bias_ref, skip_ref, glu_ref = take(7)
    states_ref, slow_ref, cw_ref, out_ref, dglu_ref, gp_ref = take(6)
    grads = take(len(orders))
    act_ref, acc_ref = take(2)
    rows, feats = x_ref.shape
    channels = own * parts
    steps = rows // SUB
    me = me_ref[0]
    gather_rows(me, blocks, own, channels, cw_ref)
    pr, pi = cst_ref[0:1, :channels], cst_ref[0:1, channels:]
    qr, qi = cst_ref[1:2, :channels], cst_ref[1:2, channels:]
    wr, wi = cst_ref[2:3, :channels], cst_ref[2:3, channels:]
    dr, di = device_entry(recvs, channels, wr, wi, group, True)
    hr, hi = seg_enter(end_ref[:, :channels], end_ref[:, channels:], qr, qi, dr, di, group, True)
    states_ref[0:SUB, :] = jnp.concatenate([hr, hi], axis=1)
    br = jnp.broadcast_to(pr, (SUB, channels))
    bi = jnp.broadcast_to(pi, (SUB, channels))

    def step(j, h):
        base = pl.multiple_of(j * SUB, SUB)
        u = drive_ref[pl.ds(base, SUB), :]
        nr, ni = cmul(br, bi, h[0], h[1])
        nr, ni = nr + u[:, :channels], ni + u[:, channels:]
        at = pl.ds(pl.multiple_of(base + SUB, SUB), SUB)
        states_ref[at, :channels] = nr
        states_ref[at, channels:] = ni
        return nr, ni

    lax.fori_loop(0, steps, step, (hr, hi), unroll=8)

    def chunk(c, carry):
        base = pl.multiple_of(c * CHUNK, CHUNK)
        at = pl.ds(base, CHUNK)
        states = states_ref[pl.ds(pl.multiple_of(base + SUB, SUB), CHUNK), :]
        slow = jnp.concatenate([states[:, :channels], -states[:, channels:]], axis=1).astype(BF16)
        slow_ref[at, :] = slow
        normed = unit_ref[at, :] * gain_ref[...] + bias_ref[...]
        v = nn(slow, cw_ref[...]) + skip_ref[...] * normed
        t = jnp.tanh(GELU_A * (v + GELU_B * (v * v * v)))
        half = 0.5 * (1.0 + t)
        gp_ref[at, :] = half + (0.5 * GELU_A) * v * (1.0 - t * t) * (1.0 + (3.0 * GELU_B) * (v * v))
        act = (v * half).astype(BF16)
        act_ref[at, :] = act
        glu = nn(act, glu_ref[...])
        mask = wide(row_mask(base, CHUNK, group, steps, me, lens_ref), feats)
        value = glu[:, :feats]
        gate = jax.nn.sigmoid(glu[:, feats:])
        branch = mask * gate
        out_ref[at, :] = (x_ref[at, :].astype(F32) + branch * value).astype(BF16)
        d_value = branch * cot_ref[at, :].astype(F32)
        dglu_ref[at, :feats] = d_value.astype(BF16)
        dglu_ref[at, feats:] = (d_value * value * (1.0 - gate)).astype(BF16)
        return carry

    lax.fori_loop(0, rows // CHUNK, chunk, 0)
    width = 256

    def tile(c, carry):
        at = pl.ds(pl.multiple_of(c * width, width), width)
        acc_ref[:, at] = tn(act_ref[...], dglu_ref[:, at])
        return carry

    lax.fori_loop(0, 2 * feats // width, tile, 0)
    spread(acc_ref, place_ref[0], orders, grads)


def spread(acc_ref, place, orders, grads):
    for order, ref in zip(orders, grads):
        _, size, _ = ref.shape
        for k, m in enumerate(order):
            at = pl.ds(pl.multiple_of((place ^ m) * size, size), size)
            ref[k] = acc_ref[at, :].astype(ref.dtype)


def spread_pairs(acc_ref, place, own, channels, orders, grads):
    for order, ref in zip(orders, grads):
        for k, m in enumerate(order):
            off = pl.multiple_of((place ^ m) * own, own)
            ref[k, 0:own] = acc_ref[pl.ds(off, own), :].astype(ref.dtype)
            also = pl.ds(pl.multiple_of(channels + off, own), own)
            ref[k, own : 2 * own] = acc_ref[also, :].astype(ref.dtype)


def back_kernel(own, group, orders, me_ref, *refs):
    it = iter(refs)
    take = lambda n: [next(it) for _ in range(n)]
    dglu_ref, gp_ref, unit_ref, gain_ref, bias_ref, glu_ref, cw_ref, slow_ref, cst_ref = take(9)
    dpre_ref, dst_ref, start_ref, skip_ref = take(4)
    grads = take(len(orders))
    dmix_ref, acc_ref = take(2)
    rows, feats = gp_ref.shape
    channels = cw_ref.shape[0] // 2
    steps = rows // SUB
    me = me_ref[0]

    def chunk(c, total):
        at = pl.ds(pl.multiple_of(c * CHUNK, CHUNK), CHUNK)
        d_pre = nt(dglu_ref[at, :], glu_ref[...]) * gp_ref[at, :]
        dpre_ref[at, :] = d_pre
        normed = unit_ref[at, :] * gain_ref[...] + bias_ref[...]
        total = total + jnp.sum((d_pre * normed).reshape(CHUNK // SUB, SUB, feats), axis=0)
        d_mixed = d_pre.astype(BF16)
        dmix_ref[at, :] = d_mixed
        dst_ref[at, :] = nt(d_mixed, cw_ref[...])
        return total

    total = lax.fori_loop(0, rows // CHUNK, chunk, jnp.zeros((SUB, feats), F32))
    skip_ref[...] = total
    pr, pi = cst_ref[0:1, :channels], cst_ref[0:1, channels:]
    br = jnp.broadcast_to(pr, (SUB, channels))
    bi = jnp.broadcast_to(-pi, (SUB, channels))

    def step(k, a):
        base = pl.multiple_of((steps - 1 - k) * SUB, SUB)
        u = dst_ref[pl.ds(base, SUB), :]
        nr, ni = cmul(br, bi, a[0], a[1])
        return nr + u[:, :channels], ni - u[:, channels:]

    zero = jnp.zeros((SUB, channels), F32)
    ar, ai = lax.fori_loop(0, steps, step, (zero, zero), unroll=8)
    qr, qi = cst_ref[1:2, :channels], -cst_ref[1:2, channels:]
    ar, ai = seg_prefix(ar, ai, qr, qi, group, False)
    start_ref[...] = jnp.concatenate([ar, ai], axis=1)
    width = 256

    def tile(c, carry):
        at = pl.ds(pl.multiple_of(c * width, width), width)
        acc_ref[:, at] = tn(slow_ref[...], dmix_ref[:, at])
        return carry

    lax.fori_loop(0, feats // width, tile, 0)
    spread_pairs(acc_ref, me, own, channels, orders, grads)


def adjoint_kernel(n_recv, own, group, orders, me_ref, lens_ref, *refs):
    it = iter(refs)
    take = lambda n: [next(it) for _ in range(n)]
    dst_ref, start_ref, cst_ref = take(3)
    recvs = take(n_recv)
    states_ref, drive_ref, low_ref = take(3)
    dproj_ref, sums_ref = take(2)
    grads = take(len(orders))
    adj_ref, acc_ref = take(2)
    rows = dst_ref.shape[0]
    channels = dst_ref.shape[1] // 2
    steps = rows // SUB
    me = me_ref[0]
    pr, pi = cst_ref[0:1, :channels], -cst_ref[0:1, channels:]
    qr, qi = cst_ref[1:2, :channels], -cst_ref[1:2, channels:]
    wr, wi = cst_ref[2:3, :channels], -cst_ref[2:3, channels:]
    dr, di = device_entry(recvs, channels, wr, wi, group, False)
    ar, ai = seg_enter(start_ref[:, :channels], start_ref[:, channels:], qr, qi, dr, di, group, False)
    br = jnp.broadcast_to(pr, (SUB, channels))
    bi = jnp.broadcast_to(pi, (SUB, channels))

    def step(k, carry):
        ar, ai, sr, si, sg = carry
        base = pl.multiple_of((steps - 1 - k) * SUB, SUB)
        at = pl.ds(base, SUB)
        d = dst_ref[at, :]
        nr, ni = cmul(br, bi, ar, ai)
        ar, ai = nr + d[:, :channels], ni - d[:, channels:]
        adj_ref[at, :channels] = ar
        adj_ref[at, channels:] = ai
        h = states_ref[at, :]
        hr, hi = h[:, :channels], h[:, channels:]
        u = drive_ref[at, :]
        sr = sr + (ar * hr + ai * hi)
        si = si + (ai * hr - ar * hi)
        sg = sg + (ar * u[:, :channels] + ai * u[:, channels:])
        return ar, ai, sr, si, sg

    zero = jnp.zeros((SUB, channels), F32)
    out = lax.fori_loop(0, steps, step, (ar, ai, zero, zero, zero), unroll=4)
    sums_ref[:, :channels] = out[2]
    sums_ref[:, channels : 2 * channels] = out[3]
    sums_ref[:, 2 * channels : 3 * channels] = out[4]
    gains = cst_ref[3:4, :]

    def chunk(c, carry):
        base = pl.multiple_of(c * CHUNK, CHUNK)
        at = pl.ds(base, CHUNK)
        mask = row_mask(base, CHUNK, group, steps, me, lens_ref)
        dproj_ref[at, :] = (adj_ref[at, :] * (gains * wide(mask, 2 * channels))).astype(BF16)
        return carry

    lax.fori_loop(0, rows // CHUNK, chunk, 0)
    width = 256
    feats = low_ref.shape[1]

    def tile(c, carry):
        at = pl.ds(pl.multiple_of(c * width, width), width)
        acc_ref[:, at] = tn(dproj_ref[...], low_ref[:, at])
        return carry

    lax.fori_loop(0, feats // width, tile, 0)
    spread_pairs(acc_ref, me, own, channels, orders, grads)


def tokens_kernel(dproj_ref, win_ref, dpre_ref, skip_ref, unit_ref, inv_ref, gain_ref, cot_ref, out_ref, sums_ref):
    rows, feats = dpre_ref.shape

    def chunk(c, carry):
        total_gain, total_bias = carry
        at = pl.ds(pl.multiple_of(c * CHUNK, CHUNK), CHUNK)
        d_normed = dpre_ref[at, :] * skip_ref[...] + nn(dproj_ref[at, :], win_ref[...])
        unit = unit_ref[at, :]
        total_gain = total_gain + jnp.sum((d_normed * unit).reshape(CHUNK // SUB, SUB, feats), axis=0)
        total_bias = total_bias + jnp.sum(d_normed.reshape(CHUNK // SUB, SUB, feats), axis=0)
        d_unit = d_normed * gain_ref[...]
        first = jnp.mean(d_unit, axis=1, keepdims=True)
        second = jnp.mean(d_unit * unit, axis=1, keepdims=True)
        inv = wide(inv_ref[at, :], feats)
        out_ref[at, :] = cot_ref[at, :].astype(F32) + inv * (d_unit - first - unit * second)
        return total_gain, total_bias

    zero = jnp.zeros((SUB, feats), F32)
    total_gain, total_bias = lax.fori_loop(0, rows // CHUNK, chunk, (zero, zero))
    sums_ref[:, :feats] = total_gain
    sums_ref[:, feats:] = total_bias


def place_kernel(n, place_ref, *refs):
    blocks, out_ref = refs[:n], refs[n]
    size = blocks[0].shape[0]
    for m, block in enumerate(blocks):
        at = pl.ds(pl.multiple_of((place_ref[0] ^ m) * size, size), size)
        out_ref[at, :] = block[...].astype(F32)


def exchange(x, axis, bit):
    return lax.ppermute(x, axis, [(i, i ^ bit) for i in range(lax.axis_size(axis))])


def bits_of(n):
    return [1 << k for k in range(n.bit_length() - 1)]


def stage_orders(bits):
    kept = [0]
    orders = [[0]]
    for bit in reversed(bits):
        send = [m ^ bit for m in kept]
        orders.insert(0, send)
        kept = send + kept
    return orders


def halve(parts, stages):
    for axis, bit in stages:
        got = exchange(parts[0].astype(BF16), axis, bit)
        rest, off = [], 0
        for p in parts[1:]:
            n = p.shape[0]
            rest.append(p.astype(F32) + got[off : off + n].astype(F32))
            off += n
        parts = rest
    return parts[0][0]


def double(x, stages):
    for axis, bit in stages:
        low = lax.reduce_precision(x, 8, 7).astype(BF16)
        x = low.astype(F32) + exchange(low, axis, bit).astype(F32)
    return x


def double_f32(x, stages):
    for axis, bit in stages:
        x = x + exchange(x, axis, bit)
    return x


def gather_blocks(own, stages):
    blocks = {0: own}
    for axis, bit, unit in stages:
        for m in list(blocks):
            blocks[m ^ unit] = exchange(blocks[m], axis, bit)
    return [blocks[m] for m in range(len(blocks))]


def three_parts(x):
    high = lax.reduce_precision(x, 8, 7)
    mid = lax.reduce_precision(x - high, 8, 7)
    return [high, mid, x - high - mid]


def shards(
    tokens,
    norm_gain,
    norm_bias,
    input_weight,
    output_weight,
    log_rate,
    log_angle,
    log_gain,
    skip_gain,
    glu_weight,
    lengths,
    cotangent,
):
    span, group, feats = tokens.shape
    own = log_rate.shape[0]
    parts = lax.axis_size("state")
    n_seq = lax.axis_size("seq")
    channels = own * parts
    rows = span * group
    me = lax.axis_index("state")
    seq_index = lax.axis_index("seq")
    me_ref = me.reshape(1)
    state_bits, seq_bits = bits_of(parts), bits_of(n_seq)
    place_ref = (me + parts * (seq_index & 1)).reshape(1)
    gather_stages = [("state", b, b) for b in reversed(state_bits)]

    decay = jnp.exp(log_rate)
    angle = jnp.exp(log_angle)
    pole_re = jnp.exp(-decay) * jnp.cos(angle)
    pole_im = jnp.exp(-decay) * jnp.sin(angle)
    small = jnp.stack(three_parts(pole_re) + three_parts(pole_im) + three_parts(jnp.exp(log_gain)))
    mine = (jnp.arange(feats, dtype=jnp.int32) // own) == me
    reps = feats // own
    small = jnp.where(mine[None, :], jnp.tile(small, (1, reps)), 0.0)
    small = jnp.pad(small, ((0, PARAM_ROWS - small.shape[0]), (0, 0))).astype(BF16)
    b_own = input_weight.transpose(2, 1, 0).reshape(2 * own, feats)
    b_own = jnp.concatenate([b_own, small], axis=0)
    c_own = output_weight.transpose(1, 0, 2).reshape(2 * own, feats)
    b_blocks = gather_blocks(b_own, gather_stages)
    c_blocks = gather_blocks(c_own, gather_stages)

    gain_row, bias_row, skip_row = (v.reshape(1, feats) for v in (norm_gain, norm_bias, skip_gain))
    x = to_rows(tokens)
    cot = to_rows(cotangent)
    low, unit, inv = call(
        norm_kernel,
        [((rows, feats), BF16), ((rows, feats), F32), ((rows, 128), F32)],
        [x, gain_row, bias_row],
        [],
        [],
        8,
        rows * feats * 10,
        "norm",
    )
    full = rows * feats * 2 * channels * 2
    drive, end, win, cst = call(
        functools.partial(project_kernel, parts, own, group),
        [
            ((rows, 2 * channels), F32),
            ((SUB, 2 * channels), F32),
            ((2 * channels, feats), BF16),
            ((SUB, 2 * channels), F32),
        ],
        [low] + b_blocks,
        [me_ref, lengths],
        [],
        12,
        full,
        "project",
    )
    forward = [
        lax.ppermute(end, "state", [(i, i + k) for i in range(parts - k)]) for k in range(1, parts)
    ]
    glu_bits = state_bits + [parts]
    glu_orders = stage_orders(glu_bits)
    glu_stages = [("state", b) for b in state_bits] + [("seq", 1)]
    glu_blocks = 2 * parts
    glu_rows = feats // glu_blocks
    glu_outs = [
        ((len(o), glu_rows, 2 * feats), BF16 if k == 0 else F32) for k, o in enumerate(glu_orders)
    ]
    states, slow, cw, out_rows, d_glu, slope, *glu_parts = call(
        functools.partial(mix_kernel, parts, len(forward), own, group, glu_orders),
        [
            ((rows + SUB, 2 * channels), F32),
            ((rows, 2 * channels), BF16),
            ((2 * channels, feats), BF16),
            ((rows, feats), BF16),
            ((rows, 2 * feats), BF16),
            ((rows, feats), F32),
        ]
        + glu_outs,
        [drive, end, cst]
        + forward
        + c_blocks
        + [x, unit, cot, gain_row, bias_row, skip_row, glu_weight],
        [me_ref, place_ref, lengths],
        [pltpu.VMEM((rows, feats), BF16), pltpu.VMEM((feats, 2 * feats), F32)],
        20,
        5 * full,
        "mix",
    )
    state_orders = stage_orders(state_bits)
    state_stages = [("state", b) for b in state_bits]
    seq_stages = [("seq", b) for b in seq_bits]
    pair_outs = [
        ((len(o), 2 * own, feats), BF16 if k == 0 else F32) for k, o in enumerate(state_orders)
    ]
    d_pre, d_states, start, skip_sum, *out_parts = call(
        functools.partial(back_kernel, own, group, state_orders),
        [
            ((rows, feats), F32),
            ((rows, 2 * channels), F32),
            ((SUB, 2 * channels), F32),
            ((SUB, feats), F32),
        ]
        + pair_outs,
        [d_glu, slope, unit, gain_row, bias_row, glu_weight, cw, slow, cst],
        [me_ref],
        [pltpu.VMEM((rows, feats), BF16), pltpu.VMEM((2 * channels, feats), F32)],
        16,
        4 * full,
        "back",
    )
    backward = [
        lax.ppermute(start, "state", [(i + k, i) for i in range(parts - k)]) for k in range(1, parts)
    ]
    d_proj, channel_sums, *in_parts = call(
        functools.partial(adjoint_kernel, len(backward), own, group, state_orders),
        [((rows, 2 * channels), BF16), ((SUB, 3 * channels), F32)] + pair_outs,
        [d_states, start, cst] + backward + [states, drive, low],
        [me_ref, lengths],
        [pltpu.VMEM((rows, 2 * channels), F32), pltpu.VMEM((2 * channels, feats), F32)],
        16,
        2 * full,
        "adjoint",
    )
    grad_rows, feature_sums = call(
        tokens_kernel,
        [((rows, feats), F32), ((SUB, 2 * feats), F32)],
        [d_proj, win, d_pre, skip_row, unit, inv, gain_row, cot],
        [],
        [],
        12,
        full,
        "tokens",
    )

    glu_own = halve(glu_parts, glu_stages)
    glu_own = double(glu_own, [("seq", b) for b in seq_bits[1:]])
    glu_all = gather_blocks(
        lax.reduce_precision(glu_own, 8, 7).astype(BF16),
        [("seq", 1, parts)] + gather_stages,
    )
    (grad_glu,) = call(
        functools.partial(place_kernel, glu_blocks),
        [((feats, 2 * feats), F32)],
        glu_all,
        [place_ref],
        [],
        8,
        feats * feats,
        "place",
    )
    grad_out = double(halve(out_parts, state_stages), seq_stages)
    grad_in = double(halve(in_parts, state_stages), seq_stages)

    sums = jnp.concatenate([channel_sums, feature_sums, skip_sum], axis=1)
    sums = jnp.sum(sums, axis=0, keepdims=True)
    sums = double_f32(sums, state_stages + seq_stages)[0]
    sum_re, sum_im, gain_sum = (
        lax.dynamic_slice(sums, (k * channels + me * own,), (own,)) for k in range(3)
    )
    base = 3 * channels
    grad_gain, grad_bias, grad_skip = (
        sums[base + k * feats : base + (k + 1) * feats] for k in range(3)
    )
    grad_rate = -decay * (sum_re * pole_re + sum_im * pole_im)
    grad_angle = angle * (sum_im * pole_re - sum_re * pole_im)
    return (
        from_rows(out_rows, group),
        from_rows(grad_rows, group),
        grad_gain,
        grad_bias,
        grad_in.reshape(2, own, feats).transpose(2, 1, 0),
        grad_out.reshape(2, own, feats).transpose(1, 0, 2),
        grad_rate,
        grad_angle,
        gain_sum,
        grad_skip,
        grad_glu,
    )


def solution(mesh):
    placed = (
        P("state", "seq", None),
        P(),
        P(),
        P(None, "state", None),
        P("state", None, None),
        P("state"),
        P("state"),
        P("state"),
        P(),
        P(),
        P("seq"),
        P("state", "seq", None),
    )
    return jax.shard_map(
        shards,
        mesh=mesh,
        in_specs=placed,
        out_specs=(
            P("state", "seq", None),
            P("state", "seq", None),
            P(),
            P(),
            P(None, "state", None),
            P("state", None, None),
            P("state"),
            P("state"),
            P("state"),
            P(),
            P(),
        ),
        check_vma=False,
    )
```

profile of v0, /device:TPU:0, one launch (start us, length us, event | category | flops | bytes accessed | tf_op | source)
XLA Modules:
  0.0 158.3 jit_solution(13377891545867681512)
XLA Ops:
  2.7 0.9 copy.24
  3.7 3.0 %collective-permute-start.1 = (bf16[144,512]{1,0:T(8,128)(2,1)S(1)}, bf16[144,512]{1,0:T(8,128)(2,1)}, u32[]{:S(2)}, u32[]{:S(2)}) collective-permute-start(bf16[144,512]{1,0:T(8,128)(2,1)S(1)} %fusion.1.refs_0_), channel_id=1, source_target_pairs={{0,2},{1,3},{2,0},{3,1},{4,6},{5,7},{6,4},{7,5},{8,10},{9,11},{10,... | collective-permute-start | bytes 442376 | tf_op jit(solution)/shard_map/ppermute | solution.py:462
  6.7 0.9 copy.25
  7.8 3.5 %collective-permute-done.1.refs_2_ = bf16[144,512]{1,0:T(8,128)(2,1)} collective-permute-done((bf16[144,512]{1,0:T(8,128)(2,1)S(1)}, bf16[144,512]{1,0:T(8,128)(2,1)}, u32[]{:S(2)}, u32[]{:S(2)}) %collective-permute-start.1) | collective-permute-done | bytes 147488 | tf_op jit(solution)/shard_map/ppermute | solution.py:462
  11.8 1.7 %collective-permute-done.7.refs_8_ = bf16[128,512]{1,0:T(8,128)(2,1)} collective-permute-done((bf16[128,512]{1,0:T(8,128)(2,1)S(1)}, bf16[128,512]{1,0:T(8,128)(2,1)}, u32[]{:S(2)}, u32[]{:S(2)}) %collective-permute-start.7) | collective-permute-done | bytes 131104 | tf_op jit(solution)/shard_map/ppermute | solution.py:462
  13.5 2.0 %copy.36 = bf16[4,128,2,512]{3,2,0,1:T(2,128)(2,1)S(1)} copy(bf16[4,128,2,512]{3,2,1,0:T(2,128)(2,1)} %bitcast.87) | data formatting | bytes 2097152 | tf_op jit(solution)/shard_map/reshape | solution.py:40
  15.9 1.1 norm.1
  17.0 0.8 copy-done.11
  17.8 3.6 %project.1 = (f32[1024,512]{1,0:T(8,128)S(1)}, f32[8,512]{1,0:T(8,128)S(1)}, bf16[512,512]{1,0:T(8,128)(2,1)S(1)}, f32[8,512]{1,0:T(8,128)S(1)}) custom-call(s32[1]{0:T(128)} %bitcast.me_ref, s32[2]{0:T(128)S(1)} %copy-done.34, bf16[1024,512]{1,0:T(8,128)(2,1)S(1)} %get-tuple-element.42.low_ref.refs_8_, bf16[144,512]{1,0:T(8,128)(2,1)S(1)} %fusion.1.refs_0_, ...), custom_call_target="tpu_custom_call" | custom-call | flops 536870912 | bytes 4194304 | tf_op jit(solution)/shard_map/project/pallas_call | solution.py:67
  21.5 1.3 copy-done.4
  22.8 0.8 copy-done.13
  23.6 2.4 %collective-permute-start.3 = (f32[8,512]{1,0:T(8,128)S(1)}, f32[8,512]{1,0:T(8,128)S(1)}, u32[]{:S(2)}, u32[]{:S(2)}) collective-permute-start(f32[8,512]{1,0:T(8,128)S(1)} %get-tuple-element.44.refs_1_), channel_id=1, source_target_pairs={{0,1},{1,2},{2,3},{4,5},{5,6},{6,7},{8,9},{9,10},{10,11},{12,13},{... | collective-permute-start | bytes 49160 | tf_op jit(solution)/shard_map/ppermute | solution.py:590
  26.0 3.7 %collective-permute-start.4 = (f32[8,512]{1,0:T(8,128)S(1)}, f32[8,512]{1,0:T(8,128)S(1)}, u32[]{:S(2)}, u32[]{:S(2)}) collective-permute-start(f32[8,512]{1,0:T(8,128)S(1)} %get-tuple-element.44.refs_1_), channel_id=1, source_target_pairs={{0,2},{1,3},{4,6},{5,7},{8,10},{9,11},{12,14},{13,15},{16,18},{17,... | collective-permute-start | bytes 49160 | tf_op jit(solution)/shard_map/ppermute | solution.py:590
  29.7 1.3 collective-permute-start.5
  31.0 2.9 %copy.35 = bf16[4,128,2,512]{3,2,0,1:T(2,128)(2,1)} copy(bf16[4,128,2,512]{3,2,1,0:T(2,128)(2,1)} %bitcast.88) | data formatting | bytes 2097152 | tf_op jit(solution)/shard_map/reshape | solution.py:40
  33.9 1.5 reshape.112.refs_12_.cot_ref
  37.3 1.2 copy-done.1
  38.5 1.6 %copy-done.5 = f32[1024,512]{1,0:T(8,128)S(1)} copy-done((f32[1024,512]{1,0:T(8,128)S(1)}, f32[1024,512]{1,0:T(8,128)}, u32[]{:S(2)}) %copy-start.5) | copy-done | bytes 2097176
  40.1 1.2 copy-done.10
  46.9 8.7 %mix.1 = (f32[1032,512]{1,0:T(8,128)S(1)}, bf16[1024,512]{1,0:T(8,128)(2,1)S(1)}, bf16[512,512]{1,0:T(8,128)(2,1)S(1)}, bf16[1024,512]{1,0:T(8,128)(2,1)S(1)}, b...) custom-call(s32[1]{0:T(128)} %bitcast.me_ref, ...), custom_call_target="tpu_custom_call" | custom-call | flops 2684354560 | bytes 4194304 | tf_op jit(solution)/shard_map/mix/pallas_call | solution.py:67
  55.6 1.0 copy-done.7
  57.4 4.4 %back.1 = (f32[1024,512]{1,0:T(8,128)S(1)}, f32[1024,512]{1,0:T(8,128)S(1)}, f32[8,512]{1,0:T(8,128)S(1)}, f32[8,512]{1,0:T(8,128)S(1)}, bf16[2,128,512]{2,1,0:T...) custom-call(s32[1]{0:T(128)} %bitcast.me_ref, ...), custom_call_target="tpu_custom_call" | custom-call | flops 2147483648 | bytes 4194304 | tf_op jit(solution)/shard_map/back/pallas_call | solution.py:67
  61.8 1.3 collective-permute-start.9
  63.1 1.3 collective-permute-start.10
  64.4 1.5 collective-permute-start.11
  65.9 2.9 %collective-permute-done.10.refs_4_ = f32[8,512]{1,0:T(8,128)S(1)} collective-permute-done((f32[8,512]{1,0:T(8,128)S(1)}, f32[8,512]{1,0:T(8,128)S(1)}, u32[]{:S(2)}, u32[]{:S(2)}) %collective-permute-start.10) | collective-permute-done | bytes 16416 | tf_op jit(solution)/shard_map/ppermute | solution.py:644
  68.8 1.4 collective-permute-done.11.refs_5_
  70.3 3.5 %adjoint.1 = (bf16[1024,512]{1,0:T(8,128)(2,1)S(1)}, f32[8,768]{1,0:T(8,128)S(1)}, bf16[2,128,512]{2,1,0:T(8,128)(2,1)S(1)}, f32[1,128,512]{2,1,0:T(8,128)S(1)}, f32[1,128,512]{2,1,0:T(8,128)S(1)}) custom-call(s32[1]{0:T(128)} %bitcast.me_ref, s32[2]{0:T(128)S(1)} %copy-done.36, f32[1024,512]{1,0:T(8,128)S(1)} %get-tuple-element.52.refs_0_, ...), custom_call_target="tpu_custom_call" | custom-call | flops 1073741824 | bytes 4194304 | tf_op jit(solution)/shard_map/adjoint/pallas_call | solution.py:67
  74.5 2.0 %tokens.1 = (f32[1024,512]{1,0:T(8,128)S(1)}, f32[8,1024]{1,0:T(8,128)S(1)}) custom-call(bf16[1024,512]{1,0:T(8,128)(2,1)S(1)} %get-tuple-element.55.dproj_ref, bf16[512,512]{1,0:T(8,128)(2,1)S(1)} %copy-done.14, f32[1024,512]{1,0:T(8,128)S(1)} %get-tuple-element.57.dpre_ref, f32[1,512]{1,0:T(1,128)S(1)} %bitcast.81, ...), custom_call_target="tpu_custom_call" | custom-call | flops 536870912 | bytes 4194304 | tf_op jit(solution)/shard_map/tokens/pallas_call | solution.py:67
  76.5 1.3 copy-done.2
  78.0 1.2 collective-permute-done.12
  79.2 3.6 %collective-permute-done.13 = f32[1,2304]{1,0:T(1,128)S(1)} collective-permute-done((f32[1,2304]{1,0:T(1,128)S(1)}, f32[1,2304]{1,0:T(1,128)S(1)}, u32[]{:S(2)}, u32[]{:S(2)}) %collective-permute-start.13) | collective-permute-done | bytes 9248 | tf_op jit(solution)/shard_map/ppermute | solution.py:462
  82.9 1.6 collective-permute-start.14
  84.5 2.2 %collective-permute-done.14 = f32[1,2304]{1,0:T(1,128)S(1)} collective-permute-done((f32[1,2304]{1,0:T(1,128)S(1)}, f32[1,2304]{1,0:T(1,128)S(1)}, u32[]{:S(2)}, u32[]{:S(2)}) %collective-permute-start.14) | collective-permute-done | bytes 9248 | tf_op jit(solution)/shard_map/ppermute | solution.py:462
  86.6 1.6 %collective-permute-start.15 = (f32[1,2304]{1,0:T(1,128)S(1)}, f32[1,2304]{1,0:T(1,128)S(1)}, u32[]{:S(2)}, u32[]{:S(2)}) collective-permute-start(f32[1,2304]{1,0:T(1,128)S(1)} %add.104), channel_id=1, source_target_pairs={{0,8},{4,12},{8,0},{12,4},{16,24},{20,28},{24,16},{28,20},{1,9},{5... | collective-permute-start | bytes 27656 | tf_op jit(solution)/shard_map/ppermute | solution.py:462
  88.3 2.1 %collective-permute-done.15 = f32[1,2304]{1,0:T(1,128)S(1)} collective-permute-done((f32[1,2304]{1,0:T(1,128)S(1)}, f32[1,2304]{1,0:T(1,128)S(1)}, u32[]{:S(2)}, u32[]{:S(2)}) %collective-permute-start.15) | collective-permute-done | bytes 9248 | tf_op jit(solution)/shard_map/ppermute | solution.py:462
  90.4 2.6 %collective-permute-start.16 = (f32[1,2304]{1,0:T(1,128)S(1)}, f32[1,2304]{1,0:T(1,128)S(1)}, u32[]{:S(2)}, u32[]{:S(2)}) collective-permute-start(f32[1,2304]{1,0:T(1,128)S(1)} %add.105), channel_id=1, source_target_pairs={{0,16},{4,20},{8,24},{12,28},{16,0},{20,4},{24,8},{28,12},{1,17},{... | collective-permute-start | bytes 27656 | tf_op jit(solution)/shard_map/ppermute | solution.py:462
  93.0 2.4 %reshape.114 = bf16[128,4,2,512]{3,2,1,0:T(2,128)(2,1)} reshape(bf16[1024,512]{1,0:T(8,128)(2,1)} %copy-done.7) | data formatting | bytes 2097152 | tf_op jit(solution)/shard_map/reshape | solution.py:46
  95.4 2.9 %copy.27 = bf16[4,128,2,512]{3,2,1,0:T(2,128)(2,1)} copy(bf16[4,128,2,512]{3,2,0,1:T(2,128)(2,1)} %bitcast.83) | data formatting | bytes 2097152 | tf_op jit(solution)/shard_map/transpose | solution.py:46
  98.8 2.2 %reshape.116 = f32[128,4,2,512]{3,2,1,0:T(2,128)} reshape(f32[1024,512]{1,0:T(8,128)S(1)} %copy-done.3) | data formatting | bytes 4194304 | tf_op jit(solution)/shard_map/reshape | solution.py:46
  101.1 3.7 %copy.28 = f32[4,128,2,512]{3,2,1,0:T(2,128)} copy(f32[4,128,2,512]{3,2,0,1:T(2,128)} %bitcast.82) | data formatting | bytes 4194304 | tf_op jit(solution)/shard_map/transpose | solution.py:46
  107.0 2.1 %collective-permute-start.18 = (bf16[1,128,512]{2,1,0:T(8,128)(2,1)S(1)}, bf16[1,128,512]{2,1,0:T(8,128)(2,1)S(1)}, u32[]{:S(2)}, u32[]{:S(2)}) collective-permute-start(bf16[1,128,512]{2,1,0:T(8,128)(2,1)S(1)} %add_convert_fusion.3), channel_id=1, source_target_pairs={{0,2},{1,3},{2,0},{3,1},{4,6},{5,7},{6,4},{7,5},{8,10},{9,11},{10,... | collective-permute-start | bytes 393224 | tf_op jit(solution)/shard_map/ppermute | solution.py:462
  109.0 1.0 add_convert_fusion
  110.1 3.1 %collective-permute-done.23 = bf16[1,128,512]{2,1,0:T(8,128)(2,1)S(1)} collective-permute-done((bf16[1,128,512]{2,1,0:T(8,128)(2,1)S(1)}, bf16[1,128,512]{2,1,0:T(8,128)(2,1)S(1)}, u32[]{:S(2)}, u32[]{:S(2)}) %collective-permute-start.23) | collective-permute-done | bytes 131104 | tf_op jit(solution)/shard_map/ppermute | solution.py:462
  113.3 1.6 %collective-permute-start.24 = (bf16[128,512]{1,0:T(8,128)(2,1)S(1)}, bf16[128,512]{1,0:T(8,128)(2,1)S(1)}, u32[]{:S(2)}, u32[]{:S(2)}) collective-permute-start(bf16[128,512]{1,0:T(8,128)(2,1)S(1)} %fusion.3), channel_id=1, source_target_pairs={{0,4},{4,0},{8,12},{12,8},{16,20},{20,16},{24,28},{28,24},{1,5},{5... | collective-permute-start | bytes 393224 | tf_op jit(solution)/shard_map/ppermute | solution.py:462
  114.9 1.2 collective-permute-done.18
  116.1 1.6 %collective-permute-start.19 = (bf16[128,512]{1,0:T(8,128)(2,1)S(1)}, bf16[128,512]{1,0:T(8,128)(2,1)S(1)}, u32[]{:S(2)}, u32[]{:S(2)}) collective-permute-start(bf16[128,512]{1,0:T(8,128)(2,1)S(1)} %fusion.2), channel_id=1, source_target_pairs={{0,4},{4,0},{8,12},{12,8},{16,20},{20,16},{24,28},{28,24},{1,5},{5... | collective-permute-start | bytes 393224 | tf_op jit(solution)/shard_map/ppermute | solution.py:462
  117.7 3.5 %collective-permute-done.28 = bf16[2,64,1024]{2,1,0:T(8,128)(2,1)S(1)} collective-permute-done((bf16[2,64,1024]{2,1,0:T(8,128)(2,1)S(1)}, bf16[2,64,1024]{2,1,0:T(8,128)(2,1)S(1)}, u32[]{:S(2)}, u32[]{:S(2)}) %collective-permute-start.28) | collective-permute-done | bytes 262176 | tf_op jit(solution)/shard_map/ppermute | solution.py:462
  121.2 1.0 add_convert_fusion.1
  122.1 1.6 %collective-permute-start.29 = (bf16[1,64,1024]{2,1,0:T(8,128)(2,1)S(1)}, bf16[1,64,1024]{2,1,0:T(8,128)(2,1)S(1)}, u32[]{:S(2)}, u32[]{:S(2)}) collective-permute-start(bf16[1,64,1024]{2,1,0:T(8,128)(2,1)S(1)} %add_convert_fusion.1), channel_id=1, source_target_pairs={{0,4},{4,0},{8,12},{12,8},{16,20},{20,16},{24,28},{28,24},{1,5},{5... | collective-permute-start | bytes 393224 | tf_op jit(solution)/shard_map/ppermute | solution.py:462
  123.8 1.6 %collective-permute-start.25 = (bf16[128,512]{1,0:T(8,128)(2,1)S(1)}, bf16[128,512]{1,0:T(8,128)(2,1)S(1)}, u32[]{:S(2)}, u32[]{:S(2)}) collective-permute-start(bf16[128,512]{1,0:T(8,128)(2,1)S(1)} %reduce-precision_convert_fusion.4), channel_id=1, source_target_pairs={{0,8},{4,12},{8,0},{12,4},{16,24},{20,28},{24,16},{28,20},{1,9},{5... | collective-permute-start | bytes 393224 | tf_op jit(solution)/shard_map/ppermute | solution.py:462
  125.4 1.8 %collective-permute-done.29 = bf16[1,64,1024]{2,1,0:T(8,128)(2,1)S(1)} collective-permute-done((bf16[1,64,1024]{2,1,0:T(8,128)(2,1)S(1)}, bf16[1,64,1024]{2,1,0:T(8,128)(2,1)S(1)}, u32[]{:S(2)}, u32[]{:S(2)}) %collective-permute-start.29) | collective-permute-done | bytes 131104 | tf_op jit(solution)/shard_map/ppermute | solution.py:462
  127.3 1.0 fusion.4
  128.2 1.6 %collective-permute-start.30 = (bf16[64,1024]{1,0:T(8,128)(2,1)S(1)}, bf16[64,1024]{1,0:T(8,128)(2,1)S(1)}, u32[]{:S(2)}, u32[]{:S(2)}) collective-permute-start(bf16[64,1024]{1,0:T(8,128)(2,1)S(1)} %fusion.4), channel_id=1, source_target_pairs={{0,8},{4,12},{8,0},{12,4},{16,24},{20,28},{24,16},{28,20},{1,9},{5... | collective-permute-start | bytes 393224 | tf_op jit(solution)/shard_map/ppermute | solution.py:462
  130.4 3.4 %collective-permute-done.30 = bf16[64,1024]{1,0:T(8,128)(2,1)S(1)} collective-permute-done((bf16[64,1024]{1,0:T(8,128)(2,1)S(1)}, bf16[64,1024]{1,0:T(8,128)(2,1)S(1)}, u32[]{:S(2)}, u32[]{:S(2)}) %collective-permute-start.30) | collective-permute-done | bytes 131104 | tf_op jit(solution)/shard_map/ppermute | solution.py:462
  134.3 2.6 %collective-permute-start.26 = (bf16[128,512]{1,0:T(8,128)(2,1)S(1)}, bf16[128,512]{1,0:T(8,128)(2,1)S(1)}, u32[]{:S(2)}, u32[]{:S(2)}) collective-permute-start(bf16[128,512]{1,0:T(8,128)(2,1)S(1)} %reduce-precision_convert_fusion.3), channel_id=1, source_target_pairs={{0,16},{4,20},{8,24},{12,28},{16,0},{20,4},{24,8},{28,12},{1,17},{... | collective-permute-start | bytes 393224 | tf_op jit(solution)/shard_map/ppermute | solution.py:462
  137.0 8.5 %collective-permute-done.31 = bf16[64,1024]{1,0:T(8,128)(2,1)S(1)} collective-permute-done((bf16[64,1024]{1,0:T(8,128)(2,1)S(1)}, bf16[64,1024]{1,0:T(8,128)(2,1)S(1)}, u32[]{:S(2)}, u32[]{:S(2)}) %collective-permute-start.31) | collective-permute-done | bytes 131104 | tf_op jit(solution)/shard_map/ppermute | solution.py:462
  145.5 1.6 %collective-permute-start.35 = (bf16[64,1024]{1,0:T(8,128)(2,1)S(1)}, bf16[64,1024]{1,0:T(8,128)(2,1)S(1)}, u32[]{:S(2)}, u32[]{:S(2)}) collective-permute-start(bf16[64,1024]{1,0:T(8,128)(2,1)S(1)} %reduce-precision_convert_fusion.refs_0_), channel_id=1, source_target_pairs={{0,4},{4,0},{8,12},{12,8},{16,20},{20,16},{24,28},{28,24},{1,5},{5... | collective-permute-start | bytes 393224 | tf_op jit(solution)/shard_map/ppermute | solution.py:462
  147.2 0.8 collective-permute-start.33
  148.1 2.5 %collective-permute-done.35.refs_4_ = bf16[64,1024]{1,0:T(8,128)(2,1)S(1)} collective-permute-done((bf16[64,1024]{1,0:T(8,128)(2,1)S(1)}, bf16[64,1024]{1,0:T(8,128)(2,1)S(1)}, u32[]{:S(2)}, u32[]{:S(2)}) %collective-permute-start.35) | collective-permute-done | bytes 131104 | tf_op jit(solution)/shard_map/ppermute | solution.py:462
  151.4 0.9 copy.37
  152.8 2.7 %collective-permute-done.37.refs_6_ = bf16[64,1024]{1,0:T(8,128)(2,1)S(1)} collective-permute-done((bf16[64,1024]{1,0:T(8,128)(2,1)S(1)}, bf16[64,1024]{1,0:T(8,128)(2,1)S(1)}, u32[]{:S(2)}, u32[]{:S(2)}) %collective-permute-start.37) | collective-permute-done | bytes 131104 | tf_op jit(solution)/shard_map/ppermute | solution.py:462
  155.6 0.9 copy.38
  156.9 1.5 place.1
  (181 shorter events, 18.2 us)
Async XLA Ops:
  3.7 7.6 %collective-permute-start.1 = (bf16[144,512]{1,0:T(8,128)(2,1)S(1)}, bf16[144,512]{1,0:T(8,128)(2,1)}, u32[]{:S(2)}, u32[]{:S(2)}) collective-permute-start(bf16[144,512]{1,0:T(8,128)(2,1)S(1)} %fusion.1.refs_0_), channel_id=1, source_target_pairs={{0,2},{1,3},{2,0},{3,1},{4,6},{5,7},{6,4},{7,5},{8,10},{9,11},{10,... | collective-permute-start | bytes 442376 | tf_op jit(solution)/shard_map/ppermute | solution.py:462
  7.6 5.8 %collective-permute-start.7 = (bf16[128,512]{1,0:T(8,128)(2,1)S(1)}, bf16[128,512]{1,0:T(8,128)(2,1)}, u32[]{:S(2)}, u32[]{:S(2)}) collective-permute-start(bf16[128,512]{1,0:T(8,128)(2,1)S(1)} %bitcast.70), channel_id=1, source_target_pairs={{0,2},{1,3},{2,0},{3,1},{4,6},{5,7},{6,4},{7,5},{8,10},{9,11},{10,... | collective-permute-start | bytes 393224 | tf_op jit(solution)/shard_map/ppermute | solution.py:462
  7.7 10.1 %collective-permute-start = (bf16[144,512]{1,0:T(8,128)(2,1)S(1)}, bf16[144,512]{1,0:T(8,128)(2,1)}, u32[]{:S(2)}, u32[]{:S(2)}) collective-permute-start(bf16[144,512]{1,0:T(8,128)(2,1)S(1)} %fusion.1.refs_0_), channel_id=1, source_target_pairs={{0,1},{1,0},{2,3},{3,2},{4,5},{5,4},{6,7},{7,6},{8,9},{9,8},{10,11... | collective-permute-start | bytes 442376 | tf_op jit(solution)/shard_map/ppermute | solution.py:462
  11.3 6.5 %collective-permute-start.2 = (bf16[144,512]{1,0:T(8,128)(2,1)}, bf16[144,512]{1,0:T(8,128)(2,1)}, u32[]{:S(2)}, u32[]{:S(2)}) collective-permute-start(bf16[144,512]{1,0:T(8,128)(2,1)} %collective-permute-done.1.refs_2_), channel_id=1, source_target_pairs={{0,1},{1,0},{2,3},{3,2},{4,5},{5,4},{6,7},{7,6},{8,9},{9,8},{10,11... | collective-permute-start | bytes 442376 | tf_op jit(solution)/shard_map/ppermute | solution.py:462
  11.3 24.1 %collective-permute-start.6 = (bf16[128,512]{1,0:T(8,128)(2,1)S(1)}, bf16[128,512]{1,0:T(8,128)(2,1)}, u32[]{:S(2)}, u32[]{:S(2)}) collective-permute-start(bf16[128,512]{1,0:T(8,128)(2,1)S(1)} %bitcast.71), channel_id=1, source_target_pairs={{0,1},{1,0},{2,3},{3,2},{4,5},{5,4},{6,7},{7,6},{8,9},{9,8},{10,11... | collective-permute-start | bytes 393224 | tf_op jit(solution)/shard_map/ppermute | solution.py:462
  13.5 22.0 %collective-permute-start.8 = (bf16[128,512]{1,0:T(8,128)(2,1)}, bf16[128,512]{1,0:T(8,128)(2,1)}, u32[]{:S(2)}, u32[]{:S(2)}) collective-permute-start(bf16[128,512]{1,0:T(8,128)(2,1)} %collective-permute-done.7.refs_8_), channel_id=1, source_target_pairs={{0,1},{1,0},{2,3},{3,2},{4,5},{5,4},{6,7},{7,6},{8,9},{9,8},{10,11... | collective-permute-start | bytes 393224 | tf_op jit(solution)/shard_map/ppermute | solution.py:462
  15.9 18.0 %copy-start = (bf16[1024,512]{1,0:T(8,128)(2,1)}, bf16[1024,512]{1,0:T(8,128)(2,1)S(1)}, u32[]{:S(2)}) copy-start(bf16[1024,512]{1,0:T(8,128)(2,1)S(1)} %reshape.106.x_ref.refs_10_) | copy-start | bytes 3145732
  23.6 11.8 %copy-start.43 = (f32[8,512]{1,0:T(8,128)}, f32[8,512]{1,0:T(8,128)S(1)}, u32[]{:S(2)}) copy-start(f32[8,512]{1,0:T(8,128)S(1)} %get-tuple-element.44.refs_1_) | copy-start | bytes 49156
  23.6 11.8 %collective-permute-start.3 = (f32[8,512]{1,0:T(8,128)S(1)}, f32[8,512]{1,0:T(8,128)S(1)}, u32[]{:S(2)}, u32[]{:S(2)}) collective-permute-start(f32[8,512]{1,0:T(8,128)S(1)} %get-tuple-element.44.refs_1_), channel_id=1, source_target_pairs={{0,1},{1,2},{2,3},{4,5},{5,6},{6,7},{8,9},{9,10},{10,11},{12,13},{... | collective-permute-start | bytes 49160 | tf_op jit(solution)/shard_map/ppermute | solution.py:590
  26.0 10.0 %collective-permute-start.4 = (f32[8,512]{1,0:T(8,128)S(1)}, f32[8,512]{1,0:T(8,128)S(1)}, u32[]{:S(2)}, u32[]{:S(2)}) collective-permute-start(f32[8,512]{1,0:T(8,128)S(1)} %get-tuple-element.44.refs_1_), channel_id=1, source_target_pairs={{0,2},{1,3},{4,6},{5,7},{8,10},{9,11},{12,14},{13,15},{16,18},{17,... | collective-permute-start | bytes 49160 | tf_op jit(solution)/shard_map/ppermute | solution.py:590
  29.7 7.0 %collective-permute-start.5 = (f32[8,512]{1,0:T(8,128)S(1)}, f32[8,512]{1,0:T(8,128)S(1)}, u32[]{:S(2)}, u32[]{:S(2)}) collective-permute-start(f32[8,512]{1,0:T(8,128)S(1)} %get-tuple-element.44.refs_1_), channel_id=1, source_target_pairs={{0,3},{4,7},{8,11},{12,15},{16,19},{20,23},{24,27},{28,31}} | collective-permute-start | bytes 49160 | tf_op jit(solution)/shard_map/ppermute | solution.py:590
  46.9 10.5 %copy-start.31 = (f32[512]{0:T(512)S(1)}, f32[512]{0:T(512)}, u32[]{:S(2)}) copy-start(f32[512]{0:T(512)} %param.14) | copy-start | bytes 6148
  57.4 4.4 %copy-start.17 = (f32[1,64,1024]{2,1,0:T(8,128)}, f32[1,64,1024]{2,1,0:T(8,128)S(1)}, u32[]{:S(2)}) copy-start(f32[1,64,1024]{2,1,0:T(8,128)S(1)} %get-tuple-element.72) | copy-start | bytes 786436
  57.4 4.4 %copy-start.37 = (bf16[4,64,1024]{2,1,0:T(8,128)(2,1)}, bf16[4,64,1024]{2,1,0:T(8,128)(2,1)S(1)}, u32[]{:S(2)}) copy-start(bf16[4,64,1024]{2,1,0:T(8,128)(2,1)S(1)} %get-tuple-element.70) | copy-start | bytes 1572868
  57.4 12.8 %copy-start.6 = (f32[1024,512]{1,0:T(8,128)S(1)}, f32[1024,512]{1,0:T(8,128)}, u32[]{:S(2)}) copy-start(f32[1024,512]{1,0:T(8,128)} %copy-done.4) | copy-start | bytes 6291460
  57.4 12.8 %copy-start.9 = (bf16[1024,512]{1,0:T(8,128)(2,1)S(1)}, bf16[1024,512]{1,0:T(8,128)(2,1)}, u32[]{:S(2)}) copy-start(bf16[1024,512]{1,0:T(8,128)(2,1)} %copy-done.8) | copy-start | bytes 3145732
  57.4 12.8 %copy-start.36 = (s32[2]{0:T(128)S(1)}, s32[2]{0:T(128)}, u32[]{:S(2)}) copy-start(s32[2]{0:T(128)} %lens_ref.5) | copy-start | bytes 28
  61.8 11.9 %copy-start.19 = (f32[1,128,512]{2,1,0:T(8,128)}, f32[1,128,512]{2,1,0:T(8,128)S(1)}, u32[]{:S(2)}) copy-start(f32[1,128,512]{2,1,0:T(8,128)S(1)} %get-tuple-element.66) | copy-start | bytes 786436
  61.8 11.9 %copy-start.23 = (f32[1,128,512]{2,1,0:T(8,128)}, f32[1,128,512]{2,1,0:T(8,128)S(1)}, u32[]{:S(2)}) copy-start(f32[1,128,512]{2,1,0:T(8,128)S(1)} %get-tuple-element.68) | copy-start | bytes 786436
  61.8 11.9 %copy-start.39 = (bf16[2,128,512]{2,1,0:T(8,128)(2,1)}, bf16[2,128,512]{2,1,0:T(8,128)(2,1)S(1)}, u32[]{:S(2)}) copy-start(bf16[2,128,512]{2,1,0:T(8,128)(2,1)S(1)} %get-tuple-element.67) | copy-start | bytes 786436
  61.8 4.1 %collective-permute-start.9 = (f32[8,512]{1,0:T(8,128)S(1)}, f32[8,512]{1,0:T(8,128)S(1)}, u32[]{:S(2)}, u32[]{:S(2)}) collective-permute-start(f32[8,512]{1,0:T(8,128)S(1)} %get-tuple-element.53.refs_1_), channel_id=1, source_target_pairs={{1,0},{2,1},{3,2},{5,4},{6,5},{7,6},{9,8},{10,9},{11,10},{13,12},{... | collective-permute-start | bytes 49160 | tf_op jit(solution)/shard_map/ppermute | solution.py:644
  63.1 5.6 %collective-permute-start.10 = (f32[8,512]{1,0:T(8,128)S(1)}, f32[8,512]{1,0:T(8,128)S(1)}, u32[]{:S(2)}, u32[]{:S(2)}) collective-permute-start(f32[8,512]{1,0:T(8,128)S(1)} %get-tuple-element.53.refs_1_), channel_id=1, source_target_pairs={{2,0},{3,1},{6,4},{7,5},{10,8},{11,9},{14,12},{15,13},{18,16},{19,... | collective-permute-start | bytes 49160 | tf_op jit(solution)/shard_map/ppermute | solution.py:644
  64.4 5.8 %collective-permute-start.11 = (f32[8,512]{1,0:T(8,128)S(1)}, f32[8,512]{1,0:T(8,128)S(1)}, u32[]{:S(2)}, u32[]{:S(2)}) collective-permute-start(f32[8,512]{1,0:T(8,128)S(1)} %get-tuple-element.53.refs_1_), channel_id=1, source_target_pairs={{3,0},{7,4},{11,8},{15,12},{19,16},{23,20},{27,24},{31,28}} | collective-permute-start | bytes 49160 | tf_op jit(solution)/shard_map/ppermute | solution.py:644
  70.2 4.2 %copy-start.12 = (f32[1024,128]{1,0:T(8,128)S(1)}, f32[1024,128]{1,0:T(8,128)}, u32[]{:S(2)}) copy-start(f32[1024,128]{1,0:T(8,128)} %copy-done.11) | copy-start | bytes 1572868
  77.9 1.2 collective-permute-start.12
  79.1 3.7 %collective-permute-start.13 = (f32[1,2304]{1,0:T(1,128)S(1)}, f32[1,2304]{1,0:T(1,128)S(1)}, u32[]{:S(2)}, u32[]{:S(2)}) collective-permute-start(f32[1,2304]{1,0:T(1,128)S(1)} %reshape_add_fusion), channel_id=1, source_target_pairs={{0,2},{1,3},{2,0},{3,1},{4,6},{5,7},{6,4},{7,5},{8,10},{9,11},{10,... | collective-permute-start | bytes 27656 | tf_op jit(solution)/shard_map/ppermute | solution.py:462
  82.9 3.7 %collective-permute-start.14 = (f32[1,2304]{1,0:T(1,128)S(1)}, f32[1,2304]{1,0:T(1,128)S(1)}, u32[]{:S(2)}, u32[]{:S(2)}) collective-permute-start(f32[1,2304]{1,0:T(1,128)S(1)} %add.103), channel_id=1, source_target_pairs={{0,4},{4,0},{8,12},{12,8},{16,20},{20,16},{24,28},{28,24},{1,5},{5... | collective-permute-start | bytes 27656 | tf_op jit(solution)/shard_map/ppermute | solution.py:462
  86.6 3.7 %collective-permute-start.15 = (f32[1,2304]{1,0:T(1,128)S(1)}, f32[1,2304]{1,0:T(1,128)S(1)}, u32[]{:S(2)}, u32[]{:S(2)}) collective-permute-start(f32[1,2304]{1,0:T(1,128)S(1)} %add.104), channel_id=1, source_target_pairs={{0,8},{4,12},{8,0},{12,4},{16,24},{20,28},{24,16},{28,20},{1,9},{5... | collective-permute-start | bytes 27656 | tf_op jit(solution)/shard_map/ppermute | solution.py:462
  90.4 14.6 %collective-permute-start.16 = (f32[1,2304]{1,0:T(1,128)S(1)}, f32[1,2304]{1,0:T(1,128)S(1)}, u32[]{:S(2)}, u32[]{:S(2)}) collective-permute-start(f32[1,2304]{1,0:T(1,128)S(1)} %add.105), channel_id=1, source_target_pairs={{0,16},{4,20},{8,24},{12,28},{16,0},{20,4},{24,8},{28,12},{1,17},{... | collective-permute-start | bytes 27656 | tf_op jit(solution)/shard_map/ppermute | solution.py:462
  93.0 5.3 %copy-start.40 = (bf16[2,128,512]{2,1,0:T(8,128)(2,1)S(1)}, bf16[2,128,512]{2,1,0:T(8,128)(2,1)}, u32[]{:S(2)}) copy-start(bf16[2,128,512]{2,1,0:T(8,128)(2,1)} %copy-done.39) | copy-start | bytes 786436
  93.0 5.3 %copy-start.38 = (bf16[4,64,1024]{2,1,0:T(8,128)(2,1)S(1)}, bf16[4,64,1024]{2,1,0:T(8,128)(2,1)}, u32[]{:S(2)}) copy-start(bf16[4,64,1024]{2,1,0:T(8,128)(2,1)} %copy-done.37) | copy-start | bytes 1572868
  93.0 5.8 %copy-start.3 = (f32[1024,512]{1,0:T(8,128)S(1)}, f32[1024,512]{1,0:T(8,128)}, u32[]{:S(2)}) copy-start(f32[1024,512]{1,0:T(8,128)} %copy-done.2) | copy-start | bytes 6291460
  98.3 8.5 %collective-permute-start.22 = (bf16[2,128,512]{2,1,0:T(8,128)(2,1)S(1)}, bf16[2,128,512]{2,1,0:T(8,128)(2,1)S(1)}, u32[]{:S(2)}, u32[]{:S(2)}) collective-permute-start(bf16[2,128,512]{2,1,0:T(8,128)(2,1)S(1)} %copy-done.40), channel_id=1, source_target_pairs={{0,1},{1,0},{2,3},{3,2},{4,5},{5,4},{6,7},{7,6},{8,9},{9,8},{10,11... | collective-permute-start | bytes 786440 | tf_op jit(solution)/shard_map/ppermute | solution.py:462
  98.3 10.7 %collective-permute-start.27 = (bf16[4,64,1024]{2,1,0:T(8,128)(2,1)S(1)}, bf16[4,64,1024]{2,1,0:T(8,128)(2,1)}, u32[]{:S(2)}, u32[]{:S(2)}) collective-permute-start(bf16[4,64,1024]{2,1,0:T(8,128)(2,1)S(1)} %copy-done.38), channel_id=1, source_target_pairs={{0,1},{1,0},{2,3},{3,2},{4,5},{5,4},{6,7},{7,6},{8,9},{9,8},{10,11... | collective-permute-start | bytes 1572872 | tf_op jit(solution)/shard_map/ppermute | solution.py:462
  101.1 4.5 %copy-start.52 = (f32[64]{0:T(128)S(1)}, f32[64]{0:T(128)}, u32[]{:S(2)}) copy-start(f32[64]{0:T(128)} %copy-done.51) | copy-start | bytes 772
  101.1 4.5 %copy-start.54 = (f32[64]{0:T(128)S(1)}, f32[64]{0:T(128)}, u32[]{:S(2)}) copy-start(f32[64]{0:T(128)} %copy-done.53) | copy-start | bytes 772
  101.1 4.5 %copy-start.55 = (f32[64]{0:T(128)S(1)}, f32[64]{0:T(128)}, u32[]{:S(2)}) copy-start(f32[64]{0:T(128)} %param.18) | copy-start | bytes 772
  101.1 4.5 %copy-start.56 = (f32[64]{0:T(128)S(1)}, f32[64]{0:T(128)}, u32[]{:S(2)}) copy-start(f32[64]{0:T(128)} %param.17) | copy-start | bytes 772
  101.1 5.7 %copy-start.24 = (f32[1,128,512]{2,1,0:T(8,128)S(1)}, f32[1,128,512]{2,1,0:T(8,128)}, u32[]{:S(2)}) copy-start(f32[1,128,512]{2,1,0:T(8,128)} %copy-done.23) | copy-start | bytes 786436
  101.1 5.8 %copy-start.26 = (f32[1,128,512]{2,1,0:T(8,128)S(1)}, f32[1,128,512]{2,1,0:T(8,128)}, u32[]{:S(2)}) copy-start(f32[1,128,512]{2,1,0:T(8,128)} %copy-done.25) | copy-start | bytes 786436
  101.1 7.9 %copy-start.16 = (f32[2,64,1024]{2,1,0:T(8,128)S(1)}, f32[2,64,1024]{2,1,0:T(8,128)}, u32[]{:S(2)}) copy-start(f32[2,64,1024]{2,1,0:T(8,128)} %copy-done.15) | copy-start | bytes 1572868
  104.8 8.4 %copy-start.20 = (f32[1,128,512]{2,1,0:T(8,128)S(1)}, f32[1,128,512]{2,1,0:T(8,128)}, u32[]{:S(2)}) copy-start(f32[1,128,512]{2,1,0:T(8,128)} %copy-done.19) | copy-start | bytes 786436
  104.8 11.2 %copy-start.22 = (f32[1,128,512]{2,1,0:T(8,128)S(1)}, f32[1,128,512]{2,1,0:T(8,128)}, u32[]{:S(2)}) copy-start(f32[1,128,512]{2,1,0:T(8,128)} %copy-done.21) | copy-start | bytes 786436
  104.8 16.3 %copy-start.18 = (f32[1,64,1024]{2,1,0:T(8,128)S(1)}, f32[1,64,1024]{2,1,0:T(8,128)}, u32[]{:S(2)}) copy-start(f32[1,64,1024]{2,1,0:T(8,128)} %copy-done.17) | copy-start | bytes 786436
  104.9 2.1 %collective-permute-start.17 = (bf16[2,128,512]{2,1,0:T(8,128)(2,1)S(1)}, bf16[2,128,512]{2,1,0:T(8,128)(2,1)S(1)}, u32[]{:S(2)}, u32[]{:S(2)}) collective-permute-start(bf16[2,128,512]{2,1,0:T(8,128)(2,1)S(1)} %copy-done.42), channel_id=1, source_target_pairs={{0,1},{1,0},{2,3},{3,2},{4,5},{5,4},{6,7},{7,6},{8,9},{9,8},{10,11... | collective-permute-start | bytes 786440 | tf_op jit(solution)/shard_map/ppermute | solution.py:462
  106.8 6.4 %collective-permute-start.23 = (bf16[1,128,512]{2,1,0:T(8,128)(2,1)S(1)}, bf16[1,128,512]{2,1,0:T(8,128)(2,1)S(1)}, u32[]{:S(2)}, u32[]{:S(2)}) collective-permute-start(bf16[1,128,512]{2,1,0:T(8,128)(2,1)S(1)} %add_convert_fusion.2), channel_id=1, source_target_pairs={{0,2},{1,3},{2,0},{3,1},{4,6},{5,7},{6,4},{7,5},{8,10},{9,11},{10,... | collective-permute-start | bytes 393224 | tf_op jit(solution)/shard_map/ppermute | solution.py:462
  107.0 9.0 %collective-permute-start.18 = (bf16[1,128,512]{2,1,0:T(8,128)(2,1)S(1)}, bf16[1,128,512]{2,1,0:T(8,128)(2,1)S(1)}, u32[]{:S(2)}, u32[]{:S(2)}) collective-permute-start(bf16[1,128,512]{2,1,0:T(8,128)(2,1)S(1)} %add_convert_fusion.3), channel_id=1, source_target_pairs={{0,2},{1,3},{2,0},{3,1},{4,6},{5,7},{6,4},{7,5},{8,10},{9,11},{10,... | collective-permute-start | bytes 393224 | tf_op jit(solution)/shard_map/ppermute | solution.py:462
  110.0 11.1 %collective-permute-start.28 = (bf16[2,64,1024]{2,1,0:T(8,128)(2,1)S(1)}, bf16[2,64,1024]{2,1,0:T(8,128)(2,1)S(1)}, u32[]{:S(2)}, u32[]{:S(2)}) collective-permute-start(bf16[2,64,1024]{2,1,0:T(8,128)(2,1)S(1)} %add_convert_fusion), channel_id=1, source_target_pairs={{0,2},{1,3},{2,0},{3,1},{4,6},{5,7},{6,4},{7,5},{8,10},{9,11},{10,... | collective-permute-start | bytes 786440 | tf_op jit(solution)/shard_map/ppermute | solution.py:462
  113.3 10.5 %collective-permute-start.24 = (bf16[128,512]{1,0:T(8,128)(2,1)S(1)}, bf16[128,512]{1,0:T(8,128)(2,1)S(1)}, u32[]{:S(2)}, u32[]{:S(2)}) collective-permute-start(bf16[128,512]{1,0:T(8,128)(2,1)S(1)} %fusion.3), channel_id=1, source_target_pairs={{0,4},{4,0},{8,12},{12,8},{16,20},{20,16},{24,28},{28,24},{1,5},{5... | collective-permute-start | bytes 393224 | tf_op jit(solution)/shard_map/ppermute | solution.py:462
  116.1 13.8 %collective-permute-start.19 = (bf16[128,512]{1,0:T(8,128)(2,1)S(1)}, bf16[128,512]{1,0:T(8,128)(2,1)S(1)}, u32[]{:S(2)}, u32[]{:S(2)}) collective-permute-start(bf16[128,512]{1,0:T(8,128)(2,1)S(1)} %fusion.2), channel_id=1, source_target_pairs={{0,4},{4,0},{8,12},{12,8},{16,20},{20,16},{24,28},{28,24},{1,5},{5... | collective-permute-start | bytes 393224 | tf_op jit(solution)/shard_map/ppermute | solution.py:462
  122.1 5.1 %collective-permute-start.29 = (bf16[1,64,1024]{2,1,0:T(8,128)(2,1)S(1)}, bf16[1,64,1024]{2,1,0:T(8,128)(2,1)S(1)}, u32[]{:S(2)}, u32[]{:S(2)}) collective-permute-start(bf16[1,64,1024]{2,1,0:T(8,128)(2,1)S(1)} %add_convert_fusion.1), channel_id=1, source_target_pairs={{0,4},{4,0},{8,12},{12,8},{16,20},{20,16},{24,28},{28,24},{1,5},{5... | collective-permute-start | bytes 393224 | tf_op jit(solution)/shard_map/ppermute | solution.py:462
  123.8 10.5 %collective-permute-start.25 = (bf16[128,512]{1,0:T(8,128)(2,1)S(1)}, bf16[128,512]{1,0:T(8,128)(2,1)S(1)}, u32[]{:S(2)}, u32[]{:S(2)}) collective-permute-start(bf16[128,512]{1,0:T(8,128)(2,1)S(1)} %reduce-precision_convert_fusion.4), channel_id=1, source_target_pairs={{0,8},{4,12},{8,0},{12,4},{16,24},{20,28},{24,16},{28,20},{1,9},{5... | collective-permute-start | bytes 393224 | tf_op jit(solution)/shard_map/ppermute | solution.py:462
  128.2 5.6 %collective-permute-start.30 = (bf16[64,1024]{1,0:T(8,128)(2,1)S(1)}, bf16[64,1024]{1,0:T(8,128)(2,1)S(1)}, u32[]{:S(2)}, u32[]{:S(2)}) collective-permute-start(bf16[64,1024]{1,0:T(8,128)(2,1)S(1)} %fusion.4), channel_id=1, source_target_pairs={{0,8},{4,12},{8,0},{12,4},{16,24},{20,28},{24,16},{28,20},{1,9},{5... | collective-permute-start | bytes 393224 | tf_op jit(solution)/shard_map/ppermute | solution.py:462
  129.9 17.2 %collective-permute-start.20 = (bf16[128,512]{1,0:T(8,128)(2,1)S(1)}, bf16[128,512]{1,0:T(8,128)(2,1)S(1)}, u32[]{:S(2)}, u32[]{:S(2)}) collective-permute-start(bf16[128,512]{1,0:T(8,128)(2,1)S(1)} %reduce-precision_convert_fusion.7), channel_id=1, source_target_pairs={{0,8},{4,12},{8,0},{12,4},{16,24},{20,28},{24,16},{28,20},{1,9},{5... | collective-permute-start | bytes 393224 | tf_op jit(solution)/shard_map/ppermute | solution.py:462
  133.9 11.6 %collective-permute-start.31 = (bf16[64,1024]{1,0:T(8,128)(2,1)S(1)}, bf16[64,1024]{1,0:T(8,128)(2,1)S(1)}, u32[]{:S(2)}, u32[]{:S(2)}) collective-permute-start(bf16[64,1024]{1,0:T(8,128)(2,1)S(1)} %reduce-precision_convert_fusion.1), channel_id=1, source_target_pairs={{0,16},{4,20},{8,24},{12,28},{16,0},{20,4},{24,8},{28,12},{1,17},{... | collective-permute-start | bytes 393224 | tf_op jit(solution)/shard_map/ppermute | solution.py:462
  134.3 17.0 %collective-permute-start.26 = (bf16[128,512]{1,0:T(8,128)(2,1)S(1)}, bf16[128,512]{1,0:T(8,128)(2,1)S(1)}, u32[]{:S(2)}, u32[]{:S(2)}) collective-permute-start(bf16[128,512]{1,0:T(8,128)(2,1)S(1)} %reduce-precision_convert_fusion.3), channel_id=1, source_target_pairs={{0,16},{4,20},{8,24},{12,28},{16,0},{20,4},{24,8},{28,12},{1,17},{... | collective-permute-start | bytes 393224 | tf_op jit(solution)/shard_map/ppermute | solution.py:462
  145.5 5.0 %collective-permute-start.35 = (bf16[64,1024]{1,0:T(8,128)(2,1)S(1)}, bf16[64,1024]{1,0:T(8,128)(2,1)S(1)}, u32[]{:S(2)}, u32[]{:S(2)}) collective-permute-start(bf16[64,1024]{1,0:T(8,128)(2,1)S(1)} %reduce-precision_convert_fusion.refs_0_), channel_id=1, source_target_pairs={{0,4},{4,0},{8,12},{12,8},{16,20},{20,16},{24,28},{28,24},{1,5},{5... | collective-permute-start | bytes 393224 | tf_op jit(solution)/shard_map/ppermute | solution.py:462
  147.2 8.4 %collective-permute-start.21 = (bf16[128,512]{1,0:T(8,128)(2,1)S(1)}, bf16[128,512]{1,0:T(8,128)(2,1)S(1)}, u32[]{:S(2)}, u32[]{:S(2)}) collective-permute-start(bf16[128,512]{1,0:T(8,128)(2,1)S(1)} %reduce-precision_convert_fusion.6), channel_id=1, source_target_pairs={{0,16},{4,20},{8,24},{12,28},{16,0},{20,4},{24,8},{28,12},{1,17},{... | collective-permute-start | bytes 393224 | tf_op jit(solution)/shard_map/ppermute | solution.py:462
  147.2 5.6 %collective-permute-start.33 = (bf16[64,1024]{1,0:T(8,128)(2,1)S(1)}, bf16[64,1024]{1,0:T(8,128)(2,1)S(1)}, u32[]{:S(2)}, u32[]{:S(2)}) collective-permute-start(bf16[64,1024]{1,0:T(8,128)(2,1)S(1)} %reduce-precision_convert_fusion.refs_0_), channel_id=1, source_target_pairs={{0,2},{1,3},{2,0},{3,1},{4,6},{5,7},{6,4},{7,5},{8,10},{9,11},{10,... | collective-permute-start | bytes 393224 | tf_op jit(solution)/shard_map/ppermute | solution.py:462
  150.6 5.0 %collective-permute-start.37 = (bf16[64,1024]{1,0:T(8,128)(2,1)S(1)}, bf16[64,1024]{1,0:T(8,128)(2,1)S(1)}, u32[]{:S(2)}, u32[]{:S(2)}) collective-permute-start(bf16[64,1024]{1,0:T(8,128)(2,1)S(1)} %collective-permute-done.35.refs_4_), channel_id=1, source_target_pairs={{0,2},{1,3},{2,0},{3,1},{4,6},{5,7},{6,4},{7,5},{8,10},{9,11},{10,... | collective-permute-start | bytes 393224 | tf_op jit(solution)/shard_map/ppermute | solution.py:462
  152.3 4.2 %collective-permute-start.32 = (bf16[64,1024]{1,0:T(8,128)(2,1)S(1)}, bf16[64,1024]{1,0:T(8,128)(2,1)S(1)}, u32[]{:S(2)}, u32[]{:S(2)}) collective-permute-start(bf16[64,1024]{1,0:T(8,128)(2,1)S(1)} %reduce-precision_convert_fusion.refs_0_), channel_id=1, source_target_pairs={{0,1},{1,0},{2,3},{3,2},{4,5},{5,4},{6,7},{7,6},{8,9},{9,8},{10,11... | collective-permute-start | bytes 393224 | tf_op jit(solution)/shard_map/ppermute | solution.py:462
  152.3 4.2 %collective-permute-start.36 = (bf16[64,1024]{1,0:T(8,128)(2,1)S(1)}, bf16[64,1024]{1,0:T(8,128)(2,1)S(1)}, u32[]{:S(2)}, u32[]{:S(2)}) collective-permute-start(bf16[64,1024]{1,0:T(8,128)(2,1)S(1)} %collective-permute-done.35.refs_4_), channel_id=1, source_target_pairs={{0,1},{1,0},{2,3},{3,2},{4,5},{5,4},{6,7},{7,6},{8,9},{9,8},{10,11... | collective-permute-start | bytes 393224 | tf_op jit(solution)/shard_map/ppermute | solution.py:462
  152.8 3.7 %collective-permute-start.34 = (bf16[64,1024]{1,0:T(8,128)(2,1)S(1)}, bf16[64,1024]{1,0:T(8,128)(2,1)S(1)}, u32[]{:S(2)}, u32[]{:S(2)}) collective-permute-start(bf16[64,1024]{1,0:T(8,128)(2,1)S(1)} %collective-permute-done.33.refs_2_), channel_id=1, source_target_pairs={{0,1},{1,0},{2,3},{3,2},{4,5},{5,4},{6,7},{7,6},{8,9},{9,8},{10,11... | collective-permute-start | bytes 393224 | tf_op jit(solution)/shard_map/ppermute | solution.py:462
  155.5 1.3 collective-permute-start.38
  (32 other events, 46.5 us)
where the time goes:
time: 159 us; the launch traced here: 158 us
  waiting for transfers between devices  45.7 us (29%)
  local copies, waits for them, and re-layouts  41.7 us (26%)
  starting transfers between devices  39.3 us (25%)
  Pallas kernels  24.7 us (16%)
  other arithmetic  5.45 us (3%)
    ppermute x33, waiting for transfers between devices, exchange(): lax.ppermute(x, axis, [(i, i ^ bit) for i in range(lax.axis_size(axis))])  41.4 us
    ppermute x33, starting transfers between devices, exchange(): lax.ppermute(x, axis, [(i, i ^ bit) for i in range(lax.axis_size(axis))])  27.9 us
    pallas_call x7, Pallas kernels, call(): pl.pallas_call(body, out_shape=[jax.ShapeDtypeStruct(s, d) for s, d in ou...  24.7 us
    unnamed x114, local copies, waits for them, and re-layouts  18.7 us
    ppermute x3, starting transfers between devices, shards(): lax.ppermute(end, 'state', [(i, i + k) for i in range(parts - k)])  7.34 us
    reshape x4, local copies, waits for them, and re-layouts, to_rows(): x.reshape(segs, steps, group, feats).transpose(1, 0, 2, 3)  6.79 us
    transpose x2, local copies, waits for them, and re-layouts, from_rows(): y.reshape(steps, segs, group, feats).transpose(1, 0, 2, 3)  6.64 us
    reshape x2, local copies, waits for them, and re-layouts, from_rows(): y.reshape(steps, segs, group, feats).transpose(1, 0, 2, 3)  4.61 us
  transfers between devices with their start and end apart: 39, of which 17 were waited for; matrix products, arithmetic and copies ran while one was open for 16% of the time, Pallas kernels for 3%

commit v1 on v0

v1 whole, which is shorter than its diff:
```python
import functools

import jax
import jax.numpy as jnp
from jax import lax
from jax.experimental import pallas as pl
from jax.experimental.pallas import tpu as pltpu
from jax.sharding import PartitionSpec as P

F32, BF16 = jnp.float32, jnp.bfloat16
EPSILON = 1e-05
SUB = 8
CHUNK = 256
PARAM_ROWS = 16
GELU_A = 0.7978845608028654
GELU_B = 0.044715
MIB = 1 << 20


def cmul(ar, ai, br, bi):
    return ar * br - ai * bi, ar * bi + ai * br


def nn(a, b):
    return lax.dot_general(a, b, (((1,), (0,)), ((), ())), preferred_element_type=F32)


def nt(a, b):
    return lax.dot_general(a, b, (((1,), (1,)), ((), ())), preferred_element_type=F32)


def tn(a, b):
    return lax.dot_general(a, b, (((0,), (0,)), ((), ())), preferred_element_type=F32)


def rows_in(ref, first, count):
    segs, _, group, feats = ref.shape
    x = ref[:, pl.ds(first, count)].astype(F32)
    return x.transpose(1, 0, 2, 3).reshape(count * segs * group, feats)


def rows_out(y, ref, first, count):
    segs, _, group, feats = ref.shape
    return y.reshape(count, segs, group, feats).transpose(1, 0, 2, 3)


def row_mask(base, rows, group, steps, me, lens_ref):
    segs = SUB // group
    row = lax.broadcasted_iota(jnp.int32, (rows, 128), 0) + base
    place = row & (SUB - 1)
    seq = place & (group - 1)
    position = me * (segs * steps) + (place // group) * steps + (row // SUB)
    length = jnp.full((rows, 128), lens_ref[0], jnp.int32)
    for k in range(1, group):
        length = jnp.where(seq == k, lens_ref[k], length)
    return (position < length).astype(F32)


def wide(column, lanes):
    return jnp.concatenate([column] * (lanes // column.shape[1]), axis=1)


def call(body, outs, ins, scratch, limit_mib, flops, name, small=()):
    specs = []
    for k, x in enumerate(ins):
        if x.dtype == jnp.int32:
            specs.append(pl.BlockSpec(memory_space=pltpu.SMEM))
        elif k in small:
            specs.append(pl.BlockSpec(x.shape, lambda *_, n=x.ndim: (0,) * n))
        else:
            specs.append(pl.BlockSpec(memory_space=pltpu.VMEM))
    return pl.pallas_call(
        body,
        out_shape=[jax.ShapeDtypeStruct(s, d) for s, d in outs],
        in_specs=specs,
        out_specs=[pl.BlockSpec(memory_space=pltpu.VMEM)] * len(outs),
        scratch_shapes=scratch,
        compiler_params=pltpu.CompilerParams(vmem_limit_bytes=limit_mib * MIB),
        cost_estimate=pl.CostEstimate(flops=flops, bytes_accessed=4 * MIB, transcendentals=0),
        name=name,
    )(*ins)


def split_pairs(pairs_ref, flat_ref):
    own, _, feats = pairs_ref.shape
    flat = pairs_ref[...].astype(F32).reshape(2 * own, feats)
    for c in range(feats // 128):
        flat_ref[c] = flat[:, c * 128 : (c + 1) * 128]
    take = lambda k: [flat_ref[c, pl.ds(k, own, stride=2), :] for c in range(feats // 128)]
    return [jnp.concatenate(take(k), axis=1).astype(BF16) for k in range(2)]


def three_parts(x):
    high = x.astype(BF16)
    rest = x - high.astype(F32)
    mid = rest.astype(BF16)
    return [high, mid, (rest - mid.astype(F32)).astype(BF16)]


def prep_kernel(weight_ref, rate_ref, angle_ref, level_ref, gain_ref, bias_ref, skip_ref, pay_ref, vec_ref, flat_ref):
    own, _, feats = weight_ref.shape
    for k, rows in enumerate(split_pairs(weight_ref, flat_ref)):
        pay_ref[k * own : (k + 1) * own, :] = rows
    me = lax.axis_index("state")
    lane = lax.broadcasted_iota(jnp.int32, (1, feats), 1)
    mine = (lane // own) == me
    over = lambda ref: jnp.concatenate([ref[...]] * (feats // own), axis=1)
    size = jnp.exp(-jnp.exp(over(rate_ref)))
    angle = jnp.exp(over(angle_ref))
    parts = []
    for v in (size * jnp.cos(angle), size * jnp.sin(angle), jnp.exp(over(level_ref))):
        parts += three_parts(jnp.where(mine, v, 0.0))
    parts += [jnp.zeros((PARAM_ROWS - len(parts), feats), BF16)]
    pay_ref[2 * own :, :] = jnp.concatenate([p.astype(F32) for p in parts], axis=0).astype(BF16)
    vec_ref[0:1, :] = gain_ref[...]
    vec_ref[1:2, :] = bias_ref[...]
    vec_ref[2:3, :] = skip_ref[...]


def norm_kernel(x_ref, cot_ref, weight_ref, vec_ref, lens_ref, low_ref, unit_ref, inv_ref, mask_ref, rows_ref, pay_ref, flat_ref):
    segs, steps, group, feats = x_ref.shape
    rows = steps * SUB
    own = weight_ref.shape[0]
    me = lax.axis_index("state")
    size = 128
    gain, bias = vec_ref[0:1, :], vec_ref[1:2, :]

    def chunk(c, carry):
        base = pl.multiple_of(c * size, size)
        at = pl.ds(base, size)
        first = pl.multiple_of(c * (size // SUB), size // SUB)
        x = rows_in(x_ref, first, size // SUB)
        centred = x - jnp.mean(x, axis=1, keepdims=True)
        inv = lax.rsqrt(jnp.mean(centred * centred, axis=1, keepdims=True) + EPSILON)
        unit = centred * inv
        unit_ref[at, :] = unit
        low_ref[at, :] = (unit * gain + bias).astype(BF16)
        inv_ref[at, :] = jnp.broadcast_to(inv, (size, 128))
        mask_ref[at, :] = row_mask(base, size, group, steps, me, lens_ref)
        rows_ref[at, :] = rows_in(cot_ref, first, size // SUB).astype(BF16)
        return carry

    lax.fori_loop(0, rows // size, chunk, 0)
    for k, part in enumerate(split_pairs(weight_ref, flat_ref)):
        pay_ref[k * own : (k + 1) * own, :] = part


def gather_rows(me, blocks, own, channels, dst_ref):
    for m, block in enumerate(blocks):
        off = pl.multiple_of((me ^ m) * own, own)
        dst_ref[pl.ds(off, own), :] = block[0:own, :]
        dst_ref[pl.ds(pl.multiple_of(channels + off, own), own), :] = block[own : 2 * own, :]


def seg_of(group):
    row = lax.broadcasted_iota(jnp.int32, (SUB, 128), 0)
    return row // group


def shift_rows(x, by, keep):
    return jnp.where(wide(keep, x.shape[1]), pltpu.roll(x, by % SUB, 0), 0.0)


def seg_prefix(xr, xi, qr, qi, group, forward):
    seg = seg_of(group)
    segs = SUB // group
    dist = 1
    while dist < segs:
        by = group * dist if forward else SUB - group * dist
        keep = seg >= dist if forward else seg < segs - dist
        sr, si = shift_rows(xr, by, keep), shift_rows(xi, by, keep)
        ar, ai = cmul(qr, qi, sr, si)
        xr, xi = xr + ar, xi + ai
        qr, qi = cmul(qr, qi, qr, qi)
        dist *= 2
    return xr, xi


def seg_enter(xr, xi, qr, qi, dr, di, group, forward):
    seg = seg_of(group)
    segs = SUB // group
    by = group if forward else SUB - group
    keep = seg >= 1 if forward else seg < segs - 1
    er, ei = shift_rows(xr, by, keep), shift_rows(xi, by, keep)
    gap = seg if forward else segs - 1 - seg
    pr, pi = jnp.ones_like(er), jnp.zeros_like(ei)
    bit = 1
    while bit < segs:
        nr, ni = cmul(pr, pi, qr, qi)
        take = wide((gap & bit) != 0, er.shape[1])
        pr, pi = jnp.where(take, nr, pr), jnp.where(take, ni, pi)
        qr, qi = cmul(qr, qi, qr, qi)
        bit *= 2
    ar, ai = cmul(pr, pi, dr, di)
    return er + ar, ei + ai


def device_entry(ends_ref, me, channels, qr, qi, group, forward):
    seg = seg_of(group)
    segs = SUB // group
    parts = ends_ref.shape[0]
    keep = wide(seg == (segs - 1 if forward else 0), channels)
    tr = ti = jnp.zeros((SUB, channels), F32)
    for device in range(parts - 1) if forward else range(parts - 1, 0, -1):
        end = ends_ref[me ^ device]
        nr, ni = cmul(tr, ti, qr, qi)
        counts = device < me if forward else device > me
        tr = jnp.where(counts, nr + end[:, :channels], tr)
        ti = jnp.where(counts, ni + end[:, channels:], ti)
    out = []
    for x in (tr, ti):
        x = jnp.where(keep, x, 0.0)
        y = x
        for k in range(1, segs):
            y = y + pltpu.roll(x, group * k, 0)
        out.append(y)
    return out


def project_kernel(parts, own, group, low_ref, mask_ref, *refs):
    blocks = refs[:parts]
    drive_ref, end_ref, win_ref, cst_ref = refs[parts:]
    rows = low_ref.shape[0]
    channels = own * parts
    steps = rows // SUB
    me = lax.axis_index("state")
    gather_rows(me, blocks, own, channels, win_ref)
    rows_of = []
    for k in range(3):
        total = None
        for block in blocks:
            tile = block[2 * own : 2 * own + PARAM_ROWS, :].astype(F32)
            for part in range(3):
                piece = tile[3 * k + part : 3 * k + part + 1, :channels]
                total = piece if total is None else total + piece
        rows_of.append(total)
    pr, pi, gain = rows_of
    powers = [(pr, pi)]
    span = steps * (SUB // group)
    ar, ai = pr, pi
    count = 1
    while count < span:
        ar, ai = cmul(ar, ai, ar, ai)
        count *= 2
        if count in (steps, span):
            powers.append((ar, ai))
    while len(powers) < 3:
        powers.append(powers[-1])
    for k, (r, i) in enumerate(powers):
        cst_ref[k : k + 1, :] = jnp.concatenate([r, i], axis=1)
    gains = jnp.concatenate([gain, gain], axis=1)
    cst_ref[3:4, :] = gains
    cst_ref[4:8, :] = jnp.zeros((4, 2 * channels), F32)

    def chunk(c, carry):
        base = pl.multiple_of(c * CHUNK, CHUNK)
        at = pl.ds(base, CHUNK)
        mask = mask_ref[at, :]
        drive_ref[at, :] = nt(low_ref[at, :], win_ref[...]) * (gains * wide(mask, 2 * channels))
        return carry

    lax.fori_loop(0, rows // CHUNK, chunk, 0)
    br = jnp.broadcast_to(pr, (SUB, channels))
    bi = jnp.broadcast_to(pi, (SUB, channels))

    def step(j, h):
        u = drive_ref[pl.ds(pl.multiple_of(j * SUB, SUB), SUB), :]
        nr, ni = cmul(br, bi, h[0], h[1])
        return nr + u[:, :channels], ni + u[:, channels:]

    zero = jnp.zeros((SUB, channels), F32)
    er, ei = lax.fori_loop(0, steps, step, (zero, zero), unroll=8)
    er, ei = seg_prefix(er, ei, *powers[1], group, True)
    end_ref[...] = jnp.concatenate([er, ei], axis=1)


def mix_kernel(parts, own, group, orders, *refs):
    it = iter(refs)
    take = lambda n: [next(it) for _ in range(n)]
    drive_ref, end_ref, cst_ref, ends_ref = take(4)
    blocks = take(parts)
    unit_ref, cot_ref, mask_ref, vec_ref, glu_ref = take(5)
    states_ref, slow_ref, cw_ref, branch_ref, dglu_ref, gp_ref = take(6)
    grads = take(len(orders))
    act_ref, acc_ref = take(2)
    rows, feats = unit_ref.shape
    channels = own * parts
    steps = rows // SUB
    me = lax.axis_index("state")
    place = me + parts * (lax.axis_index("seq") & 1)
    gather_rows(me, blocks, own, channels, cw_ref)
    gain, bias, skip = (vec_ref[k : k + 1, :] for k in range(3))
    pr, pi = cst_ref[0:1, :channels], cst_ref[0:1, channels:]
    qr, qi = cst_ref[1:2, :channels], cst_ref[1:2, channels:]
    wr, wi = cst_ref[2:3, :channels], cst_ref[2:3, channels:]
    dr, di = device_entry(ends_ref, me, channels, wr, wi, group, True)
    hr, hi = seg_enter(end_ref[:, :channels], end_ref[:, channels:], qr, qi, dr, di, group, True)
    states_ref[0:SUB, :] = jnp.concatenate([hr, hi], axis=1)
    br = jnp.broadcast_to(pr, (SUB, channels))
    bi = jnp.broadcast_to(pi, (SUB, channels))

    def step(j, h):
        base = pl.multiple_of(j * SUB, SUB)
        u = drive_ref[pl.ds(base, SUB), :]
        nr, ni = cmul(br, bi, h[0], h[1])
        nr, ni = nr + u[:, :channels], ni + u[:, channels:]
        at = pl.ds(pl.multiple_of(base + SUB, SUB), SUB)
        states_ref[at, :channels] = nr
        states_ref[at, channels:] = ni
        return nr, ni

    lax.fori_loop(0, steps, step, (hr, hi), unroll=8)

    def chunk(c, carry):
        base = pl.multiple_of(c * CHUNK, CHUNK)
        at = pl.ds(base, CHUNK)
        states = states_ref[pl.ds(pl.multiple_of(base + SUB, SUB), CHUNK), :]
        slow = jnp.concatenate([states[:, :channels], -states[:, channels:]], axis=1).astype(BF16)
        slow_ref[at, :] = slow
        normed = unit_ref[at, :] * gain + bias
        v = nn(slow, cw_ref[...]) + skip * normed
        t = jnp.tanh(GELU_A * (v + GELU_B * (v * v * v)))
        half = 0.5 * (1.0 + t)
        gp_ref[at, :] = half + (0.5 * GELU_A) * v * (1.0 - t * t) * (1.0 + (3.0 * GELU_B) * (v * v))
        act = (v * half).astype(BF16)
        act_ref[at, :] = act
        glu = nn(act, glu_ref[...])
        mask = wide(mask_ref[at, :], feats)
        value = glu[:, :feats]
        gate = jax.nn.sigmoid(glu[:, feats:])
        branch = mask * gate
        branch_ref[at, :] = branch * value
        d_value = branch * cot_ref[at, :].astype(F32)
        dglu_ref[at, :feats] = d_value.astype(BF16)
        dglu_ref[at, feats:] = (d_value * value * (1.0 - gate)).astype(BF16)
        return carry

    lax.fori_loop(0, rows // CHUNK, chunk, 0)
    width = 256

    def tile(c, carry):
        at = pl.ds(pl.multiple_of(c * width, width), width)
        acc_ref[:, at] = tn(act_ref[...], dglu_ref[:, at])
        return carry

    lax.fori_loop(0, 2 * feats // width, tile, 0)
    spread(acc_ref, place, orders, grads)


def spread(acc_ref, place, orders, grads):
    for order, ref in zip(orders, grads):
        _, size, _ = ref.shape
        for k, m in enumerate(order):
            at = pl.ds(pl.multiple_of((place ^ m) * size, size), size)
            ref[k] = acc_ref[at, :].astype(ref.dtype)


def spread_pairs(acc_ref, place, own, channels, orders, grads):
    for order, ref in zip(orders, grads):
        for k, m in enumerate(order):
            off = pl.multiple_of((place ^ m) * own, own)
            ref[k, 0:own] = acc_ref[pl.ds(off, own), :].astype(ref.dtype)
            also = pl.ds(pl.multiple_of(channels + off, own), own)
            ref[k, own : 2 * own] = acc_ref[also, :].astype(ref.dtype)


def back_kernel(own, group, orders, *refs):
    it = iter(refs)
    take = lambda n: [next(it) for _ in range(n)]
    dglu_ref, gp_ref, unit_ref, vec_ref, glu_ref, cw_ref, slow_ref, cst_ref = take(8)
    dpre_ref, dst_ref, start_ref, skip_ref = take(4)
    grads = take(len(orders))
    dmix_ref, acc_ref = take(2)
    rows, feats = gp_ref.shape
    channels = cw_ref.shape[0] // 2
    steps = rows // SUB
    me = lax.axis_index("state")
    gain, bias = vec_ref[0:1, :], vec_ref[1:2, :]

    def chunk(c, total):
        at = pl.ds(pl.multiple_of(c * CHUNK, CHUNK), CHUNK)
        d_pre = nt(dglu_ref[at, :], glu_ref[...]) * gp_ref[at, :]
        dpre_ref[at, :] = d_pre
        normed = unit_ref[at, :] * gain + bias
        total = total + jnp.sum((d_pre * normed).reshape(CHUNK // SUB, SUB, feats), axis=0)
        d_mixed = d_pre.astype(BF16)
        dmix_ref[at, :] = d_mixed
        dst_ref[at, :] = nt(d_mixed, cw_ref[...])
        return total

    total = lax.fori_loop(0, rows // CHUNK, chunk, jnp.zeros((SUB, feats), F32))
    skip_ref[...] = total
    pr, pi = cst_ref[0:1, :channels], cst_ref[0:1, channels:]
    br = jnp.broadcast_to(pr, (SUB, channels))
    bi = jnp.broadcast_to(-pi, (SUB, channels))

    def step(k, a):
        base = pl.multiple_of((steps - 1 - k) * SUB, SUB)
        u = dst_ref[pl.ds(base, SUB), :]
        nr, ni = cmul(br, bi, a[0], a[1])
        return nr + u[:, :channels], ni - u[:, channels:]

    zero = jnp.zeros((SUB, channels), F32)
    ar, ai = lax.fori_loop(0, steps, step, (zero, zero), unroll=8)
    qr, qi = cst_ref[1:2, :channels], -cst_ref[1:2, channels:]
    ar, ai = seg_prefix(ar, ai, qr, qi, group, False)
    start_ref[...] = jnp.concatenate([ar, ai], axis=1)
    width = 256

    def tile(c, carry):
        at = pl.ds(pl.multiple_of(c * width, width), width)
        acc_ref[:, at] = tn(slow_ref[...], dmix_ref[:, at])
        return carry

    lax.fori_loop(0, feats // width, tile, 0)
    spread_pairs(acc_ref, me, own, channels, orders, grads)


def adjoint_kernel(own, group, orders, *refs):
    it = iter(refs)
    take = lambda n: [next(it) for _ in range(n)]
    dst_ref, start_ref, cst_ref, ends_ref = take(4)
    states_ref, drive_ref, low_ref, mask_ref = take(4)
    dproj_ref, sums_ref = take(2)
    grads = take(len(orders))
    adj_ref, acc_ref = take(2)
    rows = dst_ref.shape[0]
    channels = dst_ref.shape[1] // 2
    steps = rows // SUB
    me = lax.axis_index("state")
    pr, pi = cst_ref[0:1, :channels], -cst_ref[0:1, channels:]
    qr, qi = cst_ref[1:2, :channels], -cst_ref[1:2, channels:]
    wr, wi = cst_ref[2:3, :channels], -cst_ref[2:3, channels:]
    dr, di = device_entry(ends_ref, me, channels, wr, wi, group, False)
    ar, ai = seg_enter(start_ref[:, :channels], start_ref[:, channels:], qr, qi, dr, di, group, False)
    br = jnp.broadcast_to(pr, (SUB, channels))
    bi = jnp.broadcast_to(pi, (SUB, channels))

    def step(k, carry):
        ar, ai, sr, si, sg = carry
        base = pl.multiple_of((steps - 1 - k) * SUB, SUB)
        at = pl.ds(base, SUB)
        d = dst_ref[at, :]
        nr, ni = cmul(br, bi, ar, ai)
        ar, ai = nr + d[:, :channels], ni - d[:, channels:]
        adj_ref[at, :channels] = ar
        adj_ref[at, channels:] = ai
        h = states_ref[at, :]
        hr, hi = h[:, :channels], h[:, channels:]
        u = drive_ref[at, :]
        sr = sr + (ar * hr + ai * hi)
        si = si + (ai * hr - ar * hi)
        sg = sg + (ar * u[:, :channels] + ai * u[:, channels:])
        return ar, ai, sr, si, sg

    zero = jnp.zeros((SUB, channels), F32)
    out = lax.fori_loop(0, steps, step, (ar, ai, zero, zero, zero), unroll=4)
    sums_ref[:, :channels] = out[2]
    sums_ref[:, channels : 2 * channels] = out[3]
    sums_ref[:, 2 * channels : 3 * channels] = out[4]
    gains = cst_ref[3:4, :]

    def chunk(c, carry):
        base = pl.multiple_of(c * CHUNK, CHUNK)
        at = pl.ds(base, CHUNK)
        mask = mask_ref[at, :]
        dproj_ref[at, :] = (adj_ref[at, :] * (gains * wide(mask, 2 * channels))).astype(BF16)
        return carry

    lax.fori_loop(0, rows // CHUNK, chunk, 0)
    width = 256
    feats = low_ref.shape[1]

    def tile(c, carry):
        at = pl.ds(pl.multiple_of(c * width, width), width)
        acc_ref[:, at] = tn(dproj_ref[...], low_ref[:, at])
        return carry

    lax.fori_loop(0, feats // width, tile, 0)
    spread_pairs(acc_ref, me, own, channels, orders, grads)


def out_kernel(branch_ref, x_ref, out_ref):
    segs, steps, _, _ = x_ref.shape
    size = 16

    def chunk(c, carry):
        first = pl.multiple_of(c * size, size)
        rows = branch_ref[pl.ds(pl.multiple_of(first * SUB, size * SUB), size * SUB), :]
        at = pl.ds(first, size)
        out_ref[:, at] = (x_ref[:, at].astype(F32) + rows_out(rows, x_ref, first, size)).astype(BF16)
        return carry

    lax.fori_loop(0, steps // size, chunk, 0)


def tokens_kernel(dproj_ref, win_ref, dpre_ref, unit_ref, inv_ref, vec_ref, cot_ref, out_ref, sums_ref):
    rows, feats = dpre_ref.shape
    gain, skip = vec_ref[0:1, :], vec_ref[2:3, :]
    size = 128
    steps = size // SUB

    def chunk(c, carry):
        total_gain, total_bias = carry
        at = pl.ds(pl.multiple_of(c * size, size), size)
        d_normed = dpre_ref[at, :] * skip + nn(dproj_ref[at, :], win_ref[...])
        unit = unit_ref[at, :]
        total_gain = total_gain + jnp.sum((d_normed * unit).reshape(steps, SUB, feats), axis=0)
        total_bias = total_bias + jnp.sum(d_normed.reshape(steps, SUB, feats), axis=0)
        d_unit = d_normed * gain
        first = jnp.mean(d_unit, axis=1, keepdims=True)
        second = jnp.mean(d_unit * unit, axis=1, keepdims=True)
        inv = wide(inv_ref[at, :], feats)
        rows = inv * (d_unit - first - unit * second)
        place = pl.multiple_of(c * steps, steps)
        step_at = pl.ds(place, steps)
        out_ref[:, step_at] = cot_ref[:, step_at].astype(F32) + rows_out(rows, cot_ref, place, steps)
        return total_gain, total_bias

    zero = jnp.zeros((SUB, feats), F32)
    total_gain, total_bias = lax.fori_loop(0, rows // size, chunk, (zero, zero))
    sums_ref[:, :feats] = total_gain
    sums_ref[:, feats:] = total_bias


def place_kernel(masks, parts, *refs):
    arrays, out_ref = refs[:-1], refs[-1]
    place = lax.axis_index("state") + parts * (lax.axis_index("seq") & 1)
    size = arrays[0].shape[1]
    for ms, ref in zip(masks, arrays):
        for k, m in enumerate(ms):
            at = pl.ds(pl.multiple_of((place ^ m) * size, size), size)
            out_ref[at, :] = ref[k].astype(F32)


def exchange(x, mask):
    count = lax.axis_size("seq") * lax.axis_size("state")
    return lax.ppermute(x, ("seq", "state"), [(i, i ^ mask) for i in range(count)])


def tie(x, *after):
    return lax.optimization_barrier((x, after))[0]


def bits_of(n):
    return [1 << k for k in range(n.bit_length() - 1)]


def submasks(group):
    out = [0]
    for bit in group:
        out += [m | bit for m in out]
    return out[1:]


def stage_orders(groups):
    kept = [0]
    stages = []
    for group in reversed(groups):
        sends = [[m ^ p for m in kept] for p in submasks(group)]
        stages.insert(0, sends)
        kept = sum(sends, []) + kept
    return [o for sends in stages for o in sends] + [[0]]


def halve(parts, group):
    masks = submasks(group)
    got = [exchange(p.astype(BF16), m) for p, m in zip(parts, masks)]
    rest, off = [], 0
    for p in parts[len(masks) :]:
        n = p.shape[0]
        total = p.astype(F32)
        for g in got:
            total = total + g[off : off + n].astype(F32)
        rest.append(total)
        off += n
    return rest


def double(x, mask):
    low = lax.reduce_precision(x, 8, 7).astype(BF16)
    return low.astype(F32) + exchange(low, mask).astype(F32)


def double_f32(x, mask):
    return x + exchange(x, mask)


def gather_ends(end, bits):
    g = end[None]
    for bit in reversed(bits):
        g = jnp.stack([g, exchange(g, bit)], axis=1).reshape((2 * g.shape[0],) + end.shape)
    return g


def gather_blocks(own, bits):
    blocks = {0: own}
    for bit in reversed(bits):
        for m in list(blocks):
            blocks[m ^ bit] = exchange(blocks[m], bit)
    return [blocks[m] for m in range(len(blocks))]


def shards(
    tokens,
    norm_gain,
    norm_bias,
    input_weight,
    output_weight,
    log_rate,
    log_angle,
    log_gain,
    skip_gain,
    glu_weight,
    lengths,
    cotangent,
):
    span, group, feats = tokens.shape
    own = log_rate.shape[0]
    parts = lax.axis_size("state")
    n_seq = lax.axis_size("seq")
    channels = own * parts
    rows = span * group
    segs = SUB // group
    me = lax.axis_index("state")
    state_bits = bits_of(parts)
    seq_masks = [parts * b for b in bits_of(n_seq)]
    if len(seq_masks) > 2:
        seq_masks[-1] |= seq_masks[-2]
    full = rows * feats * 2 * channels * 2

    as_row = lambda v: v.reshape(1, -1)
    x4 = tokens.reshape(segs, span // segs, group, feats)
    cot4 = cotangent.reshape(segs, span // segs, group, feats)
    b_own, vec = call(
        prep_kernel,
        [((2 * own + PARAM_ROWS, feats), BF16), ((SUB, feats), F32)],
        [input_weight.transpose(1, 2, 0)]
        + [as_row(v) for v in (log_rate, log_angle, log_gain, norm_gain, norm_bias, skip_gain)],
        [pltpu.VMEM((feats // 128, 2 * own, 128), F32)],
        8,
        MIB,
        "prep",
        small=range(7),
    )
    b_blocks = gather_blocks(b_own, state_bits)
    low, unit, inv, mask, cot, c_own = call(
        norm_kernel,
        [
            ((rows, feats), BF16),
            ((rows, feats), F32),
            ((rows, 128), F32),
            ((rows, 128), F32),
            ((rows, feats), BF16),
            ((2 * own, feats), BF16),
        ],
        [x4, cot4, output_weight, vec, lengths],
        [pltpu.VMEM((feats // 128, 2 * own, 128), F32)],
        8,
        rows * feats * 20,
        "norm",
        small=(2,),
    )
    c_blocks = gather_blocks(c_own, state_bits)
    drive, end, win, cst = call(
        functools.partial(project_kernel, parts, own, group),
        [
            ((rows, 2 * channels), F32),
            ((SUB, 2 * channels), F32),
            ((2 * channels, feats), BF16),
            ((SUB, 2 * channels), F32),
        ],
        [low, mask] + b_blocks,
        [],
        12,
        full,
        "project",
    )
    ends = gather_ends(end, state_bits)
    glu_bits = state_bits + [parts]
    glu_groups = [glu_bits[:1]] + [glu_bits[k : k + 2] for k in range(1, len(glu_bits), 2)]
    glu_orders = stage_orders(glu_groups)
    glu_rows = feats // (2 * parts)
    glu_outs = [
        ((len(o), glu_rows, 2 * feats), BF16 if k == 0 else F32) for k, o in enumerate(glu_orders)
    ]
    states, slow, cw, branch, d_glu, slope, *glu_parts = call(
        functools.partial(mix_kernel, parts, own, group, glu_orders),
        [
            ((rows + SUB, 2 * channels), F32),
            ((rows, 2 * channels), BF16),
            ((2 * channels, feats), BF16),
            ((rows, feats), F32),
            ((rows, 2 * feats), BF16),
            ((rows, feats), F32),
        ]
        + glu_outs,
        [drive, end, cst, ends] + c_blocks + [unit, cot, mask, vec, glu_weight],
        [pltpu.VMEM((rows, feats), BF16), pltpu.VMEM((feats, 2 * feats), F32)],
        20,
        5 * full,
        "mix",
    )
    glu_parts = halve(glu_parts, glu_groups[0])
    state_groups = [[b] for b in state_bits]
    pair_orders = stage_orders(state_groups)
    pair_outs = [
        ((len(o), 2 * own, feats), BF16 if k == 0 else F32) for k, o in enumerate(pair_orders)
    ]
    d_pre, d_states, start, skip_sum, *out_parts = call(
        functools.partial(back_kernel, own, group, pair_orders),
        [
            ((rows, feats), F32),
            ((rows, 2 * channels), F32),
            ((SUB, 2 * channels), F32),
            ((SUB, feats), F32),
        ]
        + pair_outs,
        [d_glu, slope, unit, vec, glu_weight, cw, slow, cst],
        [pltpu.VMEM((rows, feats), BF16), pltpu.VMEM((2 * channels, feats), F32)],
        16,
        4 * full,
        "back",
    )
    starts = gather_ends(tie(start, glu_parts), state_bits)
    for g in glu_groups[1:]:
        glu_parts = halve(glu_parts, g)
    glu_own = glu_parts[0][0]
    out_parts = halve(out_parts, state_groups[0])
    (out4,) = call(
        out_kernel,
        [(x4.shape, BF16)],
        [tie(branch, start), x4],
        [],
        8,
        MIB,
        "out",
    )
    d_proj, channel_sums, *in_parts = call(
        functools.partial(adjoint_kernel, own, group, pair_orders),
        [((rows, 2 * channels), BF16), ((SUB, 3 * channels), F32)] + pair_outs,
        [tie(d_states, out4, out_parts), start, cst, starts, states, drive, low, mask],
        [pltpu.VMEM((rows, 2 * channels), F32), pltpu.VMEM((2 * channels, feats), F32)],
        16,
        2 * full,
        "adjoint",
    )
    in_parts = halve(in_parts, state_groups[0])
    d_proj = tie(d_proj, glu_own, in_parts)
    grad4, feature_sums = call(
        tokens_kernel,
        [(cot4.shape, F32), ((SUB, 2 * feats), F32)],
        [d_proj, win, d_pre, unit, inv, vec, cot4],
        [],
        12,
        full,
        "tokens",
    )
    sums = jnp.concatenate([channel_sums, feature_sums, skip_sum], axis=1)
    sums = jnp.sum(sums, axis=0, keepdims=True)
    for g in state_groups[1:]:
        out_parts = halve(out_parts, g)
        in_parts = halve(in_parts, g)
    grad_out, grad_in = out_parts[0][0], in_parts[0][0]
    for m in state_bits:
        sums = double_f32(sums, m)
    for m in seq_masks:
        grad_out = double(grad_out, m)
        grad_in = double(grad_in, m)
        sums = double_f32(sums, m)
    sums = sums[0]

    for m in seq_masks[1:]:
        glu_own = double(glu_own, m)
    held = {0: lax.reduce_precision(glu_own, 8, 7).astype(BF16)}
    for g in reversed(glu_groups[1:]):
        for m in list(held):
            for p in submasks(g):
                held[m ^ p] = exchange(held[m], p)
    rest = [m for m in held if m]
    arrays = [held[0][None], jnp.stack([held[m] for m in rest])]
    masks = [[0], rest]
    for p in submasks(glu_groups[0]):
        arrays += [exchange(a, p) for a in arrays[:2]]
        masks += [[m ^ p for m in ms] for ms in masks[:2]]
    (grad_glu,) = call(
        functools.partial(place_kernel, masks, parts),
        [((feats, 2 * feats), F32)],
        arrays,
        [],
        8,
        feats * feats,
        "place",
    )
    sum_re, sum_im, gain_sum = (
        lax.dynamic_slice(sums, (k * channels + me * own,), (own,)) for k in range(3)
    )
    base = 3 * channels
    grad_gain, grad_bias, grad_skip = (
        sums[base + k * feats : base + (k + 1) * feats] for k in range(3)
    )
    decay = jnp.exp(log_rate)
    angle = jnp.exp(log_angle)
    pole_re = jnp.exp(-decay) * jnp.cos(angle)
    pole_im = jnp.exp(-decay) * jnp.sin(angle)
    grad_rate = -decay * (sum_re * pole_re + sum_im * pole_im)
    grad_angle = angle * (sum_im * pole_re - sum_re * pole_im)
    return (
        out4.reshape(tokens.shape),
        grad4.reshape(tokens.shape),
        grad_gain,
        grad_bias,
        grad_in.reshape(2, own, feats).transpose(2, 1, 0),
        grad_out.reshape(2, own, feats).transpose(1, 0, 2),
        grad_rate,
        grad_angle,
        gain_sum,
        grad_skip,
        grad_glu,
    )


def solution(mesh):
    placed = (
        P("state", "seq", None),
        P(),
        P(),
        P(None, "state", None),
        P("state", None, None),
        P("state"),
        P("state"),
        P("state"),
        P(),
        P(),
        P("seq"),
        P("state", "seq", None),
    )
    return jax.shard_map(
        shards,
        mesh=mesh,
        in_specs=placed,
        out_specs=(
            P("state", "seq", None),
            P("state", "seq", None),
            P(),
            P(),
            P(None, "state", None),
            P("state", None, None),
            P("state"),
            P("state"),
            P("state"),
            P(),
            P(),
        ),
        check_vma=False,
    )
```

time: 159 us -> 123 us (0.77)
  local copies, waits for them, and re-layouts: 41.7 us -> 20.1 us
  waiting for transfers between devices: 45.7 us -> 32.2 us
  starting transfers between devices: 39.3 us -> 36.1 us
  Pallas kernels: 24.7 us -> 27.8 us
    ppermute x39 -> x36, waiting for transfers between devices: 45.7 us -> 32.2 us  [exchange(): lax.ppermute(x, ('seq', 'state'), [(i, i ^ mask) for i in range(count)])]
    reshape x6 -> x0, local copies, waits for them, and re-layouts: 11.4 us -> none  [the longest x4 6.79 us: to_rows(): x.reshape(segs, steps, group, feats).transpose(1, 0, 2, 3)]
    transpose x4 -> x0, local copies, waits for them, and re-layouts: 8.48 us -> none  [the longest x2 6.64 us: from_rows(): y.reshape(steps, segs, group, feats).transpose(1, 0, 2, 3)]
    ppermute x39 -> x36, starting transfers between devices: 39.3 us -> 36.1 us  [exchange(): lax.ppermute(x, ('seq', 'state'), [(i, i ^ mask) for i in range(count)])]
    pallas_call x7 -> x9, Pallas kernels: 24.7 us -> 27.8 us  [call(): pl.pallas_call(body, out_shape=[jax.ShapeDtypeStruct(s, d) for s, d in ou...]
    convert_element_type x8, other arithmetic: 1.24 us -> 3.45 us  [double(): low = lax.reduce_precision(x, 8, 7).astype(BF16)]
    convert_element_type x5 -> x1, other arithmetic: 2.05 us -> 0.03 us  [shards(): held = {0: lax.reduce_precision(glu_own, 8, 7).astype(BF16)}]
    unnamed x114 -> x52, local copies, waits for them, and re-layouts: 18.7 us -> 17.1 us
  transfers between devices with their start and end apart: 39 -> 36, of which waited for: 17 -> 16; matrix products, arithmetic and copies ran while one was open for 16% -> 6% of each run, Pallas kernels for 3% -> 13%
where the time goes in v1:
time: 123 us
  starting transfers between devices  36.1 us (29%)
  waiting for transfers between devices  32.2 us (26%)
  Pallas kernels  27.8 us (23%)
  local copies, waits for them, and re-layouts  20.1 us (16%)
  other arithmetic  5.4 us (4%)
    ppermute x36, starting transfers between devices, exchange(): lax.ppermute(x, ('seq', 'state'), [(i, i ^ mask) for i in range(count)])  36.1 us
    ppermute x36, waiting for transfers between devices, exchange(): lax.ppermute(x, ('seq', 'state'), [(i, i ^ mask) for i in range(count)])  32.2 us
    pallas_call x9, Pallas kernels, call(): pl.pallas_call(body, out_shape=[jax.ShapeDtypeStruct(s, d) for s, d in ou...  27.8 us
    unnamed x52, local copies, waits for them, and re-layouts  17.1 us
    convert_element_type x8, other arithmetic, double(): low = lax.reduce_precision(x, 8, 7).astype(BF16)  3.45 us
  transfers between devices with their start and end apart: 36, of which 16 were waited for; matrix products, arithmetic and copies ran while one was open for 6% of the time, Pallas kernels for 13%

profile of v1, /device:TPU:0, one launch (start us, length us, event | category | flops | bytes accessed | tf_op | source)
XLA Modules:
  0.0 122.6 jit_solution(9304394386731337813)
XLA Ops:
  0.7 0.9 copy-done.15
  1.6 0.7 copy-done.16
  2.2 0.7 copy-done.17
  2.9 0.7 copy-done.18
  3.6 0.7 copy-done.19
  4.3 0.7 copy-done.21
  5.7 3.0 %collective-permute-start.1 = (bf16[144,512]{1,0:T(8,128)(2,1)S(1)}, bf16[144,512]{1,0:T(8,128)(2,1)S(1)}, u32[]{:S(2)}, u32[]{:S(2)}) collective-permute-start(bf16[144,512]{1,0:T(8,128)(2,1)S(1)} %get-tuple-element.55.refs_0_), channel_id=1, source_target_pairs={{0,2},{1,3},{2,0},{3,1},{4,6},{5,7},{6,4},{7,5},{8,10},{9,11},{10,... | collective-permute-start | bytes 442376 | tf_op jit(solution)/shard_map/ppermute | solution.py:538
  8.7 3.8 %collective-permute-done.1.refs_2_ = bf16[144,512]{1,0:T(8,128)(2,1)S(1)} collective-permute-done((bf16[144,512]{1,0:T(8,128)(2,1)S(1)}, bf16[144,512]{1,0:T(8,128)(2,1)S(1)}, u32[]{:S(2)}, u32[]{:S(2)}) %collective-permute-start.1) | collective-permute-done | bytes 147488 | tf_op jit(solution)/shard_map/ppermute | solution.py:538
  12.6 1.2 copy-done
  13.8 1.2 copy-done.2
  15.0 0.9 copy-done.14
  16.6 3.9 %norm.1 = (bf16[1024,512]{1,0:T(8,128)(2,1)S(1)}, f32[1024,512]{1,0:T(8,128)S(1)}, f32[1024,128]{1,0:T(8,128)S(1)}, f32[1024,128]{1,0:T(8,128)S(1)}, bf16[1024,5...) custom-call(bf16[4,128,2,512]{3,2,1,0:T(2,128)(2,1)S(1)} %bitcast.67, bf16[4,128,2,512]{3,2,1,0:T(2,128)(2,1)S(1)} %bitcast.65, ...), custom_call_target="tpu_custom_call" | custom-call | flops 10485760 | bytes 4194304 | tf_op jit(solution)/shard_map/norm/pallas_call | solution.py:72
  20.5 0.8 copy-done.9
  21.3 1.9 %project.1 = (f32[1024,512]{1,0:T(8,128)S(1)}, f32[8,512]{1,0:T(8,128)S(1)}, bf16[512,512]{1,0:T(8,128)(2,1)S(1)}, f32[8,512]{1,0:T(8,128)S(1)}) custom-call(bf16[1024,512]{1,0:T(8,128)(2,1)S(1)} %get-tuple-element.53.low_ref.refs_6_, f32[1024,128]{1,0:T(8,128)S(1)} %get-tuple-element.54.mask_ref.refs_10_.refs_7_, ...), custom_call_target="tpu_custom_call" | custom-call | flops 536870912 | bytes 4194304 | tf_op jit(solution)/shard_map/project/pallas_call | solution.py:72
  23.2 0.8 copy-done.11
  24.0 1.7 %collective-permute-start.3 = (f32[1,8,512]{2,1,0:T(8,128)S(1)}, f32[1,8,512]{2,1,0:T(8,128)S(1)}, u32[]{:S(2)}, u32[]{:S(2)}) collective-permute-start(f32[1,8,512]{2,1,0:T(8,128)S(1)} %bitcast.76), channel_id=1, source_target_pairs={{0,2},{1,3},{2,0},{3,1},{4,6},{5,7},{6,4},{7,5},{8,10},{9,11},{10,... | collective-permute-start | bytes 49160 | tf_op jit(solution)/shard_map/ppermute | solution.py:538
  26.1 1.7 %collective-permute-done.3 = f32[1,8,512]{2,1,0:T(8,128)S(1)} collective-permute-done((f32[1,8,512]{2,1,0:T(8,128)S(1)}, f32[1,8,512]{2,1,0:T(8,128)S(1)}, u32[]{:S(2)}, u32[]{:S(2)}) %collective-permute-start.3) | collective-permute-done | bytes 16416 | tf_op jit(solution)/shard_map/ppermute | solution.py:538
  28.3 3.1 %collective-permute-done.6.refs_6_ = bf16[128,512]{1,0:T(8,128)(2,1)S(1)} collective-permute-done((bf16[128,512]{1,0:T(8,128)(2,1)S(1)}, bf16[128,512]{1,0:T(8,128)(2,1)S(1)}, u32[]{:S(2)}, u32[]{:S(2)}) %collective-permute-start.6) | collective-permute-done | bytes 131104 | tf_op jit(solution)/shard_map/ppermute | solution.py:538
  31.4 1.3 %collective-permute-done.7.refs_7_ = bf16[128,512]{1,0:T(8,128)(2,1)S(1)} collective-permute-done((bf16[128,512]{1,0:T(8,128)(2,1)S(1)}, bf16[128,512]{1,0:T(8,128)(2,1)S(1)}, u32[]{:S(2)}, u32[]{:S(2)}) %collective-permute-start.7) | collective-permute-done | bytes 131104 | tf_op jit(solution)/shard_map/ppermute | solution.py:538
  32.8 6.9 %mix.1 = (f32[1032,512]{1,0:T(8,128)S(1)}, bf16[1024,512]{1,0:T(8,128)(2,1)S(1)}, bf16[512,512]{1,0:T(8,128)(2,1)S(1)}, f32[1024,512]{1,0:T(8,128)S(1)}, bf16[10...) custom-call(f32[1024,512]{1,0:T(8,128)S(1)} %get-tuple-element.56.re, ...), custom_call_target="tpu_custom_call" | custom-call | flops 2684354560 | bytes 4194304 | tf_op jit(solution)/shard_map/mix/pallas_call | solution.py:72
  39.8 4.3 %back.1 = (f32[1024,512]{1,0:T(8,128)S(1)}, f32[1024,512]{1,0:T(8,128)S(1)}, f32[8,512]{1,0:T(8,128)S(1)}, f32[8,512]{1,0:T(8,128)S(1)}, bf16[2,128,512]{2,1,0:T...) custom-call(bf16[1024,1024]{1,0:T(8,128)(2,1)S(1)} %get-tuple-element.63.refs_0_, ...), custom_call_target="tpu_custom_call" | custom-call | flops 2147483648 | bytes 4194304 | tf_op jit(solution)/shard_map/back/pallas_call | solution.py:72
  44.7 1.7 %collective-permute-start.14 = (bf16[1,64,1024]{2,1,0:T(8,128)(2,1)S(1)}, bf16[1,64,1024]{2,1,0:T(8,128)(2,1)S(1)}, u32[]{:S(2)}, u32[]{:S(2)}) collective-permute-start(bf16[1,64,1024]{2,1,0:T(8,128)(2,1)S(1)} %get-tuple-element.100), channel_id=1, source_target_pairs={{0,6},{1,7},{2,4},{3,5},{4,2},{5,3},{6,0},{7,1},{8,14},{9,15},{10,... | collective-permute-start | bytes 393224 | tf_op jit(solution)/shard_map/ppermute | solution.py:538
  46.9 1.4 %collective-permute-start.12 = (bf16[1,64,1024]{2,1,0:T(8,128)(2,1)S(1)}, bf16[1,64,1024]{2,1,0:T(8,128)(2,1)S(1)}, u32[]{:S(2)}, u32[]{:S(2)}) collective-permute-start(bf16[1,64,1024]{2,1,0:T(8,128)(2,1)S(1)} %get-tuple-element.102), channel_id=1, source_target_pairs={{0,2},{1,3},{2,0},{3,1},{4,6},{5,7},{6,4},{7,5},{8,10},{9,11},{10,... | collective-permute-start | bytes 393224 | tf_op jit(solution)/shard_map/ppermute | solution.py:538
  48.3 0.7 collective-permute-start.25
  49.0 3.0 %collective-permute-done.14 = bf16[1,64,1024]{2,1,0:T(8,128)(2,1)S(1)} collective-permute-done((bf16[1,64,1024]{2,1,0:T(8,128)(2,1)S(1)}, bf16[1,64,1024]{2,1,0:T(8,128)(2,1)S(1)}, u32[]{:S(2)}, u32[]{:S(2)}) %collective-permute-start.14) | collective-permute-done | bytes 131104 | tf_op jit(solution)/shard_map/ppermute | solution.py:538
  52.0 2.0 %collective-permute-done.13 = bf16[1,64,1024]{2,1,0:T(8,128)(2,1)S(1)} collective-permute-done((bf16[1,64,1024]{2,1,0:T(8,128)(2,1)S(1)}, bf16[1,64,1024]{2,1,0:T(8,128)(2,1)S(1)}, u32[]{:S(2)}, u32[]{:S(2)}) %collective-permute-start.13) | collective-permute-done | bytes 131104 | tf_op jit(solution)/shard_map/ppermute | solution.py:538
  54.0 0.9 collective-permute-done.12
  54.9 0.7 reduce-precision_convert_fusion.2
  55.7 0.7 collective-permute-start.10
  56.4 2.0 %out.1 = bf16[4,128,2,512]{3,2,1,0:T(2,128)(2,1)} custom-call(f32[1024,512]{1,0:T(8,128)S(1)} %get-tuple-element.68.branch_ref, bf16[4,128,2,512]{3,2,1,0:T(2,128)(2,1)S(1)} %bitcast.68), custom_call_target="tpu_custom_call" | custom-call | flops 1048576 | bytes 4194304 | tf_op jit(solution)/shard_map/out/pallas_call | solution.py:72
  58.4 1.0 collective-permute-done.10
  59.4 0.7 fusion.1
  60.6 2.8 %adjoint.1 = (bf16[1024,512]{1,0:T(8,128)(2,1)S(1)}, f32[8,768]{1,0:T(8,128)S(1)}, bf16[2,128,512]{2,1,0:T(8,128)(2,1)}, f32[1,128,512]{2,1,0:T(8,128)S(1)}, f32[1,128,512]{2,1,0:T(8,128)S(1)}) custom-call(f32[1024,512]{1,0:T(8,128)S(1)} %get-tuple-element.73.refs_0_, f32[8,512]{1,0:T(8,128)S(1)} %get-tuple-element.79.refs_1_, ...), custom_call_target="tpu_custom_call" | custom-call | flops 1073741824 | bytes 4194304 | tf_op jit(solution)/shard_map/adjoint/pallas_call | solution.py:72
  63.5 1.0 copy-done.7
  64.4 0.7 copy-done.13
  65.8 1.2 %collective-permute-done.15 = bf16[2,128,512]{2,1,0:T(8,128)(2,1)} collective-permute-done((bf16[2,128,512]{2,1,0:T(8,128)(2,1)}, bf16[2,128,512]{2,1,0:T(8,128)(2,1)}, u32[]{:S(2)}, u32[]{:S(2)}) %collective-permute-start.15) | collective-permute-done | bytes 262176 | tf_op jit(solution)/shard_map/ppermute | solution.py:538
  67.0 1.0 convert_add_fusion.3
  68.0 0.8 collective-permute-start.21
  68.8 2.5 %collective-permute-done.26 = bf16[128,512]{1,0:T(8,128)(2,1)S(1)} collective-permute-done((bf16[128,512]{1,0:T(8,128)(2,1)}, bf16[128,512]{1,0:T(8,128)(2,1)S(1)}, u32[]{:S(2)}, u32[]{:S(2)}) %collective-permute-start.26) | collective-permute-done | bytes 131104 | tf_op jit(solution)/shard_map/ppermute | solution.py:538
  71.3 0.9 reduce-precision_convert_fusion.4
  72.2 1.6 %collective-permute-start.27 = (bf16[128,512]{1,0:T(8,128)(2,1)S(1)}, bf16[128,512]{1,0:T(8,128)(2,1)S(1)}, u32[]{:S(2)}, u32[]{:S(2)}) collective-permute-start(bf16[128,512]{1,0:T(8,128)(2,1)S(1)} %reduce-precision_convert_fusion.4), channel_id=1, source_target_pairs={{0,8},{1,9},{2,10},{3,11},{4,12},{5,13},{6,14},{7,15},{8,0},{9,1},... | collective-permute-start | bytes 393224 | tf_op jit(solution)/shard_map/ppermute | solution.py:538
  74.3 1.0 fusion
  75.3 1.6 %copy-done.5 = f32[1024,512]{1,0:T(8,128)S(1)} copy-done((f32[1024,512]{1,0:T(8,128)S(1)}, f32[1024,512]{1,0:T(8,128)}, u32[]{:S(2)}) %copy-start.5) | copy-done | bytes 2097176
  76.9 1.2 copy-done.8
  78.1 1.0 copy-done.10
  79.1 1.0 copy-done.12
  80.2 4.4 %tokens.1 = (f32[4,128,2,512]{3,2,1,0:T(2,128)}, f32[8,1024]{1,0:T(8,128)S(1)}) custom-call(bf16[1024,512]{1,0:T(8,128)(2,1)S(1)} %copy-done.8, bf16[512,512]{1,0:T(8,128)(2,1)S(1)} %copy-done.12, f32[1024,512]{1,0:T(8,128)S(1)} %copy-done.5, f32[1024,512]{1,0:T(8,128)S(1)} %get-tuple-element.60.refs_8_.refs_2_.unit_ref, f32[1024,128]{1,0:T(8,128)S(1)} %copy-done.10, ...), custom_call_target="tpu_custom_call" | custom-call | flops 536870912 | bytes 4194304 | tf_op jit(solution)/shard_map/tokens/pallas_call | solution.py:72
  84.7 3.7 %collective-permute-start.30 = (bf16[64,1024]{1,0:T(8,128)(2,1)S(1)}, bf16[64,1024]{1,0:T(8,128)(2,1)S(1)}, u32[]{:S(2)}, u32[]{:S(2)}) collective-permute-start(bf16[64,1024]{1,0:T(8,128)(2,1)S(1)} %reduce-precision_convert_fusion.1), channel_id=1, source_target_pairs={{0,24},{1,25},{2,26},{3,27},{4,28},{5,29},{6,30},{7,31},{8,16},{9,... | collective-permute-start | bytes 393224 | tf_op jit(solution)/shard_map/ppermute | solution.py:538
  88.4 0.8 collective-permute-start.17
  89.2 1.1 collective-permute-start.28
  90.3 1.8 %collective-permute-done.17 = f32[1,2304]{1,0:T(1,128)S(1)} collective-permute-done((f32[1,2304]{1,0:T(1,128)S(1)}, f32[1,2304]{1,0:T(1,128)S(1)}, u32[]{:S(2)}, u32[]{:S(2)}) %collective-permute-start.17) | collective-permute-done | bytes 9248 | tf_op jit(solution)/shard_map/ppermute | solution.py:538
  92.7 1.8 %collective-permute-start.33 = (bf16[64,1024]{1,0:T(8,128)(2,1)S(1)}, bf16[64,1024]{1,0:T(8,128)(2,1)S(1)}, u32[]{:S(2)}, u32[]{:S(2)}) collective-permute-start(bf16[64,1024]{1,0:T(8,128)(2,1)S(1)} %reduce-precision_convert_fusion), channel_id=1, source_target_pairs={{0,6},{1,7},{2,4},{3,5},{4,2},{5,3},{6,0},{7,1},{8,14},{9,15},{10,... | collective-permute-start | bytes 393224 | tf_op jit(solution)/shard_map/ppermute | solution.py:538
  95.1 1.2 collective-permute-start.31
  96.3 1.6 %collective-permute-start.22 = (bf16[128,512]{1,0:T(8,128)(2,1)S(1)}, bf16[128,512]{1,0:T(8,128)(2,1)S(1)}, u32[]{:S(2)}, u32[]{:S(2)}) collective-permute-start(bf16[128,512]{1,0:T(8,128)(2,1)S(1)} %fusion), channel_id=1, source_target_pairs={{0,4},{1,5},{2,6},{3,7},{4,0},{5,1},{6,2},{7,3},{8,12},{9,13},{10,... | collective-permute-start | bytes 393224 | tf_op jit(solution)/shard_map/ppermute | solution.py:538
  97.9 4.6 %collective-permute-start.19 = (f32[1,2304]{1,0:T(1,128)S(1)}, f32[1,2304]{1,0:T(1,128)S(1)}, u32[]{:S(2)}, u32[]{:S(2)}) collective-permute-start(f32[1,2304]{1,0:T(1,128)S(1)} %add.107), channel_id=1, source_target_pairs={{0,8},{1,9},{2,10},{3,11},{4,12},{5,13},{6,14},{7,15},{8,0},{9,1},... | collective-permute-start | bytes 27656 | tf_op jit(solution)/shard_map/ppermute | solution.py:538
  102.5 0.9 copy.29
  103.4 0.7 collective-permute-done.19
  104.1 2.5 %collective-permute-start.20 = (f32[1,2304]{1,0:T(1,128)S(1)}, f32[1,2304]{1,0:T(1,128)S(1)}, u32[]{:S(2)}, u32[]{:S(2)}) collective-permute-start(f32[1,2304]{1,0:T(1,128)S(1)} %add.108), channel_id=1, source_target_pairs={{0,24},{1,25},{2,26},{3,27},{4,28},{5,29},{6,30},{7,31},{8,16},{9,... | collective-permute-start | bytes 27656 | tf_op jit(solution)/shard_map/ppermute | solution.py:538
  107.0 2.6 %collective-permute-done.20 = f32[1,2304]{1,0:T(1,128)S(1)} collective-permute-done((f32[1,2304]{1,0:T(1,128)S(1)}, f32[1,2304]{1,0:T(1,128)S(1)}, u32[]{:S(2)}, u32[]{:S(2)}) %collective-permute-start.20) | collective-permute-done | bytes 9248 | tf_op jit(solution)/shard_map/ppermute | solution.py:538
  110.6 4.2 %collective-permute-done.23 = bf16[128,512]{1,0:T(8,128)(2,1)S(1)} collective-permute-done((bf16[128,512]{1,0:T(8,128)(2,1)S(1)}, bf16[128,512]{1,0:T(8,128)(2,1)S(1)}, u32[]{:S(2)}, u32[]{:S(2)}) %collective-permute-start.23) | collective-permute-done | bytes 131104 | tf_op jit(solution)/shard_map/ppermute | solution.py:538
  114.8 2.5 %collective-permute-start.24 = (bf16[128,512]{1,0:T(8,128)(2,1)S(1)}, bf16[128,512]{1,0:T(8,128)(2,1)S(1)}, u32[]{:S(2)}, u32[]{:S(2)}) collective-permute-start(bf16[128,512]{1,0:T(8,128)(2,1)S(1)} %reduce-precision_convert_fusion.6), channel_id=1, source_target_pairs={{0,24},{1,25},{2,26},{3,27},{4,28},{5,29},{6,30},{7,31},{8,16},{9,... | collective-permute-start | bytes 393224 | tf_op jit(solution)/shard_map/ppermute | solution.py:538
  118.5 1.5 %place.1 = f32[512,1024]{1,0:T(8,128)} custom-call(bf16[1,64,1024]{2,1,0:T(8,128)(2,1)S(1)} %bitcast.70, bf16[3,64,1024]{2,1,0:T(8,128)(2,1)S(1)} %pad_maximum_fusion.refs_1_, bf16[1,64,1024]{2,1,0:T(8,128)(2,1)S(1)} %collective-permute-done.34.refs_2_, bf16[3,64,1024]{2,1,0:T(8,128)(2,1)S(1)} %collective-permute-done.35.refs_3_), custom_call_target="tpu_custom_call" | custom-call | flops 262144 | bytes 4194304 | tf_op jit(solution)/shard_map/place/pallas_call | solution.py:72
  120.0 1.7 %collective-permute-done.24 = bf16[128,512]{1,0:T(8,128)(2,1)S(1)} collective-permute-done((bf16[128,512]{1,0:T(8,128)(2,1)S(1)}, bf16[128,512]{1,0:T(8,128)(2,1)S(1)}, u32[]{:S(2)}, u32[]{:S(2)}) %collective-permute-start.24) | collective-permute-done | bytes 131104 | tf_op jit(solution)/shard_map/ppermute | solution.py:538
  121.7 0.9 copy.30
  (102 shorter events, 9.1 us)
Async XLA Ops:
  0.6 0.9 copy-start.15
  1.6 0.7 copy-start.16
  2.2 0.7 copy-start.17
  2.9 0.7 copy-start.18
  3.6 0.7 copy-start.19
  4.3 0.7 copy-start.21
  4.9 0.7 copy-start.23
  5.7 6.9 %collective-permute-start.1 = (bf16[144,512]{1,0:T(8,128)(2,1)S(1)}, bf16[144,512]{1,0:T(8,128)(2,1)S(1)}, u32[]{:S(2)}, u32[]{:S(2)}) collective-permute-start(bf16[144,512]{1,0:T(8,128)(2,1)S(1)} %get-tuple-element.55.refs_0_), channel_id=1, source_target_pairs={{0,2},{1,3},{2,0},{3,1},{4,6},{5,7},{6,4},{7,5},{8,10},{9,11},{10,... | collective-permute-start | bytes 442376 | tf_op jit(solution)/shard_map/ppermute | solution.py:538
  8.7 12.6 %collective-permute-start = (bf16[144,512]{1,0:T(8,128)(2,1)S(1)}, bf16[144,512]{1,0:T(8,128)(2,1)S(1)}, u32[]{:S(2)}, u32[]{:S(2)}) collective-permute-start(bf16[144,512]{1,0:T(8,128)(2,1)S(1)} %get-tuple-element.55.refs_0_), channel_id=1, source_target_pairs={{0,1},{1,0},{2,3},{3,2},{4,5},{5,4},{6,7},{7,6},{8,9},{9,8},{10,11... | collective-permute-start | bytes 442376 | tf_op jit(solution)/shard_map/ppermute | solution.py:538
  12.6 8.7 %collective-permute-start.2 = (bf16[144,512]{1,0:T(8,128)(2,1)S(1)}, bf16[144,512]{1,0:T(8,128)(2,1)S(1)}, u32[]{:S(2)}, u32[]{:S(2)}) collective-permute-start(bf16[144,512]{1,0:T(8,128)(2,1)S(1)} %collective-permute-done.1.refs_2_), channel_id=1, source_target_pairs={{0,1},{1,0},{2,3},{3,2},{4,5},{5,4},{6,7},{7,6},{8,9},{9,8},{10,11... | collective-permute-start | bytes 442376 | tf_op jit(solution)/shard_map/ppermute | solution.py:538
  12.6 1.2 copy-start
  13.8 1.2 copy-start.2
  15.0 0.9 copy-start.14
  15.9 0.7 copy-start.24
  16.6 16.2 %copy-start.6 = (bf16[512,1024]{1,0:T(8,128)(2,1)S(1)}, bf16[512,1024]{1,0:T(8,128)(2,1)}, u32[]{:S(2)}) copy-start(bf16[512,1024]{1,0:T(8,128)(2,1)} %refs_4_.1) | copy-start | bytes 3145732
  20.5 0.8 copy-start.9
  23.2 0.8 copy-start.11
  24.0 3.7 %collective-permute-start.3 = (f32[1,8,512]{2,1,0:T(8,128)S(1)}, f32[1,8,512]{2,1,0:T(8,128)S(1)}, u32[]{:S(2)}, u32[]{:S(2)}) collective-permute-start(f32[1,8,512]{2,1,0:T(8,128)S(1)} %bitcast.76), channel_id=1, source_target_pairs={{0,2},{1,3},{2,0},{3,1},{4,6},{5,7},{6,4},{7,5},{8,10},{9,11},{10,... | collective-permute-start | bytes 49160 | tf_op jit(solution)/shard_map/ppermute | solution.py:538
  25.8 5.6 %collective-permute-start.6 = (bf16[128,512]{1,0:T(8,128)(2,1)S(1)}, bf16[128,512]{1,0:T(8,128)(2,1)S(1)}, u32[]{:S(2)}, u32[]{:S(2)}) collective-permute-start(bf16[128,512]{1,0:T(8,128)(2,1)S(1)} %get-tuple-element.59.refs_4_), channel_id=1, source_target_pairs={{0,2},{1,3},{2,0},{3,1},{4,6},{5,7},{6,4},{7,5},{8,10},{9,11},{10,... | collective-permute-start | bytes 393224 | tf_op jit(solution)/shard_map/ppermute | solution.py:538
  27.8 3.6 %collective-permute-start.4 = (f32[2,8,512]{2,1,0:T(8,128)S(1)}, f32[2,8,512]{2,1,0:T(8,128)S(1)}, u32[]{:S(2)}, u32[]{:S(2)}) collective-permute-start(f32[2,8,512]{2,1,0:T(8,128)S(1)} %get-tuple-element.106), channel_id=1, source_target_pairs={{0,1},{1,0},{2,3},{3,2},{4,5},{5,4},{6,7},{7,6},{8,9},{9,8},{10,11... | collective-permute-start | bytes 98312 | tf_op jit(solution)/shard_map/ppermute | solution.py:538
  27.8 3.6 %collective-permute-start.5 = (bf16[128,512]{1,0:T(8,128)(2,1)S(1)}, bf16[128,512]{1,0:T(8,128)(2,1)S(1)}, u32[]{:S(2)}, u32[]{:S(2)}) collective-permute-start(bf16[128,512]{1,0:T(8,128)(2,1)S(1)} %get-tuple-element.59.refs_4_), channel_id=1, source_target_pairs={{0,1},{1,0},{2,3},{3,2},{4,5},{5,4},{6,7},{7,6},{8,9},{9,8},{10,11... | collective-permute-start | bytes 393224 | tf_op jit(solution)/shard_map/ppermute | solution.py:538
  31.4 1.3 %collective-permute-start.7 = (bf16[128,512]{1,0:T(8,128)(2,1)S(1)}, bf16[128,512]{1,0:T(8,128)(2,1)S(1)}, u32[]{:S(2)}, u32[]{:S(2)}) collective-permute-start(bf16[128,512]{1,0:T(8,128)(2,1)S(1)} %collective-permute-done.6.refs_6_), channel_id=1, source_target_pairs={{0,1},{1,0},{2,3},{3,2},{4,5},{5,4},{6,7},{7,6},{8,9},{9,8},{10,11... | collective-permute-start | bytes 393224 | tf_op jit(solution)/shard_map/ppermute | solution.py:538
  39.6 5.0 %collective-permute-start.9 = (bf16[4,64,1024]{2,1,0:T(8,128)(2,1)S(1)}, bf16[4,64,1024]{2,1,0:T(8,128)(2,1)S(1)}, u32[]{:S(2)}, u32[]{:S(2)}) collective-permute-start(bf16[4,64,1024]{2,1,0:T(8,128)(2,1)S(1)} %get-tuple-element.75), channel_id=1, source_target_pairs={{0,1},{1,0},{2,3},{3,2},{4,5},{5,4},{6,7},{7,6},{8,9},{9,8},{10,11... | collective-permute-start | bytes 1572872 | tf_op jit(solution)/shard_map/ppermute | solution.py:538
  44.2 14.2 %copy-start.4 = (f32[1024,512]{1,0:T(8,128)}, f32[1024,512]{1,0:T(8,128)S(1)}, u32[]{:S(2)}) copy-start(f32[1024,512]{1,0:T(8,128)S(1)} %get-tuple-element.87.dpre_ref) | copy-start | bytes 6291460
  44.2 12.2 %copy-start.3 = (bf16[512,2,512]{2,1,0:T(2,128)(2,1)S(1)}, bf16[512,2,512]{2,1,0:T(2,128)(2,1)}, u32[]{:S(2)}) copy-start(bf16[512,2,512]{2,1,0:T(2,128)(2,1)} %param.12) | copy-start | bytes 3145732
  44.2 4.1 %collective-permute-start.8 = (bf16[2,128,512]{2,1,0:T(8,128)(2,1)S(1)}, bf16[2,128,512]{2,1,0:T(8,128)(2,1)S(1)}, u32[]{:S(2)}, u32[]{:S(2)}) collective-permute-start(bf16[2,128,512]{2,1,0:T(8,128)(2,1)S(1)} %get-tuple-element.71), channel_id=1, source_target_pairs={{0,1},{1,0},{2,3},{3,2},{4,5},{5,4},{6,7},{7,6},{8,9},{9,8},{10,11... | collective-permute-start | bytes 786440 | tf_op jit(solution)/shard_map/ppermute | solution.py:538
  44.7 7.3 %collective-permute-start.14 = (bf16[1,64,1024]{2,1,0:T(8,128)(2,1)S(1)}, bf16[1,64,1024]{2,1,0:T(8,128)(2,1)S(1)}, u32[]{:S(2)}, u32[]{:S(2)}) collective-permute-start(bf16[1,64,1024]{2,1,0:T(8,128)(2,1)S(1)} %get-tuple-element.100), channel_id=1, source_target_pairs={{0,6},{1,7},{2,4},{3,5},{4,2},{5,3},{6,0},{7,1},{8,14},{9,15},{10,... | collective-permute-start | bytes 393224 | tf_op jit(solution)/shard_map/ppermute | solution.py:538
  46.4 7.6 %collective-permute-start.13 = (bf16[1,64,1024]{2,1,0:T(8,128)(2,1)S(1)}, bf16[1,64,1024]{2,1,0:T(8,128)(2,1)S(1)}, u32[]{:S(2)}, u32[]{:S(2)}) collective-permute-start(bf16[1,64,1024]{2,1,0:T(8,128)(2,1)S(1)} %get-tuple-element.101), channel_id=1, source_target_pairs={{0,4},{1,5},{2,6},{3,7},{4,0},{5,1},{6,2},{7,3},{8,12},{9,13},{10,... | collective-permute-start | bytes 393224 | tf_op jit(solution)/shard_map/ppermute | solution.py:538
  46.9 8.1 %collective-permute-start.12 = (bf16[1,64,1024]{2,1,0:T(8,128)(2,1)S(1)}, bf16[1,64,1024]{2,1,0:T(8,128)(2,1)S(1)}, u32[]{:S(2)}, u32[]{:S(2)}) collective-permute-start(bf16[1,64,1024]{2,1,0:T(8,128)(2,1)S(1)} %get-tuple-element.102), channel_id=1, source_target_pairs={{0,2},{1,3},{2,0},{3,1},{4,6},{5,7},{6,4},{7,5},{8,10},{9,11},{10,... | collective-permute-start | bytes 393224 | tf_op jit(solution)/shard_map/ppermute | solution.py:538
  48.3 11.1 %collective-permute-start.25 = (bf16[1,128,512]{2,1,0:T(8,128)(2,1)S(1)}, bf16[1,128,512]{2,1,0:T(8,128)(2,1)S(1)}, u32[]{:S(2)}, u32[]{:S(2)}) collective-permute-start(bf16[1,128,512]{2,1,0:T(8,128)(2,1)S(1)} %convert_add_fusion.9), channel_id=1, source_target_pairs={{0,2},{1,3},{2,0},{3,1},{4,6},{5,7},{6,4},{7,5},{8,10},{9,11},{10,... | collective-permute-start | bytes 393224 | tf_op jit(solution)/shard_map/ppermute | solution.py:538
  55.7 3.7 %collective-permute-start.10 = (f32[1,8,512]{2,1,0:T(8,128)S(1)}, f32[1,8,512]{2,1,0:T(8,128)S(1)}, u32[]{:S(2)}, u32[]{:S(2)}) collective-permute-start(f32[1,8,512]{2,1,0:T(8,128)S(1)} %bitcast.73), channel_id=1, source_target_pairs={{0,2},{1,3},{2,0},{3,1},{4,6},{5,7},{6,4},{7,5},{8,10},{9,11},{10,... | collective-permute-start | bytes 49160 | tf_op jit(solution)/shard_map/ppermute | solution.py:538
  59.4 1.2 collective-permute-start.11
  63.5 1.0 copy-start.7
  64.4 0.7 copy-start.13
  65.1 10.1 %copy-start.1 = (bf16[512,2,512]{2,1,0:T(2,128)(2,1)S(1)}, bf16[512,2,512]{2,1,0:T(2,128)(2,1)}, u32[]{:S(2)}) copy-start(bf16[512,2,512]{2,1,0:T(2,128)(2,1)} %param.23) | copy-start | bytes 3145732
  65.1 1.9 %collective-permute-start.15 = (bf16[2,128,512]{2,1,0:T(8,128)(2,1)}, bf16[2,128,512]{2,1,0:T(8,128)(2,1)}, u32[]{:S(2)}, u32[]{:S(2)}) collective-permute-start(bf16[2,128,512]{2,1,0:T(8,128)(2,1)} %get-tuple-element.83), channel_id=1, source_target_pairs={{0,1},{1,0},{2,3},{3,2},{4,5},{5,4},{6,7},{7,6},{8,9},{9,8},{10,11... | collective-permute-start | bytes 786440 | tf_op jit(solution)/shard_map/ppermute | solution.py:538
  65.3 6.0 %collective-permute-start.26 = (bf16[128,512]{1,0:T(8,128)(2,1)}, bf16[128,512]{1,0:T(8,128)(2,1)S(1)}, u32[]{:S(2)}, u32[]{:S(2)}) collective-permute-start(bf16[128,512]{1,0:T(8,128)(2,1)} %fusion.1), channel_id=1, source_target_pairs={{0,4},{1,5},{2,6},{3,7},{4,0},{5,1},{6,2},{7,3},{8,12},{9,13},{10,... | collective-permute-start | bytes 393224 | tf_op jit(solution)/shard_map/ppermute | solution.py:538
  68.0 6.3 %collective-permute-start.21 = (bf16[1,128,512]{2,1,0:T(8,128)(2,1)S(1)}, bf16[1,128,512]{2,1,0:T(8,128)(2,1)S(1)}, u32[]{:S(2)}, u32[]{:S(2)}) collective-permute-start(bf16[1,128,512]{2,1,0:T(8,128)(2,1)S(1)} %convert_add_fusion.3), channel_id=1, source_target_pairs={{0,2},{1,3},{2,0},{3,1},{4,6},{5,7},{6,4},{7,5},{8,10},{9,11},{10,... | collective-permute-start | bytes 393224 | tf_op jit(solution)/shard_map/ppermute | solution.py:538
  72.2 17.0 %collective-permute-start.27 = (bf16[128,512]{1,0:T(8,128)(2,1)S(1)}, bf16[128,512]{1,0:T(8,128)(2,1)S(1)}, u32[]{:S(2)}, u32[]{:S(2)}) collective-permute-start(bf16[128,512]{1,0:T(8,128)(2,1)S(1)} %reduce-precision_convert_fusion.4), channel_id=1, source_target_pairs={{0,8},{1,9},{2,10},{3,11},{4,12},{5,13},{6,14},{7,15},{8,0},{9,1},... | collective-permute-start | bytes 393224 | tf_op jit(solution)/shard_map/ppermute | solution.py:538
  73.8 10.8 %collective-permute-start.29 = (bf16[64,1024]{1,0:T(8,128)(2,1)}, bf16[64,1024]{1,0:T(8,128)(2,1)S(1)}, u32[]{:S(2)}, u32[]{:S(2)}) collective-permute-start(bf16[64,1024]{1,0:T(8,128)(2,1)} %reduce-precision_convert_fusion.2), channel_id=1, source_target_pairs={{0,8},{1,9},{2,10},{3,11},{4,12},{5,13},{6,14},{7,15},{8,0},{9,1},... | collective-permute-start | bytes 393224 | tf_op jit(solution)/shard_map/ppermute | solution.py:538
  75.3 1.6 %copy-start.5 = (f32[1024,512]{1,0:T(8,128)S(1)}, f32[1024,512]{1,0:T(8,128)}, u32[]{:S(2)}) copy-start(f32[1024,512]{1,0:T(8,128)} %copy-done.4) | copy-start | bytes 6291460
  76.9 1.2 copy-start.8
  78.1 1.0 copy-start.10
  79.1 1.0 copy-start.12
  80.2 4.5 %copy-start.25 = (bf16[64,1024]{1,0:T(8,128)(2,1)S(1)}, bf16[64,1024]{1,0:T(8,128)(2,1)}, u32[]{:S(2)}) copy-start(bf16[64,1024]{1,0:T(8,128)(2,1)} %reduce-precision_convert_fusion.2) | copy-start | bytes 393220
  84.5 32.8 %copy-start.20 = (f32[64]{0:T(128)S(1)}, f32[64]{0:T(128)}, u32[]{:S(2)}) copy-start(f32[64]{0:T(128)} %param.17) | copy-start | bytes 772
  84.5 32.8 %copy-start.22 = (f32[64]{0:T(128)S(1)}, f32[64]{0:T(128)}, u32[]{:S(2)}) copy-start(f32[64]{0:T(128)} %param.18) | copy-start | bytes 772
  84.6 3.8 %collective-permute-start.16 = (f32[1,2304]{1,0:T(1,128)S(1)}, f32[1,2304]{1,0:T(1,128)S(1)}, u32[]{:S(2)}, u32[]{:S(2)}) collective-permute-start(f32[1,2304]{1,0:T(1,128)S(1)} %broadcast_in_dim.14), channel_id=1, source_target_pairs={{0,1},{1,0},{2,3},{3,2},{4,5},{5,4},{6,7},{7,6},{8,9},{9,8},{10,11... | collective-permute-start | bytes 27656 | tf_op jit(solution)/shard_map/ppermute | solution.py:538
  84.7 8.0 %collective-permute-start.30 = (bf16[64,1024]{1,0:T(8,128)(2,1)S(1)}, bf16[64,1024]{1,0:T(8,128)(2,1)S(1)}, u32[]{:S(2)}, u32[]{:S(2)}) collective-permute-start(bf16[64,1024]{1,0:T(8,128)(2,1)S(1)} %reduce-precision_convert_fusion.1), channel_id=1, source_target_pairs={{0,24},{1,25},{2,26},{3,27},{4,28},{5,29},{6,30},{7,31},{8,16},{9,... | collective-permute-start | bytes 393224 | tf_op jit(solution)/shard_map/ppermute | solution.py:538
  88.4 3.7 %collective-permute-start.17 = (f32[1,2304]{1,0:T(1,128)S(1)}, f32[1,2304]{1,0:T(1,128)S(1)}, u32[]{:S(2)}, u32[]{:S(2)}) collective-permute-start(f32[1,2304]{1,0:T(1,128)S(1)} %reshape_add_fusion), channel_id=1, source_target_pairs={{0,2},{1,3},{2,0},{3,1},{4,6},{5,7},{6,4},{7,5},{8,10},{9,11},{10,... | collective-permute-start | bytes 27656 | tf_op jit(solution)/shard_map/ppermute | solution.py:538
  89.2 8.6 %collective-permute-start.28 = (bf16[128,512]{1,0:T(8,128)(2,1)S(1)}, bf16[128,512]{1,0:T(8,128)(2,1)S(1)}, u32[]{:S(2)}, u32[]{:S(2)}) collective-permute-start(bf16[128,512]{1,0:T(8,128)(2,1)S(1)} %reduce-precision_convert_fusion.3), channel_id=1, source_target_pairs={{0,24},{1,25},{2,26},{3,27},{4,28},{5,29},{6,30},{7,31},{8,16},{9,... | collective-permute-start | bytes 393224 | tf_op jit(solution)/shard_map/ppermute | solution.py:538
  92.2 4.1 %collective-permute-start.18 = (f32[1,2304]{1,0:T(1,128)S(1)}, f32[1,2304]{1,0:T(1,128)S(1)}, u32[]{:S(2)}, u32[]{:S(2)}) collective-permute-start(f32[1,2304]{1,0:T(1,128)S(1)} %add.106), channel_id=1, source_target_pairs={{0,4},{1,5},{2,6},{3,7},{4,0},{5,1},{6,2},{7,3},{8,12},{9,13},{10,... | collective-permute-start | bytes 27656 | tf_op jit(solution)/shard_map/ppermute | solution.py:538
  92.7 11.4 %collective-permute-start.33 = (bf16[64,1024]{1,0:T(8,128)(2,1)S(1)}, bf16[64,1024]{1,0:T(8,128)(2,1)S(1)}, u32[]{:S(2)}, u32[]{:S(2)}) collective-permute-start(bf16[64,1024]{1,0:T(8,128)(2,1)S(1)} %reduce-precision_convert_fusion), channel_id=1, source_target_pairs={{0,6},{1,7},{2,4},{3,5},{4,2},{5,3},{6,0},{7,1},{8,14},{9,15},{10,... | collective-permute-start | bytes 393224 | tf_op jit(solution)/shard_map/ppermute | solution.py:538
  94.5 12.2 %collective-permute-start.32 = (bf16[64,1024]{1,0:T(8,128)(2,1)S(1)}, bf16[64,1024]{1,0:T(8,128)(2,1)S(1)}, u32[]{:S(2)}, u32[]{:S(2)}) collective-permute-start(bf16[64,1024]{1,0:T(8,128)(2,1)S(1)} %reduce-precision_convert_fusion), channel_id=1, source_target_pairs={{0,4},{1,5},{2,6},{3,7},{4,0},{5,1},{6,2},{7,3},{8,12},{9,13},{10,... | collective-permute-start | bytes 393224 | tf_op jit(solution)/shard_map/ppermute | solution.py:538
  95.1 11.5 %collective-permute-start.31 = (bf16[64,1024]{1,0:T(8,128)(2,1)S(1)}, bf16[64,1024]{1,0:T(8,128)(2,1)S(1)}, u32[]{:S(2)}, u32[]{:S(2)}) collective-permute-start(bf16[64,1024]{1,0:T(8,128)(2,1)S(1)} %reduce-precision_convert_fusion), channel_id=1, source_target_pairs={{0,2},{1,3},{2,0},{3,1},{4,6},{5,7},{6,4},{7,5},{8,10},{9,11},{10,... | collective-permute-start | bytes 393224 | tf_op jit(solution)/shard_map/ppermute | solution.py:538
  96.3 13.4 %collective-permute-start.22 = (bf16[128,512]{1,0:T(8,128)(2,1)S(1)}, bf16[128,512]{1,0:T(8,128)(2,1)S(1)}, u32[]{:S(2)}, u32[]{:S(2)}) collective-permute-start(bf16[128,512]{1,0:T(8,128)(2,1)S(1)} %fusion), channel_id=1, source_target_pairs={{0,4},{1,5},{2,6},{3,7},{4,0},{5,1},{6,2},{7,3},{8,12},{9,13},{10,... | collective-permute-start | bytes 393224 | tf_op jit(solution)/shard_map/ppermute | solution.py:538
  97.9 6.2 %collective-permute-start.19 = (f32[1,2304]{1,0:T(1,128)S(1)}, f32[1,2304]{1,0:T(1,128)S(1)}, u32[]{:S(2)}, u32[]{:S(2)}) collective-permute-start(f32[1,2304]{1,0:T(1,128)S(1)} %add.107), channel_id=1, source_target_pairs={{0,8},{1,9},{2,10},{3,11},{4,12},{5,13},{6,14},{7,15},{8,0},{9,1},... | collective-permute-start | bytes 27656 | tf_op jit(solution)/shard_map/ppermute | solution.py:538
  104.1 14.4 %collective-permute-start.34 = (bf16[1,64,1024]{2,1,0:T(8,128)(2,1)S(1)}, bf16[1,64,1024]{2,1,0:T(8,128)(2,1)S(1)}, u32[]{:S(2)}, u32[]{:S(2)}) collective-permute-start(bf16[1,64,1024]{2,1,0:T(8,128)(2,1)S(1)} %bitcast.69), channel_id=1, source_target_pairs={{0,1},{1,0},{2,3},{3,2},{4,5},{5,4},{6,7},{7,6},{8,9},{9,8},{10,11... | collective-permute-start | bytes 393224 | tf_op jit(solution)/shard_map/ppermute | solution.py:538
  104.1 5.5 %collective-permute-start.20 = (f32[1,2304]{1,0:T(1,128)S(1)}, f32[1,2304]{1,0:T(1,128)S(1)}, u32[]{:S(2)}, u32[]{:S(2)}) collective-permute-start(f32[1,2304]{1,0:T(1,128)S(1)} %add.108), channel_id=1, source_target_pairs={{0,24},{1,25},{2,26},{3,27},{4,28},{5,29},{6,30},{7,31},{8,16},{9,... | collective-permute-start | bytes 27656 | tf_op jit(solution)/shard_map/ppermute | solution.py:538
  106.7 11.8 %collective-permute-start.35 = (bf16[3,64,1024]{2,1,0:T(8,128)(2,1)S(1)}, bf16[3,64,1024]{2,1,0:T(8,128)(2,1)S(1)}, u32[]{:S(2)}, u32[]{:S(2)}) collective-permute-start(bf16[3,64,1024]{2,1,0:T(8,128)(2,1)S(1)} %pad_maximum_fusion.refs_1_), channel_id=1, source_target_pairs={{0,1},{1,0},{2,3},{3,2},{4,5},{5,4},{6,7},{7,6},{8,9},{9,8},{10,11... | collective-permute-start | bytes 1179656 | tf_op jit(solution)/shard_map/ppermute | solution.py:538
  109.7 5.0 %collective-permute-start.23 = (bf16[128,512]{1,0:T(8,128)(2,1)S(1)}, bf16[128,512]{1,0:T(8,128)(2,1)S(1)}, u32[]{:S(2)}, u32[]{:S(2)}) collective-permute-start(bf16[128,512]{1,0:T(8,128)(2,1)S(1)} %reduce-precision_convert_fusion.7), channel_id=1, source_target_pairs={{0,8},{1,9},{2,10},{3,11},{4,12},{5,13},{6,14},{7,15},{8,0},{9,1},... | collective-permute-start | bytes 393224 | tf_op jit(solution)/shard_map/ppermute | solution.py:538
  114.8 6.9 %collective-permute-start.24 = (bf16[128,512]{1,0:T(8,128)(2,1)S(1)}, bf16[128,512]{1,0:T(8,128)(2,1)S(1)}, u32[]{:S(2)}, u32[]{:S(2)}) collective-permute-start(bf16[128,512]{1,0:T(8,128)(2,1)S(1)} %reduce-precision_convert_fusion.6), channel_id=1, source_target_pairs={{0,24},{1,25},{2,26},{3,27},{4,28},{5,29},{6,30},{7,31},{8,16},{9,... | collective-permute-start | bytes 393224 | tf_op jit(solution)/shard_map/ppermute | solution.py:538

commit v2 on v1

--- a/solution.py
+++ b/solution.py
@@ -39,9 +39,9 @@
     return x.transpose(1, 0, 2, 3).reshape(count * segs * group, feats)
 
 
-def rows_out(y, ref, first, count):
+def rows_out(y, ref):
     segs, _, group, feats = ref.shape
-    return y.reshape(count, segs, group, feats).transpose(1, 0, 2, 3)
+    return y.reshape(y.shape[0] // SUB, segs, group, feats).transpose(1, 0, 2, 3)
 
 
 def row_mask(base, rows, group, steps, me, lens_ref):
@@ -60,15 +60,10 @@
     return jnp.concatenate([column] * (lanes // column.shape[1]), axis=1)
 
 
-def call(body, outs, ins, scratch, limit_mib, flops, name, small=()):
-    specs = []
-    for k, x in enumerate(ins):
-        if x.dtype == jnp.int32:
-            specs.append(pl.BlockSpec(memory_space=pltpu.SMEM))
-        elif k in small:
-            specs.append(pl.BlockSpec(x.shape, lambda *_, n=x.ndim: (0,) * n))
-        else:
-            specs.append(pl.BlockSpec(memory_space=pltpu.VMEM))
+def call(body, outs, ins, scratch, limit_mib, flops, name, fetched=()):
+    specs = [
+        pl.BlockSpec(memory_space=pltpu.HBM if k in fetched else pltpu.VMEM) for k in range(len(ins))
+    ]
     return pl.pallas_call(
         body,
         out_shape=[jax.ShapeDtypeStruct(s, d) for s, d in outs],
@@ -81,6 +76,17 @@
     )(*ins)
 
 
+def start_copies(sources, targets, sems):
+    copies = [pltpu.make_async_copy(a, b, sems.at[k]) for k, (a, b) in enumerate(zip(sources, targets))]
+    for c in copies:
+        c.start()
+    return copies
+
+
+def held(x):
+    return pltpu.VMEM(x.shape, x.dtype)
+
+
 def split_pairs(pairs_ref, flat_ref):
     own, _, feats = pairs_ref.shape
     flat = pairs_ref[...].astype(F32).reshape(2 * own, feats)
@@ -97,33 +103,52 @@
     return [high, mid, (rest - mid.astype(F32)).astype(BF16)]
 
 
-def prep_kernel(weight_ref, rate_ref, angle_ref, level_ref, gain_ref, bias_ref, skip_ref, pay_ref, vec_ref, flat_ref):
+def prep_kernel(*refs):
+    sources, (pay_ref, vec_ref) = refs[:7], refs[7:9]
+    targets, flat_ref, sems = refs[9:16], refs[16], refs[17]
+    weight_ref, rate_ref, angle_ref, level_ref = targets[:4]
     own, _, feats = weight_ref.shape
-    for k, rows in enumerate(split_pairs(weight_ref, flat_ref)):
-        pay_ref[k * own : (k + 1) * own, :] = rows
+    copies = start_copies(sources, targets, sems)
+    for c in copies[1:]:
+        c.wait()
     me = lax.axis_index("state")
     lane = lax.broadcasted_iota(jnp.int32, (1, feats), 1)
     mine = (lane // own) == me
     over = lambda ref: jnp.concatenate([ref[...]] * (feats // own), axis=1)
-    size = jnp.exp(-jnp.exp(over(rate_ref)))
+    decay = jnp.exp(over(rate_ref))
+    size = jnp.exp(-decay)
     angle = jnp.exp(over(angle_ref))
+    pole_re, pole_im = size * jnp.cos(angle), size * jnp.sin(angle)
     parts = []
-    for v in (size * jnp.cos(angle), size * jnp.sin(angle), jnp.exp(over(level_ref))):
+    for v in (pole_re, pole_im, jnp.exp(over(level_ref))):
         parts += three_parts(jnp.where(mine, v, 0.0))
     parts += [jnp.zeros((PARAM_ROWS - len(parts), feats), BF16)]
     pay_ref[2 * own :, :] = jnp.concatenate([p.astype(F32) for p in parts], axis=0).astype(BF16)
-    vec_ref[0:1, :] = gain_ref[...]
-    vec_ref[1:2, :] = bias_ref[...]
-    vec_ref[2:3, :] = skip_ref[...]
-
-
-def norm_kernel(x_ref, cot_ref, weight_ref, vec_ref, lens_ref, low_ref, unit_ref, inv_ref, mask_ref, rows_ref, pay_ref, flat_ref):
+    rows = [t[...] for t in targets[4:]] + [pole_re, pole_im, decay, angle]
+    for k, row in enumerate(rows):
+        vec_ref[k : k + 1, :] = row
+    vec_ref[len(rows) :, :] = jnp.zeros((SUB - len(rows), feats), F32)
+    copies[0].wait()
+    for k, part in enumerate(split_pairs(weight_ref, flat_ref)):
+        pay_ref[k * own : (k + 1) * own, :] = part
+
+
+def norm_kernel(x_hbm, cot_hbm, weight_hbm, lens_hbm, vec_ref, low_ref, unit_ref, inv_ref, mask_ref, rows_ref, pay_ref, *scratch):
+    x_ref, cot_ref, weight_ref, lens_ref, flat_ref, sems = scratch
     segs, steps, group, feats = x_ref.shape
     rows = steps * SUB
     own = weight_ref.shape[0]
     me = lax.axis_index("state")
     size = 128
+    cut = steps // 4
     gain, bias = vec_ref[0:1, :], vec_ref[1:2, :]
+    sources, targets = [lens_hbm], [lens_ref]
+    for k in range(4):
+        at = pl.ds(k * cut, cut)
+        sources += [x_hbm.at[:, at], cot_hbm.at[:, at]]
+        targets += [x_ref.at[:, at], cot_ref.at[:, at]]
+    copies = start_copies(sources + [weight_hbm], targets + [weight_ref], sems)
+    copies[0].wait()
 
     def chunk(c, carry):
         base = pl.multiple_of(c * size, size)
@@ -140,7 +165,12 @@
         rows_ref[at, :] = rows_in(cot_ref, first, size // SUB).astype(BF16)
         return carry
 
-    lax.fori_loop(0, rows // size, chunk, 0)
+    turns = rows // size // 4
+    for k in range(4):
+        copies[1 + 2 * k].wait()
+        copies[2 + 2 * k].wait()
+        lax.fori_loop(k * turns, (k + 1) * turns, chunk, 0)
+    copies[9].wait()
     for k, part in enumerate(split_pairs(weight_ref, flat_ref)):
         pay_ref[k * own : (k + 1) * own, :] = part
 
@@ -374,7 +404,7 @@
     rows, feats = gp_ref.shape
     channels = cw_ref.shape[0] // 2
     steps = rows // SUB
-    me = lax.axis_index("state")
+    place = lax.axis_index("state") + lax.axis_size("state") * (lax.axis_index("seq") & 1)
     gain, bias = vec_ref[0:1, :], vec_ref[1:2, :]
 
     def chunk(c, total):
@@ -413,7 +443,7 @@
         return carry
 
     lax.fori_loop(0, feats // width, tile, 0)
-    spread_pairs(acc_ref, me, own, channels, orders, grads)
+    spread(acc_ref, place, orders, grads)
 
 
 def adjoint_kernel(own, group, orders, *refs):
@@ -480,47 +510,108 @@
     spread_pairs(acc_ref, me, own, channels, orders, grads)
 
 
-def out_kernel(branch_ref, x_ref, out_ref):
+def out_kernel(x_hbm, branch_ref, out_ref, x_ref, sems):
     segs, steps, _, _ = x_ref.shape
     size = 16
+    cut = steps // 4
+    places = [pl.ds(k * cut, cut) for k in range(4)]
+    copies = start_copies([x_hbm.at[:, p] for p in places], [x_ref.at[:, p] for p in places], sems)
 
     def chunk(c, carry):
         first = pl.multiple_of(c * size, size)
         rows = branch_ref[pl.ds(pl.multiple_of(first * SUB, size * SUB), size * SUB), :]
         at = pl.ds(first, size)
-        out_ref[:, at] = (x_ref[:, at].astype(F32) + rows_out(rows, x_ref, first, size)).astype(BF16)
+        out_ref[:, at] = (x_ref[:, at].astype(F32) + rows_out(rows, x_ref)).astype(BF16)
         return carry
 
-    lax.fori_loop(0, steps // size, chunk, 0)
-
-
-def tokens_kernel(dproj_ref, win_ref, dpre_ref, unit_ref, inv_ref, vec_ref, cot_ref, out_ref, sums_ref):
+    for k in range(4):
+        copies[k].wait()
+        lax.fori_loop(k * cut // size, (k + 1) * cut // size, chunk, 0)
+
+
+def normed_kernel(dproj_ref, win_ref, dpre_ref, unit_ref, vec_ref, channel_ref, skip_ref, dnorm_ref, sums_ref):
     rows, feats = dpre_ref.shape
-    gain, skip = vec_ref[0:1, :], vec_ref[2:3, :]
+    skip = vec_ref[2:3, :]
+
+    def chunk(c, carry):
+        total_gain, total_bias = carry
+        at = pl.ds(pl.multiple_of(c * CHUNK, CHUNK), CHUNK)
+        d_normed = dpre_ref[at, :] * skip + nn(dproj_ref[at, :], win_ref[...])
+        dnorm_ref[at, :] = d_normed
+        folded = lambda v: jnp.sum(v.reshape(CHUNK // SUB, SUB, feats), axis=0)
+        return total_gain + folded(d_normed * unit_ref[at, :]), total_bias + folded(d_normed)
+
+    zero = jnp.zeros((SUB, feats), F32)
+    total_gain, total_bias = lax.fori_loop(0, rows // CHUNK, chunk, (zero, zero))
+    over = lambda v: jnp.sum(v, axis=0, keepdims=True)
+    channel = over(channel_ref[...])
+    wide_at = channel.shape[1] - feats
+    sums_ref[0:1, :] = channel[:, :feats]
+    sums_ref[1:2, :] = jnp.zeros((1, feats), F32)
+    sums_ref[1:2, :wide_at] = channel[:, feats:]
+    sums_ref[2:3, :] = over(total_gain)
+    sums_ref[3:4, :] = over(total_bias)
+    sums_ref[4:5, :] = over(skip_ref[...])
+    sums_ref[5:8, :] = jnp.zeros((3, feats), F32)
+
+
+def tokens_kernel(cot_hbm, dnorm_ref, unit_ref, inv_ref, vec_ref, out_ref, cot_ref, sems):
+    rows, feats = dnorm_ref.shape
+    gain = vec_ref[0:1, :]
     size = 128
     steps = size // SUB
+    cut = cot_ref.shape[1] // 4
+    places = [pl.ds(k * cut, cut) for k in range(4)]
+    copies = start_copies([cot_hbm.at[:, p] for p in places], [cot_ref.at[:, p] for p in places], sems)
 
     def chunk(c, carry):
-        total_gain, total_bias = carry
         at = pl.ds(pl.multiple_of(c * size, size), size)
-        d_normed = dpre_ref[at, :] * skip + nn(dproj_ref[at, :], win_ref[...])
         unit = unit_ref[at, :]
-        total_gain = total_gain + jnp.sum((d_normed * unit).reshape(steps, SUB, feats), axis=0)
-        total_bias = total_bias + jnp.sum(d_normed.reshape(steps, SUB, feats), axis=0)
-        d_unit = d_normed * gain
+        d_unit = dnorm_ref[at, :] * gain
         first = jnp.mean(d_unit, axis=1, keepdims=True)
         second = jnp.mean(d_unit * unit, axis=1, keepdims=True)
-        inv = wide(inv_ref[at, :], feats)
-        rows = inv * (d_unit - first - unit * second)
-        place = pl.multiple_of(c * steps, steps)
-        step_at = pl.ds(place, steps)
-        out_ref[:, step_at] = cot_ref[:, step_at].astype(F32) + rows_out(rows, cot_ref, place, steps)
-        return total_gain, total_bias
-
-    zero = jnp.zeros((SUB, feats), F32)
-    total_gain, total_bias = lax.fori_loop(0, rows // size, chunk, (zero, zero))
-    sums_ref[:, :feats] = total_gain
-    sums_ref[:, feats:] = total_bias
+        rows = wide(inv_ref[at, :], feats) * (d_unit - first - unit * second)
+        step_at = pl.ds(pl.multiple_of(c * steps, steps), steps)
+        out_ref[:, step_at] = cot_ref[:, step_at].astype(F32) + rows_out(rows, cot_ref)
+        return carry
+
+    for k in range(4):
+        copies[k].wait()
+        lax.fori_loop(k * cut // steps, (k + 1) * cut // steps, chunk, 0)
+
+
+def join_pairs(parts, flat_ref, out_ref):
+    own, _, feats = out_ref.shape
+    for k, part in enumerate(parts):
+        for c in range(feats // 128):
+            flat_ref[c, pl.ds(k, own, stride=2), :] = part[:, c * 128 : (c + 1) * 128]
+    rows = jnp.concatenate([flat_ref[c] for c in range(feats // 128)], axis=1)
+    out_ref[...] = rows.reshape(own, 2, feats)
+
+
+def halves_kernel(mine_ref, other_ref, out_ref, flat_ref):
+    own = out_ref.shape[0]
+    first = (lax.axis_index("seq") & 1) == 0
+    a, b = mine_ref[...].astype(F32), other_ref[...].astype(F32)
+    join_pairs([jnp.where(first, a, b), jnp.where(first, b, a)], flat_ref, out_ref)
+
+
+def finish_kernel(low_ref, got_ref, sums_ref, more_ref, vec_ref, in_ref, feat_ref, rate_ref, angle_ref, level_ref, flat_ref):
+    own, _, feats = in_ref.shape
+    total = low_ref[...].astype(F32) + got_ref[0 : 2 * own, :].astype(F32)
+    join_pairs([total[:own, :], total[own:, :]], flat_ref, in_ref)
+    sums = sums_ref[...] + more_ref[...]
+    feat_ref[...] = sums[2:5, :]
+    me = lax.axis_index("state")
+    channels = lax.axis_size("state") * own
+    pick = lambda row: sum(
+        jnp.where(me == d, row[:, d * own : (d + 1) * own], 0.0) for d in range(channels // own)
+    )
+    sum_re, sum_im = pick(sums[0:1, :channels]), pick(sums[0:1, channels:])
+    pole_re, pole_im, decay, angle = (vec_ref[k : k + 1, :own] for k in range(3, 7))
+    rate_ref[...] = -decay * (sum_re * pole_re + sum_im * pole_im)
+    angle_ref[...] = angle * (sum_im * pole_re - sum_re * pole_im)
+    level_ref[...] = pick(sums[1:2, :channels])
 
 
 def place_kernel(masks, parts, *refs):
@@ -563,9 +654,12 @@
     return [o for sends in stages for o in sends] + [[0]]
 
 
-def halve(parts, group):
+def halve(parts, group, after=None):
     masks = submasks(group)
-    got = [exchange(p.astype(BF16), m) for p, m in zip(parts, masks)]
+    sends = [p.astype(BF16) for p in parts[: len(masks)]]
+    got = [exchange(p, m) for p, m in zip(sends, masks)]
+    if after is not None:
+        got = tie(got, after)
     rest, off = [], 0
     for p in parts[len(masks) :]:
         n = p.shape[0]
@@ -577,13 +671,22 @@
     return rest
 
 
+def rounded(x):
+    return lax.reduce_precision(x, 8, 7)
+
+
 def double(x, mask):
-    low = lax.reduce_precision(x, 8, 7).astype(BF16)
+    low = rounded(x).astype(BF16)
     return low.astype(F32) + exchange(low, mask).astype(F32)
 
 
-def double_f32(x, mask):
-    return x + exchange(x, mask)
+def two_parts(x):
+    high = rounded(x)
+    return [high.astype(BF16), rounded(x - high).astype(BF16)]
+
+
+def sum_of(parts):
+    return parts[0].astype(F32) + parts[1].astype(F32)
 
 
 def gather_ends(end, bits):
@@ -630,18 +733,20 @@
     full = rows * feats * 2 * channels * 2
 
     as_row = lambda v: v.reshape(1, -1)
+    flat = pltpu.VMEM((feats // 128, 2 * own, 128), F32)
     x4 = tokens.reshape(segs, span // segs, group, feats)
     cot4 = cotangent.reshape(segs, span // segs, group, feats)
+    ins = [input_weight.transpose(1, 2, 0)]
+    ins += [as_row(v) for v in (log_rate, log_angle, log_gain, norm_gain, norm_bias, skip_gain)]
     b_own, vec = call(
         prep_kernel,
         [((2 * own + PARAM_ROWS, feats), BF16), ((SUB, feats), F32)],
-        [input_weight.transpose(1, 2, 0)]
-        + [as_row(v) for v in (log_rate, log_angle, log_gain, norm_gain, norm_bias, skip_gain)],
-        [pltpu.VMEM((feats // 128, 2 * own, 128), F32)],
+        ins,
+        [held(x) for x in ins] + [flat, pltpu.SemaphoreType.DMA((7,))],
         8,
         MIB,
         "prep",
-        small=range(7),
+        fetched=range(7),
     )
     b_blocks = gather_blocks(b_own, state_bits)
     low, unit, inv, mask, cot, c_own = call(
@@ -654,12 +759,13 @@
             ((rows, feats), BF16),
             ((2 * own, feats), BF16),
         ],
-        [x4, cot4, output_weight, vec, lengths],
-        [pltpu.VMEM((feats // 128, 2 * own, 128), F32)],
-        8,
+        [x4, cot4, output_weight, lengths, vec],
+        [held(x4), held(cot4), held(output_weight), pltpu.SMEM(lengths.shape, jnp.int32)]
+        + [flat, pltpu.SemaphoreType.DMA((10,))],
+        12,
         rows * feats * 20,
         "norm",
-        small=(2,),
+        fetched=range(4),
     )
     c_blocks = gather_blocks(c_own, state_bits)
     drive, end, win, cst = call(
@@ -677,15 +783,15 @@
         "project",
     )
     ends = gather_ends(end, state_bits)
-    glu_bits = state_bits + [parts]
-    glu_groups = [glu_bits[:1]] + [glu_bits[k : k + 2] for k in range(1, len(glu_bits), 2)]
-    glu_orders = stage_orders(glu_groups)
+    all_bits = state_bits + [parts]
+    all_groups = [all_bits[:1]] + [all_bits[k : k + 2] for k in range(1, len(all_bits), 2)]
+    all_orders = stage_orders(all_groups)
     glu_rows = feats // (2 * parts)
-    glu_outs = [
-        ((len(o), glu_rows, 2 * feats), BF16 if k == 0 else F32) for k, o in enumerate(glu_orders)
+    block_outs = lambda rows, width, orders: [
+        ((len(o), rows, width), BF16 if k == 0 else F32) for k, o in enumerate(orders)
     ]
     states, slow, cw, branch, d_glu, slope, *glu_parts = call(
-        functools.partial(mix_kernel, parts, own, group, glu_orders),
+        functools.partial(mix_kernel, parts, own, group, all_orders),
         [
             ((rows + SUB, 2 * channels), F32),
             ((rows, 2 * channels), BF16),
@@ -694,95 +800,135 @@
             ((rows, 2 * feats), BF16),
             ((rows, feats), F32),
         ]
-        + glu_outs,
+        + block_outs(glu_rows, 2 * feats, all_orders),
         [drive, end, cst, ends] + c_blocks + [unit, cot, mask, vec, glu_weight],
         [pltpu.VMEM((rows, feats), BF16), pltpu.VMEM((feats, 2 * feats), F32)],
         20,
         5 * full,
         "mix",
     )
-    glu_parts = halve(glu_parts, glu_groups[0])
-    state_groups = [[b] for b in state_bits]
-    pair_orders = stage_orders(state_groups)
-    pair_outs = [
-        ((len(o), 2 * own, feats), BF16 if k == 0 else F32) for k, o in enumerate(pair_orders)
-    ]
     d_pre, d_states, start, skip_sum, *out_parts = call(
-        functools.partial(back_kernel, own, group, pair_orders),
+        functools.partial(back_kernel, own, group, all_orders),
         [
             ((rows, feats), F32),
             ((rows, 2 * channels), F32),
             ((SUB, 2 * channels), F32),
             ((SUB, feats), F32),
         ]
-        + pair_outs,
+        + block_outs(own, feats, all_orders),
         [d_glu, slope, unit, vec, glu_weight, cw, slow, cst],
         [pltpu.VMEM((rows, feats), BF16), pltpu.VMEM((2 * channels, feats), F32)],
         16,
         4 * full,
         "back",
     )
-    starts = gather_ends(tie(start, glu_parts), state_bits)
-    for g in glu_groups[1:]:
-        glu_parts = halve(glu_parts, g)
-    glu_own = glu_parts[0][0]
-    out_parts = halve(out_parts, state_groups[0])
+    starts = gather_ends(start, state_bits)
     (out4,) = call(
         out_kernel,
         [(x4.shape, BF16)],
-        [tie(branch, start), x4],
-        [],
+        [x4, tie(branch, start)],
+        [held(x4), pltpu.SemaphoreType.DMA((4,))],
         8,
         MIB,
         "out",
-    )
+        fetched=(0,),
+    )
+    glu_parts = halve(glu_parts, all_groups[0], after=start)
+    out_parts = halve(out_parts, all_groups[0])
+    both = [jnp.concatenate(p, axis=-1) for p in zip(glu_parts, out_parts)]
+    state_groups = [[b] for b in state_bits]
+    pair_orders = stage_orders(state_groups)
     d_proj, channel_sums, *in_parts = call(
         functools.partial(adjoint_kernel, own, group, pair_orders),
-        [((rows, 2 * channels), BF16), ((SUB, 3 * channels), F32)] + pair_outs,
-        [tie(d_states, out4, out_parts), start, cst, starts, states, drive, low, mask],
+        [((rows, 2 * channels), BF16), ((SUB, 3 * channels), F32)]
+        + block_outs(2 * own, feats, pair_orders),
+        [tie(d_states, out4), start, cst, starts, states, drive, low, mask],
         [pltpu.VMEM((rows, 2 * channels), F32), pltpu.VMEM((2 * channels, feats), F32)],
         16,
         2 * full,
         "adjoint",
     )
+    for g in all_groups[1:]:
+        both = halve(both, g, after=channel_sums)
+    both = both[0][0]
     in_parts = halve(in_parts, state_groups[0])
-    d_proj = tie(d_proj, glu_own, in_parts)
-    grad4, feature_sums = call(
-        tokens_kernel,
-        [(cot4.shape, F32), ((SUB, 2 * feats), F32)],
-        [d_proj, win, d_pre, unit, inv, vec, cot4],
+    d_normed, sums = call(
+        normed_kernel,
+        [((rows, feats), F32), ((SUB, feats), F32)],
+        [d_proj, win, d_pre, unit, vec, channel_sums, skip_sum],
         [],
         12,
         full,
+        "normed",
+    )
+    for g in state_groups[1:]:
+        keep = in_parts[1:]
+        own_sums = two_parts(sums)
+        send = jnp.concatenate([in_parts[0].astype(BF16).reshape(-1, feats)] + own_sums, axis=0)
+        got = exchange(send, g[0])
+        in_parts, off = [], 0
+        for p in keep:
+            n = p.shape[0] * p.shape[1]
+            in_parts.append(p + got[off : off + n].reshape(p.shape).astype(F32))
+            off += n
+        sums = sum_of(own_sums) + sum_of([got[off : off + SUB], got[off + SUB :]])
+        send = in_parts[0]
+    total = in_parts[0][0]
+    (grad4,) = call(
+        tokens_kernel,
+        [(cot4.shape, F32)],
+        [cot4, tie(d_normed, both, send), unit, inv, vec],
+        [held(cot4), pltpu.SemaphoreType.DMA((4,))],
+        12,
+        full,
         "tokens",
-    )
-    sums = jnp.concatenate([channel_sums, feature_sums, skip_sum], axis=1)
-    sums = jnp.sum(sums, axis=0, keepdims=True)
-    for g in state_groups[1:]:
-        out_parts = halve(out_parts, g)
-        in_parts = halve(in_parts, g)
-    grad_out, grad_in = out_parts[0][0], in_parts[0][0]
-    for m in state_bits:
-        sums = double_f32(sums, m)
+        fetched=(0,),
+    )
     for m in seq_masks:
-        grad_out = double(grad_out, m)
-        grad_in = double(grad_in, m)
-        sums = double_f32(sums, m)
-    sums = sums[0]
+        low_total = rounded(total).astype(BF16)
+        own_sums = two_parts(sums)
+        got = exchange(jnp.concatenate([low_total] + own_sums, axis=0), m)
+        total = low_total.astype(F32) + got[: 2 * own].astype(F32)
+        got_sums = [got[2 * own : 2 * own + SUB], got[2 * own + SUB :]]
+        sums = sum_of(own_sums) + sum_of(got_sums)
+    grad_in, feature_grads, grad_rate, grad_angle, grad_level = call(
+        finish_kernel,
+        [((own, 2, feats), F32), ((3, feats), F32)] + [((1, own), F32)] * 3,
+        [low_total, got, sums, exchange(sums, state_bits[0]), vec],
+        [flat],
+        8,
+        MIB,
+        "finish",
+    )
 
     for m in seq_masks[1:]:
-        glu_own = double(glu_own, m)
-    held = {0: lax.reduce_precision(glu_own, 8, 7).astype(BF16)}
-    for g in reversed(glu_groups[1:]):
-        for m in list(held):
+        both = double(both, m)
+    both = rounded(both).astype(BF16)
+    blocks = {0: both[:, : 2 * feats]}
+    for g in reversed(all_groups[1:]):
+        for m in list(blocks):
             for p in submasks(g):
-                held[m ^ p] = exchange(held[m], p)
-    rest = [m for m in held if m]
-    arrays = [held[0][None], jnp.stack([held[m] for m in rest])]
+                if m == 0 and p == parts:
+                    got = exchange(both, p)
+                    blocks[p] = got[:, : 2 * feats]
+                    other_half = got[:, 2 * feats :]
+                else:
+                    blocks[m ^ p] = exchange(blocks[m], p)
+    rest = [m for m in blocks if m]
+    arrays = [blocks[0][None], jnp.stack([blocks[m] for m in rest])]
     masks = [[0], rest]
-    for p in submasks(glu_groups[0]):
+    for p in submasks(all_groups[0]):
         arrays += [exchange(a, p) for a in arrays[:2]]
         masks += [[m ^ p for m in ms] for ms in masks[:2]]
+    (grad_out,) = call(
+        halves_kernel,
+        [((own, 2, feats), F32)],
+        [both[:, 2 * feats :], other_half],
+        [flat],
+        8,
+        MIB,
+        "halves",
+    )
     (grad_glu,) = call(
         functools.partial(place_kernel, masks, parts),
         [((feats, 2 * feats), F32)],
@@ -792,30 +938,17 @@
         feats * feats,
         "place",
     )
-    sum_re, sum_im, gain_sum = (
-        lax.dynamic_slice(sums, (k * channels + me * own,), (own,)) for k in range(3)
-    )
-    base = 3 * channels
-    grad_gain, grad_bias, grad_skip = (
-        sums[base + k * feats : base + (k + 1) * feats] for k in range(3)
-    )
-    decay = jnp.exp(log_rate)
-    angle = jnp.exp(log_angle)
-    pole_re = jnp.exp(-decay) * jnp.cos(angle)
-    pole_im = jnp.exp(-decay) * jnp.sin(angle)
-    grad_rate = -decay * (sum_re * pole_re + sum_im * pole_im)
-    grad_angle = angle * (sum_im * pole_re - sum_re * pole_im)
     return (
         out4.reshape(tokens.shape),
         grad4.reshape(tokens.shape),
-        grad_gain,
-        grad_bias,
-        grad_in.reshape(2, own, feats).transpose(2, 1, 0),
-        grad_out.reshape(2, own, feats).transpose(1, 0, 2),
-        grad_rate,
-        grad_angle,
-        gain_sum,
-        grad_skip,
+        feature_grads[0],
+        feature_grads[1],
+        grad_in.transpose(2, 0, 1),
+        grad_out,
+        grad_rate.reshape(own),
+        grad_angle.reshape(own),
+        grad_level.reshape(own),
+        feature_grads[2],
         grad_glu,
     )
 

time: 123 us -> 107 us (0.87)
  the two profiles are of different devices: /device:TPU:0 before, /device:TPU:17 now
where the time goes in v2:
time: 107 us
  waiting for transfers between devices  38.7 us (36%)
  Pallas kernels  28.9 us (27%)
  starting transfers between devices  28.2 us (26%)
  local copies, waits for them, and re-layouts  9.57 us (9%)
    ppermute x28, waiting for transfers between devices, exchange(): lax.ppermute(x, ('seq', 'state'), [(i, i ^ mask) for i in range(count)])  38.7 us
    pallas_call x12, Pallas kernels, call(): pl.pallas_call(body, out_shape=[jax.ShapeDtypeStruct(s, d) for s, d in ou...  28.9 us
    ppermute x28, starting transfers between devices, exchange(): lax.ppermute(x, ('seq', 'state'), [(i, i ^ mask) for i in range(count)])  28.2 us
    unnamed x28, local copies, waits for them, and re-layouts  8.93 us
  transfers between devices with their start and end apart: 28, of which 13 were waited for; matrix products, arithmetic and copies ran while one was open for 1% of the time, Pallas kernels for 13%

profile of v2, /device:TPU:17, one launch (start us, length us, event | category | flops | bytes accessed | tf_op | source)
XLA Modules:
  0.0 107.2 jit_solution(11101053006369228374)
XLA Ops:
  0.7 0.9 copy-done.6
  1.6 0.7 copy-done.7
  2.2 0.7 copy-done.8
  2.9 0.7 copy-done.9
  3.6 0.7 copy-done.10
  4.3 0.7 copy-done.11
  4.9 0.7 copy-done.12
  5.6 0.4 prep.1
  6.0 1.3 %collective-permute-start.1 = (bf16[144,512]{1,0:T(8,128)(2,1)S(1)}, bf16[144,512]{1,0:T(8,128)(2,1)S(1)}, u32[]{:S(2)}, u32[]{:S(2)}) collective-permute-start(bf16[144,512]{1,0:T(8,128)(2,1)S(1)} %get-tuple-element.65.refs_0_), channel_id=1, source_target_pairs={{0,2},{1,3},{2,0},{3,1},{4,6},{5,7},{6,4},{7,5},{8,10},{9,11},{10,... | collective-permute-start | bytes 442376 | tf_op jit(solution)/shard_map/ppermute | solution.py:629
  7.3 1.0 collective-permute-start
  8.3 2.5 %collective-permute-done.1.refs_2_ = bf16[144,512]{1,0:T(8,128)(2,1)S(1)} collective-permute-done((bf16[144,512]{1,0:T(8,128)(2,1)S(1)}, bf16[144,512]{1,0:T(8,128)(2,1)S(1)}, u32[]{:S(2)}, u32[]{:S(2)}) %collective-permute-start.1) | collective-permute-done | bytes 147488 | tf_op jit(solution)/shard_map/ppermute | solution.py:629
  10.8 1.5 %collective-permute-start.2 = (bf16[144,512]{1,0:T(8,128)(2,1)S(1)}, bf16[144,512]{1,0:T(8,128)(2,1)S(1)}, u32[]{:S(2)}, u32[]{:S(2)}) collective-permute-start(bf16[144,512]{1,0:T(8,128)(2,1)S(1)} %collective-permute-done.1.refs_2_), channel_id=1, source_target_pairs={{0,1},{1,0},{2,3},{3,2},{4,5},{5,4},{6,7},{7,6},{8,9},{9,8},{10,11... | collective-permute-start | bytes 442376 | tf_op jit(solution)/shard_map/ppermute | solution.py:629
  12.4 1.2 %copy-done = bf16[512,2,512]{2,1,0:T(2,128)(2,1)S(1)} copy-done((bf16[512,2,512]{2,1,0:T(2,128)(2,1)S(1)}, bf16[512,2,512]{2,1,0:T(2,128)(2,1)}, u32[]{:S(2)}) %copy-start) | copy-done | bytes 1048600
  13.6 1.2 %copy-done.2 = bf16[512,2,512]{2,1,0:T(2,128)(2,1)S(1)} copy-done((bf16[512,2,512]{2,1,0:T(2,128)(2,1)S(1)}, bf16[512,2,512]{2,1,0:T(2,128)(2,1)}, u32[]{:S(2)}) %copy-start.2) | copy-done | bytes 1048600
  14.8 0.9 copy-done.5
  15.7 0.7 copy-done.13
  16.4 4.1 %norm.1 = (bf16[1024,512]{1,0:T(8,128)(2,1)S(1)}, f32[1024,512]{1,0:T(8,128)S(1)}, f32[1024,128]{1,0:T(8,128)S(1)}, f32[1024,128]{1,0:T(8,128)S(1)}, bf16[1024,5...) custom-call(bf16[4,128,2,512]{3,2,1,0:T(2,128)(2,1)S(1)} %bitcast.57, bf16[4,128,2,512]{3,2,1,0:T(2,128)(2,1)S(1)} %bitcast.55, ...), custom_call_target="tpu_custom_call" | custom-call | flops 10485760 | bytes 4194304 | tf_op jit(solution)/shard_map/norm/pallas_call | solution.py:67
  20.5 1.9 %project.1 = (f32[1024,512]{1,0:T(8,128)S(1)}, f32[8,512]{1,0:T(8,128)S(1)}, bf16[512,512]{1,0:T(8,128)(2,1)S(1)}, f32[8,512]{1,0:T(8,128)S(1)}) custom-call(bf16[1024,512]{1,0:T(8,128)(2,1)S(1)} %get-tuple-element.63.low_ref.refs_6_, f32[1024,128]{1,0:T(8,128)S(1)} %get-tuple-element.64.mask_ref.refs_10_.refs_7_, ...), custom_call_target="tpu_custom_call" | custom-call | flops 536870912 | bytes 4194304 | tf_op jit(solution)/shard_map/project/pallas_call | solution.py:67
  22.4 1.3 %collective-permute-start.3 = (f32[1,8,512]{2,1,0:T(8,128)S(1)}, f32[1,8,512]{2,1,0:T(8,128)S(1)}, u32[]{:S(2)}, u32[]{:S(2)}) collective-permute-start(f32[1,8,512]{2,1,0:T(8,128)S(1)} %bitcast.64), channel_id=1, source_target_pairs={{0,2},{1,3},{2,0},{3,1},{4,6},{5,7},{6,4},{7,5},{8,10},{9,11},{10,... | collective-permute-start | bytes 49160 | tf_op jit(solution)/shard_map/ppermute | solution.py:629
  23.6 0.3 collective-permute-start.6
  23.9 1.1 %collective-permute-done.3 = f32[1,8,512]{2,1,0:T(8,128)S(1)} collective-permute-done((f32[1,8,512]{2,1,0:T(8,128)S(1)}, f32[1,8,512]{2,1,0:T(8,128)S(1)}, u32[]{:S(2)}, u32[]{:S(2)}) %collective-permute-start.3) | collective-permute-done | bytes 16416 | tf_op jit(solution)/shard_map/ppermute | solution.py:629
  25.0 1.2 %collective-permute-start.4 = (f32[2,8,512]{2,1,0:T(8,128)S(1)}, f32[2,8,512]{2,1,0:T(8,128)S(1)}, u32[]{:S(2)}, u32[]{:S(2)}) collective-permute-start(f32[2,8,512]{2,1,0:T(8,128)S(1)} %get-tuple-element.136), channel_id=1, source_target_pairs={{0,1},{1,0},{2,3},{3,2},{4,5},{5,4},{6,7},{7,6},{8,9},{9,8},{10,11... | collective-permute-start | bytes 98312 | tf_op jit(solution)/shard_map/ppermute | solution.py:629
  26.2 2.2 %collective-permute-done.6.refs_6_ = bf16[128,512]{1,0:T(8,128)(2,1)S(1)} collective-permute-done((bf16[128,512]{1,0:T(8,128)(2,1)S(1)}, bf16[128,512]{1,0:T(8,128)(2,1)S(1)}, u32[]{:S(2)}, u32[]{:S(2)}) %collective-permute-start.6) | collective-permute-done | bytes 131104 | tf_op jit(solution)/shard_map/ppermute | solution.py:629
  28.4 1.1 %collective-permute-start.7 = (bf16[128,512]{1,0:T(8,128)(2,1)S(1)}, bf16[128,512]{1,0:T(8,128)(2,1)S(1)}, u32[]{:S(2)}, u32[]{:S(2)}) collective-permute-start(bf16[128,512]{1,0:T(8,128)(2,1)S(1)} %collective-permute-done.6.refs_6_), channel_id=1, source_target_pairs={{0,1},{1,0},{2,3},{3,2},{4,5},{5,4},{6,7},{7,6},{8,9},{9,8},{10,11... | collective-permute-start | bytes 393224 | tf_op jit(solution)/shard_map/ppermute | solution.py:629
  29.6 0.9 collective-permute-done.7.refs_7_
  30.5 6.9 %mix.1 = (f32[1032,512]{1,0:T(8,128)S(1)}, bf16[1024,512]{1,0:T(8,128)(2,1)S(1)}, bf16[512,512]{1,0:T(8,128)(2,1)S(1)}, f32[1024,512]{1,0:T(8,128)S(1)}, bf16[10...) custom-call(f32[1024,512]{1,0:T(8,128)S(1)} %get-tuple-element.66.re, ...), custom_call_target="tpu_custom_call" | custom-call | flops 2684354560 | bytes 4194304 | tf_op jit(solution)/shard_map/mix/pallas_call | solution.py:67
  37.4 4.3 %back.1 = (f32[1024,512]{1,0:T(8,128)S(1)}, f32[1024,512]{1,0:T(8,128)S(1)}, f32[8,512]{1,0:T(8,128)S(1)}, f32[8,512]{1,0:T(8,128)S(1)}, bf16[4,64,512]{2,1,0:T(...) custom-call(bf16[1024,1024]{1,0:T(8,128)(2,1)S(1)} %get-tuple-elemen, ...), custom_call_target="tpu_custom_call" | custom-call | flops 2147483648 | bytes 4194304 | tf_op jit(solution)/shard_map/back/pallas_call | solution.py:67
  41.8 0.5 collective-permute-start.8
  42.3 2.2 %collective-permute-done.8 = f32[1,8,512]{2,1,0:T(8,128)S(1)} collective-permute-done((f32[1,8,512]{2,1,0:T(8,128)S(1)}, f32[1,8,512]{2,1,0:T(8,128)S(1)}, u32[]{:S(2)}, u32[]{:S(2)}) %collective-permute-start.8) | collective-permute-done | bytes 16416 | tf_op jit(solution)/shard_map/ppermute | solution.py:629
  44.4 1.5 %collective-permute-start.9 = (f32[2,8,512]{2,1,0:T(8,128)S(1)}, f32[2,8,512]{2,1,0:T(8,128)S(1)}, u32[]{:S(2)}, u32[]{:S(2)}) collective-permute-start(f32[2,8,512]{2,1,0:T(8,128)S(1)} %get-tuple-element.134), channel_id=1, source_target_pairs={{0,1},{1,0},{2,3},{3,2},{4,5},{5,4},{6,7},{7,6},{8,9},{9,8},{10,11... | collective-permute-start | bytes 98312 | tf_op jit(solution)/shard_map/ppermute | solution.py:629
  46.0 2.1 %out.1 = bf16[4,128,2,512]{3,2,1,0:T(2,128)(2,1)} custom-call(bf16[4,128,2,512]{3,2,1,0:T(2,128)(2,1)S(1)} %bitcast.58, f32[1024,512]{1,0:T(8,128)S(1)} %get-tuple-element.78.branch_ref), custom_call_target="tpu_custom_call" | custom-call | flops 1048576 | bytes 4194304 | tf_op jit(solution)/shard_map/out/pallas_call | solution.py:67
  48.1 0.5 collective-permute-start.11
  48.7 2.1 %adjoint.1 = (bf16[1024,512]{1,0:T(8,128)(2,1)S(1)}, f32[8,768]{1,0:T(8,128)S(1)}, bf16[2,128,512]{2,1,0:T(8,128)(2,1)S(1)}, f32[1,128,512]{2,1,0:T(8,128)S(1)}, f32[1,128,512]{2,1,0:T(8,128)S(1)}) custom-call(f32[1024,512]{1,0:T(8,128)S(1)} %get-tuple-element.80.refs_0_, f32[8,512]{1,0:T(8,128)S(1)} %get-tuple-element.77.refs_1_, ...), custom_call_target="tpu_custom_call" | custom-call | flops 1073741824 | bytes 4194304 | tf_op jit(solution)/shard_map/adjoint/pallas_call | solution.py:67
  50.8 0.1 collective-permute-start.15
  50.9 1.3 %normed.1 = (f32[1024,512]{1,0:T(8,128)S(1)}, f32[8,512]{1,0:T(8,128)S(1)}) custom-call(bf16[1024,512]{1,0:T(8,128)(2,1)S(1)} %get-tuple-element.82.dproj_ref, bf16[512,512]{1,0:T(8,128)(2,1)S(1)} %get-tuple-element.83.win_ref, f32[1024,512]{1,0:T(8,128)S(1)} %get-tuple-element.84.dpre_ref, f32[1024,512]{1,0:T(8,128)S(1)} %get-tuple-element.70.refs_8_.refs_2_.unit_ref, ...), custom_call_target="tpu_custom_call" | custom-call | flops 536870912 | bytes 4194304 | tf_op jit(solution)/shard_map/normed/pallas_call | solution.py:67
  52.2 0.2 collective-permute-done.15
  52.4 0.5 collective-permute-start.16
  53.0 4.7 %collective-permute-done.16 = bf16[144,512]{1,0:T(8,128)(2,1)S(1)} collective-permute-done((bf16[144,512]{1,0:T(8,128)(2,1)S(1)}, bf16[144,512]{1,0:T(8,128)(2,1)S(1)}, u32[]{:S(2)}, u32[]{:S(2)}) %collective-permute-start.16) | collective-permute-done | bytes 147488 | tf_op jit(solution)/shard_map/ppermute | solution.py:629
  57.8 1.3 %collective-permute-start.17 = (bf16[144,512]{1,0:T(8,128)(2,1)S(1)}, bf16[144,512]{1,0:T(8,128)(2,1)S(1)}, u32[]{:S(2)}, u32[]{:S(2)}) collective-permute-start(bf16[144,512]{1,0:T(8,128)(2,1)S(1)} %pad_maximum_fusion.5), channel_id=1, source_target_pairs={{0,4},{1,5},{2,6},{3,7},{4,0},{5,1},{6,2},{7,3},{8,12},{9,13},{10,... | collective-permute-start | bytes 442376 | tf_op jit(solution)/shard_map/ppermute | solution.py:629
  59.1 0.1 convert_add_fusion.1
  59.2 0.5 collective-permute-start.12
  59.8 0.3 collective-permute-start.13
  60.1 2.1 %collective-permute-start.14 = (bf16[1,64,1536]{2,1,0:T(8,128)(2,1)S(1)}, bf16[1,64,1536]{2,1,0:T(8,128)(2,1)S(1)}, u32[]{:S(2)}, u32[]{:S(2)}) collective-permute-start(bf16[1,64,1536]{2,1,0:T(8,128)(2,1)S(1)} %pad_maximum_fusion.3), channel_id=1, source_target_pairs={{0,6},{1,7},{2,4},{3,5},{4,2},{5,3},{6,0},{7,1},{8,14},{9,15},{10,... | collective-permute-start | bytes 589832 | tf_op jit(solution)/shard_map/ppermute | solution.py:629
  62.2 1.4 %collective-permute-start.18 = (bf16[144,512]{1,0:T(8,128)(2,1)S(1)}, bf16[144,512]{1,0:T(8,128)(2,1)S(1)}, u32[]{:S(2)}, u32[]{:S(2)}) collective-permute-start(bf16[144,512]{1,0:T(8,128)(2,1)S(1)} %pad_maximum_fusion.6), channel_id=1, source_target_pairs={{0,8},{1,9},{2,10},{3,11},{4,12},{5,13},{6,14},{7,15},{8,0},{9,1},... | collective-permute-start | bytes 442376 | tf_op jit(solution)/shard_map/ppermute | solution.py:629
  63.6 0.7 collective-permute-done.12
  64.3 6.6 %collective-permute-done.13 = bf16[1,64,1536]{2,1,0:T(8,128)(2,1)S(1)} collective-permute-done((bf16[1,64,1536]{2,1,0:T(8,128)(2,1)S(1)}, bf16[1,64,1536]{2,1,0:T(8,128)(2,1)S(1)}, u32[]{:S(2)}, u32[]{:S(2)}) %collective-permute-start.13) | collective-permute-done | bytes 196640 | tf_op jit(solution)/shard_map/ppermute | solution.py:629
  70.9 0.1 reduce-precision_convert_fusion.2
  71.0 1.4 %collective-permute-start.21 = (bf16[64,1536]{1,0:T(8,128)(2,1)S(1)}, bf16[64,1536]{1,0:T(8,128)(2,1)S(1)}, u32[]{:S(2)}, u32[]{:S(2)}) collective-permute-start(bf16[64,1536]{1,0:T(8,128)(2,1)S(1)} %reduce-precision_convert_fusion.2), channel_id=1, source_target_pairs={{0,8},{1,9},{2,10},{3,11},{4,12},{5,13},{6,14},{7,15},{8,0},{9,1},... | collective-permute-start | bytes 589832 | tf_op jit(solution)/shard_map/ppermute | solution.py:629
  72.4 3.2 %collective-permute-done.21 = bf16[64,1536]{1,0:T(8,128)(2,1)S(1)} collective-permute-done((bf16[64,1536]{1,0:T(8,128)(2,1)S(1)}, bf16[64,1536]{1,0:T(8,128)(2,1)S(1)}, u32[]{:S(2)}, u32[]{:S(2)}) %collective-permute-start.21) | collective-permute-done | bytes 196640 | tf_op jit(solution)/shard_map/ppermute | solution.py:629
  75.6 0.2 collective-permute-start.22
  75.9 1.4 %collective-permute-start.19 = (bf16[144,512]{1,0:T(8,128)(2,1)S(1)}, bf16[144,512]{1,0:T(8,128)(2,1)S(1)}, u32[]{:S(2)}, u32[]{:S(2)}) collective-permute-start(bf16[144,512]{1,0:T(8,128)(2,1)S(1)} %pad_maximum_fusion.7), channel_id=1, source_target_pairs={{0,24},{1,25},{2,26},{3,27},{4,28},{5,29},{6,30},{7,31},{8,16},{9,... | collective-permute-start | bytes 442376 | tf_op jit(solution)/shard_map/ppermute | solution.py:629
  77.3 10.7 %collective-permute-done.22 = bf16[64,1536]{1,0:T(8,128)(2,1)S(1)} collective-permute-done((bf16[64,1536]{1,0:T(8,128)(2,1)S(1)}, bf16[64,1536]{1,0:T(8,128)(2,1)S(1)}, u32[]{:S(2)}, u32[]{:S(2)}) %collective-permute-start.22) | collective-permute-done | bytes 196640 | tf_op jit(solution)/shard_map/ppermute | solution.py:629
  88.1 1.0 collective-permute-start.24
  89.1 1.7 %collective-permute-start.25 = (bf16[64,1024]{1,0:T(8,128)(2,1)S(1)}, bf16[64,1024]{1,0:T(8,128)(2,1)S(1)}, u32[]{:S(2)}, u32[]{:S(2)}) collective-permute-start(bf16[64,1024]{1,0:T(8,128)(2,1)S(1)} %get-tuple-element.125), channel_id=1, source_target_pairs={{0,6},{1,7},{2,4},{3,5},{4,2},{5,3},{6,0},{7,1},{8,14},{9,15},{10,... | collective-permute-start | bytes 393224 | tf_op jit(solution)/shard_map/ppermute | solution.py:629
  90.8 2.1 %collective-permute-done.23 = bf16[64,1536]{1,0:T(8,128)(2,1)S(1)} collective-permute-done((bf16[64,1536]{1,0:T(8,128)(2,1)S(1)}, bf16[64,1536]{1,0:T(8,128)(2,1)S(1)}, u32[]{:S(2)}, u32[]{:S(2)}) %collective-permute-start.23) | collective-permute-done | bytes 196640 | tf_op jit(solution)/shard_map/ppermute | solution.py:629
  92.9 1.7 %collective-permute-done.25 = bf16[64,1024]{1,0:T(8,128)(2,1)S(1)} collective-permute-done((bf16[64,1024]{1,0:T(8,128)(2,1)S(1)}, bf16[64,1024]{1,0:T(8,128)(2,1)S(1)}, u32[]{:S(2)}, u32[]{:S(2)}) %collective-permute-start.25) | collective-permute-done | bytes 131104 | tf_op jit(solution)/shard_map/ppermute | solution.py:629
  94.6 5.5 %collective-permute-start.27 = (bf16[3,64,1024]{2,1,0:T(8,128)(2,1)S(1)}, bf16[3,64,1024]{2,1,0:T(8,128)(2,1)S(1)}, u32[]{:S(2)}, u32[]{:S(2)}) collective-permute-start(bf16[3,64,1024]{2,1,0:T(8,128)(2,1)S(1)} %pad_maximum_fusion.refs_1_), channel_id=1, source_target_pairs={{0,1},{1,0},{2,3},{3,2},{4,5},{5,4},{6,7},{7,6},{8,9},{9,8},{10,11... | collective-permute-start | bytes 1179656 | tf_op jit(solution)/shard_map/ppermute | solution.py:629
  100.1 0.1 collective-permute-start.20
  100.2 2.8 %tokens.1 = f32[4,128,2,512]{3,2,1,0:T(2,128)} custom-call(bf16[4,128,2,512]{3,2,1,0:T(2,128)(2,1)S(1)} %bitcast.56, f32[1024,512]{1,0:T(8,128)S(1)} %get-tuple-element.106.dnorm_ref, f32[1024,512]{1,0:T(8,128)S(1)} %get-tuple-element.70.refs_8_.refs_2_.unit_ref, f32[1024,128]{1,0:T(8,128)S(1)} %get-tuple-element.107.inv_ref, ...), custom_call_target="tpu_custom_call" | custom-call | flops 536870912 | bytes 4194304 | tf_op jit(solution)/shard_map/tokens/pallas_call | solution.py:67
  103.0 0.8 finish.1
  103.8 0.5 collective-permute-start.26
  104.3 0.6 fusion.19
  104.9 0.8 halves.1
  105.7 1.5 %place.1 = f32[512,1024]{1,0:T(8,128)} custom-call(bf16[1,64,1024]{2,1,0:T(8,128)(2,1)S(1)} %get-tuple-element.126.refs_0_, bf16[3,64,1024]{2,1,0:T(8,128)(2,1)S(1)} %pad_maximum_fusion.refs_1_, bf16[1,64,1024]{2,1,0:T(8,128)(2,1)S(1)} %collective-permute-done.26.refs_2_, bf16[3,64,1024]{2,1,0:T(8,128)(2,1)S(1)} %collective-permute-done.27.refs_3_), custom_call_target="tpu_custom_call" | custom-call | flops 262144 | bytes 4194304 | tf_op jit(solution)/shard_map/place/pallas_call | solution.py:67
  (65 shorter events, 0.9 us)
Async XLA Ops:
  0.6 0.9 copy-start.6
  1.6 0.7 copy-start.7
  2.2 0.7 copy-start.8
  2.9 0.7 copy-start.9
  3.6 0.7 copy-start.10
  4.3 0.7 copy-start.11
  4.9 0.7 copy-start.12
  6.0 4.8 %collective-permute-start.1 = (bf16[144,512]{1,0:T(8,128)(2,1)S(1)}, bf16[144,512]{1,0:T(8,128)(2,1)S(1)}, u32[]{:S(2)}, u32[]{:S(2)}) collective-permute-start(bf16[144,512]{1,0:T(8,128)(2,1)S(1)} %get-tuple-element.65.refs_0_), channel_id=1, source_target_pairs={{0,2},{1,3},{2,0},{3,1},{4,6},{5,7},{6,4},{7,5},{8,10},{9,11},{10,... | collective-permute-start | bytes 442376 | tf_op jit(solution)/shard_map/ppermute | solution.py:629
  7.3 13.1 %collective-permute-start = (bf16[144,512]{1,0:T(8,128)(2,1)S(1)}, bf16[144,512]{1,0:T(8,128)(2,1)S(1)}, u32[]{:S(2)}, u32[]{:S(2)}) collective-permute-start(bf16[144,512]{1,0:T(8,128)(2,1)S(1)} %get-tuple-element.65.refs_0_), channel_id=1, source_target_pairs={{0,1},{1,0},{2,3},{3,2},{4,5},{5,4},{6,7},{7,6},{8,9},{9,8},{10,11... | collective-permute-start | bytes 442376 | tf_op jit(solution)/shard_map/ppermute | solution.py:629
  10.8 9.6 %collective-permute-start.2 = (bf16[144,512]{1,0:T(8,128)(2,1)S(1)}, bf16[144,512]{1,0:T(8,128)(2,1)S(1)}, u32[]{:S(2)}, u32[]{:S(2)}) collective-permute-start(bf16[144,512]{1,0:T(8,128)(2,1)S(1)} %collective-permute-done.1.refs_2_), channel_id=1, source_target_pairs={{0,1},{1,0},{2,3},{3,2},{4,5},{5,4},{6,7},{7,6},{8,9},{9,8},{10,11... | collective-permute-start | bytes 442376 | tf_op jit(solution)/shard_map/ppermute | solution.py:629
  12.3 1.2 %copy-start = (bf16[512,2,512]{2,1,0:T(2,128)(2,1)S(1)}, bf16[512,2,512]{2,1,0:T(2,128)(2,1)}, u32[]{:S(2)}) copy-start(bf16[512,2,512]{2,1,0:T(2,128)(2,1)} %param.23) | copy-start | bytes 3145732
  13.6 1.2 %copy-start.2 = (bf16[512,2,512]{2,1,0:T(2,128)(2,1)S(1)}, bf16[512,2,512]{2,1,0:T(2,128)(2,1)}, u32[]{:S(2)}) copy-start(bf16[512,2,512]{2,1,0:T(2,128)(2,1)} %param.12) | copy-start | bytes 3145732
  14.8 0.9 copy-start.5
  15.7 0.7 copy-start.13
  16.4 14.2 %copy-start.4 = (bf16[512,1024]{1,0:T(8,128)(2,1)S(1)}, bf16[512,1024]{1,0:T(8,128)(2,1)}, u32[]{:S(2)}) copy-start(bf16[512,1024]{1,0:T(8,128)(2,1)} %refs_4_.1) | copy-start | bytes 3145732
  22.4 2.7 %collective-permute-start.3 = (f32[1,8,512]{2,1,0:T(8,128)S(1)}, f32[1,8,512]{2,1,0:T(8,128)S(1)}, u32[]{:S(2)}, u32[]{:S(2)}) collective-permute-start(f32[1,8,512]{2,1,0:T(8,128)S(1)} %bitcast.64), channel_id=1, source_target_pairs={{0,2},{1,3},{2,0},{3,1},{4,6},{5,7},{6,4},{7,5},{8,10},{9,11},{10,... | collective-permute-start | bytes 49160 | tf_op jit(solution)/shard_map/ppermute | solution.py:629
  23.6 4.8 %collective-permute-start.6 = (bf16[128,512]{1,0:T(8,128)(2,1)S(1)}, bf16[128,512]{1,0:T(8,128)(2,1)S(1)}, u32[]{:S(2)}, u32[]{:S(2)}) collective-permute-start(bf16[128,512]{1,0:T(8,128)(2,1)S(1)} %get-tuple-element.69.refs_4_), channel_id=1, source_target_pairs={{0,2},{1,3},{2,0},{3,1},{4,6},{5,7},{6,4},{7,5},{8,10},{9,11},{10,... | collective-permute-start | bytes 393224 | tf_op jit(solution)/shard_map/ppermute | solution.py:629
  25.0 4.5 %collective-permute-start.4 = (f32[2,8,512]{2,1,0:T(8,128)S(1)}, f32[2,8,512]{2,1,0:T(8,128)S(1)}, u32[]{:S(2)}, u32[]{:S(2)}) collective-permute-start(f32[2,8,512]{2,1,0:T(8,128)S(1)} %get-tuple-element.136), channel_id=1, source_target_pairs={{0,1},{1,0},{2,3},{3,2},{4,5},{5,4},{6,7},{7,6},{8,9},{9,8},{10,11... | collective-permute-start | bytes 98312 | tf_op jit(solution)/shard_map/ppermute | solution.py:629
  26.2 3.4 %collective-permute-start.5 = (bf16[128,512]{1,0:T(8,128)(2,1)S(1)}, bf16[128,512]{1,0:T(8,128)(2,1)S(1)}, u32[]{:S(2)}, u32[]{:S(2)}) collective-permute-start(bf16[128,512]{1,0:T(8,128)(2,1)S(1)} %get-tuple-element.69.refs_4_), channel_id=1, source_target_pairs={{0,1},{1,0},{2,3},{3,2},{4,5},{5,4},{6,7},{7,6},{8,9},{9,8},{10,11... | collective-permute-start | bytes 393224 | tf_op jit(solution)/shard_map/ppermute | solution.py:629
  28.4 2.1 %collective-permute-start.7 = (bf16[128,512]{1,0:T(8,128)(2,1)S(1)}, bf16[128,512]{1,0:T(8,128)(2,1)S(1)}, u32[]{:S(2)}, u32[]{:S(2)}) collective-permute-start(bf16[128,512]{1,0:T(8,128)(2,1)S(1)} %collective-permute-done.6.refs_6_), channel_id=1, source_target_pairs={{0,1},{1,0},{2,3},{3,2},{4,5},{5,4},{6,7},{7,6},{8,9},{9,8},{10,11... | collective-permute-start | bytes 393224 | tf_op jit(solution)/shard_map/ppermute | solution.py:629
  37.4 8.6 %copy-start.3 = (bf16[512,2,512]{2,1,0:T(2,128)(2,1)S(1)}, bf16[512,2,512]{2,1,0:T(2,128)(2,1)}, u32[]{:S(2)}) copy-start(bf16[512,2,512]{2,1,0:T(2,128)(2,1)} %param.12) | copy-start | bytes 3145732
  41.8 2.7 %collective-permute-start.8 = (f32[1,8,512]{2,1,0:T(8,128)S(1)}, f32[1,8,512]{2,1,0:T(8,128)S(1)}, u32[]{:S(2)}, u32[]{:S(2)}) collective-permute-start(f32[1,8,512]{2,1,0:T(8,128)S(1)} %bitcast.61), channel_id=1, source_target_pairs={{0,2},{1,3},{2,0},{3,1},{4,6},{5,7},{6,4},{7,5},{8,10},{9,11},{10,... | collective-permute-start | bytes 49160 | tf_op jit(solution)/shard_map/ppermute | solution.py:629
  44.4 4.2 %collective-permute-start.9 = (f32[2,8,512]{2,1,0:T(8,128)S(1)}, f32[2,8,512]{2,1,0:T(8,128)S(1)}, u32[]{:S(2)}, u32[]{:S(2)}) collective-permute-start(f32[2,8,512]{2,1,0:T(8,128)S(1)} %get-tuple-element.134), channel_id=1, source_target_pairs={{0,1},{1,0},{2,3},{3,2},{4,5},{5,4},{6,7},{7,6},{8,9},{9,8},{10,11... | collective-permute-start | bytes 98312 | tf_op jit(solution)/shard_map/ppermute | solution.py:629
  45.9 13.2 %collective-permute-start.10 = (bf16[4,64,1024]{2,1,0:T(8,128)(2,1)S(1)}, bf16[4,64,1024]{2,1,0:T(8,128)(2,1)S(1)}, u32[]{:S(2)}, u32[]{:S(2)}) collective-permute-start(bf16[4,64,1024]{2,1,0:T(8,128)(2,1)S(1)} %get-tuple-element.89), channel_id=1, source_target_pairs={{0,1},{1,0},{2,3},{3,2},{4,5},{5,4},{6,7},{7,6},{8,9},{9,8},{10,11... | collective-permute-start | bytes 1572872 | tf_op jit(solution)/shard_map/ppermute | solution.py:629
  48.1 4.8 %collective-permute-start.11 = (bf16[4,64,512]{2,1,0:T(8,128)(2,1)S(1)}, bf16[4,64,512]{2,1,0:T(8,128)(2,1)S(1)}, u32[]{:S(2)}, u32[]{:S(2)}) collective-permute-start(bf16[4,64,512]{2,1,0:T(8,128)(2,1)S(1)} %get-tuple-element.92), channel_id=1, source_target_pairs={{0,1},{1,0},{2,3},{3,2},{4,5},{5,4},{6,7},{7,6},{8,9},{9,8},{10,11... | collective-permute-start | bytes 786440 | tf_op jit(solution)/shard_map/ppermute | solution.py:629
  50.8 1.6 %collective-permute-start.15 = (bf16[2,128,512]{2,1,0:T(8,128)(2,1)S(1)}, bf16[2,128,512]{2,1,0:T(8,128)(2,1)S(1)}, u32[]{:S(2)}, u32[]{:S(2)}) collective-permute-start(bf16[2,128,512]{2,1,0:T(8,128)(2,1)S(1)} %get-tuple-element.103), channel_id=1, source_target_pairs={{0,1},{1,0},{2,3},{3,2},{4,5},{5,4},{6,7},{7,6},{8,9},{9,8},{10,11... | collective-permute-start | bytes 786440 | tf_op jit(solution)/shard_map/ppermute | solution.py:629
  52.4 5.2 %collective-permute-start.16 = (bf16[144,512]{1,0:T(8,128)(2,1)S(1)}, bf16[144,512]{1,0:T(8,128)(2,1)S(1)}, u32[]{:S(2)}, u32[]{:S(2)}) collective-permute-start(bf16[144,512]{1,0:T(8,128)(2,1)S(1)} %pad_maximum_fusion.4), channel_id=1, source_target_pairs={{0,2},{1,3},{2,0},{3,1},{4,6},{5,7},{6,4},{7,5},{8,10},{9,11},{10,... | collective-permute-start | bytes 442376 | tf_op jit(solution)/shard_map/ppermute | solution.py:629
  57.8 4.4 %collective-permute-start.17 = (bf16[144,512]{1,0:T(8,128)(2,1)S(1)}, bf16[144,512]{1,0:T(8,128)(2,1)S(1)}, u32[]{:S(2)}, u32[]{:S(2)}) collective-permute-start(bf16[144,512]{1,0:T(8,128)(2,1)S(1)} %pad_maximum_fusion.5), channel_id=1, source_target_pairs={{0,4},{1,5},{2,6},{3,7},{4,0},{5,1},{6,2},{7,3},{8,12},{9,13},{10,... | collective-permute-start | bytes 442376 | tf_op jit(solution)/shard_map/ppermute | solution.py:629
  59.2 5.1 %collective-permute-start.12 = (bf16[1,64,1536]{2,1,0:T(8,128)(2,1)S(1)}, bf16[1,64,1536]{2,1,0:T(8,128)(2,1)S(1)}, u32[]{:S(2)}, u32[]{:S(2)}) collective-permute-start(bf16[1,64,1536]{2,1,0:T(8,128)(2,1)S(1)} %pad_maximum_fusion.1), channel_id=1, source_target_pairs={{0,2},{1,3},{2,0},{3,1},{4,6},{5,7},{6,4},{7,5},{8,10},{9,11},{10,... | collective-permute-start | bytes 589832 | tf_op jit(solution)/shard_map/ppermute | solution.py:629
  59.8 11.1 %collective-permute-start.13 = (bf16[1,64,1536]{2,1,0:T(8,128)(2,1)S(1)}, bf16[1,64,1536]{2,1,0:T(8,128)(2,1)S(1)}, u32[]{:S(2)}, u32[]{:S(2)}) collective-permute-start(bf16[1,64,1536]{2,1,0:T(8,128)(2,1)S(1)} %pad_maximum_fusion.2), channel_id=1, source_target_pairs={{0,4},{1,5},{2,6},{3,7},{4,0},{5,1},{6,2},{7,3},{8,12},{9,13},{10,... | collective-permute-start | bytes 589832 | tf_op jit(solution)/shard_map/ppermute | solution.py:629
  60.1 10.8 %collective-permute-start.14 = (bf16[1,64,1536]{2,1,0:T(8,128)(2,1)S(1)}, bf16[1,64,1536]{2,1,0:T(8,128)(2,1)S(1)}, u32[]{:S(2)}, u32[]{:S(2)}) collective-permute-start(bf16[1,64,1536]{2,1,0:T(8,128)(2,1)S(1)} %pad_maximum_fusion.3), channel_id=1, source_target_pairs={{0,6},{1,7},{2,4},{3,5},{4,2},{5,3},{6,0},{7,1},{8,14},{9,15},{10,... | collective-permute-start | bytes 589832 | tf_op jit(solution)/shard_map/ppermute | solution.py:629
  62.2 10.1 %collective-permute-start.18 = (bf16[144,512]{1,0:T(8,128)(2,1)S(1)}, bf16[144,512]{1,0:T(8,128)(2,1)S(1)}, u32[]{:S(2)}, u32[]{:S(2)}) collective-permute-start(bf16[144,512]{1,0:T(8,128)(2,1)S(1)} %pad_maximum_fusion.6), channel_id=1, source_target_pairs={{0,8},{1,9},{2,10},{3,11},{4,12},{5,13},{6,14},{7,15},{8,0},{9,1},... | collective-permute-start | bytes 442376 | tf_op jit(solution)/shard_map/ppermute | solution.py:629
  70.9 29.3 %copy-start.1 = (bf16[512,2,512]{2,1,0:T(2,128)(2,1)S(1)}, bf16[512,2,512]{2,1,0:T(2,128)(2,1)}, u32[]{:S(2)}) copy-start(bf16[512,2,512]{2,1,0:T(2,128)(2,1)} %param.23) | copy-start | bytes 3145732
  71.0 4.6 %collective-permute-start.21 = (bf16[64,1536]{1,0:T(8,128)(2,1)S(1)}, bf16[64,1536]{1,0:T(8,128)(2,1)S(1)}, u32[]{:S(2)}, u32[]{:S(2)}) collective-permute-start(bf16[64,1536]{1,0:T(8,128)(2,1)S(1)} %reduce-precision_convert_fusion.2), channel_id=1, source_target_pairs={{0,8},{1,9},{2,10},{3,11},{4,12},{5,13},{6,14},{7,15},{8,0},{9,1},... | collective-permute-start | bytes 589832 | tf_op jit(solution)/shard_map/ppermute | solution.py:629
  75.6 12.3 %collective-permute-start.22 = (bf16[64,1536]{1,0:T(8,128)(2,1)S(1)}, bf16[64,1536]{1,0:T(8,128)(2,1)S(1)}, u32[]{:S(2)}, u32[]{:S(2)}) collective-permute-start(bf16[64,1536]{1,0:T(8,128)(2,1)S(1)} %reduce-precision_convert_fusion.1), channel_id=1, source_target_pairs={{0,24},{1,25},{2,26},{3,27},{4,28},{5,29},{6,30},{7,31},{8,16},{9,... | collective-permute-start | bytes 589832 | tf_op jit(solution)/shard_map/ppermute | solution.py:629
  75.9 24.2 %collective-permute-start.19 = (bf16[144,512]{1,0:T(8,128)(2,1)S(1)}, bf16[144,512]{1,0:T(8,128)(2,1)S(1)}, u32[]{:S(2)}, u32[]{:S(2)}) collective-permute-start(bf16[144,512]{1,0:T(8,128)(2,1)S(1)} %pad_maximum_fusion.7), channel_id=1, source_target_pairs={{0,24},{1,25},{2,26},{3,27},{4,28},{5,29},{6,30},{7,31},{8,16},{9,... | collective-permute-start | bytes 442376 | tf_op jit(solution)/shard_map/ppermute | solution.py:629
  88.0 4.9 %collective-permute-start.23 = (bf16[64,1536]{1,0:T(8,128)(2,1)S(1)}, bf16[64,1536]{1,0:T(8,128)(2,1)S(1)}, u32[]{:S(2)}, u32[]{:S(2)}) collective-permute-start(bf16[64,1536]{1,0:T(8,128)(2,1)S(1)} %reduce-precision_convert_fusion), channel_id=1, source_target_pairs={{0,4},{1,5},{2,6},{3,7},{4,0},{5,1},{6,2},{7,3},{8,12},{9,13},{10,... | collective-permute-start | bytes 589832 | tf_op jit(solution)/shard_map/ppermute | solution.py:629
  88.1 4.8 %collective-permute-start.24 = (bf16[64,1024]{1,0:T(8,128)(2,1)S(1)}, bf16[64,1024]{1,0:T(8,128)(2,1)S(1)}, u32[]{:S(2)}, u32[]{:S(2)}) collective-permute-start(bf16[64,1024]{1,0:T(8,128)(2,1)S(1)} %get-tuple-element.125), channel_id=1, source_target_pairs={{0,2},{1,3},{2,0},{3,1},{4,6},{5,7},{6,4},{7,5},{8,10},{9,11},{10,... | collective-permute-start | bytes 393224 | tf_op jit(solution)/shard_map/ppermute | solution.py:629
  89.1 5.4 %collective-permute-start.25 = (bf16[64,1024]{1,0:T(8,128)(2,1)S(1)}, bf16[64,1024]{1,0:T(8,128)(2,1)S(1)}, u32[]{:S(2)}, u32[]{:S(2)}) collective-permute-start(bf16[64,1024]{1,0:T(8,128)(2,1)S(1)} %get-tuple-element.125), channel_id=1, source_target_pairs={{0,6},{1,7},{2,4},{3,5},{4,2},{5,3},{6,0},{7,1},{8,14},{9,15},{10,... | collective-permute-start | bytes 393224 | tf_op jit(solution)/shard_map/ppermute | solution.py:629
  94.6 11.1 %collective-permute-start.27 = (bf16[3,64,1024]{2,1,0:T(8,128)(2,1)S(1)}, bf16[3,64,1024]{2,1,0:T(8,128)(2,1)S(1)}, u32[]{:S(2)}, u32[]{:S(2)}) collective-permute-start(bf16[3,64,1024]{2,1,0:T(8,128)(2,1)S(1)} %pad_maximum_fusion.refs_1_), channel_id=1, source_target_pairs={{0,1},{1,0},{2,3},{3,2},{4,5},{5,4},{6,7},{7,6},{8,9},{9,8},{10,11... | collective-permute-start | bytes 1179656 | tf_op jit(solution)/shard_map/ppermute | solution.py:629
  100.1 2.9 %collective-permute-start.20 = (f32[8,512]{1,0:T(8,128)S(1)}, f32[8,512]{1,0:T(8,128)S(1)}, u32[]{:S(2)}, u32[]{:S(2)}) collective-permute-start(f32[8,512]{1,0:T(8,128)S(1)} %add_add_fusion.sums_ref), channel_id=1, source_target_pairs={{0,1},{1,0},{2,3},{3,2},{4,5},{5,4},{6,7},{7,6},{8,9},{9,8},{10,11... | collective-permute-start | bytes 49160 | tf_op jit(solution)/shard_map/ppermute | solution.py:629
  103.8 1.9 %collective-permute-start.26 = (bf16[1,64,1024]{2,1,0:T(8,128)(2,1)S(1)}, bf16[1,64,1024]{2,1,0:T(8,128)(2,1)S(1)}, u32[]{:S(2)}, u32[]{:S(2)}) collective-permute-start(bf16[1,64,1024]{2,1,0:T(8,128)(2,1)S(1)} %get-tuple-element.126.refs_0_), channel_id=1, source_target_pairs={{0,1},{1,0},{2,3},{3,2},{4,5},{5,4},{6,7},{7,6},{8,9},{9,8},{10,11... | collective-permute-start | bytes 393224 | tf_op jit(solution)/shard_map/ppermute | solution.py:629

commit v3 on v2

--- a/solution.py
+++ b/solution.py
@@ -44,15 +44,15 @@
     return y.reshape(y.shape[0] // SUB, segs, group, feats).transpose(1, 0, 2, 3)
 
 
-def row_mask(base, rows, group, steps, me, lens_ref):
+def row_mask(base, rows, group, steps, me, lengths):
     segs = SUB // group
     row = lax.broadcasted_iota(jnp.int32, (rows, 128), 0) + base
     place = row & (SUB - 1)
     seq = place & (group - 1)
-    position = me * (segs * steps) + (place // group) * steps + (row // SUB)
-    length = jnp.full((rows, 128), lens_ref[0], jnp.int32)
+    position = (me * (segs * steps) + (place // group) * steps + (row // SUB)).astype(F32)
+    length = jnp.broadcast_to(lengths[:, 0:1], (rows, 128))
     for k in range(1, group):
-        length = jnp.where(seq == k, lens_ref[k], length)
+        length = jnp.where(seq == k, lengths[:, k : k + 1], length)
     return (position < length).astype(F32)
 
 
@@ -61,9 +61,10 @@
 
 
 def call(body, outs, ins, scratch, limit_mib, flops, name, fetched=()):
-    specs = [
-        pl.BlockSpec(memory_space=pltpu.HBM if k in fetched else pltpu.VMEM) for k in range(len(ins))
-    ]
+    specs = []
+    for k, x in enumerate(ins):
+        space = pltpu.SMEM if x.dtype == jnp.int32 else pltpu.HBM if k in fetched else pltpu.VMEM
+        specs.append(pl.BlockSpec(memory_space=space))
     return pl.pallas_call(
         body,
         out_shape=[jax.ShapeDtypeStruct(s, d) for s, d in outs],
@@ -103,83 +104,74 @@
     return [high, mid, (rest - mid.astype(F32)).astype(BF16)]
 
 
-def prep_kernel(*refs):
-    sources, (pay_ref, vec_ref) = refs[:7], refs[7:9]
-    targets, flat_ref, sems = refs[9:16], refs[16], refs[17]
-    weight_ref, rate_ref, angle_ref, level_ref = targets[:4]
-    own, _, feats = weight_ref.shape
-    copies = start_copies(sources, targets, sems)
-    for c in copies[1:]:
-        c.wait()
+def prep_kernel(own, group, small_ref, pay_ref, vec_ref):
+    feats = vec_ref.shape[1]
     me = lax.axis_index("state")
     lane = lax.broadcasted_iota(jnp.int32, (1, feats), 1)
     mine = (lane // own) == me
-    over = lambda ref: jnp.concatenate([ref[...]] * (feats // own), axis=1)
-    decay = jnp.exp(over(rate_ref))
+    base = 3 * feats
+    logs = [small_ref[:, base + k * own : base + (k + 1) * own] for k in range(3)]
+    rate, turn, level = (jnp.concatenate([v] * (feats // own), axis=1) for v in logs)
+    decay = jnp.exp(rate)
     size = jnp.exp(-decay)
-    angle = jnp.exp(over(angle_ref))
+    angle = jnp.exp(turn)
     pole_re, pole_im = size * jnp.cos(angle), size * jnp.sin(angle)
     parts = []
-    for v in (pole_re, pole_im, jnp.exp(over(level_ref))):
+    for v in (pole_re, pole_im, jnp.exp(level)):
         parts += three_parts(jnp.where(mine, v, 0.0))
     parts += [jnp.zeros((PARAM_ROWS - len(parts), feats), BF16)]
-    pay_ref[2 * own :, :] = jnp.concatenate([p.astype(F32) for p in parts], axis=0).astype(BF16)
-    rows = [t[...] for t in targets[4:]] + [pole_re, pole_im, decay, angle]
+    flat = jnp.concatenate([p.astype(F32) for p in parts], axis=0)
+    pay_ref[...] = flat.reshape(PARAM_ROWS // 2, 2, feats).astype(BF16)
+    rows = [small_ref[:, k * feats : (k + 1) * feats] for k in range(3)] + [pole_re, pole_im, decay, angle]
     for k, row in enumerate(rows):
         vec_ref[k : k + 1, :] = row
+    base += 3 * own
     vec_ref[len(rows) :, :] = jnp.zeros((SUB - len(rows), feats), F32)
-    copies[0].wait()
-    for k, part in enumerate(split_pairs(weight_ref, flat_ref)):
-        pay_ref[k * own : (k + 1) * own, :] = part
-
-
-def norm_kernel(x_hbm, cot_hbm, weight_hbm, lens_hbm, vec_ref, low_ref, unit_ref, inv_ref, mask_ref, rows_ref, pay_ref, *scratch):
-    x_ref, cot_ref, weight_ref, lens_ref, flat_ref, sems = scratch
+    vec_ref[7:8, :group] = small_ref[:, base : base + group]
+
+
+def cotangent_kernel(cot_ref, rows_ref):
+    steps = 16
+    for c in range(cot_ref.shape[1] // steps):
+        at = pl.ds(c * steps * SUB, steps * SUB)
+        rows_ref[at, :] = rows_in(cot_ref, c * steps, steps).astype(BF16)
+
+
+def weights_kernel(*refs):
+    blocks, (out_ref, flat_ref) = refs[:-2], refs[-2:]
+    gather_rows(lax.axis_index("state"), blocks, flat_ref, out_ref)
+
+
+def norm_kernel(x_ref, vec_ref, low_ref, unit_ref, inv_ref, mask_ref):
     segs, steps, group, feats = x_ref.shape
     rows = steps * SUB
-    own = weight_ref.shape[0]
     me = lax.axis_index("state")
     size = 128
-    cut = steps // 4
     gain, bias = vec_ref[0:1, :], vec_ref[1:2, :]
-    sources, targets = [lens_hbm], [lens_ref]
-    for k in range(4):
-        at = pl.ds(k * cut, cut)
-        sources += [x_hbm.at[:, at], cot_hbm.at[:, at]]
-        targets += [x_ref.at[:, at], cot_ref.at[:, at]]
-    copies = start_copies(sources + [weight_hbm], targets + [weight_ref], sems)
-    copies[0].wait()
 
     def chunk(c, carry):
         base = pl.multiple_of(c * size, size)
         at = pl.ds(base, size)
-        first = pl.multiple_of(c * (size // SUB), size // SUB)
-        x = rows_in(x_ref, first, size // SUB)
+        x = rows_in(x_ref, pl.multiple_of(c * (size // SUB), size // SUB), size // SUB)
         centred = x - jnp.mean(x, axis=1, keepdims=True)
         inv = lax.rsqrt(jnp.mean(centred * centred, axis=1, keepdims=True) + EPSILON)
         unit = centred * inv
         unit_ref[at, :] = unit
         low_ref[at, :] = (unit * gain + bias).astype(BF16)
         inv_ref[at, :] = jnp.broadcast_to(inv, (size, 128))
-        mask_ref[at, :] = row_mask(base, size, group, steps, me, lens_ref)
-        rows_ref[at, :] = rows_in(cot_ref, first, size // SUB).astype(BF16)
+        mask_ref[at, :] = row_mask(base, size, group, steps, me, vec_ref[7:8, :])
         return carry
 
-    turns = rows // size // 4
-    for k in range(4):
-        copies[1 + 2 * k].wait()
-        copies[2 + 2 * k].wait()
-        lax.fori_loop(k * turns, (k + 1) * turns, chunk, 0)
-    copies[9].wait()
-    for k, part in enumerate(split_pairs(weight_ref, flat_ref)):
-        pay_ref[k * own : (k + 1) * own, :] = part
-
-
-def gather_rows(me, blocks, own, channels, dst_ref):
+    lax.fori_loop(0, rows // size, chunk, 0)
+
+
+def gather_rows(me, blocks, flat_ref, dst_ref):
+    own = flat_ref.shape[1] // 2
+    channels = own * len(blocks)
     for m, block in enumerate(blocks):
-        off = pl.multiple_of((me ^ m) * own, own)
-        dst_ref[pl.ds(off, own), :] = block[0:own, :]
-        dst_ref[pl.ds(pl.multiple_of(channels + off, own), own), :] = block[own : 2 * own, :]
+        for k, part in enumerate(split_pairs(block.at[0:own], flat_ref)):
+            at = pl.multiple_of(k * channels + (me ^ m) * own, own)
+            dst_ref[pl.ds(at, own), :] = part
 
 
 def seg_of(group):
@@ -249,17 +241,17 @@
 
 def project_kernel(parts, own, group, low_ref, mask_ref, *refs):
     blocks = refs[:parts]
-    drive_ref, end_ref, win_ref, cst_ref = refs[parts:]
+    drive_ref, end_ref, win_ref, cst_ref, flat_ref = refs[parts:]
     rows = low_ref.shape[0]
     channels = own * parts
     steps = rows // SUB
     me = lax.axis_index("state")
-    gather_rows(me, blocks, own, channels, win_ref)
+    gather_rows(me, blocks, flat_ref, win_ref)
     rows_of = []
     for k in range(3):
         total = None
         for block in blocks:
-            tile = block[2 * own : 2 * own + PARAM_ROWS, :].astype(F32)
+            tile = block[own : own + PARAM_ROWS // 2].astype(F32).reshape(PARAM_ROWS, -1)
             for part in range(3):
                 piece = tile[3 * k + part : 3 * k + part + 1, :channels]
                 total = piece if total is None else total + piece
@@ -308,9 +300,8 @@
     it = iter(refs)
     take = lambda n: [next(it) for _ in range(n)]
     drive_ref, end_ref, cst_ref, ends_ref = take(4)
-    blocks = take(parts)
-    unit_ref, cot_ref, mask_ref, vec_ref, glu_ref = take(5)
-    states_ref, slow_ref, cw_ref, branch_ref, dglu_ref, gp_ref = take(6)
+    cw_ref, unit_ref, cot_ref, mask_ref, vec_ref, glu_ref = take(6)
+    states_ref, slow_ref, branch_ref, dglu_ref, gp_ref = take(5)
     grads = take(len(orders))
     act_ref, acc_ref = take(2)
     rows, feats = unit_ref.shape
@@ -318,7 +309,6 @@
     steps = rows // SUB
     me = lax.axis_index("state")
     place = me + parts * (lax.axis_index("seq") & 1)
-    gather_rows(me, blocks, own, channels, cw_ref)
     gain, bias, skip = (vec_ref[k : k + 1, :] for k in range(3))
     pr, pi = cst_ref[0:1, :channels], cst_ref[0:1, channels:]
     qr, qi = cst_ref[1:2, :channels], cst_ref[1:2, channels:]
@@ -654,14 +644,14 @@
     return [o for sends in stages for o in sends] + [[0]]
 
 
-def halve(parts, group, after=None):
+def swap(parts, group):
     masks = submasks(group)
-    sends = [p.astype(BF16) for p in parts[: len(masks)]]
-    got = [exchange(p, m) for p, m in zip(sends, masks)]
-    if after is not None:
-        got = tie(got, after)
+    return [exchange(p.astype(BF16), m) for p, m in zip(parts, masks)]
+
+
+def add_up(parts, got):
     rest, off = [], 0
-    for p in parts[len(masks) :]:
+    for p in parts[len(got) :]:
         n = p.shape[0]
         total = p.astype(F32)
         for g in got:
@@ -671,13 +661,12 @@
     return rest
 
 
+def halve(parts, group):
+    return add_up(parts, swap(parts, group))
+
+
 def rounded(x):
     return lax.reduce_precision(x, 8, 7)
-
-
-def double(x, mask):
-    low = rounded(x).astype(BF16)
-    return low.astype(F32) + exchange(low, mask).astype(F32)
 
 
 def two_parts(x):
@@ -696,12 +685,16 @@
     return g
 
 
-def gather_blocks(own, bits):
-    blocks = {0: own}
-    for bit in reversed(bits):
-        for m in list(blocks):
-            blocks[m ^ bit] = exchange(blocks[m], bit)
-    return [blocks[m] for m in range(len(blocks))]
+def gather_blocks(arrays, bits, ready=None):
+    blocks = [{0: a} for a in arrays]
+    for n, bit in enumerate(reversed(bits)):
+        for held_blocks in blocks:
+            for m in list(held_blocks):
+                x = held_blocks[m]
+                if m and n and ready is not None:
+                    x = tie(x, ready)
+                held_blocks[m ^ bit] = exchange(x, bit)
+    return [[b[m] for m in range(len(b))] for b in blocks]
 
 
 def shards(
@@ -732,42 +725,33 @@
         seq_masks[-1] |= seq_masks[-2]
     full = rows * feats * 2 * channels * 2
 
-    as_row = lambda v: v.reshape(1, -1)
     flat = pltpu.VMEM((feats // 128, 2 * own, 128), F32)
     x4 = tokens.reshape(segs, span // segs, group, feats)
     cot4 = cotangent.reshape(segs, span // segs, group, feats)
-    ins = [input_weight.transpose(1, 2, 0)]
-    ins += [as_row(v) for v in (log_rate, log_angle, log_gain, norm_gain, norm_bias, skip_gain)]
-    b_own, vec = call(
-        prep_kernel,
-        [((2 * own + PARAM_ROWS, feats), BF16), ((SUB, feats), F32)],
-        ins,
-        [held(x) for x in ins] + [flat, pltpu.SemaphoreType.DMA((7,))],
+    small = jnp.concatenate(
+        [norm_gain, norm_bias, skip_gain, log_rate, log_angle, log_gain, lengths.astype(F32)]
+    )
+    small = jnp.pad(small, (0, -small.shape[0] % 128)).reshape(1, -1)
+    small_own, vec = call(
+        functools.partial(prep_kernel, own, group),
+        [((PARAM_ROWS // 2, 2, feats), BF16), ((SUB, feats), F32)],
+        [small],
+        [],
         8,
         MIB,
         "prep",
-        fetched=range(7),
-    )
-    b_blocks = gather_blocks(b_own, state_bits)
-    low, unit, inv, mask, cot, c_own = call(
+    )
+    b_own = jnp.concatenate([input_weight.transpose(1, 2, 0), small_own], axis=0)
+    low, unit, inv, mask = call(
         norm_kernel,
-        [
-            ((rows, feats), BF16),
-            ((rows, feats), F32),
-            ((rows, 128), F32),
-            ((rows, 128), F32),
-            ((rows, feats), BF16),
-            ((2 * own, feats), BF16),
-        ],
-        [x4, cot4, output_weight, lengths, vec],
-        [held(x4), held(cot4), held(output_weight), pltpu.SMEM(lengths.shape, jnp.int32)]
-        + [flat, pltpu.SemaphoreType.DMA((10,))],
+        [((rows, feats), BF16), ((rows, feats), F32), ((rows, 128), F32), ((rows, 128), F32)],
+        [x4, vec],
+        [],
         12,
         rows * feats * 20,
         "norm",
-        fetched=range(4),
-    )
-    c_blocks = gather_blocks(c_own, state_bits)
+    )
+    b_blocks, c_blocks = gather_blocks([b_own, tie(output_weight, b_own)], state_bits, low)
     drive, end, win, cst = call(
         functools.partial(project_kernel, parts, own, group),
         [
@@ -777,12 +761,22 @@
             ((SUB, 2 * channels), F32),
         ],
         [low, mask] + b_blocks,
-        [],
+        [flat],
         12,
         full,
         "project",
     )
     ends = gather_ends(end, state_bits)
+    (cot,) = call(cotangent_kernel, [((rows, feats), BF16)], [tie(cot4, end)], [], 8, MIB, "cotangent")
+    (cw,) = call(
+        weights_kernel,
+        [((2 * channels, feats), BF16)],
+        [tie(c_blocks[0], end)] + c_blocks[1:],
+        [flat],
+        8,
+        MIB,
+        "weights",
+    )
     all_bits = state_bits + [parts]
     all_groups = [all_bits[:1]] + [all_bits[k : k + 2] for k in range(1, len(all_bits), 2)]
     all_orders = stage_orders(all_groups)
@@ -790,18 +784,17 @@
     block_outs = lambda rows, width, orders: [
         ((len(o), rows, width), BF16 if k == 0 else F32) for k, o in enumerate(orders)
     ]
-    states, slow, cw, branch, d_glu, slope, *glu_parts = call(
+    states, slow, branch, d_glu, slope, *glu_parts = call(
         functools.partial(mix_kernel, parts, own, group, all_orders),
         [
             ((rows + SUB, 2 * channels), F32),
             ((rows, 2 * channels), BF16),
-            ((2 * channels, feats), BF16),
             ((rows, feats), F32),
             ((rows, 2 * feats), BF16),
             ((rows, feats), F32),
         ]
         + block_outs(glu_rows, 2 * feats, all_orders),
-        [drive, end, cst, ends] + c_blocks + [unit, cot, mask, vec, glu_weight],
+        [drive, end, cst, ends, cw, unit, cot, mask, vec, glu_weight],
         [pltpu.VMEM((rows, feats), BF16), pltpu.VMEM((feats, 2 * feats), F32)],
         20,
         5 * full,
@@ -822,18 +815,9 @@
         4 * full,
         "back",
     )
-    starts = gather_ends(start, state_bits)
-    (out4,) = call(
-        out_kernel,
-        [(x4.shape, BF16)],
-        [x4, tie(branch, start)],
-        [held(x4), pltpu.SemaphoreType.DMA((4,))],
-        8,
-        MIB,
-        "out",
-        fetched=(0,),
-    )
-    glu_parts = halve(glu_parts, all_groups[0], after=start)
+    got = swap(glu_parts, all_groups[0])
+    starts = gather_ends(tie(start, got), state_bits)
+    glu_parts = add_up(glu_parts, tie(got, start))
     out_parts = halve(out_parts, all_groups[0])
     both = [jnp.concatenate(p, axis=-1) for p in zip(glu_parts, out_parts)]
     state_groups = [[b] for b in state_bits]
@@ -842,15 +826,12 @@
         functools.partial(adjoint_kernel, own, group, pair_orders),
         [((rows, 2 * channels), BF16), ((SUB, 3 * channels), F32)]
         + block_outs(2 * own, feats, pair_orders),
-        [tie(d_states, out4), start, cst, starts, states, drive, low, mask],
+        [tie(d_states, both), start, cst, starts, states, drive, low, mask],
         [pltpu.VMEM((rows, 2 * channels), F32), pltpu.VMEM((2 * channels, feats), F32)],
         16,
         2 * full,
         "adjoint",
     )
-    for g in all_groups[1:]:
-        both = halve(both, g, after=channel_sums)
-    both = both[0][0]
     in_parts = halve(in_parts, state_groups[0])
     d_normed, sums = call(
         normed_kernel,
@@ -861,33 +842,26 @@
         full,
         "normed",
     )
+    sent = []
     for g in state_groups[1:]:
-        keep = in_parts[1:]
         own_sums = two_parts(sums)
-        send = jnp.concatenate([in_parts[0].astype(BF16).reshape(-1, feats)] + own_sums, axis=0)
-        got = exchange(send, g[0])
-        in_parts, off = [], 0
-        for p in keep:
+        sent.append(
+            jnp.concatenate([in_parts[0].astype(BF16).reshape(-1, feats)] + own_sums, axis=0)
+        )
+        got = exchange(sent[-1], g[0])
+        rest, off = [], 0
+        for p in in_parts[1:]:
             n = p.shape[0] * p.shape[1]
-            in_parts.append(p + got[off : off + n].reshape(p.shape).astype(F32))
+            rest.append(p + got[off : off + n].reshape(p.shape).astype(F32))
             off += n
+        in_parts = rest
         sums = sum_of(own_sums) + sum_of([got[off : off + SUB], got[off + SUB :]])
-        send = in_parts[0]
     total = in_parts[0][0]
-    (grad4,) = call(
-        tokens_kernel,
-        [(cot4.shape, F32)],
-        [cot4, tie(d_normed, both, send), unit, inv, vec],
-        [held(cot4), pltpu.SemaphoreType.DMA((4,))],
-        12,
-        full,
-        "tokens",
-        fetched=(0,),
-    )
     for m in seq_masks:
         low_total = rounded(total).astype(BF16)
         own_sums = two_parts(sums)
-        got = exchange(jnp.concatenate([low_total] + own_sums, axis=0), m)
+        sent.append(jnp.concatenate([low_total] + own_sums, axis=0))
+        got = exchange(sent[-1], m)
         total = low_total.astype(F32) + got[: 2 * own].astype(F32)
         got_sums = [got[2 * own : 2 * own + SUB], got[2 * own + SUB :]]
         sums = sum_of(own_sums) + sum_of(got_sums)
@@ -901,9 +875,35 @@
         "finish",
     )
 
-    for m in seq_masks[1:]:
-        both = double(both, m)
-    both = rounded(both).astype(BF16)
+    for n, g in enumerate(all_groups[1:]):
+        both = add_up(both, tie(swap(both, g), sent[0]))
+    both = both[0][0]
+    (grad4,) = call(
+        tokens_kernel,
+        [(cot4.shape, F32)],
+        [cot4, tie(d_normed, both, sent[0]), unit, inv, vec],
+        [held(cot4), pltpu.SemaphoreType.DMA((4,))],
+        12,
+        full,
+        "tokens",
+        fetched=(0,),
+    )
+    (out4,) = call(
+        out_kernel,
+        [(x4.shape, BF16)],
+        [x4, tie(branch, both, sent[0])],
+        [held(x4), pltpu.SemaphoreType.DMA((4,))],
+        8,
+        MIB,
+        "out",
+        fetched=(0,),
+    )
+    at = lambda k: sent[max(0, min(k, len(sent) - 1))]
+    for n, m in enumerate(reversed(seq_masks[1:])):
+        mine = tie(rounded(both).astype(BF16), at(2 * n - 1))
+        got = tie(exchange(mine, m), at(2 * n + 1), grad4, out4)
+        both = mine.astype(F32) + got.astype(F32)
+    both = tie(rounded(both).astype(BF16), sent[-1])
     blocks = {0: both[:, : 2 * feats]}
     for g in reversed(all_groups[1:]):
         for m in list(blocks):

time: 107 us -> 81.2 us (0.76)
  the two profiles are of different devices: /device:TPU:17 before, /device:TPU:0 now
where the time goes in v3:
time: 81.2 us; the launch traced here: 81 us
  Pallas kernels  28.9 us (36%)
  starting transfers between devices  26.1 us (32%)
  waiting for transfers between devices  19.7 us (24%)
  local copies, waits for them, and re-layouts  2.71 us (3%)
  other arithmetic  2.6 us (3%)
  between operations  1.03 us (1%)
    pallas_call x14, Pallas kernels, call(): pl.pallas_call(body, out_shape=[jax.ShapeDtypeStruct(s, d) for s, d in ou...  28.9 us
    ppermute x28, starting transfers between devices, exchange(): lax.ppermute(x, ('seq', 'state'), [(i, i ^ mask) for i in range(count)])  26.1 us
    ppermute x28, waiting for transfers between devices, exchange(): lax.ppermute(x, ('seq', 'state'), [(i, i ^ mask) for i in range(count)])  19.7 us
  transfers between devices with their start and end apart: 28, of which 13 were waited for; matrix products, arithmetic and copies ran while one was open for 2% of the time, Pallas kernels for 25%

profile of v3, /device:TPU:0, one launch (start us, length us, event | category | flops | bytes accessed | tf_op | source)
XLA Modules:
  0.0 81.0 jit_solution(8871498144570931093)
XLA Ops:
  0.7 0.7 convert_element_type.197
  1.4 0.8 concatenate.57
  2.2 0.1 prep.1
  2.4 1.1 %pad_maximum_fusion.5.refs_0_ = bf16[72,2,512]{2,1,0:T(2,128)(2,1)S(1)} fusion(bf16[8,2,512]{2,1,0:T(2,128)(2,1)S(1)} %get-tuple-element.73, bf16[64,2,512]{2,1,0:T(2,128)(2,1)} %bitcast.60), kind=kLoop, calls=%fused_computation.19 | loop fusion | flops 73728 | bytes 294912 | tf_op jit(solution)/shard_map/concatenate | solution.py:744
  3.5 3.0 %collective-permute-start.1 = (bf16[72,2,512]{2,1,0:T(2,128)(2,1)S(1)}, bf16[72,2,512]{2,1,0:T(2,128)(2,1)S(1)}, u32[]{:S(2)}, u32[]{:S(2)}) collective-permute-start(bf16[72,2,512]{2,1,0:T(2,128)(2,1)S(1)} %pad_maximum_fusion.5.refs_0_), channel_id=1, source_target_pairs={{0,2},{1,3},{2,0},{3,1},{4,6},{5,7},{6,4},{7,5},{8,10},{9,11},{10,... | collective-permute-start | bytes 442376 | tf_op jit(solution)/shard_map/ppermute | solution.py:619
  6.5 1.2 %copy-done.1 = bf16[512,2,512]{2,1,0:T(2,128)(2,1)S(1)} copy-done((bf16[512,2,512]{2,1,0:T(2,128)(2,1)S(1)}, bf16[512,2,512]{2,1,0:T(2,128)(2,1)}, u32[]{:S(2)}) %copy-start.1) | copy-done | bytes 1048600
  7.7 3.4 %norm.1 = (bf16[1024,512]{1,0:T(8,128)(2,1)S(1)}, f32[1024,512]{1,0:T(8,128)S(1)}, f32[1024,128]{1,0:T(8,128)S(1)}, f32[1024,128]{1,0:T(8,128)S(1)}) custom-call(bf16[4,128,2,512]{3,2,1,0:T(2,128)(2,1)S(1)} %bitcast.50, f32[8,512]{1,0:T(8,128)S(1)} %get-tuple-element.70.vec_ref.refs_8_.refs_3_), custom_call_target="tpu_custom_call" | custom-call | flops 10485760 | bytes 4194304 | tf_op jit(solution)/shard_map/norm/pallas_call | solution.py:68
  11.1 0.6 collective-permute-start.2
  11.7 0.4 collective-permute-start.6
  12.1 0.6 collective-permute-done.2.refs_3_
  12.7 2.2 %project.1 = (f32[1024,512]{1,0:T(8,128)S(1)}, f32[8,512]{1,0:T(8,128)S(1)}, bf16[512,512]{1,0:T(8,128)(2,1)S(1)}, f32[8,512]{1,0:T(8,128)S(1)}) custom-call(bf16[1024,512]{1,0:T(8,128)(2,1)S(1)} %get-tuple-element.71.low_ref.refs_6_, f32[1024,128]{1,0:T(8,128)S(1)} %get-tuple-element.72.mask_ref.refs_7_, bf16[72,2,512]{2,1,0:T(2,128)(2,1)S(1)} %pad_maximum_fusion.5.refs_0_, ...), custom_call_target="tpu_custom_call" | custom-call | flops 536870912 | bytes 4194304 | tf_op jit(solution)/shard_map/project/pallas_call | solution.py:68
  14.9 0.0 copy-start.3
  14.9 1.1 %collective-permute-start.3 = (f32[1,8,512]{2,1,0:T(8,128)S(1)}, f32[1,8,512]{2,1,0:T(8,128)S(1)}, u32[]{:S(2)}, u32[]{:S(2)}) collective-permute-start(f32[1,8,512]{2,1,0:T(8,128)S(1)} %bitcast.56), channel_id=1, source_target_pairs={{0,2},{1,3},{2,0},{3,1},{4,6},{5,7},{6,4},{7,5},{8,10},{9,11},{10,... | collective-permute-start | bytes 49160 | tf_op jit(solution)/shard_map/ppermute | solution.py:619
  16.0 1.3 %collective-permute-done.6.refs_2_ = bf16[64,2,512]{2,1,0:T(2,128)(2,1)S(1)} collective-permute-done((bf16[64,2,512]{2,1,0:T(2,128)(2,1)}, bf16[64,2,512]{2,1,0:T(2,128)(2,1)S(1)}, u32[]{:S(2)}, u32[]{:S(2)}) %collective-permute-start.6) | collective-permute-done | bytes 131104 | tf_op jit(solution)/shard_map/ppermute | solution.py:619
  17.4 1.4 %collective-permute-done.3 = f32[1,8,512]{2,1,0:T(8,128)S(1)} collective-permute-done((f32[1,8,512]{2,1,0:T(8,128)S(1)}, f32[1,8,512]{2,1,0:T(8,128)S(1)}, u32[]{:S(2)}, u32[]{:S(2)}) %collective-permute-start.3) | collective-permute-done | bytes 16416 | tf_op jit(solution)/shard_map/ppermute | solution.py:619
  18.8 0.3 cotangent.1.refs_6_
  19.1 0.4 weights.1.refs_4_.refs_5_
  19.5 0.5 collective-permute-done.4
  20.0 6.8 %mix.1 = (f32[1032,512]{1,0:T(8,128)S(1)}, bf16[1024,512]{1,0:T(8,128)(2,1)S(1)}, f32[1024,512]{1,0:T(8,128)S(1)}, bf16[1024,1024]{1,0:T(8,128)(2,1)S(1)}, f32[1...) custom-call(f32[1024,512]{1,0:T(8,128)S(1)} %get-tuple-element.75.re, ...), custom_call_target="tpu_custom_call" | custom-call | flops 2684354560 | bytes 4194304 | tf_op jit(solution)/shard_map/mix/pallas_call | solution.py:68
  26.8 0.2 collective-permute-start.8
  27.1 4.3 %back.1 = (f32[1024,512]{1,0:T(8,128)S(1)}, f32[1024,512]{1,0:T(8,128)S(1)}, f32[8,512]{1,0:T(8,128)S(1)}, f32[8,512]{1,0:T(8,128)S(1)}, bf16[4,64,512]{2,1,0:T(...) custom-call(bf16[1024,1024]{1,0:T(8,128)(2,1)S(1)} %get-tuple-elemen, ...), custom_call_target="tpu_custom_call" | custom-call | flops 2147483648 | bytes 4194304 | tf_op jit(solution)/shard_map/back/pallas_call | solution.py:68
  31.4 0.4 collective-permute-start.9
  31.8 1.2 %collective-permute-done.9 = bf16[4,64,512]{2,1,0:T(8,128)(2,1)S(1)} collective-permute-done((bf16[4,64,512]{2,1,0:T(8,128)(2,1)S(1)}, bf16[4,64,512]{2,1,0:T(8,128)(2,1)S(1)}, u32[]{:S(2)}, u32[]{:S(2)}) %collective-permute-start.9) | collective-permute-done | bytes 262176 | tf_op jit(solution)/shard_map/ppermute | solution.py:619
  33.0 0.1 convert_add_fusion.2
  33.1 1.1 %collective-permute-start.13 = (f32[1,8,512]{2,1,0:T(8,128)S(1)}, f32[1,8,512]{2,1,0:T(8,128)S(1)}, u32[]{:S(2)}, u32[]{:S(2)}) collective-permute-start(f32[1,8,512]{2,1,0:T(8,128)S(1)} %bitcast.53), channel_id=1, source_target_pairs={{0,2},{1,3},{2,0},{3,1},{4,6},{5,7},{6,4},{7,5},{8,10},{9,11},{10,... | collective-permute-start | bytes 49160 | tf_op jit(solution)/shard_map/ppermute | solution.py:619
  34.1 0.1 convert_add_fusion.1
  34.3 1.1 %collective-permute-start.10 = (bf16[1,64,1536]{2,1,0:T(8,128)(2,1)S(1)}, bf16[1,64,1536]{2,1,0:T(8,128)(2,1)S(1)}, u32[]{:S(2)}, u32[]{:S(2)}) collective-permute-start(bf16[1,64,1536]{2,1,0:T(8,128)(2,1)S(1)} %pad_maximum_fusion.2), channel_id=1, source_target_pairs={{0,2},{1,3},{2,0},{3,1},{4,6},{5,7},{6,4},{7,5},{8,10},{9,11},{10,... | collective-permute-start | bytes 589832 | tf_op jit(solution)/shard_map/ppermute | solution.py:619
  35.4 1.6 %collective-permute-start.11 = (bf16[1,64,1536]{2,1,0:T(8,128)(2,1)S(1)}, bf16[1,64,1536]{2,1,0:T(8,128)(2,1)S(1)}, u32[]{:S(2)}, u32[]{:S(2)}) collective-permute-start(bf16[1,64,1536]{2,1,0:T(8,128)(2,1)S(1)} %pad_maximum_fusion.3), channel_id=1, source_target_pairs={{0,4},{1,5},{2,6},{3,7},{4,0},{5,1},{6,2},{7,3},{8,12},{9,13},{10,... | collective-permute-start | bytes 589832 | tf_op jit(solution)/shard_map/ppermute | solution.py:619
  37.0 0.1 collective-permute-start.14
  37.1 1.8 %collective-permute-start.12 = (bf16[1,64,1536]{2,1,0:T(8,128)(2,1)S(1)}, bf16[1,64,1536]{2,1,0:T(8,128)(2,1)S(1)}, u32[]{:S(2)}, u32[]{:S(2)}) collective-permute-start(bf16[1,64,1536]{2,1,0:T(8,128)(2,1)S(1)} %pad_maximum_fusion.4), channel_id=1, source_target_pairs={{0,6},{1,7},{2,4},{3,5},{4,2},{5,3},{6,0},{7,1},{8,14},{9,15},{10,... | collective-permute-start | bytes 589832 | tf_op jit(solution)/shard_map/ppermute | solution.py:619
  39.0 2.1 %adjoint.1 = (bf16[1024,512]{1,0:T(8,128)(2,1)S(1)}, f32[8,768]{1,0:T(8,128)S(1)}, bf16[2,128,512]{2,1,0:T(8,128)(2,1)S(1)}, f32[1,128,512]{2,1,0:T(8,128)S(1)}, f32[1,128,512]{2,1,0:T(8,128)S(1)}) custom-call(f32[1024,512]{1,0:T(8,128)S(1)} %get-tuple-element.100.refs_0_, f32[8,512]{1,0:T(8,128)S(1)} %get-tuple-element.101.refs_1_, ...), custom_call_target="tpu_custom_call" | custom-call | flops 1073741824 | bytes 4194304 | tf_op jit(solution)/shard_map/adjoint/pallas_call | solution.py:68
  41.1 0.3 collective-permute-start.15
  41.4 1.3 %normed.1 = (f32[1024,512]{1,0:T(8,128)S(1)}, f32[8,512]{1,0:T(8,128)S(1)}) custom-call(bf16[1024,512]{1,0:T(8,128)(2,1)S(1)} %get-tuple-element.105.dproj_ref, bf16[512,512]{1,0:T(8,128)(2,1)S(1)} %get-tuple-element.106.win_ref, f32[1024,512]{1,0:T(8,128)S(1)} %get-tuple-element.107.dpre_ref, f32[1024,512]{1,0:T(8,128)S(1)} %get-tuple-element.81.refs_5_.refs_2_.unit_ref, ...), custom_call_target="tpu_custom_call" | custom-call | flops 536870912 | bytes 4194304 | tf_op jit(solution)/shard_map/normed/pallas_call | solution.py:68
  42.7 0.0 copy-start.2
  42.7 0.0 collective-permute-done.15
  42.8 1.1 %collective-permute-start.16 = (bf16[144,512]{1,0:T(8,128)(2,1)S(1)}, bf16[144,512]{1,0:T(8,128)(2,1)S(1)}, u32[]{:S(2)}, u32[]{:S(2)}) collective-permute-start(bf16[144,512]{1,0:T(8,128)(2,1)S(1)} %pad_maximum_fusion.6), channel_id=1, source_target_pairs={{0,2},{1,3},{2,0},{3,1},{4,6},{5,7},{6,4},{7,5},{8,10},{9,11},{10,... | collective-permute-start | bytes 442376 | tf_op jit(solution)/shard_map/ppermute | solution.py:619
  43.8 1.5 %collective-permute-done.11 = bf16[1,64,1536]{2,1,0:T(8,128)(2,1)S(1)} collective-permute-done((bf16[1,64,1536]{2,1,0:T(8,128)(2,1)S(1)}, bf16[1,64,1536]{2,1,0:T(8,128)(2,1)S(1)}, u32[]{:S(2)}, u32[]{:S(2)}) %collective-permute-start.11) | collective-permute-done | bytes 196640 | tf_op jit(solution)/shard_map/ppermute | solution.py:619
  45.3 1.6 %collective-permute-done.12 = bf16[1,64,1536]{2,1,0:T(8,128)(2,1)S(1)} collective-permute-done((bf16[1,64,1536]{2,1,0:T(8,128)(2,1)S(1)}, bf16[1,64,1536]{2,1,0:T(8,128)(2,1)S(1)}, u32[]{:S(2)}, u32[]{:S(2)}) %collective-permute-start.12) | collective-permute-done | bytes 196640 | tf_op jit(solution)/shard_map/ppermute | solution.py:619
  46.9 0.1 reduce-precision_convert_fusion.2
  47.0 3.7 %collective-permute-start.21 = (bf16[64,1536]{1,0:T(8,128)(2,1)S(1)}, bf16[64,1536]{1,0:T(8,128)(2,1)S(1)}, u32[]{:S(2)}, u32[]{:S(2)}) collective-permute-start(bf16[64,1536]{1,0:T(8,128)(2,1)S(1)} %reduce-precision_convert_fusion.2), channel_id=1, source_target_pairs={{0,24},{1,25},{2,26},{3,27},{4,28},{5,29},{6,30},{7,31},{8,16},{9,... | collective-permute-start | bytes 589832 | tf_op jit(solution)/shard_map/ppermute | solution.py:619
  50.7 0.1 fusion.3
  50.8 0.9 %collective-permute-start.17 = (bf16[144,512]{1,0:T(8,128)(2,1)S(1)}, bf16[144,512]{1,0:T(8,128)(2,1)S(1)}, u32[]{:S(2)}, u32[]{:S(2)}) collective-permute-start(bf16[144,512]{1,0:T(8,128)(2,1)S(1)} %pad_maximum_fusion.7), channel_id=1, source_target_pairs={{0,4},{1,5},{2,6},{3,7},{4,0},{5,1},{6,2},{7,3},{8,12},{9,13},{10,... | collective-permute-start | bytes 442376 | tf_op jit(solution)/shard_map/ppermute | solution.py:619
  51.7 2.1 %out.1 = bf16[4,128,2,512]{3,2,1,0:T(2,128)(2,1)} custom-call(bf16[4,128,2,512]{3,2,1,0:T(2,128)(2,1)S(1)} %bitcast.51, f32[1024,512]{1,0:T(8,128)S(1)} %get-tuple-element.114.branch_ref), custom_call_target="tpu_custom_call" | custom-call | flops 1048576 | bytes 4194304 | tf_op jit(solution)/shard_map/out/pallas_call | solution.py:68
  53.9 2.8 %tokens.1 = f32[4,128,2,512]{3,2,1,0:T(2,128)} custom-call(bf16[4,128,2,512]{3,2,1,0:T(2,128)(2,1)S(1)} %bitcast.49, f32[1024,512]{1,0:T(8,128)S(1)} %get-tuple-element.116.dnorm_ref, f32[1024,512]{1,0:T(8,128)S(1)} %get-tuple-element.81.refs_5_.refs_2_.unit_ref, f32[1024,128]{1,0:T(8,128)S(1)} %get-tuple-element.117.inv_ref, ...), custom_call_target="tpu_custom_call" | custom-call | flops 536870912 | bytes 4194304 | tf_op jit(solution)/shard_map/tokens/pallas_call | solution.py:68
  56.8 1.8 %collective-permute-start.18 = (bf16[144,512]{1,0:T(8,128)(2,1)S(1)}, bf16[144,512]{1,0:T(8,128)(2,1)S(1)}, u32[]{:S(2)}, u32[]{:S(2)}) collective-permute-start(bf16[144,512]{1,0:T(8,128)(2,1)S(1)} %pad_maximum_fusion.8), channel_id=1, source_target_pairs={{0,8},{1,9},{2,10},{3,11},{4,12},{5,13},{6,14},{7,15},{8,0},{9,1},... | collective-permute-start | bytes 442376 | tf_op jit(solution)/shard_map/ppermute | solution.py:619
  58.6 0.4 collective-permute-start.22
  59.0 4.6 %collective-permute-done.18 = bf16[144,512]{1,0:T(8,128)(2,1)S(1)} collective-permute-done((bf16[144,512]{1,0:T(8,128)(2,1)S(1)}, bf16[144,512]{1,0:T(8,128)(2,1)S(1)}, u32[]{:S(2)}, u32[]{:S(2)}) %collective-permute-start.18) | collective-permute-done | bytes 147488 | tf_op jit(solution)/shard_map/ppermute | solution.py:619
  63.7 2.2 %collective-permute-start.19 = (bf16[144,512]{1,0:T(8,128)(2,1)S(1)}, bf16[144,512]{1,0:T(8,128)(2,1)S(1)}, u32[]{:S(2)}, u32[]{:S(2)}) collective-permute-start(bf16[144,512]{1,0:T(8,128)(2,1)S(1)} %pad_maximum_fusion.9), channel_id=1, source_target_pairs={{0,24},{1,25},{2,26},{3,27},{4,28},{5,29},{6,30},{7,31},{8,16},{9,... | collective-permute-start | bytes 442376 | tf_op jit(solution)/shard_map/ppermute | solution.py:619
  65.9 1.3 %collective-permute-done.22 = bf16[64,1536]{1,0:T(8,128)(2,1)S(1)} collective-permute-done((bf16[64,1536]{1,0:T(8,128)(2,1)S(1)}, bf16[64,1536]{1,0:T(8,128)(2,1)S(1)}, u32[]{:S(2)}, u32[]{:S(2)}) %collective-permute-start.22) | collective-permute-done | bytes 196640 | tf_op jit(solution)/shard_map/ppermute | solution.py:619
  67.2 0.1 reduce-precision_convert_fusion
  67.3 1.3 %collective-permute-start.23 = (bf16[64,1536]{1,0:T(8,128)(2,1)S(1)}, bf16[64,1536]{1,0:T(8,128)(2,1)S(1)}, u32[]{:S(2)}, u32[]{:S(2)}) collective-permute-start(bf16[64,1536]{1,0:T(8,128)(2,1)S(1)} %reduce-precision_convert_fusion), channel_id=1, source_target_pairs={{0,4},{1,5},{2,6},{3,7},{4,0},{5,1},{6,2},{7,3},{8,12},{9,13},{10,... | collective-permute-start | bytes 589832 | tf_op jit(solution)/shard_map/ppermute | solution.py:619
  68.6 1.1 %collective-permute-start.24 = (bf16[64,1024]{1,0:T(8,128)(2,1)S(1)}, bf16[64,1024]{1,0:T(8,128)(2,1)S(1)}, u32[]{:S(2)}, u32[]{:S(2)}) collective-permute-start(bf16[64,1024]{1,0:T(8,128)(2,1)S(1)} %get-tuple-element.139), channel_id=1, source_target_pairs={{0,2},{1,3},{2,0},{3,1},{4,6},{5,7},{6,4},{7,5},{8,10},{9,11},{10,... | collective-permute-start | bytes 393224 | tf_op jit(solution)/shard_map/ppermute | solution.py:619
  69.7 1.3 %collective-permute-start.25 = (bf16[64,1024]{1,0:T(8,128)(2,1)S(1)}, bf16[64,1024]{1,0:T(8,128)(2,1)S(1)}, u32[]{:S(2)}, u32[]{:S(2)}) collective-permute-start(bf16[64,1024]{1,0:T(8,128)(2,1)S(1)} %get-tuple-element.139), channel_id=1, source_target_pairs={{0,6},{1,7},{2,4},{3,5},{4,2},{5,3},{6,0},{7,1},{8,14},{9,15},{10,... | collective-permute-start | bytes 393224 | tf_op jit(solution)/shard_map/ppermute | solution.py:619
  70.9 2.1 %collective-permute-done.23 = bf16[64,1536]{1,0:T(8,128)(2,1)S(1)} collective-permute-done((bf16[64,1536]{1,0:T(8,128)(2,1)S(1)}, bf16[64,1536]{1,0:T(8,128)(2,1)S(1)}, u32[]{:S(2)}, u32[]{:S(2)}) %collective-permute-start.23) | collective-permute-done | bytes 196640 | tf_op jit(solution)/shard_map/ppermute | solution.py:619
  73.0 0.6 collective-permute-done.24
  73.6 1.9 %collective-permute-done.25 = bf16[64,1024]{1,0:T(8,128)(2,1)S(1)} collective-permute-done((bf16[64,1024]{1,0:T(8,128)(2,1)S(1)}, bf16[64,1024]{1,0:T(8,128)(2,1)S(1)}, u32[]{:S(2)}, u32[]{:S(2)}) %collective-permute-start.25) | collective-permute-done | bytes 131104 | tf_op jit(solution)/shard_map/ppermute | solution.py:619
  75.6 0.1 collective-permute-start.27
  75.7 0.5 collective-permute-start.20
  76.2 0.1 collective-permute-start.26
  76.3 1.1 %collective-permute-done.20.more_ref = f32[8,512]{1,0:T(8,128)S(1)} collective-permute-done((f32[8,512]{1,0:T(8,128)S(1)}, f32[8,512]{1,0:T(8,128)S(1)}, u32[]{:S(2)}, u32[]{:S(2)}) %collective-permute-start.20) | collective-permute-done | bytes 16416 | tf_op jit(solution)/shard_map/ppermute | solution.py:619
  77.4 0.8 finish.1
  78.2 0.6 fusion.17
  78.8 0.8 halves.1
  79.6 1.5 %place.1 = f32[512,1024]{1,0:T(8,128)} custom-call(bf16[1,64,1024]{2,1,0:T(8,128)(2,1)S(1)} %get-tuple-element.140.refs_0_, bf16[3,64,1024]{2,1,0:T(8,128)(2,1)S(1)} %pad_maximum_fusion.1.refs_1_, bf16[1,64,1024]{2,1,0:T(8,128)(2,1)S(1)} %collective-permute-done.26.refs_2_, bf16[3,64,1024]{2,1,0:T(8,128)(2,1)S(1)} %collective-permute-done.27.refs_3_), custom_call_target="tpu_custom_call" | custom-call | flops 262144 | bytes 4194304 | tf_op jit(solution)/shard_map/place/pallas_call | solution.py:68
  (54 shorter events, 0.5 us)
Async XLA Ops:
  0.6 18.1 %copy-start = (bf16[512,2,512]{2,1,0:T(2,128)(2,1)S(1)}, bf16[512,2,512]{2,1,0:T(2,128)(2,1)}, u32[]{:S(2)}) copy-start(bf16[512,2,512]{2,1,0:T(2,128)(2,1)} %param.23) | copy-start | bytes 3145732
  3.5 7.6 %collective-permute-start.1 = (bf16[72,2,512]{2,1,0:T(2,128)(2,1)S(1)}, bf16[72,2,512]{2,1,0:T(2,128)(2,1)S(1)}, u32[]{:S(2)}, u32[]{:S(2)}) collective-permute-start(bf16[72,2,512]{2,1,0:T(2,128)(2,1)S(1)} %pad_maximum_fusion.5.refs_0_), channel_id=1, source_target_pairs={{0,2},{1,3},{2,0},{3,1},{4,6},{5,7},{6,4},{7,5},{8,10},{9,11},{10,... | collective-permute-start | bytes 442376 | tf_op jit(solution)/shard_map/ppermute | solution.py:619
  6.5 5.6 %collective-permute-start = (bf16[72,2,512]{2,1,0:T(2,128)(2,1)S(1)}, bf16[72,2,512]{2,1,0:T(2,128)(2,1)S(1)}, u32[]{:S(2)}, u32[]{:S(2)}) collective-permute-start(bf16[72,2,512]{2,1,0:T(2,128)(2,1)S(1)} %pad_maximum_fusion.5.refs_0_), channel_id=1, source_target_pairs={{0,1},{1,0},{2,3},{3,2},{4,5},{5,4},{6,7},{7,6},{8,9},{9,8},{10,11... | collective-permute-start | bytes 442376 | tf_op jit(solution)/shard_map/ppermute | solution.py:619
  6.5 1.2 %copy-start.1 = (bf16[512,2,512]{2,1,0:T(2,128)(2,1)S(1)}, bf16[512,2,512]{2,1,0:T(2,128)(2,1)}, u32[]{:S(2)}) copy-start(bf16[512,2,512]{2,1,0:T(2,128)(2,1)} %param.12) | copy-start | bytes 3145732
  7.7 8.3 %copy-start.4 = (bf16[64,2,512]{2,1,0:T(2,128)(2,1)S(1)}, bf16[64,2,512]{2,1,0:T(2,128)(2,1)}, u32[]{:S(2)}) copy-start(bf16[64,2,512]{2,1,0:T(2,128)(2,1)} %refs_0_) | copy-start | bytes 393220
  11.1 1.6 %collective-permute-start.2 = (bf16[72,2,512]{2,1,0:T(2,128)(2,1)S(1)}, bf16[72,2,512]{2,1,0:T(2,128)(2,1)S(1)}, u32[]{:S(2)}, u32[]{:S(2)}) collective-permute-start(bf16[72,2,512]{2,1,0:T(2,128)(2,1)S(1)} %collective-permute-done.1.refs_2_), channel_id=1, source_target_pairs={{0,1},{1,0},{2,3},{3,2},{4,5},{5,4},{6,7},{7,6},{8,9},{9,8},{10,11... | collective-permute-start | bytes 442376 | tf_op jit(solution)/shard_map/ppermute | solution.py:619
  11.7 5.7 %collective-permute-start.6 = (bf16[64,2,512]{2,1,0:T(2,128)(2,1)}, bf16[64,2,512]{2,1,0:T(2,128)(2,1)S(1)}, u32[]{:S(2)}, u32[]{:S(2)}) collective-permute-start(bf16[64,2,512]{2,1,0:T(2,128)(2,1)} %refs_0_), channel_id=1, source_target_pairs={{0,2},{1,3},{2,0},{3,1},{4,6},{5,7},{6,4},{7,5},{8,10},{9,11},{10,... | collective-permute-start | bytes 393224 | tf_op jit(solution)/shard_map/ppermute | solution.py:619
  14.9 5.1 %copy-start.3 = (bf16[512,1024]{1,0:T(8,128)(2,1)S(1)}, bf16[512,1024]{1,0:T(8,128)(2,1)}, u32[]{:S(2)}) copy-start(bf16[512,1024]{1,0:T(8,128)(2,1)} %refs_4_.1) | copy-start | bytes 3145732
  14.9 3.8 %collective-permute-start.3 = (f32[1,8,512]{2,1,0:T(8,128)S(1)}, f32[1,8,512]{2,1,0:T(8,128)S(1)}, u32[]{:S(2)}, u32[]{:S(2)}) collective-permute-start(f32[1,8,512]{2,1,0:T(8,128)S(1)} %bitcast.56), channel_id=1, source_target_pairs={{0,2},{1,3},{2,0},{3,1},{4,6},{5,7},{6,4},{7,5},{8,10},{9,11},{10,... | collective-permute-start | bytes 49160 | tf_op jit(solution)/shard_map/ppermute | solution.py:619
  16.0 3.1 %collective-permute-start.5 = (bf16[64,2,512]{2,1,0:T(2,128)(2,1)S(1)}, bf16[64,2,512]{2,1,0:T(2,128)(2,1)S(1)}, u32[]{:S(2)}, u32[]{:S(2)}) collective-permute-start(bf16[64,2,512]{2,1,0:T(2,128)(2,1)S(1)} %copy-done.4), channel_id=1, source_target_pairs={{0,1},{1,0},{2,3},{3,2},{4,5},{5,4},{6,7},{7,6},{8,9},{9,8},{10,11... | collective-permute-start | bytes 393224 | tf_op jit(solution)/shard_map/ppermute | solution.py:619
  17.4 1.7 %collective-permute-start.7 = (bf16[64,2,512]{2,1,0:T(2,128)(2,1)S(1)}, bf16[64,2,512]{2,1,0:T(2,128)(2,1)S(1)}, u32[]{:S(2)}, u32[]{:S(2)}) collective-permute-start(bf16[64,2,512]{2,1,0:T(2,128)(2,1)S(1)} %collective-permute-done.6.refs_2_), channel_id=1, source_target_pairs={{0,1},{1,0},{2,3},{3,2},{4,5},{5,4},{6,7},{7,6},{8,9},{9,8},{10,11... | collective-permute-start | bytes 393224 | tf_op jit(solution)/shard_map/ppermute | solution.py:619
  18.7 1.2 %collective-permute-start.4 = (f32[2,8,512]{2,1,0:T(8,128)S(1)}, f32[2,8,512]{2,1,0:T(8,128)S(1)}, u32[]{:S(2)}, u32[]{:S(2)}) collective-permute-start(f32[2,8,512]{2,1,0:T(8,128)S(1)} %get-tuple-element.150), channel_id=1, source_target_pairs={{0,1},{1,0},{2,3},{3,2},{4,5},{5,4},{6,7},{7,6},{8,9},{9,8},{10,11... | collective-permute-start | bytes 98312 | tf_op jit(solution)/shard_map/ppermute | solution.py:619
  26.8 6.2 %collective-permute-start.8 = (bf16[4,64,1024]{2,1,0:T(8,128)(2,1)S(1)}, bf16[4,64,1024]{2,1,0:T(8,128)(2,1)S(1)}, u32[]{:S(2)}, u32[]{:S(2)}) collective-permute-start(bf16[4,64,1024]{2,1,0:T(8,128)(2,1)S(1)} %get-tuple-element.85), channel_id=1, source_target_pairs={{0,1},{1,0},{2,3},{3,2},{4,5},{5,4},{6,7},{7,6},{8,9},{9,8},{10,11... | collective-permute-start | bytes 1572872 | tf_op jit(solution)/shard_map/ppermute | solution.py:619
  31.4 1.6 %collective-permute-start.9 = (bf16[4,64,512]{2,1,0:T(8,128)(2,1)S(1)}, bf16[4,64,512]{2,1,0:T(8,128)(2,1)S(1)}, u32[]{:S(2)}, u32[]{:S(2)}) collective-permute-start(bf16[4,64,512]{2,1,0:T(8,128)(2,1)S(1)} %get-tuple-element.92), channel_id=1, source_target_pairs={{0,1},{1,0},{2,3},{3,2},{4,5},{5,4},{6,7},{7,6},{8,9},{9,8},{10,11... | collective-permute-start | bytes 786440 | tf_op jit(solution)/shard_map/ppermute | solution.py:619
  33.1 3.9 %collective-permute-start.13 = (f32[1,8,512]{2,1,0:T(8,128)S(1)}, f32[1,8,512]{2,1,0:T(8,128)S(1)}, u32[]{:S(2)}, u32[]{:S(2)}) collective-permute-start(f32[1,8,512]{2,1,0:T(8,128)S(1)} %bitcast.53), channel_id=1, source_target_pairs={{0,2},{1,3},{2,0},{3,1},{4,6},{5,7},{6,4},{7,5},{8,10},{9,11},{10,... | collective-permute-start | bytes 49160 | tf_op jit(solution)/shard_map/ppermute | solution.py:619
  34.3 9.5 %collective-permute-start.10 = (bf16[1,64,1536]{2,1,0:T(8,128)(2,1)S(1)}, bf16[1,64,1536]{2,1,0:T(8,128)(2,1)S(1)}, u32[]{:S(2)}, u32[]{:S(2)}) collective-permute-start(bf16[1,64,1536]{2,1,0:T(8,128)(2,1)S(1)} %pad_maximum_fusion.2), channel_id=1, source_target_pairs={{0,2},{1,3},{2,0},{3,1},{4,6},{5,7},{6,4},{7,5},{8,10},{9,11},{10,... | collective-permute-start | bytes 589832 | tf_op jit(solution)/shard_map/ppermute | solution.py:619
  35.4 9.9 %collective-permute-start.11 = (bf16[1,64,1536]{2,1,0:T(8,128)(2,1)S(1)}, bf16[1,64,1536]{2,1,0:T(8,128)(2,1)S(1)}, u32[]{:S(2)}, u32[]{:S(2)}) collective-permute-start(bf16[1,64,1536]{2,1,0:T(8,128)(2,1)S(1)} %pad_maximum_fusion.3), channel_id=1, source_target_pairs={{0,4},{1,5},{2,6},{3,7},{4,0},{5,1},{6,2},{7,3},{8,12},{9,13},{10,... | collective-permute-start | bytes 589832 | tf_op jit(solution)/shard_map/ppermute | solution.py:619
  37.0 2.0 %collective-permute-start.14 = (f32[2,8,512]{2,1,0:T(8,128)S(1)}, f32[2,8,512]{2,1,0:T(8,128)S(1)}, u32[]{:S(2)}, u32[]{:S(2)}) collective-permute-start(f32[2,8,512]{2,1,0:T(8,128)S(1)} %get-tuple-element.148), channel_id=1, source_target_pairs={{0,1},{1,0},{2,3},{3,2},{4,5},{5,4},{6,7},{7,6},{8,9},{9,8},{10,11... | collective-permute-start | bytes 98312 | tf_op jit(solution)/shard_map/ppermute | solution.py:619
  37.1 9.8 %collective-permute-start.12 = (bf16[1,64,1536]{2,1,0:T(8,128)(2,1)S(1)}, bf16[1,64,1536]{2,1,0:T(8,128)(2,1)S(1)}, u32[]{:S(2)}, u32[]{:S(2)}) collective-permute-start(bf16[1,64,1536]{2,1,0:T(8,128)(2,1)S(1)} %pad_maximum_fusion.4), channel_id=1, source_target_pairs={{0,6},{1,7},{2,4},{3,5},{4,2},{5,3},{6,0},{7,1},{8,14},{9,15},{10,... | collective-permute-start | bytes 589832 | tf_op jit(solution)/shard_map/ppermute | solution.py:619
  41.1 1.6 %collective-permute-start.15 = (bf16[2,128,512]{2,1,0:T(8,128)(2,1)S(1)}, bf16[2,128,512]{2,1,0:T(8,128)(2,1)S(1)}, u32[]{:S(2)}, u32[]{:S(2)}) collective-permute-start(bf16[2,128,512]{2,1,0:T(8,128)(2,1)S(1)} %get-tuple-element.104), channel_id=1, source_target_pairs={{0,1},{1,0},{2,3},{3,2},{4,5},{5,4},{6,7},{7,6},{8,9},{9,8},{10,11... | collective-permute-start | bytes 786440 | tf_op jit(solution)/shard_map/ppermute | solution.py:619
  42.7 9.1 %copy-start.2 = (bf16[512,2,512]{2,1,0:T(2,128)(2,1)S(1)}, bf16[512,2,512]{2,1,0:T(2,128)(2,1)}, u32[]{:S(2)}) copy-start(bf16[512,2,512]{2,1,0:T(2,128)(2,1)} %param.12) | copy-start | bytes 3145732
  42.8 7.9 %collective-permute-start.16 = (bf16[144,512]{1,0:T(8,128)(2,1)S(1)}, bf16[144,512]{1,0:T(8,128)(2,1)S(1)}, u32[]{:S(2)}, u32[]{:S(2)}) collective-permute-start(bf16[144,512]{1,0:T(8,128)(2,1)S(1)} %pad_maximum_fusion.6), channel_id=1, source_target_pairs={{0,2},{1,3},{2,0},{3,1},{4,6},{5,7},{6,4},{7,5},{8,10},{9,11},{10,... | collective-permute-start | bytes 442376 | tf_op jit(solution)/shard_map/ppermute | solution.py:619
  47.0 9.7 %collective-permute-start.21 = (bf16[64,1536]{1,0:T(8,128)(2,1)S(1)}, bf16[64,1536]{1,0:T(8,128)(2,1)S(1)}, u32[]{:S(2)}, u32[]{:S(2)}) collective-permute-start(bf16[64,1536]{1,0:T(8,128)(2,1)S(1)} %reduce-precision_convert_fusion.2), channel_id=1, source_target_pairs={{0,24},{1,25},{2,26},{3,27},{4,28},{5,29},{6,30},{7,31},{8,16},{9,... | collective-permute-start | bytes 589832 | tf_op jit(solution)/shard_map/ppermute | solution.py:619
  50.8 5.9 %collective-permute-start.17 = (bf16[144,512]{1,0:T(8,128)(2,1)S(1)}, bf16[144,512]{1,0:T(8,128)(2,1)S(1)}, u32[]{:S(2)}, u32[]{:S(2)}) collective-permute-start(bf16[144,512]{1,0:T(8,128)(2,1)S(1)} %pad_maximum_fusion.7), channel_id=1, source_target_pairs={{0,4},{1,5},{2,6},{3,7},{4,0},{5,1},{6,2},{7,3},{8,12},{9,13},{10,... | collective-permute-start | bytes 442376 | tf_op jit(solution)/shard_map/ppermute | solution.py:619
  56.8 6.8 %collective-permute-start.18 = (bf16[144,512]{1,0:T(8,128)(2,1)S(1)}, bf16[144,512]{1,0:T(8,128)(2,1)S(1)}, u32[]{:S(2)}, u32[]{:S(2)}) collective-permute-start(bf16[144,512]{1,0:T(8,128)(2,1)S(1)} %pad_maximum_fusion.8), channel_id=1, source_target_pairs={{0,8},{1,9},{2,10},{3,11},{4,12},{5,13},{6,14},{7,15},{8,0},{9,1},... | collective-permute-start | bytes 442376 | tf_op jit(solution)/shard_map/ppermute | solution.py:619
  58.6 8.6 %collective-permute-start.22 = (bf16[64,1536]{1,0:T(8,128)(2,1)S(1)}, bf16[64,1536]{1,0:T(8,128)(2,1)S(1)}, u32[]{:S(2)}, u32[]{:S(2)}) collective-permute-start(bf16[64,1536]{1,0:T(8,128)(2,1)S(1)} %reduce-precision_convert_fusion.1), channel_id=1, source_target_pairs={{0,8},{1,9},{2,10},{3,11},{4,12},{5,13},{6,14},{7,15},{8,0},{9,1},... | collective-permute-start | bytes 589832 | tf_op jit(solution)/shard_map/ppermute | solution.py:619
  63.7 12.0 %collective-permute-start.19 = (bf16[144,512]{1,0:T(8,128)(2,1)S(1)}, bf16[144,512]{1,0:T(8,128)(2,1)S(1)}, u32[]{:S(2)}, u32[]{:S(2)}) collective-permute-start(bf16[144,512]{1,0:T(8,128)(2,1)S(1)} %pad_maximum_fusion.9), channel_id=1, source_target_pairs={{0,24},{1,25},{2,26},{3,27},{4,28},{5,29},{6,30},{7,31},{8,16},{9,... | collective-permute-start | bytes 442376 | tf_op jit(solution)/shard_map/ppermute | solution.py:619
  67.3 5.7 %collective-permute-start.23 = (bf16[64,1536]{1,0:T(8,128)(2,1)S(1)}, bf16[64,1536]{1,0:T(8,128)(2,1)S(1)}, u32[]{:S(2)}, u32[]{:S(2)}) collective-permute-start(bf16[64,1536]{1,0:T(8,128)(2,1)S(1)} %reduce-precision_convert_fusion), channel_id=1, source_target_pairs={{0,4},{1,5},{2,6},{3,7},{4,0},{5,1},{6,2},{7,3},{8,12},{9,13},{10,... | collective-permute-start | bytes 589832 | tf_op jit(solution)/shard_map/ppermute | solution.py:619
  68.6 5.0 %collective-permute-start.24 = (bf16[64,1024]{1,0:T(8,128)(2,1)S(1)}, bf16[64,1024]{1,0:T(8,128)(2,1)S(1)}, u32[]{:S(2)}, u32[]{:S(2)}) collective-permute-start(bf16[64,1024]{1,0:T(8,128)(2,1)S(1)} %get-tuple-element.139), channel_id=1, source_target_pairs={{0,2},{1,3},{2,0},{3,1},{4,6},{5,7},{6,4},{7,5},{8,10},{9,11},{10,... | collective-permute-start | bytes 393224 | tf_op jit(solution)/shard_map/ppermute | solution.py:619
  69.7 5.9 %collective-permute-start.25 = (bf16[64,1024]{1,0:T(8,128)(2,1)S(1)}, bf16[64,1024]{1,0:T(8,128)(2,1)S(1)}, u32[]{:S(2)}, u32[]{:S(2)}) collective-permute-start(bf16[64,1024]{1,0:T(8,128)(2,1)S(1)} %get-tuple-element.139), channel_id=1, source_target_pairs={{0,6},{1,7},{2,4},{3,5},{4,2},{5,3},{6,0},{7,1},{8,14},{9,15},{10,... | collective-permute-start | bytes 393224 | tf_op jit(solution)/shard_map/ppermute | solution.py:619
  75.6 4.0 %collective-permute-start.27 = (bf16[3,64,1024]{2,1,0:T(8,128)(2,1)S(1)}, bf16[3,64,1024]{2,1,0:T(8,128)(2,1)S(1)}, u32[]{:S(2)}, u32[]{:S(2)}) collective-permute-start(bf16[3,64,1024]{2,1,0:T(8,128)(2,1)S(1)} %pad_maximum_fusion.1.refs_1_), channel_id=1, source_target_pairs={{0,1},{1,0},{2,3},{3,2},{4,5},{5,4},{6,7},{7,6},{8,9},{9,8},{10,11... | collective-permute-start | bytes 1179656 | tf_op jit(solution)/shard_map/ppermute | solution.py:619
  75.7 1.7 %collective-permute-start.20 = (f32[8,512]{1,0:T(8,128)S(1)}, f32[8,512]{1,0:T(8,128)S(1)}, u32[]{:S(2)}, u32[]{:S(2)}) collective-permute-start(f32[8,512]{1,0:T(8,128)S(1)} %add_add_fusion.sums_ref), channel_id=1, source_target_pairs={{0,1},{1,0},{2,3},{3,2},{4,5},{5,4},{6,7},{7,6},{8,9},{9,8},{10,11... | collective-permute-start | bytes 49160 | tf_op jit(solution)/shard_map/ppermute | solution.py:619
  76.2 3.3 %collective-permute-start.26 = (bf16[1,64,1024]{2,1,0:T(8,128)(2,1)S(1)}, bf16[1,64,1024]{2,1,0:T(8,128)(2,1)S(1)}, u32[]{:S(2)}, u32[]{:S(2)}) collective-permute-start(bf16[1,64,1024]{2,1,0:T(8,128)(2,1)S(1)} %get-tuple-element.140.refs_0_), channel_id=1, source_target_pairs={{0,1},{1,0},{2,3},{3,2},{4,5},{5,4},{6,7},{7,6},{8,9},{9,8},{10,11... | collective-permute-start | bytes 393224 | tf_op jit(solution)/shard_map/ppermute | solution.py:619

commit v4 on v3

--- a/solution.py
+++ b/solution.py
@@ -15,6 +15,12 @@
 GELU_A = 0.7978845608028654
 GELU_B = 0.044715
 MIB = 1 << 20
+
+
+def repeat(first, last, body, carry):
+    for k in range(first, last):
+        carry = body(k, carry)
+    return carry
 
 
 def cmul(ar, ai, br, bi):
@@ -150,9 +156,9 @@
     gain, bias = vec_ref[0:1, :], vec_ref[1:2, :]
 
     def chunk(c, carry):
-        base = pl.multiple_of(c * size, size)
+        base = c * size
         at = pl.ds(base, size)
-        x = rows_in(x_ref, pl.multiple_of(c * (size // SUB), size // SUB), size // SUB)
+        x = rows_in(x_ref, c * (size // SUB), size // SUB)
         centred = x - jnp.mean(x, axis=1, keepdims=True)
         inv = lax.rsqrt(jnp.mean(centred * centred, axis=1, keepdims=True) + EPSILON)
         unit = centred * inv
@@ -162,7 +168,7 @@
         mask_ref[at, :] = row_mask(base, size, group, steps, me, vec_ref[7:8, :])
         return carry
 
-    lax.fori_loop(0, rows // size, chunk, 0)
+    repeat(0, rows // size, chunk, 0)
 
 
 def gather_rows(me, blocks, flat_ref, dst_ref):
@@ -275,13 +281,13 @@
     cst_ref[4:8, :] = jnp.zeros((4, 2 * channels), F32)
 
     def chunk(c, carry):
-        base = pl.multiple_of(c * CHUNK, CHUNK)
+        base = c * CHUNK
         at = pl.ds(base, CHUNK)
         mask = mask_ref[at, :]
         drive_ref[at, :] = nt(low_ref[at, :], win_ref[...]) * (gains * wide(mask, 2 * channels))
         return carry
 
-    lax.fori_loop(0, rows // CHUNK, chunk, 0)
+    repeat(0, rows // CHUNK, chunk, 0)
     br = jnp.broadcast_to(pr, (SUB, channels))
     bi = jnp.broadcast_to(pi, (SUB, channels))
 
@@ -332,7 +338,7 @@
     lax.fori_loop(0, steps, step, (hr, hi), unroll=8)
 
     def chunk(c, carry):
-        base = pl.multiple_of(c * CHUNK, CHUNK)
+        base = c * CHUNK
         at = pl.ds(base, CHUNK)
         states = states_ref[pl.ds(pl.multiple_of(base + SUB, SUB), CHUNK), :]
         slow = jnp.concatenate([states[:, :channels], -states[:, channels:]], axis=1).astype(BF16)
@@ -355,15 +361,15 @@
         dglu_ref[at, feats:] = (d_value * value * (1.0 - gate)).astype(BF16)
         return carry
 
-    lax.fori_loop(0, rows // CHUNK, chunk, 0)
+    repeat(0, rows // CHUNK, chunk, 0)
     width = 256
 
     def tile(c, carry):
-        at = pl.ds(pl.multiple_of(c * width, width), width)
+        at = pl.ds(c * width, width)
         acc_ref[:, at] = tn(act_ref[...], dglu_ref[:, at])
         return carry
 
-    lax.fori_loop(0, 2 * feats // width, tile, 0)
+    repeat(0, 2 * feats // width, tile, 0)
     spread(acc_ref, place, orders, grads)
 
 
@@ -398,7 +404,7 @@
     gain, bias = vec_ref[0:1, :], vec_ref[1:2, :]
 
     def chunk(c, total):
-        at = pl.ds(pl.multiple_of(c * CHUNK, CHUNK), CHUNK)
+        at = pl.ds(c * CHUNK, CHUNK)
         d_pre = nt(dglu_ref[at, :], glu_ref[...]) * gp_ref[at, :]
         dpre_ref[at, :] = d_pre
         normed = unit_ref[at, :] * gain + bias
@@ -408,7 +414,7 @@
         dst_ref[at, :] = nt(d_mixed, cw_ref[...])
         return total
 
-    total = lax.fori_loop(0, rows // CHUNK, chunk, jnp.zeros((SUB, feats), F32))
+    total = repeat(0, rows // CHUNK, chunk, jnp.zeros((SUB, feats), F32))
     skip_ref[...] = total
     pr, pi = cst_ref[0:1, :channels], cst_ref[0:1, channels:]
     br = jnp.broadcast_to(pr, (SUB, channels))
@@ -428,11 +434,11 @@
     width = 256
 
     def tile(c, carry):
-        at = pl.ds(pl.multiple_of(c * width, width), width)
+        at = pl.ds(c * width, width)
         acc_ref[:, at] = tn(slow_ref[...], dmix_ref[:, at])
         return carry
 
-    lax.fori_loop(0, feats // width, tile, 0)
+    repeat(0, feats // width, tile, 0)
     spread(acc_ref, place, orders, grads)
 
 
@@ -481,22 +487,22 @@
     gains = cst_ref[3:4, :]
 
     def chunk(c, carry):
-        base = pl.multiple_of(c * CHUNK, CHUNK)
+        base = c * CHUNK
         at = pl.ds(base, CHUNK)
         mask = mask_ref[at, :]
         dproj_ref[at, :] = (adj_ref[at, :] * (gains * wide(mask, 2 * channels))).astype(BF16)
         return carry
 
-    lax.fori_loop(0, rows // CHUNK, chunk, 0)
+    repeat(0, rows // CHUNK, chunk, 0)
     width = 256
     feats = low_ref.shape[1]
 
     def tile(c, carry):
-        at = pl.ds(pl.multiple_of(c * width, width), width)
+        at = pl.ds(c * width, width)
         acc_ref[:, at] = tn(dproj_ref[...], low_ref[:, at])
         return carry
 
-    lax.fori_loop(0, feats // width, tile, 0)
+    repeat(0, feats // width, tile, 0)
     spread_pairs(acc_ref, me, own, channels, orders, grads)
 
 
@@ -508,7 +514,7 @@
     copies = start_copies([x_hbm.at[:, p] for p in places], [x_ref.at[:, p] for p in places], sems)
 
     def chunk(c, carry):
-        first = pl.multiple_of(c * size, size)
+        first = c * size
         rows = branch_ref[pl.ds(pl.multiple_of(first * SUB, size * SUB), size * SUB), :]
         at = pl.ds(first, size)
         out_ref[:, at] = (x_ref[:, at].astype(F32) + rows_out(rows, x_ref)).astype(BF16)
@@ -516,7 +522,7 @@
 
     for k in range(4):
         copies[k].wait()
-        lax.fori_loop(k * cut // size, (k + 1) * cut // size, chunk, 0)
+        repeat(k * cut // size, (k + 1) * cut // size, chunk, 0)
 
 
 def normed_kernel(dproj_ref, win_ref, dpre_ref, unit_ref, vec_ref, channel_ref, skip_ref, dnorm_ref, sums_ref):
@@ -525,14 +531,14 @@
 
     def chunk(c, carry):
         total_gain, total_bias = carry
-        at = pl.ds(pl.multiple_of(c * CHUNK, CHUNK), CHUNK)
+        at = pl.ds(c * CHUNK, CHUNK)
         d_normed = dpre_ref[at, :] * skip + nn(dproj_ref[at, :], win_ref[...])
         dnorm_ref[at, :] = d_normed
         folded = lambda v: jnp.sum(v.reshape(CHUNK // SUB, SUB, feats), axis=0)
         return total_gain + folded(d_normed * unit_ref[at, :]), total_bias + folded(d_normed)
 
     zero = jnp.zeros((SUB, feats), F32)
-    total_gain, total_bias = lax.fori_loop(0, rows // CHUNK, chunk, (zero, zero))
+    total_gain, total_bias = repeat(0, rows // CHUNK, chunk, (zero, zero))
     over = lambda v: jnp.sum(v, axis=0, keepdims=True)
     channel = over(channel_ref[...])
     wide_at = channel.shape[1] - feats
@@ -555,19 +561,19 @@
     copies = start_copies([cot_hbm.at[:, p] for p in places], [cot_ref.at[:, p] for p in places], sems)
 
     def chunk(c, carry):
-        at = pl.ds(pl.multiple_of(c * size, size), size)
+        at = pl.ds(c * size, size)
         unit = unit_ref[at, :]
         d_unit = dnorm_ref[at, :] * gain
         first = jnp.mean(d_unit, axis=1, keepdims=True)
         second = jnp.mean(d_unit * unit, axis=1, keepdims=True)
         rows = wide(inv_ref[at, :], feats) * (d_unit - first - unit * second)
-        step_at = pl.ds(pl.multiple_of(c * steps, steps), steps)
+        step_at = pl.ds(c * steps, steps)
         out_ref[:, step_at] = cot_ref[:, step_at].astype(F32) + rows_out(rows, cot_ref)
         return carry
 
     for k in range(4):
         copies[k].wait()
-        lax.fori_loop(k * cut // steps, (k + 1) * cut // steps, chunk, 0)
+        repeat(k * cut // steps, (k + 1) * cut // steps, chunk, 0)
 
 
 def join_pairs(parts, flat_ref, out_ref):

time: 81.2 us -> 78 us (0.961)
  Pallas kernels: 28.9 us -> 23.8 us
  waiting for transfers between devices: 19.7 us -> 21 us
    pallas_call x14, Pallas kernels: 28.9 us -> 23.8 us  [call(): pl.pallas_call(body, out_shape=[jax.ShapeDtypeStruct(s, d) for s, d in ou...]
    ppermute x28, waiting for transfers between devices: 19.7 us -> 21 us  [exchange(): lax.ppermute(x, ('seq', 'state'), [(i, i ^ mask) for i in range(count)])]
  transfers between devices with their start and end apart: 28 -> 28, of which waited for: 13 -> 15; matrix products, arithmetic and copies ran while one was open for 2% -> 2% of each run, Pallas kernels for 25% -> 22%
where the time goes in v4:
time: 78 us; the launch traced here: 77.8 us
  starting transfers between devices  26.6 us (34%)
  Pallas kernels  23.8 us (31%)
  waiting for transfers between devices  21 us (27%)
  local copies, waits for them, and re-layouts  2.71 us (3%)
  other arithmetic  2.6 us (3%)
  between operations  1.02 us (1%)
    ppermute x28, starting transfers between devices, exchange(): lax.ppermute(x, ('seq', 'state'), [(i, i ^ mask) for i in range(count)])  26.6 us
    pallas_call x14, Pallas kernels, call(): pl.pallas_call(body, out_shape=[jax.ShapeDtypeStruct(s, d) for s, d in ou...  23.8 us
    ppermute x28, waiting for transfers between devices, exchange(): lax.ppermute(x, ('seq', 'state'), [(i, i ^ mask) for i in range(count)])  21 us
  transfers between devices with their start and end apart: 28, of which 15 were waited for; matrix products, arithmetic and copies ran while one was open for 2% of the time, Pallas kernels for 22%

profile of v4, /device:TPU:0, one launch (start us, length us, event | category | flops | bytes accessed | tf_op | source)
XLA Modules:
  0.0 77.8 jit_solution(8739689252819539978)
XLA Ops:
  0.7 0.7 convert_element_type.197
  1.4 0.8 %concatenate.57 = f32[1730]{0:T(1024)S(1)} concatenate(f32[512]{0:T(512)} %param.13, f32[512]{0:T(512)} %param.14, f32[512]{0:T(512)} %param.20, f32[64]{0:T(128)} %param.17, f32[64]{0:T(128)} %param.18, f32[64]{0:T(128)} %param.19, f32[2]{0:T(128)S(1)} %convert_element_type.197), dimensions={0} | concatenate | bytes 13840 | tf_op jit(solution)/shard_map/concatenate | solution.py:737
  2.2 0.1 prep.1
  2.4 1.1 %pad_maximum_fusion.5.refs_0_ = bf16[72,2,512]{2,1,0:T(2,128)(2,1)S(1)} fusion(bf16[8,2,512]{2,1,0:T(2,128)(2,1)S(1)} %get-tuple-element.73, bf16[64,2,512]{2,1,0:T(2,128)(2,1)} %bitcast.60), kind=kLoop, calls=%fused_computation.19 | loop fusion | flops 73728 | bytes 294912 | tf_op jit(solution)/shard_map/concatenate | solution.py:750
  3.5 3.0 %collective-permute-start.1 = (bf16[72,2,512]{2,1,0:T(2,128)(2,1)S(1)}, bf16[72,2,512]{2,1,0:T(2,128)(2,1)S(1)}, u32[]{:S(2)}, u32[]{:S(2)}) collective-permute-start(bf16[72,2,512]{2,1,0:T(2,128)(2,1)S(1)} %pad_maximum_fusion.5.refs_0_), channel_id=1, source_target_pairs={{0,2},{1,3},{2,0},{3,1},{4,6},{5,7},{6,4},{7,5},{8,10},{9,11},{10,... | collective-permute-start | bytes 442376 | tf_op jit(solution)/shard_map/ppermute | solution.py:625
  6.5 1.2 %copy-done.1 = bf16[512,2,512]{2,1,0:T(2,128)(2,1)S(1)} copy-done((bf16[512,2,512]{2,1,0:T(2,128)(2,1)S(1)}, bf16[512,2,512]{2,1,0:T(2,128)(2,1)}, u32[]{:S(2)}) %copy-start.1) | copy-done | bytes 1048600
  7.7 2.1 %norm.1 = (bf16[1024,512]{1,0:T(8,128)(2,1)S(1)}, f32[1024,512]{1,0:T(8,128)S(1)}, f32[1024,128]{1,0:T(8,128)S(1)}, f32[1024,128]{1,0:T(8,128)S(1)}) custom-call(bf16[4,128,2,512]{3,2,1,0:T(2,128)(2,1)S(1)} %bitcast.50, f32[8,512]{1,0:T(8,128)S(1)} %get-tuple-element.70.vec_ref.refs_8_.refs_3_), custom_call_target="tpu_custom_call" | custom-call | flops 10485760 | bytes 4194304 | tf_op jit(solution)/shard_map/norm/pallas_call | solution.py:74
  9.8 0.5 collective-permute-done.1.refs_2_
  10.3 0.1 collective-permute-start.2
  10.4 1.7 %collective-permute-start.6 = (bf16[64,2,512]{2,1,0:T(2,128)(2,1)}, bf16[64,2,512]{2,1,0:T(2,128)(2,1)S(1)}, u32[]{:S(2)}, u32[]{:S(2)}) collective-permute-start(bf16[64,2,512]{2,1,0:T(2,128)(2,1)} %refs_0_), channel_id=1, source_target_pairs={{0,2},{1,3},{2,0},{3,1},{4,6},{5,7},{6,4},{7,5},{8,10},{9,11},{10,... | collective-permute-start | bytes 393224 | tf_op jit(solution)/shard_map/ppermute | solution.py:625
  12.1 1.8 %project.1 = (f32[1024,512]{1,0:T(8,128)S(1)}, f32[8,512]{1,0:T(8,128)S(1)}, bf16[512,512]{1,0:T(8,128)(2,1)S(1)}, f32[8,512]{1,0:T(8,128)S(1)}) custom-call(bf16[1024,512]{1,0:T(8,128)(2,1)S(1)} %get-tuple-element.71.low_ref.refs_6_, f32[1024,128]{1,0:T(8,128)S(1)} %get-tuple-element.72.mask_ref.refs_7_, bf16[72,2,512]{2,1,0:T(2,128)(2,1)S(1)} %pad_maximum_fusion.5.refs_0_, ...), custom_call_target="tpu_custom_call" | custom-call | flops 536870912 | bytes 4194304 | tf_op jit(solution)/shard_map/project/pallas_call | solution.py:74
  13.9 1.4 %collective-permute-start.3 = (f32[1,8,512]{2,1,0:T(8,128)S(1)}, f32[1,8,512]{2,1,0:T(8,128)S(1)}, u32[]{:S(2)}, u32[]{:S(2)}) collective-permute-start(f32[1,8,512]{2,1,0:T(8,128)S(1)} %bitcast.56), channel_id=1, source_target_pairs={{0,2},{1,3},{2,0},{3,1},{4,6},{5,7},{6,4},{7,5},{8,10},{9,11},{10,... | collective-permute-start | bytes 49160 | tf_op jit(solution)/shard_map/ppermute | solution.py:625
  15.3 1.1 %collective-permute-done.6.refs_2_ = bf16[64,2,512]{2,1,0:T(2,128)(2,1)S(1)} collective-permute-done((bf16[64,2,512]{2,1,0:T(2,128)(2,1)}, bf16[64,2,512]{2,1,0:T(2,128)(2,1)S(1)}, u32[]{:S(2)}, u32[]{:S(2)}) %collective-permute-start.6) | collective-permute-done | bytes 131104 | tf_op jit(solution)/shard_map/ppermute | solution.py:625
  16.5 1.2 %collective-permute-done.3 = f32[1,8,512]{2,1,0:T(8,128)S(1)} collective-permute-done((f32[1,8,512]{2,1,0:T(8,128)S(1)}, f32[1,8,512]{2,1,0:T(8,128)S(1)}, u32[]{:S(2)}, u32[]{:S(2)}) %collective-permute-start.3) | collective-permute-done | bytes 16416 | tf_op jit(solution)/shard_map/ppermute | solution.py:625
  17.7 0.3 cotangent.1.refs_6_
  18.1 0.4 weights.1.refs_4_.refs_5_
  18.4 0.5 collective-permute-done.4
  18.9 5.4 %mix.1 = (f32[1032,512]{1,0:T(8,128)S(1)}, bf16[1024,512]{1,0:T(8,128)(2,1)S(1)}, f32[1024,512]{1,0:T(8,128)S(1)}, bf16[1024,1024]{1,0:T(8,128)(2,1)S(1)}, f32[1...) custom-call(f32[1024,512]{1,0:T(8,128)S(1)} %get-tuple-element.75.re, ...), custom_call_target="tpu_custom_call" | custom-call | flops 2684354560 | bytes 4194304 | tf_op jit(solution)/shard_map/mix/pallas_call | solution.py:74
  24.3 0.2 collective-permute-start.8
  24.6 3.5 %back.1 = (f32[1024,512]{1,0:T(8,128)S(1)}, f32[1024,512]{1,0:T(8,128)S(1)}, f32[8,512]{1,0:T(8,128)S(1)}, f32[8,512]{1,0:T(8,128)S(1)}, bf16[4,64,512]{2,1,0:T(...) custom-call(bf16[1024,1024]{1,0:T(8,128)(2,1)S(1)} %get-tuple-elemen, ...), custom_call_target="tpu_custom_call" | custom-call | flops 2147483648 | bytes 4194304 | tf_op jit(solution)/shard_map/back/pallas_call | solution.py:74
  28.0 0.4 collective-permute-start.9
  28.4 1.2 %collective-permute-done.9 = bf16[4,64,512]{2,1,0:T(8,128)(2,1)S(1)} collective-permute-done((bf16[4,64,512]{2,1,0:T(8,128)(2,1)S(1)}, bf16[4,64,512]{2,1,0:T(8,128)(2,1)S(1)}, u32[]{:S(2)}, u32[]{:S(2)}) %collective-permute-start.9) | collective-permute-done | bytes 262176 | tf_op jit(solution)/shard_map/ppermute | solution.py:625
  29.6 0.1 convert_add_fusion.2
  29.7 1.4 %collective-permute-start.13 = (f32[1,8,512]{2,1,0:T(8,128)S(1)}, f32[1,8,512]{2,1,0:T(8,128)S(1)}, u32[]{:S(2)}, u32[]{:S(2)}) collective-permute-start(f32[1,8,512]{2,1,0:T(8,128)S(1)} %bitcast.53), channel_id=1, source_target_pairs={{0,2},{1,3},{2,0},{3,1},{4,6},{5,7},{6,4},{7,5},{8,10},{9,11},{10,... | collective-permute-start | bytes 49160 | tf_op jit(solution)/shard_map/ppermute | solution.py:625
  31.1 0.1 convert_add_fusion.1
  31.3 0.7 collective-permute-start.10
  32.0 1.6 %collective-permute-start.11 = (bf16[1,64,1536]{2,1,0:T(8,128)(2,1)S(1)}, bf16[1,64,1536]{2,1,0:T(8,128)(2,1)S(1)}, u32[]{:S(2)}, u32[]{:S(2)}) collective-permute-start(bf16[1,64,1536]{2,1,0:T(8,128)(2,1)S(1)} %pad_maximum_fusion.3), channel_id=1, source_target_pairs={{0,4},{1,5},{2,6},{3,7},{4,0},{5,1},{6,2},{7,3},{8,12},{9,13},{10,... | collective-permute-start | bytes 589832 | tf_op jit(solution)/shard_map/ppermute | solution.py:625
  33.6 0.1 collective-permute-start.14
  33.7 2.4 %collective-permute-start.12 = (bf16[1,64,1536]{2,1,0:T(8,128)(2,1)S(1)}, bf16[1,64,1536]{2,1,0:T(8,128)(2,1)S(1)}, u32[]{:S(2)}, u32[]{:S(2)}) collective-permute-start(bf16[1,64,1536]{2,1,0:T(8,128)(2,1)S(1)} %pad_maximum_fusion.4), channel_id=1, source_target_pairs={{0,6},{1,7},{2,4},{3,5},{4,2},{5,3},{6,0},{7,1},{8,14},{9,15},{10,... | collective-permute-start | bytes 589832 | tf_op jit(solution)/shard_map/ppermute | solution.py:625
  36.1 1.7 %adjoint.1 = (bf16[1024,512]{1,0:T(8,128)(2,1)S(1)}, f32[8,768]{1,0:T(8,128)S(1)}, bf16[2,128,512]{2,1,0:T(8,128)(2,1)S(1)}, f32[1,128,512]{2,1,0:T(8,128)S(1)}, f32[1,128,512]{2,1,0:T(8,128)S(1)}) custom-call(f32[1024,512]{1,0:T(8,128)S(1)} %get-tuple-element.100.refs_0_, f32[8,512]{1,0:T(8,128)S(1)} %get-tuple-element.101.refs_1_, ...), custom_call_target="tpu_custom_call" | custom-call | flops 1073741824 | bytes 4194304 | tf_op jit(solution)/shard_map/adjoint/pallas_call | solution.py:74
  37.9 0.3 collective-permute-start.15
  38.2 0.8 %normed.1 = (f32[1024,512]{1,0:T(8,128)S(1)}, f32[8,512]{1,0:T(8,128)S(1)}) custom-call(bf16[1024,512]{1,0:T(8,128)(2,1)S(1)} %get-tuple-element.105.dproj_ref, bf16[512,512]{1,0:T(8,128)(2,1)S(1)} %get-tuple-element.106.win_ref, f32[1024,512]{1,0:T(8,128)S(1)} %get-tuple-element.107.dpre_ref, f32[1024,512]{1,0:T(8,128)S(1)} %get-tuple-element.81.refs_5_.refs_2_.unit_ref, ...), custom_call_target="tpu_custom_call" | custom-call | flops 536870912 | bytes 4194304 | tf_op jit(solution)/shard_map/normed/pallas_call | solution.py:74
  39.0 0.0 copy-start.2
  39.0 0.5 collective-permute-done.15
  39.5 0.5 collective-permute-start.16
  40.1 1.9 %collective-permute-done.11 = bf16[1,64,1536]{2,1,0:T(8,128)(2,1)S(1)} collective-permute-done((bf16[1,64,1536]{2,1,0:T(8,128)(2,1)S(1)}, bf16[1,64,1536]{2,1,0:T(8,128)(2,1)S(1)}, u32[]{:S(2)}, u32[]{:S(2)}) %collective-permute-start.11) | collective-permute-done | bytes 196640 | tf_op jit(solution)/shard_map/ppermute | solution.py:625
  42.0 2.3 %collective-permute-done.12 = bf16[1,64,1536]{2,1,0:T(8,128)(2,1)S(1)} collective-permute-done((bf16[1,64,1536]{2,1,0:T(8,128)(2,1)S(1)}, bf16[1,64,1536]{2,1,0:T(8,128)(2,1)S(1)}, u32[]{:S(2)}, u32[]{:S(2)}) %collective-permute-start.12) | collective-permute-done | bytes 196640 | tf_op jit(solution)/shard_map/ppermute | solution.py:625
  44.3 0.1 reduce-precision_convert_fusion.2
  44.4 3.7 %collective-permute-start.21 = (bf16[64,1536]{1,0:T(8,128)(2,1)S(1)}, bf16[64,1536]{1,0:T(8,128)(2,1)S(1)}, u32[]{:S(2)}, u32[]{:S(2)}) collective-permute-start(bf16[64,1536]{1,0:T(8,128)(2,1)S(1)} %reduce-precision_convert_fusion.2), channel_id=1, source_target_pairs={{0,24},{1,25},{2,26},{3,27},{4,28},{5,29},{6,30},{7,31},{8,16},{9,... | collective-permute-start | bytes 589832 | tf_op jit(solution)/shard_map/ppermute | solution.py:625
  48.1 0.1 fusion.3
  48.1 0.2 collective-permute-start.17
  48.4 2.3 %out.1 = bf16[4,128,2,512]{3,2,1,0:T(2,128)(2,1)} custom-call(bf16[4,128,2,512]{3,2,1,0:T(2,128)(2,1)S(1)} %bitcast.51, f32[1024,512]{1,0:T(8,128)S(1)} %get-tuple-element.114.branch_ref), custom_call_target="tpu_custom_call" | custom-call | flops 1048576 | bytes 4194304 | tf_op jit(solution)/shard_map/out/pallas_call | solution.py:74
  50.7 2.5 %tokens.1 = f32[4,128,2,512]{3,2,1,0:T(2,128)} custom-call(bf16[4,128,2,512]{3,2,1,0:T(2,128)(2,1)S(1)} %bitcast.49, f32[1024,512]{1,0:T(8,128)S(1)} %get-tuple-element.116.dnorm_ref, f32[1024,512]{1,0:T(8,128)S(1)} %get-tuple-element.81.refs_5_.refs_2_.unit_ref, f32[1024,128]{1,0:T(8,128)S(1)} %get-tuple-element.117.inv_ref, ...), custom_call_target="tpu_custom_call" | custom-call | flops 536870912 | bytes 4194304 | tf_op jit(solution)/shard_map/tokens/pallas_call | solution.py:74
  53.1 0.2 collective-permute-done.17
  53.4 2.1 %collective-permute-start.18 = (bf16[144,512]{1,0:T(8,128)(2,1)S(1)}, bf16[144,512]{1,0:T(8,128)(2,1)S(1)}, u32[]{:S(2)}, u32[]{:S(2)}) collective-permute-start(bf16[144,512]{1,0:T(8,128)(2,1)S(1)} %pad_maximum_fusion.8), channel_id=1, source_target_pairs={{0,8},{1,9},{2,10},{3,11},{4,12},{5,13},{6,14},{7,15},{8,0},{9,1},... | collective-permute-start | bytes 442376 | tf_op jit(solution)/shard_map/ppermute | solution.py:625
  55.6 0.1 collective-permute-start.22
  55.7 4.6 %collective-permute-done.18 = bf16[144,512]{1,0:T(8,128)(2,1)S(1)} collective-permute-done((bf16[144,512]{1,0:T(8,128)(2,1)S(1)}, bf16[144,512]{1,0:T(8,128)(2,1)S(1)}, u32[]{:S(2)}, u32[]{:S(2)}) %collective-permute-start.18) | collective-permute-done | bytes 147488 | tf_op jit(solution)/shard_map/ppermute | solution.py:625
  60.4 2.4 %collective-permute-start.19 = (bf16[144,512]{1,0:T(8,128)(2,1)S(1)}, bf16[144,512]{1,0:T(8,128)(2,1)S(1)}, u32[]{:S(2)}, u32[]{:S(2)}) collective-permute-start(bf16[144,512]{1,0:T(8,128)(2,1)S(1)} %pad_maximum_fusion.9), channel_id=1, source_target_pairs={{0,24},{1,25},{2,26},{3,27},{4,28},{5,29},{6,30},{7,31},{8,16},{9,... | collective-permute-start | bytes 442376 | tf_op jit(solution)/shard_map/ppermute | solution.py:625
  62.8 1.5 %collective-permute-done.22 = bf16[64,1536]{1,0:T(8,128)(2,1)S(1)} collective-permute-done((bf16[64,1536]{1,0:T(8,128)(2,1)S(1)}, bf16[64,1536]{1,0:T(8,128)(2,1)S(1)}, u32[]{:S(2)}, u32[]{:S(2)}) %collective-permute-start.22) | collective-permute-done | bytes 196640 | tf_op jit(solution)/shard_map/ppermute | solution.py:625
  64.2 0.1 reduce-precision_convert_fusion
  64.3 1.0 %collective-permute-start.23 = (bf16[64,1536]{1,0:T(8,128)(2,1)S(1)}, bf16[64,1536]{1,0:T(8,128)(2,1)S(1)}, u32[]{:S(2)}, u32[]{:S(2)}) collective-permute-start(bf16[64,1536]{1,0:T(8,128)(2,1)S(1)} %reduce-precision_convert_fusion), channel_id=1, source_target_pairs={{0,4},{1,5},{2,6},{3,7},{4,0},{5,1},{6,2},{7,3},{8,12},{9,13},{10,... | collective-permute-start | bytes 589832 | tf_op jit(solution)/shard_map/ppermute | solution.py:625
  65.3 1.1 %collective-permute-start.24 = (bf16[64,1024]{1,0:T(8,128)(2,1)S(1)}, bf16[64,1024]{1,0:T(8,128)(2,1)S(1)}, u32[]{:S(2)}, u32[]{:S(2)}) collective-permute-start(bf16[64,1024]{1,0:T(8,128)(2,1)S(1)} %get-tuple-element.139), channel_id=1, source_target_pairs={{0,2},{1,3},{2,0},{3,1},{4,6},{5,7},{6,4},{7,5},{8,10},{9,11},{10,... | collective-permute-start | bytes 393224 | tf_op jit(solution)/shard_map/ppermute | solution.py:625
  66.4 1.5 %collective-permute-start.25 = (bf16[64,1024]{1,0:T(8,128)(2,1)S(1)}, bf16[64,1024]{1,0:T(8,128)(2,1)S(1)}, u32[]{:S(2)}, u32[]{:S(2)}) collective-permute-start(bf16[64,1024]{1,0:T(8,128)(2,1)S(1)} %get-tuple-element.139), channel_id=1, source_target_pairs={{0,6},{1,7},{2,4},{3,5},{4,2},{5,3},{6,0},{7,1},{8,14},{9,15},{10,... | collective-permute-start | bytes 393224 | tf_op jit(solution)/shard_map/ppermute | solution.py:625
  67.9 2.3 %collective-permute-done.23 = bf16[64,1536]{1,0:T(8,128)(2,1)S(1)} collective-permute-done((bf16[64,1536]{1,0:T(8,128)(2,1)S(1)}, bf16[64,1536]{1,0:T(8,128)(2,1)S(1)}, u32[]{:S(2)}, u32[]{:S(2)}) %collective-permute-start.23) | collective-permute-done | bytes 196640 | tf_op jit(solution)/shard_map/ppermute | solution.py:625
  70.2 0.1 collective-permute-done.24
  70.3 2.0 %collective-permute-done.25 = bf16[64,1024]{1,0:T(8,128)(2,1)S(1)} collective-permute-done((bf16[64,1024]{1,0:T(8,128)(2,1)S(1)}, bf16[64,1024]{1,0:T(8,128)(2,1)S(1)}, u32[]{:S(2)}, u32[]{:S(2)}) %collective-permute-start.25) | collective-permute-done | bytes 131104 | tf_op jit(solution)/shard_map/ppermute | solution.py:625
  72.3 0.1 collective-permute-start.27
  72.5 0.5 collective-permute-start.20
  73.0 0.1 collective-permute-start.26
  73.1 1.1 %collective-permute-done.20.more_ref = f32[8,512]{1,0:T(8,128)S(1)} collective-permute-done((f32[8,512]{1,0:T(8,128)S(1)}, f32[8,512]{1,0:T(8,128)S(1)}, u32[]{:S(2)}, u32[]{:S(2)}) %collective-permute-start.20) | collective-permute-done | bytes 16416 | tf_op jit(solution)/shard_map/ppermute | solution.py:625
  74.2 0.8 %finish.1 = (f32[64,2,512]{2,1,0:T(2,128)}, f32[3,512]{1,0:T(4,128)S(1)}, f32[1,64]{1,0:T(1,128)}, f32[1,64]{1,0:T(1,128)}, f32[1,64]{1,0:T(1,128)}) custom-call(bf16[128,512]{1,0:T(8,128)(2,1)S(1)} %reduce-precision_convert_fusion.3.low_ref, bf16[144,512]{1,0:T(8,128)(2,1)S(1)} %collective-permute-done.19.got_ref, f32[8,512]{1,0:T(8,128)S(1)} %add_add_fusion.sums_ref, ...), custom_call_target="tpu_custom_call" | custom-call | flops 1048576 | bytes 4194304 | tf_op jit(solution)/shard_map/finish/pallas_call | solution.py:74
  74.9 0.6 fusion.17
  75.5 0.8 halves.1
  76.3 1.5 %place.1 = f32[512,1024]{1,0:T(8,128)} custom-call(bf16[1,64,1024]{2,1,0:T(8,128)(2,1)S(1)} %get-tuple-element.140.refs_0_, bf16[3,64,1024]{2,1,0:T(8,128)(2,1)S(1)} %pad_maximum_fusion.1.refs_1_, bf16[1,64,1024]{2,1,0:T(8,128)(2,1)S(1)} %collective-permute-done.26.refs_2_, bf16[3,64,1024]{2,1,0:T(8,128)(2,1)S(1)} %collective-permute-done.27.refs_3_), custom_call_target="tpu_custom_call" | custom-call | flops 262144 | bytes 4194304 | tf_op jit(solution)/shard_map/place/pallas_call | solution.py:74
  (54 shorter events, 0.5 us)
Async XLA Ops:
  0.6 17.1 %copy-start = (bf16[512,2,512]{2,1,0:T(2,128)(2,1)S(1)}, bf16[512,2,512]{2,1,0:T(2,128)(2,1)}, u32[]{:S(2)}) copy-start(bf16[512,2,512]{2,1,0:T(2,128)(2,1)} %param.23) | copy-start | bytes 3145732
  3.5 6.9 %collective-permute-start.1 = (bf16[72,2,512]{2,1,0:T(2,128)(2,1)S(1)}, bf16[72,2,512]{2,1,0:T(2,128)(2,1)S(1)}, u32[]{:S(2)}, u32[]{:S(2)}) collective-permute-start(bf16[72,2,512]{2,1,0:T(2,128)(2,1)S(1)} %pad_maximum_fusion.5.refs_0_), channel_id=1, source_target_pairs={{0,2},{1,3},{2,0},{3,1},{4,6},{5,7},{6,4},{7,5},{8,10},{9,11},{10,... | collective-permute-start | bytes 442376 | tf_op jit(solution)/shard_map/ppermute | solution.py:625
  6.5 5.6 %collective-permute-start = (bf16[72,2,512]{2,1,0:T(2,128)(2,1)S(1)}, bf16[72,2,512]{2,1,0:T(2,128)(2,1)S(1)}, u32[]{:S(2)}, u32[]{:S(2)}) collective-permute-start(bf16[72,2,512]{2,1,0:T(2,128)(2,1)S(1)} %pad_maximum_fusion.5.refs_0_), channel_id=1, source_target_pairs={{0,1},{1,0},{2,3},{3,2},{4,5},{5,4},{6,7},{7,6},{8,9},{9,8},{10,11... | collective-permute-start | bytes 442376 | tf_op jit(solution)/shard_map/ppermute | solution.py:625
  6.5 1.2 %copy-start.1 = (bf16[512,2,512]{2,1,0:T(2,128)(2,1)S(1)}, bf16[512,2,512]{2,1,0:T(2,128)(2,1)}, u32[]{:S(2)}) copy-start(bf16[512,2,512]{2,1,0:T(2,128)(2,1)} %param.12) | copy-start | bytes 3145732
  7.7 7.6 %copy-start.4 = (bf16[64,2,512]{2,1,0:T(2,128)(2,1)S(1)}, bf16[64,2,512]{2,1,0:T(2,128)(2,1)}, u32[]{:S(2)}) copy-start(bf16[64,2,512]{2,1,0:T(2,128)(2,1)} %refs_0_) | copy-start | bytes 393220
  10.3 1.8 %collective-permute-start.2 = (bf16[72,2,512]{2,1,0:T(2,128)(2,1)S(1)}, bf16[72,2,512]{2,1,0:T(2,128)(2,1)S(1)}, u32[]{:S(2)}, u32[]{:S(2)}) collective-permute-start(bf16[72,2,512]{2,1,0:T(2,128)(2,1)S(1)} %collective-permute-done.1.refs_2_), channel_id=1, source_target_pairs={{0,1},{1,0},{2,3},{3,2},{4,5},{5,4},{6,7},{7,6},{8,9},{9,8},{10,11... | collective-permute-start | bytes 442376 | tf_op jit(solution)/shard_map/ppermute | solution.py:625
  10.4 6.1 %collective-permute-start.6 = (bf16[64,2,512]{2,1,0:T(2,128)(2,1)}, bf16[64,2,512]{2,1,0:T(2,128)(2,1)S(1)}, u32[]{:S(2)}, u32[]{:S(2)}) collective-permute-start(bf16[64,2,512]{2,1,0:T(2,128)(2,1)} %refs_0_), channel_id=1, source_target_pairs={{0,2},{1,3},{2,0},{3,1},{4,6},{5,7},{6,4},{7,5},{8,10},{9,11},{10,... | collective-permute-start | bytes 393224 | tf_op jit(solution)/shard_map/ppermute | solution.py:625
  13.9 5.0 %copy-start.3 = (bf16[512,1024]{1,0:T(8,128)(2,1)S(1)}, bf16[512,1024]{1,0:T(8,128)(2,1)}, u32[]{:S(2)}) copy-start(bf16[512,1024]{1,0:T(8,128)(2,1)} %refs_4_.1) | copy-start | bytes 3145732
  13.9 3.8 %collective-permute-start.3 = (f32[1,8,512]{2,1,0:T(8,128)S(1)}, f32[1,8,512]{2,1,0:T(8,128)S(1)}, u32[]{:S(2)}, u32[]{:S(2)}) collective-permute-start(f32[1,8,512]{2,1,0:T(8,128)S(1)} %bitcast.56), channel_id=1, source_target_pairs={{0,2},{1,3},{2,0},{3,1},{4,6},{5,7},{6,4},{7,5},{8,10},{9,11},{10,... | collective-permute-start | bytes 49160 | tf_op jit(solution)/shard_map/ppermute | solution.py:625
  15.3 2.7 %collective-permute-start.5 = (bf16[64,2,512]{2,1,0:T(2,128)(2,1)S(1)}, bf16[64,2,512]{2,1,0:T(2,128)(2,1)S(1)}, u32[]{:S(2)}, u32[]{:S(2)}) collective-permute-start(bf16[64,2,512]{2,1,0:T(2,128)(2,1)S(1)} %copy-done.4), channel_id=1, source_target_pairs={{0,1},{1,0},{2,3},{3,2},{4,5},{5,4},{6,7},{7,6},{8,9},{9,8},{10,11... | collective-permute-start | bytes 393224 | tf_op jit(solution)/shard_map/ppermute | solution.py:625
  16.5 1.6 %collective-permute-start.7 = (bf16[64,2,512]{2,1,0:T(2,128)(2,1)S(1)}, bf16[64,2,512]{2,1,0:T(2,128)(2,1)S(1)}, u32[]{:S(2)}, u32[]{:S(2)}) collective-permute-start(bf16[64,2,512]{2,1,0:T(2,128)(2,1)S(1)} %collective-permute-done.6.refs_2_), channel_id=1, source_target_pairs={{0,1},{1,0},{2,3},{3,2},{4,5},{5,4},{6,7},{7,6},{8,9},{9,8},{10,11... | collective-permute-start | bytes 393224 | tf_op jit(solution)/shard_map/ppermute | solution.py:625
  17.7 1.2 %collective-permute-start.4 = (f32[2,8,512]{2,1,0:T(8,128)S(1)}, f32[2,8,512]{2,1,0:T(8,128)S(1)}, u32[]{:S(2)}, u32[]{:S(2)}) collective-permute-start(f32[2,8,512]{2,1,0:T(8,128)S(1)} %get-tuple-element.150), channel_id=1, source_target_pairs={{0,1},{1,0},{2,3},{3,2},{4,5},{5,4},{6,7},{7,6},{8,9},{9,8},{10,11... | collective-permute-start | bytes 98312 | tf_op jit(solution)/shard_map/ppermute | solution.py:625
  24.3 5.4 %collective-permute-start.8 = (bf16[4,64,1024]{2,1,0:T(8,128)(2,1)S(1)}, bf16[4,64,1024]{2,1,0:T(8,128)(2,1)S(1)}, u32[]{:S(2)}, u32[]{:S(2)}) collective-permute-start(bf16[4,64,1024]{2,1,0:T(8,128)(2,1)S(1)} %get-tuple-element.85), channel_id=1, source_target_pairs={{0,1},{1,0},{2,3},{3,2},{4,5},{5,4},{6,7},{7,6},{8,9},{9,8},{10,11... | collective-permute-start | bytes 1572872 | tf_op jit(solution)/shard_map/ppermute | solution.py:625
  28.0 1.6 %collective-permute-start.9 = (bf16[4,64,512]{2,1,0:T(8,128)(2,1)S(1)}, bf16[4,64,512]{2,1,0:T(8,128)(2,1)S(1)}, u32[]{:S(2)}, u32[]{:S(2)}) collective-permute-start(bf16[4,64,512]{2,1,0:T(8,128)(2,1)S(1)} %get-tuple-element.92), channel_id=1, source_target_pairs={{0,1},{1,0},{2,3},{3,2},{4,5},{5,4},{6,7},{7,6},{8,9},{9,8},{10,11... | collective-permute-start | bytes 786440 | tf_op jit(solution)/shard_map/ppermute | solution.py:625
  29.7 3.9 %collective-permute-start.13 = (f32[1,8,512]{2,1,0:T(8,128)S(1)}, f32[1,8,512]{2,1,0:T(8,128)S(1)}, u32[]{:S(2)}, u32[]{:S(2)}) collective-permute-start(f32[1,8,512]{2,1,0:T(8,128)S(1)} %bitcast.53), channel_id=1, source_target_pairs={{0,2},{1,3},{2,0},{3,1},{4,6},{5,7},{6,4},{7,5},{8,10},{9,11},{10,... | collective-permute-start | bytes 49160 | tf_op jit(solution)/shard_map/ppermute | solution.py:625
  31.3 8.8 %collective-permute-start.10 = (bf16[1,64,1536]{2,1,0:T(8,128)(2,1)S(1)}, bf16[1,64,1536]{2,1,0:T(8,128)(2,1)S(1)}, u32[]{:S(2)}, u32[]{:S(2)}) collective-permute-start(bf16[1,64,1536]{2,1,0:T(8,128)(2,1)S(1)} %pad_maximum_fusion.2), channel_id=1, source_target_pairs={{0,2},{1,3},{2,0},{3,1},{4,6},{5,7},{6,4},{7,5},{8,10},{9,11},{10,... | collective-permute-start | bytes 589832 | tf_op jit(solution)/shard_map/ppermute | solution.py:625
  32.0 9.9 %collective-permute-start.11 = (bf16[1,64,1536]{2,1,0:T(8,128)(2,1)S(1)}, bf16[1,64,1536]{2,1,0:T(8,128)(2,1)S(1)}, u32[]{:S(2)}, u32[]{:S(2)}) collective-permute-start(bf16[1,64,1536]{2,1,0:T(8,128)(2,1)S(1)} %pad_maximum_fusion.3), channel_id=1, source_target_pairs={{0,4},{1,5},{2,6},{3,7},{4,0},{5,1},{6,2},{7,3},{8,12},{9,13},{10,... | collective-permute-start | bytes 589832 | tf_op jit(solution)/shard_map/ppermute | solution.py:625
  33.6 2.5 %collective-permute-start.14 = (f32[2,8,512]{2,1,0:T(8,128)S(1)}, f32[2,8,512]{2,1,0:T(8,128)S(1)}, u32[]{:S(2)}, u32[]{:S(2)}) collective-permute-start(f32[2,8,512]{2,1,0:T(8,128)S(1)} %get-tuple-element.148), channel_id=1, source_target_pairs={{0,1},{1,0},{2,3},{3,2},{4,5},{5,4},{6,7},{7,6},{8,9},{9,8},{10,11... | collective-permute-start | bytes 98312 | tf_op jit(solution)/shard_map/ppermute | solution.py:625
  33.7 10.6 %collective-permute-start.12 = (bf16[1,64,1536]{2,1,0:T(8,128)(2,1)S(1)}, bf16[1,64,1536]{2,1,0:T(8,128)(2,1)S(1)}, u32[]{:S(2)}, u32[]{:S(2)}) collective-permute-start(bf16[1,64,1536]{2,1,0:T(8,128)(2,1)S(1)} %pad_maximum_fusion.4), channel_id=1, source_target_pairs={{0,6},{1,7},{2,4},{3,5},{4,2},{5,3},{6,0},{7,1},{8,14},{9,15},{10,... | collective-permute-start | bytes 589832 | tf_op jit(solution)/shard_map/ppermute | solution.py:625
  37.9 1.6 %collective-permute-start.15 = (bf16[2,128,512]{2,1,0:T(8,128)(2,1)S(1)}, bf16[2,128,512]{2,1,0:T(8,128)(2,1)S(1)}, u32[]{:S(2)}, u32[]{:S(2)}) collective-permute-start(bf16[2,128,512]{2,1,0:T(8,128)(2,1)S(1)} %get-tuple-element.104), channel_id=1, source_target_pairs={{0,1},{1,0},{2,3},{3,2},{4,5},{5,4},{6,7},{7,6},{8,9},{9,8},{10,11... | collective-permute-start | bytes 786440 | tf_op jit(solution)/shard_map/ppermute | solution.py:625
  39.0 9.4 %copy-start.2 = (bf16[512,2,512]{2,1,0:T(2,128)(2,1)S(1)}, bf16[512,2,512]{2,1,0:T(2,128)(2,1)}, u32[]{:S(2)}) copy-start(bf16[512,2,512]{2,1,0:T(2,128)(2,1)} %param.12) | copy-start | bytes 3145732
  39.5 8.5 %collective-permute-start.16 = (bf16[144,512]{1,0:T(8,128)(2,1)S(1)}, bf16[144,512]{1,0:T(8,128)(2,1)S(1)}, u32[]{:S(2)}, u32[]{:S(2)}) collective-permute-start(bf16[144,512]{1,0:T(8,128)(2,1)S(1)} %pad_maximum_fusion.6), channel_id=1, source_target_pairs={{0,2},{1,3},{2,0},{3,1},{4,6},{5,7},{6,4},{7,5},{8,10},{9,11},{10,... | collective-permute-start | bytes 442376 | tf_op jit(solution)/shard_map/ppermute | solution.py:625
  44.4 8.7 %collective-permute-start.21 = (bf16[64,1536]{1,0:T(8,128)(2,1)S(1)}, bf16[64,1536]{1,0:T(8,128)(2,1)S(1)}, u32[]{:S(2)}, u32[]{:S(2)}) collective-permute-start(bf16[64,1536]{1,0:T(8,128)(2,1)S(1)} %reduce-precision_convert_fusion.2), channel_id=1, source_target_pairs={{0,24},{1,25},{2,26},{3,27},{4,28},{5,29},{6,30},{7,31},{8,16},{9,... | collective-permute-start | bytes 589832 | tf_op jit(solution)/shard_map/ppermute | solution.py:625
  48.1 5.2 %collective-permute-start.17 = (bf16[144,512]{1,0:T(8,128)(2,1)S(1)}, bf16[144,512]{1,0:T(8,128)(2,1)S(1)}, u32[]{:S(2)}, u32[]{:S(2)}) collective-permute-start(bf16[144,512]{1,0:T(8,128)(2,1)S(1)} %pad_maximum_fusion.7), channel_id=1, source_target_pairs={{0,4},{1,5},{2,6},{3,7},{4,0},{5,1},{6,2},{7,3},{8,12},{9,13},{10,... | collective-permute-start | bytes 442376 | tf_op jit(solution)/shard_map/ppermute | solution.py:625
  53.4 6.9 %collective-permute-start.18 = (bf16[144,512]{1,0:T(8,128)(2,1)S(1)}, bf16[144,512]{1,0:T(8,128)(2,1)S(1)}, u32[]{:S(2)}, u32[]{:S(2)}) collective-permute-start(bf16[144,512]{1,0:T(8,128)(2,1)S(1)} %pad_maximum_fusion.8), channel_id=1, source_target_pairs={{0,8},{1,9},{2,10},{3,11},{4,12},{5,13},{6,14},{7,15},{8,0},{9,1},... | collective-permute-start | bytes 442376 | tf_op jit(solution)/shard_map/ppermute | solution.py:625
  55.6 8.6 %collective-permute-start.22 = (bf16[64,1536]{1,0:T(8,128)(2,1)S(1)}, bf16[64,1536]{1,0:T(8,128)(2,1)S(1)}, u32[]{:S(2)}, u32[]{:S(2)}) collective-permute-start(bf16[64,1536]{1,0:T(8,128)(2,1)S(1)} %reduce-precision_convert_fusion.1), channel_id=1, source_target_pairs={{0,8},{1,9},{2,10},{3,11},{4,12},{5,13},{6,14},{7,15},{8,0},{9,1},... | collective-permute-start | bytes 589832 | tf_op jit(solution)/shard_map/ppermute | solution.py:625
  60.4 12.1 %collective-permute-start.19 = (bf16[144,512]{1,0:T(8,128)(2,1)S(1)}, bf16[144,512]{1,0:T(8,128)(2,1)S(1)}, u32[]{:S(2)}, u32[]{:S(2)}) collective-permute-start(bf16[144,512]{1,0:T(8,128)(2,1)S(1)} %pad_maximum_fusion.9), channel_id=1, source_target_pairs={{0,24},{1,25},{2,26},{3,27},{4,28},{5,29},{6,30},{7,31},{8,16},{9,... | collective-permute-start | bytes 442376 | tf_op jit(solution)/shard_map/ppermute | solution.py:625
  64.3 5.9 %collective-permute-start.23 = (bf16[64,1536]{1,0:T(8,128)(2,1)S(1)}, bf16[64,1536]{1,0:T(8,128)(2,1)S(1)}, u32[]{:S(2)}, u32[]{:S(2)}) collective-permute-start(bf16[64,1536]{1,0:T(8,128)(2,1)S(1)} %reduce-precision_convert_fusion), channel_id=1, source_target_pairs={{0,4},{1,5},{2,6},{3,7},{4,0},{5,1},{6,2},{7,3},{8,12},{9,13},{10,... | collective-permute-start | bytes 589832 | tf_op jit(solution)/shard_map/ppermute | solution.py:625
  65.3 5.0 %collective-permute-start.24 = (bf16[64,1024]{1,0:T(8,128)(2,1)S(1)}, bf16[64,1024]{1,0:T(8,128)(2,1)S(1)}, u32[]{:S(2)}, u32[]{:S(2)}) collective-permute-start(bf16[64,1024]{1,0:T(8,128)(2,1)S(1)} %get-tuple-element.139), channel_id=1, source_target_pairs={{0,2},{1,3},{2,0},{3,1},{4,6},{5,7},{6,4},{7,5},{8,10},{9,11},{10,... | collective-permute-start | bytes 393224 | tf_op jit(solution)/shard_map/ppermute | solution.py:625
  66.4 5.9 %collective-permute-start.25 = (bf16[64,1024]{1,0:T(8,128)(2,1)S(1)}, bf16[64,1024]{1,0:T(8,128)(2,1)S(1)}, u32[]{:S(2)}, u32[]{:S(2)}) collective-permute-start(bf16[64,1024]{1,0:T(8,128)(2,1)S(1)} %get-tuple-element.139), channel_id=1, source_target_pairs={{0,6},{1,7},{2,4},{3,5},{4,2},{5,3},{6,0},{7,1},{8,14},{9,15},{10,... | collective-permute-start | bytes 393224 | tf_op jit(solution)/shard_map/ppermute | solution.py:625
  72.3 4.0 %collective-permute-start.27 = (bf16[3,64,1024]{2,1,0:T(8,128)(2,1)S(1)}, bf16[3,64,1024]{2,1,0:T(8,128)(2,1)S(1)}, u32[]{:S(2)}, u32[]{:S(2)}) collective-permute-start(bf16[3,64,1024]{2,1,0:T(8,128)(2,1)S(1)} %pad_maximum_fusion.1.refs_1_), channel_id=1, source_target_pairs={{0,1},{1,0},{2,3},{3,2},{4,5},{5,4},{6,7},{7,6},{8,9},{9,8},{10,11... | collective-permute-start | bytes 1179656 | tf_op jit(solution)/shard_map/ppermute | solution.py:625
  72.5 1.7 %collective-permute-start.20 = (f32[8,512]{1,0:T(8,128)S(1)}, f32[8,512]{1,0:T(8,128)S(1)}, u32[]{:S(2)}, u32[]{:S(2)}) collective-permute-start(f32[8,512]{1,0:T(8,128)S(1)} %add_add_fusion.sums_ref), channel_id=1, source_target_pairs={{0,1},{1,0},{2,3},{3,2},{4,5},{5,4},{6,7},{7,6},{8,9},{9,8},{10,11... | collective-permute-start | bytes 49160 | tf_op jit(solution)/shard_map/ppermute | solution.py:625
  73.0 3.3 %collective-permute-start.26 = (bf16[1,64,1024]{2,1,0:T(8,128)(2,1)S(1)}, bf16[1,64,1024]{2,1,0:T(8,128)(2,1)S(1)}, u32[]{:S(2)}, u32[]{:S(2)}) collective-permute-start(bf16[1,64,1024]{2,1,0:T(8,128)(2,1)S(1)} %get-tuple-element.140.refs_0_), channel_id=1, source_target_pairs={{0,1},{1,0},{2,3},{3,2},{4,5},{5,4},{6,7},{7,6},{8,9},{9,8},{10,11... | collective-permute-start | bytes 393224 | tf_op jit(solution)/shard_map/ppermute | solution.py:625

commit v5 on v4

--- a/solution.py
+++ b/solution.py
@@ -10,7 +10,7 @@
 F32, BF16 = jnp.float32, jnp.bfloat16
 EPSILON = 1e-05
 SUB = 8
-CHUNK = 256
+CHUNK = 512
 PARAM_ROWS = 16
 GELU_A = 0.7978845608028654
 GELU_B = 0.044715
@@ -50,16 +50,9 @@
     return y.reshape(y.shape[0] // SUB, segs, group, feats).transpose(1, 0, 2, 3)
 
 
-def row_mask(base, rows, group, steps, me, lengths):
-    segs = SUB // group
-    row = lax.broadcasted_iota(jnp.int32, (rows, 128), 0) + base
-    place = row & (SUB - 1)
-    seq = place & (group - 1)
-    position = (me * (segs * steps) + (place // group) * steps + (row // SUB)).astype(F32)
-    length = jnp.broadcast_to(lengths[:, 0:1], (rows, 128))
-    for k in range(1, group):
-        length = jnp.where(seq == k, lengths[:, k : k + 1], length)
-    return (position < length).astype(F32)
+def valid(first, count, limit_ref):
+    step = lax.broadcasted_iota(jnp.int32, (count, SUB, 128), 0) + first
+    return (step < limit_ref[...][None]).astype(F32).reshape(count * SUB, 128)
 
 
 def wide(column, lanes):
@@ -69,7 +62,7 @@
 def call(body, outs, ins, scratch, limit_mib, flops, name, fetched=()):
     specs = []
     for k, x in enumerate(ins):
-        space = pltpu.SMEM if x.dtype == jnp.int32 else pltpu.HBM if k in fetched else pltpu.VMEM
+        space = pltpu.SMEM if x.ndim == 1 else pltpu.HBM if k in fetched else pltpu.VMEM
         specs.append(pl.BlockSpec(memory_space=space))
     return pl.pallas_call(
         body,
@@ -110,7 +103,7 @@
     return [high, mid, (rest - mid.astype(F32)).astype(BF16)]
 
 
-def prep_kernel(own, group, small_ref, pay_ref, vec_ref):
+def prep_kernel(own, small_ref, pay_ref, vec_ref):
     feats = vec_ref.shape[1]
     me = lax.axis_index("state")
     lane = lax.broadcasted_iota(jnp.int32, (1, feats), 1)
@@ -131,9 +124,7 @@
     rows = [small_ref[:, k * feats : (k + 1) * feats] for k in range(3)] + [pole_re, pole_im, decay, angle]
     for k, row in enumerate(rows):
         vec_ref[k : k + 1, :] = row
-    base += 3 * own
     vec_ref[len(rows) :, :] = jnp.zeros((SUB - len(rows), feats), F32)
-    vec_ref[7:8, :group] = small_ref[:, base : base + group]
 
 
 def cotangent_kernel(cot_ref, rows_ref):
@@ -148,10 +139,19 @@
     gather_rows(lax.axis_index("state"), blocks, flat_ref, out_ref)
 
 
-def norm_kernel(x_ref, vec_ref, low_ref, unit_ref, inv_ref, mask_ref):
+def limit_kernel(group, steps, lens_ref, limit_ref):
+    segs = SUB // group
+    place = lax.broadcasted_iota(jnp.int32, (SUB, 128), 0)
+    seq = place & (group - 1)
+    length = jnp.full((SUB, 128), lens_ref[0], jnp.int32)
+    for k in range(1, group):
+        length = jnp.where(seq == k, lens_ref[k], length)
+    limit_ref[...] = length - (lax.axis_index("state") * segs + place // group) * steps
+
+
+def norm_kernel(x_ref, vec_ref, low_ref, unit_ref, inv_ref):
     segs, steps, group, feats = x_ref.shape
     rows = steps * SUB
-    me = lax.axis_index("state")
     size = 128
     gain, bias = vec_ref[0:1, :], vec_ref[1:2, :]
 
@@ -165,7 +165,6 @@
         unit_ref[at, :] = unit
         low_ref[at, :] = (unit * gain + bias).astype(BF16)
         inv_ref[at, :] = jnp.broadcast_to(inv, (size, 128))
-        mask_ref[at, :] = row_mask(base, size, group, steps, me, vec_ref[7:8, :])
         return carry
 
     repeat(0, rows // size, chunk, 0)
@@ -245,7 +244,7 @@
     return out
 
 
-def project_kernel(parts, own, group, low_ref, mask_ref, *refs):
+def project_kernel(parts, own, group, low_ref, limit_ref, *refs):
     blocks = refs[:parts]
     drive_ref, end_ref, win_ref, cst_ref, flat_ref = refs[parts:]
     rows = low_ref.shape[0]
@@ -283,7 +282,7 @@
     def chunk(c, carry):
         base = c * CHUNK
         at = pl.ds(base, CHUNK)
-        mask = mask_ref[at, :]
+        mask = valid(base // SUB, CHUNK // SUB, limit_ref)
         drive_ref[at, :] = nt(low_ref[at, :], win_ref[...]) * (gains * wide(mask, 2 * channels))
         return carry
 
@@ -297,7 +296,7 @@
         return nr + u[:, :channels], ni + u[:, channels:]
 
     zero = jnp.zeros((SUB, channels), F32)
-    er, ei = lax.fori_loop(0, steps, step, (zero, zero), unroll=8)
+    er, ei = lax.fori_loop(0, steps, step, (zero, zero), unroll=16)
     er, ei = seg_prefix(er, ei, *powers[1], group, True)
     end_ref[...] = jnp.concatenate([er, ei], axis=1)
 
@@ -306,7 +305,7 @@
     it = iter(refs)
     take = lambda n: [next(it) for _ in range(n)]
     drive_ref, end_ref, cst_ref, ends_ref = take(4)
-    cw_ref, unit_ref, cot_ref, mask_ref, vec_ref, glu_ref = take(6)
+    cw_ref, unit_ref, cot_ref, limit_ref, vec_ref, glu_ref = take(6)
     states_ref, slow_ref, branch_ref, dglu_ref, gp_ref = take(5)
     grads = take(len(orders))
     act_ref, acc_ref = take(2)
@@ -335,7 +334,7 @@
         states_ref[at, channels:] = ni
         return nr, ni
 
-    lax.fori_loop(0, steps, step, (hr, hi), unroll=8)
+    lax.fori_loop(0, steps, step, (hr, hi), unroll=16)
 
     def chunk(c, carry):
         base = c * CHUNK
@@ -351,7 +350,7 @@
         act = (v * half).astype(BF16)
         act_ref[at, :] = act
         glu = nn(act, glu_ref[...])
-        mask = wide(mask_ref[at, :], feats)
+        mask = wide(valid(base // SUB, CHUNK // SUB, limit_ref), feats)
         value = glu[:, :feats]
         gate = jax.nn.sigmoid(glu[:, feats:])
         branch = mask * gate
@@ -390,16 +389,14 @@
             ref[k, own : 2 * own] = acc_ref[also, :].astype(ref.dtype)
 
 
-def back_kernel(own, group, orders, *refs):
+def back_kernel(own, orders, *refs):
     it = iter(refs)
     take = lambda n: [next(it) for _ in range(n)]
-    dglu_ref, gp_ref, unit_ref, vec_ref, glu_ref, cw_ref, slow_ref, cst_ref = take(8)
-    dpre_ref, dst_ref, start_ref, skip_ref = take(4)
+    dglu_ref, gp_ref, unit_ref, vec_ref, glu_ref, slow_ref = take(6)
+    dpre_ref, dmix_ref, skip_ref = take(3)
     grads = take(len(orders))
-    dmix_ref, acc_ref = take(2)
+    (acc_ref,) = take(1)
     rows, feats = gp_ref.shape
-    channels = cw_ref.shape[0] // 2
-    steps = rows // SUB
     place = lax.axis_index("state") + lax.axis_size("state") * (lax.axis_index("seq") & 1)
     gain, bias = vec_ref[0:1, :], vec_ref[1:2, :]
 
@@ -408,17 +405,34 @@
         d_pre = nt(dglu_ref[at, :], glu_ref[...]) * gp_ref[at, :]
         dpre_ref[at, :] = d_pre
         normed = unit_ref[at, :] * gain + bias
-        total = total + jnp.sum((d_pre * normed).reshape(CHUNK // SUB, SUB, feats), axis=0)
-        d_mixed = d_pre.astype(BF16)
-        dmix_ref[at, :] = d_mixed
-        dst_ref[at, :] = nt(d_mixed, cw_ref[...])
-        return total
-
-    total = repeat(0, rows // CHUNK, chunk, jnp.zeros((SUB, feats), F32))
-    skip_ref[...] = total
-    pr, pi = cst_ref[0:1, :channels], cst_ref[0:1, channels:]
-    br = jnp.broadcast_to(pr, (SUB, channels))
-    bi = jnp.broadcast_to(-pi, (SUB, channels))
+        dmix_ref[at, :] = d_pre.astype(BF16)
+        return total + jnp.sum((d_pre * normed).reshape(CHUNK // SUB, SUB, feats), axis=0)
+
+    skip_ref[...] = repeat(0, rows // CHUNK, chunk, jnp.zeros((SUB, feats), F32))
+    width = 256
+
+    def tile(c, carry):
+        at = pl.ds(c * width, width)
+        acc_ref[:, at] = tn(slow_ref[...], dmix_ref[:, at])
+        return carry
+
+    repeat(0, feats // width, tile, 0)
+    spread(acc_ref, place, orders, grads)
+
+
+def starts_kernel(group, dmix_ref, cw_ref, cst_ref, dst_ref, start_ref):
+    rows, feats = dmix_ref.shape
+    channels = cw_ref.shape[0] // 2
+    steps = rows // SUB
+
+    def chunk(c, carry):
+        at = pl.ds(c * CHUNK, CHUNK)
+        dst_ref[at, :] = nt(dmix_ref[at, :], cw_ref[...])
+        return carry
+
+    repeat(0, rows // CHUNK, chunk, 0)
+    br = jnp.broadcast_to(cst_ref[0:1, :channels], (SUB, channels))
+    bi = jnp.broadcast_to(-cst_ref[0:1, channels:], (SUB, channels))
 
     def step(k, a):
         base = pl.multiple_of((steps - 1 - k) * SUB, SUB)
@@ -427,26 +441,17 @@
         return nr + u[:, :channels], ni - u[:, channels:]
 
     zero = jnp.zeros((SUB, channels), F32)
-    ar, ai = lax.fori_loop(0, steps, step, (zero, zero), unroll=8)
+    ar, ai = lax.fori_loop(0, steps, step, (zero, zero), unroll=16)
     qr, qi = cst_ref[1:2, :channels], -cst_ref[1:2, channels:]
     ar, ai = seg_prefix(ar, ai, qr, qi, group, False)
     start_ref[...] = jnp.concatenate([ar, ai], axis=1)
-    width = 256
-
-    def tile(c, carry):
-        at = pl.ds(c * width, width)
-        acc_ref[:, at] = tn(slow_ref[...], dmix_ref[:, at])
-        return carry
-
-    repeat(0, feats // width, tile, 0)
-    spread(acc_ref, place, orders, grads)
 
 
 def adjoint_kernel(own, group, orders, *refs):
     it = iter(refs)
     take = lambda n: [next(it) for _ in range(n)]
     dst_ref, start_ref, cst_ref, ends_ref = take(4)
-    states_ref, drive_ref, low_ref, mask_ref = take(4)
+    states_ref, drive_ref, low_ref, limit_ref = take(4)
     dproj_ref, sums_ref = take(2)
     grads = take(len(orders))
     adj_ref, acc_ref = take(2)
@@ -480,7 +485,7 @@
         return ar, ai, sr, si, sg
 
     zero = jnp.zeros((SUB, channels), F32)
-    out = lax.fori_loop(0, steps, step, (ar, ai, zero, zero, zero), unroll=4)
+    out = lax.fori_loop(0, steps, step, (ar, ai, zero, zero, zero), unroll=8)
     sums_ref[:, :channels] = out[2]
     sums_ref[:, channels : 2 * channels] = out[3]
     sums_ref[:, 2 * channels : 3 * channels] = out[4]
@@ -489,7 +494,7 @@
     def chunk(c, carry):
         base = c * CHUNK
         at = pl.ds(base, CHUNK)
-        mask = mask_ref[at, :]
+        mask = valid(base // SUB, CHUNK // SUB, limit_ref)
         dproj_ref[at, :] = (adj_ref[at, :] * (gains * wide(mask, 2 * channels))).astype(BF16)
         return carry
 
@@ -592,12 +597,12 @@
     join_pairs([jnp.where(first, a, b), jnp.where(first, b, a)], flat_ref, out_ref)
 
 
-def finish_kernel(low_ref, got_ref, sums_ref, more_ref, vec_ref, in_ref, feat_ref, rate_ref, angle_ref, level_ref, flat_ref):
+def finish_kernel(total_ref, sums_ref, vec_ref, in_ref, gain_ref, bias_ref, skip_ref, rate_ref, angle_ref, level_ref, flat_ref):
     own, _, feats = in_ref.shape
-    total = low_ref[...].astype(F32) + got_ref[0 : 2 * own, :].astype(F32)
-    join_pairs([total[:own, :], total[own:, :]], flat_ref, in_ref)
-    sums = sums_ref[...] + more_ref[...]
-    feat_ref[...] = sums[2:5, :]
+    join_pairs([total_ref[:own, :], total_ref[own:, :]], flat_ref, in_ref)
+    sums = sums_ref[...]
+    for k, ref in enumerate((gain_ref, bias_ref, skip_ref)):
+        ref[...] = sums[2 + k : 3 + k, :]
     me = lax.axis_index("state")
     channels = lax.axis_size("state") * own
     pick = lambda row: sum(
@@ -611,13 +616,38 @@
 
 
 def place_kernel(masks, parts, *refs):
-    arrays, out_ref = refs[:-1], refs[-1]
+    arrays, out_ref, wide_ref, sems = refs[: len(masks)], refs[-3], refs[-2], refs[-1]
     place = lax.axis_index("state") + parts * (lax.axis_index("seq") & 1)
     size = arrays[0].shape[1]
+    copies = []
     for ms, ref in zip(masks, arrays):
         for k, m in enumerate(ms):
+            n = len(copies)
+            wide_ref[n] = ref[k].astype(F32)
             at = pl.ds(pl.multiple_of((place ^ m) * size, size), size)
-            out_ref[at, :] = ref[k].astype(F32)
+            copies.append(pltpu.make_async_copy(wide_ref.at[n], out_ref.at[at, :], sems.at[n]))
+            copies[-1].start()
+    for c in copies:
+        c.wait()
+
+
+def place_blocks(arrays, masks, parts, shape, out=None):
+    count = sum(len(m) for m in masks)
+    _, size, width = arrays[0].shape
+    ins = list(arrays) + ([] if out is None else [out])
+    specs = [pl.BlockSpec(memory_space=pltpu.VMEM)] * len(arrays)
+    specs += [pl.BlockSpec(memory_space=pl.ANY)] * (len(ins) - len(arrays))
+    return pl.pallas_call(
+        functools.partial(place_kernel, masks, parts),
+        out_shape=jax.ShapeDtypeStruct(shape, F32),
+        in_specs=specs,
+        out_specs=pl.BlockSpec(memory_space=pl.ANY),
+        scratch_shapes=[pltpu.VMEM((count, size, width), F32), pltpu.SemaphoreType.DMA((count,))],
+        input_output_aliases={} if out is None else {len(arrays): 0},
+        compiler_params=pltpu.CompilerParams(vmem_limit_bytes=8 * MIB),
+        cost_estimate=pl.CostEstimate(flops=MIB, bytes_accessed=2 * MIB, transcendentals=0),
+        name="place",
+    )(*ins)
 
 
 def exchange(x, mask):
@@ -734,12 +764,10 @@
     flat = pltpu.VMEM((feats // 128, 2 * own, 128), F32)
     x4 = tokens.reshape(segs, span // segs, group, feats)
     cot4 = cotangent.reshape(segs, span // segs, group, feats)
-    small = jnp.concatenate(
-        [norm_gain, norm_bias, skip_gain, log_rate, log_angle, log_gain, lengths.astype(F32)]
-    )
-    small = jnp.pad(small, (0, -small.shape[0] % 128)).reshape(1, -1)
+    small = jnp.concatenate([norm_gain, norm_bias, skip_gain, log_rate, log_angle, log_gain])
+    small = small.reshape(1, -1)
     small_own, vec = call(
-        functools.partial(prep_kernel, own, group),
+        functools.partial(prep_kernel, own),
         [((PARAM_ROWS // 2, 2, feats), BF16), ((SUB, feats), F32)],
         [small],
         [],
@@ -748,16 +776,25 @@
         "prep",
     )
     b_own = jnp.concatenate([input_weight.transpose(1, 2, 0), small_own], axis=0)
-    low, unit, inv, mask = call(
+    low, unit, inv = call(
         norm_kernel,
-        [((rows, feats), BF16), ((rows, feats), F32), ((rows, 128), F32), ((rows, 128), F32)],
+        [((rows, feats), BF16), ((rows, feats), F32), ((rows, 128), F32)],
         [x4, vec],
         [],
         12,
         rows * feats * 20,
         "norm",
     )
-    b_blocks, c_blocks = gather_blocks([b_own, tie(output_weight, b_own)], state_bits, low)
+    (limit,) = call(
+        functools.partial(limit_kernel, group, rows // SUB),
+        [((SUB, 128), jnp.int32)],
+        [tie(lengths, low)],
+        [],
+        8,
+        MIB,
+        "limit",
+    )
+    b_blocks, c_blocks = gather_blocks([b_own, tie(output_weight, b_own)], state_bits, (low, limit))
     drive, end, win, cst = call(
         functools.partial(project_kernel, parts, own, group),
         [
@@ -766,7 +803,7 @@
             ((2 * channels, feats), BF16),
             ((SUB, 2 * channels), F32),
         ],
-        [low, mask] + b_blocks,
+        [low, limit] + b_blocks,
         [flat],
         12,
         full,
@@ -800,31 +837,36 @@
             ((rows, feats), F32),
         ]
         + block_outs(glu_rows, 2 * feats, all_orders),
-        [drive, end, cst, ends, cw, unit, cot, mask, vec, glu_weight],
+        [drive, end, cst, ends, cw, unit, cot, limit, vec, glu_weight],
         [pltpu.VMEM((rows, feats), BF16), pltpu.VMEM((feats, 2 * feats), F32)],
         20,
         5 * full,
         "mix",
     )
-    d_pre, d_states, start, skip_sum, *out_parts = call(
-        functools.partial(back_kernel, own, group, all_orders),
-        [
-            ((rows, feats), F32),
-            ((rows, 2 * channels), F32),
-            ((SUB, 2 * channels), F32),
-            ((SUB, feats), F32),
-        ]
+    d_pre, d_mixed, skip_sum, *out_parts = call(
+        functools.partial(back_kernel, own, all_orders),
+        [((rows, feats), F32), ((rows, feats), BF16), ((SUB, feats), F32)]
         + block_outs(own, feats, all_orders),
-        [d_glu, slope, unit, vec, glu_weight, cw, slow, cst],
-        [pltpu.VMEM((rows, feats), BF16), pltpu.VMEM((2 * channels, feats), F32)],
+        [d_glu, slope, unit, vec, glu_weight, slow],
+        [pltpu.VMEM((2 * channels, feats), F32)],
         16,
-        4 * full,
+        3 * full,
         "back",
     )
+    d_states, start = call(
+        functools.partial(starts_kernel, group),
+        [((rows, 2 * channels), F32), ((SUB, 2 * channels), F32)],
+        [d_mixed, cw, cst],
+        [],
+        12,
+        full,
+        "starts",
+    )
     got = swap(glu_parts, all_groups[0])
-    starts = gather_ends(tie(start, got), state_bits)
-    glu_parts = add_up(glu_parts, tie(got, start))
-    out_parts = halve(out_parts, all_groups[0])
+    more = swap(out_parts, all_groups[0])
+    starts = gather_ends(tie(start, got, more), state_bits)
+    got, more = tie((got, more), start)
+    glu_parts, out_parts = add_up(glu_parts, got), add_up(out_parts, more)
     both = [jnp.concatenate(p, axis=-1) for p in zip(glu_parts, out_parts)]
     state_groups = [[b] for b in state_bits]
     pair_orders = stage_orders(state_groups)
@@ -832,7 +874,7 @@
         functools.partial(adjoint_kernel, own, group, pair_orders),
         [((rows, 2 * channels), BF16), ((SUB, 3 * channels), F32)]
         + block_outs(2 * own, feats, pair_orders),
-        [tie(d_states, both), start, cst, starts, states, drive, low, mask],
+        [tie(d_states, both), start, cst, starts, states, drive, low, limit],
         [pltpu.VMEM((rows, 2 * channels), F32), pltpu.VMEM((2 * channels, feats), F32)],
         16,
         2 * full,
@@ -848,46 +890,42 @@
         full,
         "normed",
     )
-    sent = []
-    for g in state_groups[1:]:
-        own_sums = two_parts(sums)
-        sent.append(
-            jnp.concatenate([in_parts[0].astype(BF16).reshape(-1, feats)] + own_sums, axis=0)
-        )
-        got = exchange(sent[-1], g[0])
-        rest, off = [], 0
-        for p in in_parts[1:]:
-            n = p.shape[0] * p.shape[1]
-            rest.append(p + got[off : off + n].reshape(p.shape).astype(F32))
-            off += n
-        in_parts = rest
-        sums = sum_of(own_sums) + sum_of([got[off : off + SUB], got[off + SUB :]])
-    total = in_parts[0][0]
-    for m in seq_masks:
-        low_total = rounded(total).astype(BF16)
-        own_sums = two_parts(sums)
-        sent.append(jnp.concatenate([low_total] + own_sums, axis=0))
-        got = exchange(sent[-1], m)
-        total = low_total.astype(F32) + got[: 2 * own].astype(F32)
-        got_sums = [got[2 * own : 2 * own + SUB], got[2 * own + SUB :]]
-        sums = sum_of(own_sums) + sum_of(got_sums)
-    grad_in, feature_grads, grad_rate, grad_angle, grad_level = call(
-        finish_kernel,
-        [((own, 2, feats), F32), ((3, feats), F32)] + [((1, own), F32)] * 3,
-        [low_total, got, sums, exchange(sums, state_bits[0]), vec],
-        [flat],
-        8,
-        MIB,
-        "finish",
-    )
-
-    for n, g in enumerate(all_groups[1:]):
-        both = add_up(both, tie(swap(both, g), sent[0]))
+    class chain:
+        parts, total, held = in_parts, None, sums
+        masks = state_bits[1:] + seq_masks[:1] + seq_masks[:0:-1]
+        sent = []
+
+        def send(after=()):
+            chain.two = two_parts(chain.held)
+            if len(chain.parts) > 1:
+                chain.low = chain.parts[0].astype(BF16).reshape(-1, feats)
+            else:
+                chain.low = rounded(chain.parts[0][0]).astype(BF16)
+            chain.sent.append(tie(jnp.concatenate([chain.low] + chain.two, axis=0), after))
+
+        def take():
+            got = exchange(chain.sent[-1], chain.masks[len(chain.sent) - 1])
+            chain.got, rest, off = got, [], 0
+            if len(chain.parts) > 1:
+                for p in chain.parts[1:]:
+                    n = p.shape[0] * p.shape[1]
+                    rest.append(p + got[off : off + n].reshape(p.shape).astype(F32))
+                    off += n
+            else:
+                off = 2 * own
+                rest.append((chain.low.astype(F32) + got[:off].astype(F32))[None])
+            chain.parts = rest
+            chain.held = sum_of(chain.two) + sum_of([got[off : off + SUB], got[off + SUB :]])
+
+    chain.send()
+    for g in all_groups[1:]:
+        got = swap(both, g)
+        both = add_up(both, tie(got, chain.sent[-1]))
     both = both[0][0]
     (grad4,) = call(
         tokens_kernel,
         [(cot4.shape, F32)],
-        [cot4, tie(d_normed, both, sent[0]), unit, inv, vec],
+        [cot4, tie(d_normed, both, chain.sent[-1]), unit, inv, vec],
         [held(cot4), pltpu.SemaphoreType.DMA((4,))],
         12,
         full,
@@ -897,19 +935,40 @@
     (out4,) = call(
         out_kernel,
         [(x4.shape, BF16)],
-        [x4, tie(branch, both, sent[0])],
+        [x4, tie(branch, both, chain.sent[-1])],
         [held(x4), pltpu.SemaphoreType.DMA((4,))],
         8,
         MIB,
         "out",
         fetched=(0,),
     )
-    at = lambda k: sent[max(0, min(k, len(sent) - 1))]
-    for n, m in enumerate(reversed(seq_masks[1:])):
-        mine = tie(rounded(both).astype(BF16), at(2 * n - 1))
-        got = tie(exchange(mine, m), at(2 * n + 1), grad4, out4)
+    chain.take()
+    chain.held = chain.held + exchange(chain.held, state_bits[0])
+    chain.send()
+    glu_masks = seq_masks[:0:-1]
+    for n, m in enumerate(glu_masks):
+        mine = rounded(both).astype(BF16)
+        got = exchange(mine, m)
+        if n:
+            chain.take()
+            chain.send(mine)
+        got = tie(got, chain.sent[-1], grad4, out4)
         both = mine.astype(F32) + got.astype(F32)
-    both = tie(rounded(both).astype(BF16), sent[-1])
+    both = rounded(both).astype(BF16)
+    while len(chain.sent) < len(chain.masks):
+        chain.take()
+        chain.send(both)
+    chain.take()
+    last = chain.got
+    grad_in, grad_gain, grad_bias, grad_skip, grad_rate, grad_angle, grad_level = call(
+        finish_kernel,
+        [((own, 2, feats), F32)] + [((1, feats), F32)] * 3 + [((1, own), F32)] * 3,
+        [chain.parts[0][0], chain.held, vec],
+        [flat],
+        8,
+        MIB,
+        "finish",
+    )
     blocks = {0: both[:, : 2 * feats]}
     for g in reversed(all_groups[1:]):
         for m in list(blocks):
@@ -920,41 +979,34 @@
                     other_half = got[:, 2 * feats :]
                 else:
                     blocks[m ^ p] = exchange(blocks[m], p)
-    rest = [m for m in blocks if m]
-    arrays = [blocks[0][None], jnp.stack([blocks[m] for m in rest])]
-    masks = [[0], rest]
-    for p in submasks(all_groups[0]):
-        arrays += [exchange(a, p) for a in arrays[:2]]
-        masks += [[m ^ p for m in ms] for ms in masks[:2]]
+    far_own = [exchange(blocks[0][None], p) for p in submasks(all_groups[0])]
     (grad_out,) = call(
         halves_kernel,
         [((own, 2, feats), F32)],
-        [both[:, 2 * feats :], other_half],
+        [both[:, 2 * feats :], tie(other_half, far_own)],
         [flat],
         8,
         MIB,
         "halves",
     )
-    (grad_glu,) = call(
-        functools.partial(place_kernel, masks, parts),
-        [((feats, 2 * feats), F32)],
-        arrays,
-        [],
-        8,
-        feats * feats,
-        "place",
-    )
+    rest = [m for m in blocks if m]
+    near = [blocks[0][None], jnp.stack(tie([blocks[m] for m in rest], grad_out, chain.sent[-1]))]
+    near_masks = [[0], rest]
+    far = [f for p, o in zip(submasks(all_groups[0]), far_own) for f in (o, exchange(near[1], p))]
+    far_masks = [[m ^ p for m in ms] for p in submasks(all_groups[0]) for ms in near_masks]
+    grad_glu = place_blocks(tie(near, last), near_masks, parts, (feats, 2 * feats))
+    grad_glu = place_blocks(tie(far, grad_in), far_masks, parts, (feats, 2 * feats), grad_glu)
     return (
         out4.reshape(tokens.shape),
         grad4.reshape(tokens.shape),
-        feature_grads[0],
-        feature_grads[1],
+        grad_gain.reshape(feats),
+        grad_bias.reshape(feats),
         grad_in.transpose(2, 0, 1),
         grad_out,
         grad_rate.reshape(own),
         grad_angle.reshape(own),
         grad_level.reshape(own),
-        feature_grads[2],
+        grad_skip.reshape(feats),
         grad_glu,
     )
 

time: 78 us -> 73.5 us (0.942)
  starting transfers between devices: 26.6 us -> 23.2 us
  waiting for transfers between devices: 21 us -> 19.9 us
    ppermute x28, starting transfers between devices: 26.6 us -> 23.2 us  [exchange(): lax.ppermute(x, ('seq', 'state'), [(i, i ^ mask) for i in range(count)])]
    pallas_call x0 -> x2, Pallas kernels: none -> 2.03 us  [place_blocks(): pl.pallas_call(functools.partial(place_kernel, masks, parts), out_shape=j...]
    pallas_call x14 -> x15, Pallas kernels: 23.8 us -> 22.2 us  [call(): pl.pallas_call(body, out_shape=[jax.ShapeDtypeStruct(s, d) for s, d in ou...]
    ppermute x28, waiting for transfers between devices: 21 us -> 19.9 us  [exchange(): lax.ppermute(x, ('seq', 'state'), [(i, i ^ mask) for i in range(count)])]
    unnamed x10 -> x12, local copies, waits for them, and re-layouts: 1.25 us -> 1.9 us
  transfers between devices with their start and end apart: 28 -> 28, of which waited for: 15 -> 15; matrix products, arithmetic and copies ran while one was open for 2% -> 1% of each run, Pallas kernels for 22% -> 24%
where the time goes in v5:
time: 73.5 us; the launch traced here: 73.3 us
  Pallas kernels  24.2 us (33%)
  starting transfers between devices  23.2 us (32%)
  waiting for transfers between devices  19.9 us (27%)
  local copies, waits for them, and re-layouts  2.85 us (4%)
  other arithmetic  1.89 us (3%)
  between operations  1.24 us (2%)
    ppermute x28, starting transfers between devices, exchange(): lax.ppermute(x, ('seq', 'state'), [(i, i ^ mask) for i in range(count)])  23.2 us
    pallas_call x15, Pallas kernels, call(): pl.pallas_call(body, out_shape=[jax.ShapeDtypeStruct(s, d) for s, d in ou...  22.2 us
    ppermute x28, waiting for transfers between devices, exchange(): lax.ppermute(x, ('seq', 'state'), [(i, i ^ mask) for i in range(count)])  19.9 us
    pallas_call x2, Pallas kernels, place_blocks(): pl.pallas_call(functools.partial(place_kernel, masks, parts), out_shape=j...  2.03 us
    unnamed x12, local copies, waits for them, and re-layouts  1.9 us
  transfers between devices with their start and end apart: 28, of which 15 were waited for; matrix products, arithmetic and copies ran while one was open for 1% of the time, Pallas kernels for 24%

profile of v5, /device:TPU:0, one launch (start us, length us, event | category | flops | bytes accessed | tf_op | source)
XLA Modules:
  0.0 73.3 jit_solution(14625058999390771228)
XLA Ops:
  0.7 0.9 %concatenate.57 = f32[1728]{0:T(1024)S(1)} concatenate(f32[512]{0:T(512)} %param.13, f32[512]{0:T(512)} %param.14, f32[512]{0:T(512)} %param.20, f32[64]{0:T(128)} %param.17, f32[64]{0:T(128)} %param.18, f32[64]{0:T(128)} %param.19), dimensions={0} | concatenate | bytes 13824 | tf_op jit(solution)/shard_map/concatenate | solution.py:767
  1.6 0.1 prep.1
  1.7 1.1 %pad_maximum_fusion.5.refs_0_ = bf16[72,2,512]{2,1,0:T(2,128)(2,1)S(1)} fusion(bf16[8,2,512]{2,1,0:T(2,128)(2,1)S(1)} %get-tuple-element.84, bf16[64,2,512]{2,1,0:T(2,128)(2,1)} %bitcast.60), kind=kLoop, calls=%fused_computation.20 | loop fusion | flops 73728 | bytes 294912 | tf_op jit(solution)/shard_map/concatenate | solution.py:778
  2.8 3.0 %collective-permute-start.1 = (bf16[72,2,512]{2,1,0:T(2,128)(2,1)S(1)}, bf16[72,2,512]{2,1,0:T(2,128)(2,1)S(1)}, u32[]{:S(2)}, u32[]{:S(2)}) collective-permute-start(bf16[72,2,512]{2,1,0:T(2,128)(2,1)S(1)} %pad_maximum_fusion.5.refs_0_), channel_id=1, source_target_pairs={{0,2},{1,3},{2,0},{3,1},{4,6},{5,7},{6,4},{7,5},{8,10},{9,11},{10,... | collective-permute-start | bytes 442376 | tf_op jit(solution)/shard_map/ppermute | solution.py:655
  5.8 1.2 %copy-done.1 = bf16[512,2,512]{2,1,0:T(2,128)(2,1)S(1)} copy-done((bf16[512,2,512]{2,1,0:T(2,128)(2,1)S(1)}, bf16[512,2,512]{2,1,0:T(2,128)(2,1)}, u32[]{:S(2)}) %copy-start.1) | copy-done | bytes 1048600
  7.1 1.6 %norm.1 = (bf16[1024,512]{1,0:T(8,128)(2,1)S(1)}, f32[1024,512]{1,0:T(8,128)S(1)}, f32[1024,128]{1,0:T(8,128)S(1)}) custom-call(bf16[4,128,2,512]{3,2,1,0:T(2,128)(2,1)S(1)} %bitcast.49, f32[8,512]{1,0:T(8,128)S(1)} %get-tuple-element.81.vec_ref.refs_8_.refs_3_), custom_call_target="tpu_custom_call" | custom-call | flops 10485760 | bytes 4194304 | tf_op jit(solution)/shard_map/norm/pallas_call | solution.py:67
  8.7 0.0 copy-start.5
  8.7 0.6 copy-done.5
  9.3 0.6 limit.1.limit_ref.refs_7_
  9.9 0.6 collective-permute-start.2
  10.5 0.9 %collective-permute-start.6 = (bf16[64,2,512]{2,1,0:T(2,128)(2,1)}, bf16[64,2,512]{2,1,0:T(2,128)(2,1)S(1)}, u32[]{:S(2)}, u32[]{:S(2)}) collective-permute-start(bf16[64,2,512]{2,1,0:T(2,128)(2,1)} %refs_0_), channel_id=1, source_target_pairs={{0,2},{1,3},{2,0},{3,1},{4,6},{5,7},{6,4},{7,5},{8,10},{9,11},{10,... | collective-permute-start | bytes 393224 | tf_op jit(solution)/shard_map/ppermute | solution.py:655
  11.4 0.1 collective-permute-done.2.refs_3_
  11.5 1.8 %project.1 = (f32[1024,512]{1,0:T(8,128)S(1)}, f32[8,512]{1,0:T(8,128)S(1)}, bf16[512,512]{1,0:T(8,128)(2,1)S(1)}, f32[8,512]{1,0:T(8,128)S(1)}) custom-call(bf16[1024,512]{1,0:T(8,128)(2,1)S(1)} %get-tuple-element.82.low_ref.refs_6_, s32[8,128]{1,0:T(8,128)S(1)} %limit.1.limit_ref.refs_7_, bf16[72,2,512]{2,1,0:T(2,128)(2,1)S(1)} %pad_maximum_fusion.5.refs_0_, ...), custom_call_target="tpu_custom_call" | custom-call | flops 536870912 | bytes 4194304 | tf_op jit(solution)/shard_map/project/pallas_call | solution.py:67
  13.3 0.0 copy-start.3
  13.3 1.4 %collective-permute-start.3 = (f32[1,8,512]{2,1,0:T(8,128)S(1)}, f32[1,8,512]{2,1,0:T(8,128)S(1)}, u32[]{:S(2)}, u32[]{:S(2)}) collective-permute-start(f32[1,8,512]{2,1,0:T(8,128)S(1)} %bitcast.55), channel_id=1, source_target_pairs={{0,2},{1,3},{2,0},{3,1},{4,6},{5,7},{6,4},{7,5},{8,10},{9,11},{10,... | collective-permute-start | bytes 49160 | tf_op jit(solution)/shard_map/ppermute | solution.py:655
  14.6 1.5 %collective-permute-done.6.refs_2_ = bf16[64,2,512]{2,1,0:T(2,128)(2,1)S(1)} collective-permute-done((bf16[64,2,512]{2,1,0:T(2,128)(2,1)}, bf16[64,2,512]{2,1,0:T(2,128)(2,1)S(1)}, u32[]{:S(2)}, u32[]{:S(2)}) %collective-permute-start.6) | collective-permute-done | bytes 131104 | tf_op jit(solution)/shard_map/ppermute | solution.py:655
  16.2 0.9 %collective-permute-done.3 = f32[1,8,512]{2,1,0:T(8,128)S(1)} collective-permute-done((f32[1,8,512]{2,1,0:T(8,128)S(1)}, f32[1,8,512]{2,1,0:T(8,128)S(1)}, u32[]{:S(2)}, u32[]{:S(2)}) %collective-permute-start.3) | collective-permute-done | bytes 16416 | tf_op jit(solution)/shard_map/ppermute | solution.py:655
  17.1 0.3 cotangent.1.refs_6_
  17.5 0.1 collective-permute-done.7.refs_3_
  17.5 0.4 weights.1.refs_4_.cw_ref
  17.9 0.4 collective-permute-done.4
  18.3 5.2 %mix.1 = (f32[1032,512]{1,0:T(8,128)S(1)}, bf16[1024,512]{1,0:T(8,128)(2,1)S(1)}, f32[1024,512]{1,0:T(8,128)S(1)}, bf16[1024,1024]{1,0:T(8,128)(2,1)S(1)}, f32[1...) custom-call(f32[1024,512]{1,0:T(8,128)S(1)} %get-tuple-element.86.re, ...), custom_call_target="tpu_custom_call" | custom-call | flops 2684354560 | bytes 4194304 | tf_op jit(solution)/shard_map/mix/pallas_call | solution.py:67
  23.5 0.2 collective-permute-start.8
  23.8 2.1 %back.1 = (f32[1024,512]{1,0:T(8,128)S(1)}, bf16[1024,512]{1,0:T(8,128)(2,1)S(1)}, f32[8,512]{1,0:T(8,128)S(1)}, bf16[4,64,512]{2,1,0:T(8,128)(2,1)S(1)}, f32[1,...) custom-call(bf16[1024,1024]{1,0:T(8,128)(2,1)S(1)} %get-tuple-element.97, ...), custom_call_target="tpu_custom_call" | custom-call | flops 1610612736 | bytes 4194304 | tf_op jit(solution)/shard_map/back/pallas_call | solution.py:67
  25.9 0.4 collective-permute-start.9
  26.3 1.2 %starts.1 = (f32[1024,512]{1,0:T(8,128)S(1)}, f32[8,512]{1,0:T(8,128)S(1)}) custom-call(bf16[1024,512]{1,0:T(8,128)(2,1)S(1)} %get-tuple-element.101.dmix_ref, bf16[512,512]{1,0:T(8,128)(2,1)S(1)} %weights.1.refs_4_.cw_ref, f32[8,512]{1,0:T(8,128)S(1)} %get-tuple-element.88.refs_2_.cst_ref), custom_call_target="tpu_custom_call" | custom-call | flops 536870912 | bytes 4194304 | tf_op jit(solution)/shard_map/starts/pallas_call | solution.py:67
  27.5 1.4 %collective-permute-start.13 = (f32[1,8,512]{2,1,0:T(8,128)S(1)}, f32[1,8,512]{2,1,0:T(8,128)S(1)}, u32[]{:S(2)}, u32[]{:S(2)}) collective-permute-start(f32[1,8,512]{2,1,0:T(8,128)S(1)} %bitcast.52), channel_id=1, source_target_pairs={{0,2},{1,3},{2,0},{3,1},{4,6},{5,7},{6,4},{7,5},{8,10},{9,11},{10,... | collective-permute-start | bytes 49160 | tf_op jit(solution)/shard_map/ppermute | solution.py:655
  28.9 0.1 convert_add_fusion.3
  28.9 0.2 convert_add_fusion.2
  29.1 0.8 %collective-permute-start.10 = (bf16[1,64,1536]{2,1,0:T(8,128)(2,1)S(1)}, bf16[1,64,1536]{2,1,0:T(8,128)(2,1)S(1)}, u32[]{:S(2)}, u32[]{:S(2)}) collective-permute-start(bf16[1,64,1536]{2,1,0:T(8,128)(2,1)S(1)} %pad_maximum_fusion.2), channel_id=1, source_target_pairs={{0,2},{1,3},{2,0},{3,1},{4,6},{5,7},{6,4},{7,5},{8,10},{9,11},{10,... | collective-permute-start | bytes 589832 | tf_op jit(solution)/shard_map/ppermute | solution.py:655
  29.9 1.6 %collective-permute-start.11 = (bf16[1,64,1536]{2,1,0:T(8,128)(2,1)S(1)}, bf16[1,64,1536]{2,1,0:T(8,128)(2,1)S(1)}, u32[]{:S(2)}, u32[]{:S(2)}) collective-permute-start(bf16[1,64,1536]{2,1,0:T(8,128)(2,1)S(1)} %pad_maximum_fusion.3), channel_id=1, source_target_pairs={{0,4},{1,5},{2,6},{3,7},{4,0},{5,1},{6,2},{7,3},{8,12},{9,13},{10,... | collective-permute-start | bytes 589832 | tf_op jit(solution)/shard_map/ppermute | solution.py:655
  31.5 0.1 collective-permute-start.14
  31.6 2.1 %collective-permute-start.12 = (bf16[1,64,1536]{2,1,0:T(8,128)(2,1)S(1)}, bf16[1,64,1536]{2,1,0:T(8,128)(2,1)S(1)}, u32[]{:S(2)}, u32[]{:S(2)}) collective-permute-start(bf16[1,64,1536]{2,1,0:T(8,128)(2,1)S(1)} %pad_maximum_fusion.4), channel_id=1, source_target_pairs={{0,6},{1,7},{2,4},{3,5},{4,2},{5,3},{6,0},{7,1},{8,14},{9,15},{10,... | collective-permute-start | bytes 589832 | tf_op jit(solution)/shard_map/ppermute | solution.py:655
  33.8 1.7 %adjoint.1 = (bf16[1024,512]{1,0:T(8,128)(2,1)S(1)}, f32[8,768]{1,0:T(8,128)S(1)}, bf16[2,128,512]{2,1,0:T(8,128)(2,1)S(1)}, f32[1,128,512]{2,1,0:T(8,128)S(1)}, f32[1,128,512]{2,1,0:T(8,128)S(1)}) custom-call(f32[1024,512]{1,0:T(8,128)S(1)} %get-tuple-element.113.refs_0_, f32[8,512]{1,0:T(8,128)S(1)} %get-tuple-element.114.refs_1_, ...), custom_call_target="tpu_custom_call" | custom-call | flops 1073741824 | bytes 4194304 | tf_op jit(solution)/shard_map/adjoint/pallas_call | solution.py:67
  35.5 0.3 collective-permute-start.15
  35.8 0.8 %normed.1 = (f32[1024,512]{1,0:T(8,128)S(1)}, f32[8,512]{1,0:T(8,128)S(1)}) custom-call(bf16[1024,512]{1,0:T(8,128)(2,1)S(1)} %get-tuple-element.118.dproj_ref, bf16[512,512]{1,0:T(8,128)(2,1)S(1)} %get-tuple-element.119.win_ref, f32[1024,512]{1,0:T(8,128)S(1)} %get-tuple-element.120.dpre_ref, f32[1024,512]{1,0:T(8,128)S(1)} %get-tuple-element.92.refs_5_.refs_2_.unit_ref, ...), custom_call_target="tpu_custom_call" | custom-call | flops 536870912 | bytes 4194304 | tf_op jit(solution)/shard_map/normed/pallas_call | solution.py:67
  36.7 0.5 collective-permute-done.15
  37.2 0.7 collective-permute-start.16
  37.9 1.9 %collective-permute-done.11 = bf16[1,64,1536]{2,1,0:T(8,128)(2,1)S(1)} collective-permute-done((bf16[1,64,1536]{2,1,0:T(8,128)(2,1)S(1)}, bf16[1,64,1536]{2,1,0:T(8,128)(2,1)S(1)}, u32[]{:S(2)}, u32[]{:S(2)}) %collective-permute-start.11) | collective-permute-done | bytes 196640 | tf_op jit(solution)/shard_map/ppermute | solution.py:655
  39.8 2.2 %collective-permute-done.12 = bf16[1,64,1536]{2,1,0:T(8,128)(2,1)S(1)} collective-permute-done((bf16[1,64,1536]{2,1,0:T(8,128)(2,1)S(1)}, bf16[1,64,1536]{2,1,0:T(8,128)(2,1)S(1)}, u32[]{:S(2)}, u32[]{:S(2)}) %collective-permute-start.12) | collective-permute-done | bytes 196640 | tf_op jit(solution)/shard_map/ppermute | solution.py:655
  42.0 0.1 reduce-precision_convert_fusion.2
  42.1 3.7 %collective-permute-start.19 = (bf16[64,1536]{1,0:T(8,128)(2,1)S(1)}, bf16[64,1536]{1,0:T(8,128)(2,1)S(1)}, u32[]{:S(2)}, u32[]{:S(2)}) collective-permute-start(bf16[64,1536]{1,0:T(8,128)(2,1)S(1)} %reduce-precision_convert_fusion.2), channel_id=1, source_target_pairs={{0,24},{1,25},{2,26},{3,27},{4,28},{5,29},{6,30},{7,31},{8,16},{9,... | collective-permute-start | bytes 589832 | tf_op jit(solution)/shard_map/ppermute | solution.py:655
  45.7 2.1 %out.1 = bf16[4,128,2,512]{3,2,1,0:T(2,128)(2,1)} custom-call(bf16[4,128,2,512]{3,2,1,0:T(2,128)(2,1)S(1)} %bitcast.50, f32[1024,512]{1,0:T(8,128)S(1)} %get-tuple-element.127.branch_ref), custom_call_target="tpu_custom_call" | custom-call | flops 1048576 | bytes 4194304 | tf_op jit(solution)/shard_map/out/pallas_call | solution.py:67
  47.8 2.7 %tokens.1 = f32[4,128,2,512]{3,2,1,0:T(2,128)} custom-call(bf16[4,128,2,512]{3,2,1,0:T(2,128)(2,1)S(1)} %bitcast.48, f32[1024,512]{1,0:T(8,128)S(1)} %get-tuple-element.129.dnorm_ref, f32[1024,512]{1,0:T(8,128)S(1)} %get-tuple-element.92.refs_5_.refs_2_.unit_ref, f32[1024,128]{1,0:T(8,128)S(1)} %get-tuple-element.130.inv_ref, ...), custom_call_target="tpu_custom_call" | custom-call | flops 536870912 | bytes 4194304 | tf_op jit(solution)/shard_map/tokens/pallas_call | solution.py:67
  50.6 0.1 collective-permute-start.17
  50.7 1.1 %collective-permute-done.17 = f32[8,512]{1,0:T(8,128)S(1)} collective-permute-done((f32[8,512]{1,0:T(8,128)S(1)}, f32[8,512]{1,0:T(8,128)S(1)}, u32[]{:S(2)}, u32[]{:S(2)}) %collective-permute-start.17) | collective-permute-done | bytes 16416 | tf_op jit(solution)/shard_map/ppermute | solution.py:655
  51.9 0.3 collective-permute-start.18
  52.3 0.8 %collective-permute-start.21 = (bf16[64,1536]{1,0:T(8,128)(2,1)S(1)}, bf16[64,1536]{1,0:T(8,128)(2,1)S(1)}, u32[]{:S(2)}, u32[]{:S(2)}) collective-permute-start(bf16[64,1536]{1,0:T(8,128)(2,1)S(1)} %reduce-precision_convert_fusion.1), channel_id=1, source_target_pairs={{0,8},{1,9},{2,10},{3,11},{4,12},{5,13},{6,14},{7,15},{8,0},{9,1},... | collective-permute-start | bytes 589832 | tf_op jit(solution)/shard_map/ppermute | solution.py:655
  53.1 4.8 %collective-permute-done.18 = bf16[144,512]{1,0:T(8,128)(2,1)S(1)} collective-permute-done((bf16[144,512]{1,0:T(8,128)(2,1)S(1)}, bf16[144,512]{1,0:T(8,128)(2,1)S(1)}, u32[]{:S(2)}, u32[]{:S(2)}) %collective-permute-start.18) | collective-permute-done | bytes 147488 | tf_op jit(solution)/shard_map/ppermute | solution.py:655
  57.9 0.3 collective-permute-start.20
  58.2 0.8 %collective-permute-done.21 = bf16[64,1536]{1,0:T(8,128)(2,1)S(1)} collective-permute-done((bf16[64,1536]{1,0:T(8,128)(2,1)S(1)}, bf16[64,1536]{1,0:T(8,128)(2,1)S(1)}, u32[]{:S(2)}, u32[]{:S(2)}) %collective-permute-start.21) | collective-permute-done | bytes 196640 | tf_op jit(solution)/shard_map/ppermute | solution.py:655
  59.1 1.8 %collective-permute-start.23 = (bf16[64,1536]{1,0:T(8,128)(2,1)S(1)}, bf16[64,1536]{1,0:T(8,128)(2,1)S(1)}, u32[]{:S(2)}, u32[]{:S(2)}) collective-permute-start(bf16[64,1536]{1,0:T(8,128)(2,1)S(1)} %reduce-precision_convert_fusion), channel_id=1, source_target_pairs={{0,4},{1,5},{2,6},{3,7},{4,0},{5,1},{6,2},{7,3},{8,12},{9,13},{10,... | collective-permute-start | bytes 589832 | tf_op jit(solution)/shard_map/ppermute | solution.py:655
  60.9 0.8 %collective-permute-start.25 = (bf16[64,1024]{1,0:T(8,128)(2,1)S(1)}, bf16[64,1024]{1,0:T(8,128)(2,1)S(1)}, u32[]{:S(2)}, u32[]{:S(2)}) collective-permute-start(bf16[64,1024]{1,0:T(8,128)(2,1)S(1)} %get-tuple-element.161), channel_id=1, source_target_pairs={{0,2},{1,3},{2,0},{3,1},{4,6},{5,7},{6,4},{7,5},{8,10},{9,11},{10,... | collective-permute-start | bytes 393224 | tf_op jit(solution)/shard_map/ppermute | solution.py:655
  61.7 1.0 %collective-permute-start.26 = (bf16[64,1024]{1,0:T(8,128)(2,1)S(1)}, bf16[64,1024]{1,0:T(8,128)(2,1)S(1)}, u32[]{:S(2)}, u32[]{:S(2)}) collective-permute-start(bf16[64,1024]{1,0:T(8,128)(2,1)S(1)} %get-tuple-element.161), channel_id=1, source_target_pairs={{0,6},{1,7},{2,4},{3,5},{4,2},{5,3},{6,0},{7,1},{8,14},{9,15},{10,... | collective-permute-start | bytes 393224 | tf_op jit(solution)/shard_map/ppermute | solution.py:655
  62.8 2.2 %collective-permute-done.20 = bf16[144,512]{1,0:T(8,128)(2,1)S(1)} collective-permute-done((bf16[144,512]{1,0:T(8,128)(2,1)S(1)}, bf16[144,512]{1,0:T(8,128)(2,1)S(1)}, u32[]{:S(2)}, u32[]{:S(2)}) %collective-permute-start.20) | collective-permute-done | bytes 147488 | tf_op jit(solution)/shard_map/ppermute | solution.py:655
  65.1 0.9 %collective-permute-start.22 = (bf16[144,512]{1,0:T(8,128)(2,1)S(1)}, bf16[144,512]{1,0:T(8,128)(2,1)S(1)}, u32[]{:S(2)}, u32[]{:S(2)}) collective-permute-start(bf16[144,512]{1,0:T(8,128)(2,1)S(1)} %pad_maximum_fusion.9), channel_id=1, source_target_pairs={{0,8},{1,9},{2,10},{3,11},{4,12},{5,13},{6,14},{7,15},{8,0},{9,1},... | collective-permute-start | bytes 442376 | tf_op jit(solution)/shard_map/ppermute | solution.py:655
  66.0 0.4 collective-permute-done.23
  66.5 0.8 %halves.1 = f32[64,2,512]{2,1,0:T(2,128)} custom-call(bf16[64,512]{1,0:T(8,128)(2,1)S(1)} %slice.118.mine_ref, bf16[64,512]{1,0:T(8,128)(2,1)S(1)} %slice.119.other_ref), custom_call_target="tpu_custom_call" | custom-call | flops 1048576 | bytes 4194304 | tf_op jit(solution)/shard_map/halves/pallas_call | solution.py:67
  67.3 0.6 collective-permute-done.26
  67.9 0.1 collective-permute-start.27
  68.0 2.3 %collective-permute-done.22 = bf16[144,512]{1,0:T(8,128)(2,1)S(1)} collective-permute-done((bf16[144,512]{1,0:T(8,128)(2,1)S(1)}, bf16[144,512]{1,0:T(8,128)(2,1)S(1)}, u32[]{:S(2)}, u32[]{:S(2)}) %collective-permute-start.22) | collective-permute-done | bytes 147488 | tf_op jit(solution)/shard_map/ppermute | solution.py:655
  70.3 0.8 %finish.1 = (f32[64,2,512]{2,1,0:T(2,128)}, f32[1,512]{1,0:T(1,128)}, f32[1,512]{1,0:T(1,128)}, f32[1,512]{1,0:T(1,128)}, f32[1,64]{1,0:T(1,128)}, /*index=5*/f32[1,64]{1,0:T(1,128)}, f32[1,64]{1,0:T(1,128)}) custom-call(f32[128,512]{1,0:T(8,128)S(1)} %convert_add_fusion.1.total_ref, f32[8,512]{1,0:T(8,128)S(1)} %add_add_fusion.sums_ref, ...), custom_call_target="tpu_custom_call" | custom-call | flops 1048576 | bytes 4194304 | tf_op jit(solution)/shard_map/finish/pallas_call | solution.py:67
  71.1 1.0 %place.2.refs_2_ = f32[512,1024]{1,0:T(8,128)} custom-call(bf16[1,64,1024]{2,1,0:T(8,128)(2,1)S(1)} %get-tuple-element.149.refs_0_, bf16[3,64,1024]{2,1,0:T(8,128)(2,1)S(1)} %pad_maximum_fusion.1.refs_1_), custom_call_target="tpu_custom_call" | custom-call | flops 1048576 | bytes 2097152 | tf_op jit(solution)/shard_map/place/pallas_call | solution.py:640
  72.1 1.0 %place.3 = f32[512,1024]{1,0:T(8,128)} custom-call(bf16[1,64,1024]{2,1,0:T(8,128)(2,1)S(1)} %collective-permute-done.24.refs_0_, bf16[3,64,1024]{2,1,0:T(8,128)(2,1)S(1)} %collective-permute-done.27.refs_1_, f32[512,1024]{1,0:T(8,128)} %place.2.refs_2_), custom_call_target="tpu_custom_call", output_to_operand_aliasing={{}: (2, {})} | custom-call | flops 1048576 | bytes 2097152 | tf_op jit(solution)/shard_map/place/pallas_call | solution.py:640
  (58 shorter events, 0.6 us)
Async XLA Ops:
  0.6 16.5 %copy-start = (bf16[512,2,512]{2,1,0:T(2,128)(2,1)S(1)}, bf16[512,2,512]{2,1,0:T(2,128)(2,1)}, u32[]{:S(2)}) copy-start(bf16[512,2,512]{2,1,0:T(2,128)(2,1)} %param.23) | copy-start | bytes 3145732
  2.8 7.1 %collective-permute-start.1 = (bf16[72,2,512]{2,1,0:T(2,128)(2,1)S(1)}, bf16[72,2,512]{2,1,0:T(2,128)(2,1)S(1)}, u32[]{:S(2)}, u32[]{:S(2)}) collective-permute-start(bf16[72,2,512]{2,1,0:T(2,128)(2,1)S(1)} %pad_maximum_fusion.5.refs_0_), channel_id=1, source_target_pairs={{0,2},{1,3},{2,0},{3,1},{4,6},{5,7},{6,4},{7,5},{8,10},{9,11},{10,... | collective-permute-start | bytes 442376 | tf_op jit(solution)/shard_map/ppermute | solution.py:655
  5.8 5.6 %collective-permute-start = (bf16[72,2,512]{2,1,0:T(2,128)(2,1)S(1)}, bf16[72,2,512]{2,1,0:T(2,128)(2,1)S(1)}, u32[]{:S(2)}, u32[]{:S(2)}) collective-permute-start(bf16[72,2,512]{2,1,0:T(2,128)(2,1)S(1)} %pad_maximum_fusion.5.refs_0_), channel_id=1, source_target_pairs={{0,1},{1,0},{2,3},{3,2},{4,5},{5,4},{6,7},{7,6},{8,9},{9,8},{10,11... | collective-permute-start | bytes 442376 | tf_op jit(solution)/shard_map/ppermute | solution.py:655
  5.8 1.2 %copy-start.1 = (bf16[512,2,512]{2,1,0:T(2,128)(2,1)S(1)}, bf16[512,2,512]{2,1,0:T(2,128)(2,1)}, u32[]{:S(2)}) copy-start(bf16[512,2,512]{2,1,0:T(2,128)(2,1)} %param.12) | copy-start | bytes 3145732
  7.1 7.6 %copy-start.4 = (bf16[64,2,512]{2,1,0:T(2,128)(2,1)S(1)}, bf16[64,2,512]{2,1,0:T(2,128)(2,1)}, u32[]{:S(2)}) copy-start(bf16[64,2,512]{2,1,0:T(2,128)(2,1)} %refs_0_) | copy-start | bytes 393220
  8.7 0.7 copy-start.5
  9.9 1.6 %collective-permute-start.2 = (bf16[72,2,512]{2,1,0:T(2,128)(2,1)S(1)}, bf16[72,2,512]{2,1,0:T(2,128)(2,1)S(1)}, u32[]{:S(2)}, u32[]{:S(2)}) collective-permute-start(bf16[72,2,512]{2,1,0:T(2,128)(2,1)S(1)} %collective-permute-done.1.refs_2_), channel_id=1, source_target_pairs={{0,1},{1,0},{2,3},{3,2},{4,5},{5,4},{6,7},{7,6},{8,9},{9,8},{10,11... | collective-permute-start | bytes 442376 | tf_op jit(solution)/shard_map/ppermute | solution.py:655
  10.5 5.7 %collective-permute-start.6 = (bf16[64,2,512]{2,1,0:T(2,128)(2,1)}, bf16[64,2,512]{2,1,0:T(2,128)(2,1)S(1)}, u32[]{:S(2)}, u32[]{:S(2)}) collective-permute-start(bf16[64,2,512]{2,1,0:T(2,128)(2,1)} %refs_0_), channel_id=1, source_target_pairs={{0,2},{1,3},{2,0},{3,1},{4,6},{5,7},{6,4},{7,5},{8,10},{9,11},{10,... | collective-permute-start | bytes 393224 | tf_op jit(solution)/shard_map/ppermute | solution.py:655
  13.3 5.1 %copy-start.3 = (bf16[512,1024]{1,0:T(8,128)(2,1)S(1)}, bf16[512,1024]{1,0:T(8,128)(2,1)}, u32[]{:S(2)}) copy-start(bf16[512,1024]{1,0:T(8,128)(2,1)} %refs_4_.1) | copy-start | bytes 3145732
  13.3 3.8 %collective-permute-start.3 = (f32[1,8,512]{2,1,0:T(8,128)S(1)}, f32[1,8,512]{2,1,0:T(8,128)S(1)}, u32[]{:S(2)}, u32[]{:S(2)}) collective-permute-start(f32[1,8,512]{2,1,0:T(8,128)S(1)} %bitcast.55), channel_id=1, source_target_pairs={{0,2},{1,3},{2,0},{3,1},{4,6},{5,7},{6,4},{7,5},{8,10},{9,11},{10,... | collective-permute-start | bytes 49160 | tf_op jit(solution)/shard_map/ppermute | solution.py:655
  14.6 2.8 %collective-permute-start.5 = (bf16[64,2,512]{2,1,0:T(2,128)(2,1)S(1)}, bf16[64,2,512]{2,1,0:T(2,128)(2,1)S(1)}, u32[]{:S(2)}, u32[]{:S(2)}) collective-permute-start(bf16[64,2,512]{2,1,0:T(2,128)(2,1)S(1)} %copy-done.4), channel_id=1, source_target_pairs={{0,1},{1,0},{2,3},{3,2},{4,5},{5,4},{6,7},{7,6},{8,9},{9,8},{10,11... | collective-permute-start | bytes 393224 | tf_op jit(solution)/shard_map/ppermute | solution.py:655
  16.2 1.3 %collective-permute-start.7 = (bf16[64,2,512]{2,1,0:T(2,128)(2,1)S(1)}, bf16[64,2,512]{2,1,0:T(2,128)(2,1)S(1)}, u32[]{:S(2)}, u32[]{:S(2)}) collective-permute-start(bf16[64,2,512]{2,1,0:T(2,128)(2,1)S(1)} %collective-permute-done.6.refs_2_), channel_id=1, source_target_pairs={{0,1},{1,0},{2,3},{3,2},{4,5},{5,4},{6,7},{7,6},{8,9},{9,8},{10,11... | collective-permute-start | bytes 393224 | tf_op jit(solution)/shard_map/ppermute | solution.py:655
  17.1 1.2 %collective-permute-start.4 = (f32[2,8,512]{2,1,0:T(8,128)S(1)}, f32[2,8,512]{2,1,0:T(8,128)S(1)}, u32[]{:S(2)}, u32[]{:S(2)}) collective-permute-start(f32[2,8,512]{2,1,0:T(8,128)S(1)} %get-tuple-element.172), channel_id=1, source_target_pairs={{0,1},{1,0},{2,3},{3,2},{4,5},{5,4},{6,7},{7,6},{8,9},{9,8},{10,11... | collective-permute-start | bytes 98312 | tf_op jit(solution)/shard_map/ppermute | solution.py:655
  23.5 4.0 %collective-permute-start.8 = (bf16[4,64,1024]{2,1,0:T(8,128)(2,1)S(1)}, bf16[4,64,1024]{2,1,0:T(8,128)(2,1)S(1)}, u32[]{:S(2)}, u32[]{:S(2)}) collective-permute-start(bf16[4,64,1024]{2,1,0:T(8,128)(2,1)S(1)} %get-tuple-element.96), channel_id=1, source_target_pairs={{0,1},{1,0},{2,3},{3,2},{4,5},{5,4},{6,7},{7,6},{8,9},{9,8},{10,11... | collective-permute-start | bytes 1572872 | tf_op jit(solution)/shard_map/ppermute | solution.py:655
  25.9 1.6 %collective-permute-start.9 = (bf16[4,64,512]{2,1,0:T(8,128)(2,1)S(1)}, bf16[4,64,512]{2,1,0:T(8,128)(2,1)S(1)}, u32[]{:S(2)}, u32[]{:S(2)}) collective-permute-start(bf16[4,64,512]{2,1,0:T(8,128)(2,1)S(1)} %get-tuple-element.100), channel_id=1, source_target_pairs={{0,1},{1,0},{2,3},{3,2},{4,5},{5,4},{6,7},{7,6},{8,9},{9,8},{10,11... | collective-permute-start | bytes 786440 | tf_op jit(solution)/shard_map/ppermute | solution.py:655
  27.5 4.0 %collective-permute-start.13 = (f32[1,8,512]{2,1,0:T(8,128)S(1)}, f32[1,8,512]{2,1,0:T(8,128)S(1)}, u32[]{:S(2)}, u32[]{:S(2)}) collective-permute-start(f32[1,8,512]{2,1,0:T(8,128)S(1)} %bitcast.52), channel_id=1, source_target_pairs={{0,2},{1,3},{2,0},{3,1},{4,6},{5,7},{6,4},{7,5},{8,10},{9,11},{10,... | collective-permute-start | bytes 49160 | tf_op jit(solution)/shard_map/ppermute | solution.py:655
  29.1 8.8 %collective-permute-start.10 = (bf16[1,64,1536]{2,1,0:T(8,128)(2,1)S(1)}, bf16[1,64,1536]{2,1,0:T(8,128)(2,1)S(1)}, u32[]{:S(2)}, u32[]{:S(2)}) collective-permute-start(bf16[1,64,1536]{2,1,0:T(8,128)(2,1)S(1)} %pad_maximum_fusion.2), channel_id=1, source_target_pairs={{0,2},{1,3},{2,0},{3,1},{4,6},{5,7},{6,4},{7,5},{8,10},{9,11},{10,... | collective-permute-start | bytes 589832 | tf_op jit(solution)/shard_map/ppermute | solution.py:655
  29.9 9.8 %collective-permute-start.11 = (bf16[1,64,1536]{2,1,0:T(8,128)(2,1)S(1)}, bf16[1,64,1536]{2,1,0:T(8,128)(2,1)S(1)}, u32[]{:S(2)}, u32[]{:S(2)}) collective-permute-start(bf16[1,64,1536]{2,1,0:T(8,128)(2,1)S(1)} %pad_maximum_fusion.3), channel_id=1, source_target_pairs={{0,4},{1,5},{2,6},{3,7},{4,0},{5,1},{6,2},{7,3},{8,12},{9,13},{10,... | collective-permute-start | bytes 589832 | tf_op jit(solution)/shard_map/ppermute | solution.py:655
  31.5 2.2 %collective-permute-start.14 = (f32[2,8,512]{2,1,0:T(8,128)S(1)}, f32[2,8,512]{2,1,0:T(8,128)S(1)}, u32[]{:S(2)}, u32[]{:S(2)}) collective-permute-start(f32[2,8,512]{2,1,0:T(8,128)S(1)} %get-tuple-element.170), channel_id=1, source_target_pairs={{0,1},{1,0},{2,3},{3,2},{4,5},{5,4},{6,7},{7,6},{8,9},{9,8},{10,11... | collective-permute-start | bytes 98312 | tf_op jit(solution)/shard_map/ppermute | solution.py:655
  31.6 10.3 %collective-permute-start.12 = (bf16[1,64,1536]{2,1,0:T(8,128)(2,1)S(1)}, bf16[1,64,1536]{2,1,0:T(8,128)(2,1)S(1)}, u32[]{:S(2)}, u32[]{:S(2)}) collective-permute-start(bf16[1,64,1536]{2,1,0:T(8,128)(2,1)S(1)} %pad_maximum_fusion.4), channel_id=1, source_target_pairs={{0,6},{1,7},{2,4},{3,5},{4,2},{5,3},{6,0},{7,1},{8,14},{9,15},{10,... | collective-permute-start | bytes 589832 | tf_op jit(solution)/shard_map/ppermute | solution.py:655
  35.5 1.6 %collective-permute-start.15 = (bf16[2,128,512]{2,1,0:T(8,128)(2,1)S(1)}, bf16[2,128,512]{2,1,0:T(8,128)(2,1)S(1)}, u32[]{:S(2)}, u32[]{:S(2)}) collective-permute-start(bf16[2,128,512]{2,1,0:T(8,128)(2,1)S(1)} %get-tuple-element.117), channel_id=1, source_target_pairs={{0,1},{1,0},{2,3},{3,2},{4,5},{5,4},{6,7},{7,6},{8,9},{9,8},{10,11... | collective-permute-start | bytes 786440 | tf_op jit(solution)/shard_map/ppermute | solution.py:655
  36.7 9.1 %copy-start.2 = (bf16[512,2,512]{2,1,0:T(2,128)(2,1)S(1)}, bf16[512,2,512]{2,1,0:T(2,128)(2,1)}, u32[]{:S(2)}) copy-start(bf16[512,2,512]{2,1,0:T(2,128)(2,1)} %param.12) | copy-start | bytes 3145732
  37.2 13.4 %collective-permute-start.16 = (bf16[144,512]{1,0:T(8,128)(2,1)S(1)}, bf16[144,512]{1,0:T(8,128)(2,1)S(1)}, u32[]{:S(2)}, u32[]{:S(2)}) collective-permute-start(bf16[144,512]{1,0:T(8,128)(2,1)S(1)} %pad_maximum_fusion.6), channel_id=1, source_target_pairs={{0,2},{1,3},{2,0},{3,1},{4,6},{5,7},{6,4},{7,5},{8,10},{9,11},{10,... | collective-permute-start | bytes 442376 | tf_op jit(solution)/shard_map/ppermute | solution.py:655
  42.1 10.2 %collective-permute-start.19 = (bf16[64,1536]{1,0:T(8,128)(2,1)S(1)}, bf16[64,1536]{1,0:T(8,128)(2,1)S(1)}, u32[]{:S(2)}, u32[]{:S(2)}) collective-permute-start(bf16[64,1536]{1,0:T(8,128)(2,1)S(1)} %reduce-precision_convert_fusion.2), channel_id=1, source_target_pairs={{0,24},{1,25},{2,26},{3,27},{4,28},{5,29},{6,30},{7,31},{8,16},{9,... | collective-permute-start | bytes 589832 | tf_op jit(solution)/shard_map/ppermute | solution.py:655
  50.6 1.2 %collective-permute-start.17 = (f32[8,512]{1,0:T(8,128)S(1)}, f32[8,512]{1,0:T(8,128)S(1)}, u32[]{:S(2)}, u32[]{:S(2)}) collective-permute-start(f32[8,512]{1,0:T(8,128)S(1)} %add_add_fusion.3), channel_id=1, source_target_pairs={{0,1},{1,0},{2,3},{3,2},{4,5},{5,4},{6,7},{7,6},{8,9},{9,8},{10,11... | collective-permute-start | bytes 49160 | tf_op jit(solution)/shard_map/ppermute | solution.py:655
  51.9 6.0 %collective-permute-start.18 = (bf16[144,512]{1,0:T(8,128)(2,1)S(1)}, bf16[144,512]{1,0:T(8,128)(2,1)S(1)}, u32[]{:S(2)}, u32[]{:S(2)}) collective-permute-start(bf16[144,512]{1,0:T(8,128)(2,1)S(1)} %pad_maximum_fusion.7), channel_id=1, source_target_pairs={{0,4},{1,5},{2,6},{3,7},{4,0},{5,1},{6,2},{7,3},{8,12},{9,13},{10,... | collective-permute-start | bytes 442376 | tf_op jit(solution)/shard_map/ppermute | solution.py:655
  52.3 6.8 %collective-permute-start.21 = (bf16[64,1536]{1,0:T(8,128)(2,1)S(1)}, bf16[64,1536]{1,0:T(8,128)(2,1)S(1)}, u32[]{:S(2)}, u32[]{:S(2)}) collective-permute-start(bf16[64,1536]{1,0:T(8,128)(2,1)S(1)} %reduce-precision_convert_fusion.1), channel_id=1, source_target_pairs={{0,8},{1,9},{2,10},{3,11},{4,12},{5,13},{6,14},{7,15},{8,0},{9,1},... | collective-permute-start | bytes 589832 | tf_op jit(solution)/shard_map/ppermute | solution.py:655
  57.9 7.1 %collective-permute-start.20 = (bf16[144,512]{1,0:T(8,128)(2,1)S(1)}, bf16[144,512]{1,0:T(8,128)(2,1)S(1)}, u32[]{:S(2)}, u32[]{:S(2)}) collective-permute-start(bf16[144,512]{1,0:T(8,128)(2,1)S(1)} %pad_maximum_fusion.8), channel_id=1, source_target_pairs={{0,24},{1,25},{2,26},{3,27},{4,28},{5,29},{6,30},{7,31},{8,16},{9,... | collective-permute-start | bytes 442376 | tf_op jit(solution)/shard_map/ppermute | solution.py:655
  59.1 7.3 %collective-permute-start.23 = (bf16[64,1536]{1,0:T(8,128)(2,1)S(1)}, bf16[64,1536]{1,0:T(8,128)(2,1)S(1)}, u32[]{:S(2)}, u32[]{:S(2)}) collective-permute-start(bf16[64,1536]{1,0:T(8,128)(2,1)S(1)} %reduce-precision_convert_fusion), channel_id=1, source_target_pairs={{0,4},{1,5},{2,6},{3,7},{4,0},{5,1},{6,2},{7,3},{8,12},{9,13},{10,... | collective-permute-start | bytes 589832 | tf_op jit(solution)/shard_map/ppermute | solution.py:655
  60.9 6.3 %collective-permute-start.25 = (bf16[64,1024]{1,0:T(8,128)(2,1)S(1)}, bf16[64,1024]{1,0:T(8,128)(2,1)S(1)}, u32[]{:S(2)}, u32[]{:S(2)}) collective-permute-start(bf16[64,1024]{1,0:T(8,128)(2,1)S(1)} %get-tuple-element.161), channel_id=1, source_target_pairs={{0,2},{1,3},{2,0},{3,1},{4,6},{5,7},{6,4},{7,5},{8,10},{9,11},{10,... | collective-permute-start | bytes 393224 | tf_op jit(solution)/shard_map/ppermute | solution.py:655
  61.7 6.2 %collective-permute-start.26 = (bf16[64,1024]{1,0:T(8,128)(2,1)S(1)}, bf16[64,1024]{1,0:T(8,128)(2,1)S(1)}, u32[]{:S(2)}, u32[]{:S(2)}) collective-permute-start(bf16[64,1024]{1,0:T(8,128)(2,1)S(1)} %get-tuple-element.161), channel_id=1, source_target_pairs={{0,6},{1,7},{2,4},{3,5},{4,2},{5,3},{6,0},{7,1},{8,14},{9,15},{10,... | collective-permute-start | bytes 393224 | tf_op jit(solution)/shard_map/ppermute | solution.py:655
  62.8 3.7 %collective-permute-start.24 = (bf16[1,64,1024]{2,1,0:T(8,128)(2,1)S(1)}, bf16[1,64,1024]{2,1,0:T(8,128)(2,1)S(1)}, u32[]{:S(2)}, u32[]{:S(2)}) collective-permute-start(bf16[1,64,1024]{2,1,0:T(8,128)(2,1)S(1)} %get-tuple-element.149.refs_0_), channel_id=1, source_target_pairs={{0,1},{1,0},{2,3},{3,2},{4,5},{5,4},{6,7},{7,6},{8,9},{9,8},{10,11... | collective-permute-start | bytes 393224 | tf_op jit(solution)/shard_map/ppermute | solution.py:655
  65.1 5.2 %collective-permute-start.22 = (bf16[144,512]{1,0:T(8,128)(2,1)S(1)}, bf16[144,512]{1,0:T(8,128)(2,1)S(1)}, u32[]{:S(2)}, u32[]{:S(2)}) collective-permute-start(bf16[144,512]{1,0:T(8,128)(2,1)S(1)} %pad_maximum_fusion.9), channel_id=1, source_target_pairs={{0,8},{1,9},{2,10},{3,11},{4,12},{5,13},{6,14},{7,15},{8,0},{9,1},... | collective-permute-start | bytes 442376 | tf_op jit(solution)/shard_map/ppermute | solution.py:655
  67.9 4.2 %collective-permute-start.27 = (bf16[3,64,1024]{2,1,0:T(8,128)(2,1)S(1)}, bf16[3,64,1024]{2,1,0:T(8,128)(2,1)S(1)}, u32[]{:S(2)}, u32[]{:S(2)}) collective-permute-start(bf16[3,64,1024]{2,1,0:T(8,128)(2,1)S(1)} %pad_maximum_fusion.1.refs_1_), channel_id=1, source_target_pairs={{0,1},{1,0},{2,3},{3,2},{4,5},{5,4},{6,7},{7,6},{8,9},{9,8},{10,11... | collective-permute-start | bytes 1179656 | tf_op jit(solution)/shard_map/ppermute | solution.py:655

commit v6 on v5

--- a/solution.py
+++ b/solution.py
@@ -59,16 +59,16 @@
     return jnp.concatenate([column] * (lanes // column.shape[1]), axis=1)
 
 
-def call(body, outs, ins, scratch, limit_mib, flops, name, fetched=()):
+def call(body, outs, ins, scratch, limit_mib, flops, name, fetched=(), sent=False):
     specs = []
     for k, x in enumerate(ins):
-        space = pltpu.SMEM if x.ndim == 1 else pltpu.HBM if k in fetched else pltpu.VMEM
+        space = pltpu.SMEM if x.ndim == 1 else pl.ANY if k in fetched else pltpu.VMEM
         specs.append(pl.BlockSpec(memory_space=space))
     return pl.pallas_call(
         body,
         out_shape=[jax.ShapeDtypeStruct(s, d) for s, d in outs],
         in_specs=specs,
-        out_specs=[pl.BlockSpec(memory_space=pltpu.VMEM)] * len(outs),
+        out_specs=[pl.BlockSpec(memory_space=pl.ANY if sent else pltpu.VMEM)] * len(outs),
         scratch_shapes=scratch,
         compiler_params=pltpu.CompilerParams(vmem_limit_bytes=limit_mib * MIB),
         cost_estimate=pl.CostEstimate(flops=flops, bytes_accessed=4 * MIB, transcendentals=0),
@@ -149,16 +149,19 @@
     limit_ref[...] = length - (lax.axis_index("state") * segs + place // group) * steps
 
 
-def norm_kernel(x_ref, vec_ref, low_ref, unit_ref, inv_ref):
+def norm_kernel(x_hbm, vec_ref, low_ref, unit_ref, inv_ref, rows_ref, x_ref, sems):
     segs, steps, group, feats = x_ref.shape
     rows = steps * SUB
     size = 128
     gain, bias = vec_ref[0:1, :], vec_ref[1:2, :]
+    cut = steps // 4
+    places = [pl.ds(k * cut, cut) for k in range(4)]
+    copies = start_copies([x_hbm.at[:, p] for p in places], [x_ref.at[:, p] for p in places], sems)
 
     def chunk(c, carry):
-        base = c * size
-        at = pl.ds(base, size)
+        at = pl.ds(c * size, size)
         x = rows_in(x_ref, c * (size // SUB), size // SUB)
+        rows_ref[at, :] = x.astype(BF16)
         centred = x - jnp.mean(x, axis=1, keepdims=True)
         inv = lax.rsqrt(jnp.mean(centred * centred, axis=1, keepdims=True) + EPSILON)
         unit = centred * inv
@@ -167,7 +170,10 @@
         inv_ref[at, :] = jnp.broadcast_to(inv, (size, 128))
         return carry
 
-    repeat(0, rows // size, chunk, 0)
+    turns = rows // size // 4
+    for k in range(4):
+        copies[k].wait()
+        repeat(k * turns, (k + 1) * turns, chunk, 0)
 
 
 def gather_rows(me, blocks, flat_ref, dst_ref):
@@ -336,31 +342,42 @@
 
     lax.fori_loop(0, steps, step, (hr, hi), unroll=16)
 
-    def chunk(c, carry):
-        base = c * CHUNK
-        at = pl.ds(base, CHUNK)
-        states = states_ref[pl.ds(pl.multiple_of(base + SUB, SUB), CHUNK), :]
+    kept = {}
+
+    def mixed(c):
+        states = states_ref[pl.ds(c * CHUNK + SUB, CHUNK), :]
         slow = jnp.concatenate([states[:, :channels], -states[:, channels:]], axis=1).astype(BF16)
-        slow_ref[at, :] = slow
-        normed = unit_ref[at, :] * gain + bias
-        v = nn(slow, cw_ref[...]) + skip * normed
-        t = jnp.tanh(GELU_A * (v + GELU_B * (v * v * v)))
-        half = 0.5 * (1.0 + t)
-        gp_ref[at, :] = half + (0.5 * GELU_A) * v * (1.0 - t * t) * (1.0 + (3.0 * GELU_B) * (v * v))
+        slow_ref[pl.ds(c * CHUNK, CHUNK), :] = slow
+        kept["mixed", c] = nn(slow, cw_ref[...])
+
+    def activate(c):
+        at = pl.ds(c * CHUNK, CHUNK)
+        v = kept.pop(("mixed", c)) + skip * (unit_ref[at, :] * gain + bias)
+        square = v * v
+        t = jnp.tanh(v * (GELU_A + (GELU_A * GELU_B) * square))
+        half = 0.5 + 0.5 * t
+        slope = (0.5 * GELU_A) + (1.5 * GELU_A * GELU_B) * square
+        gp_ref[at, :] = half + v * (1.0 - t * t) * slope
         act = (v * half).astype(BF16)
         act_ref[at, :] = act
-        glu = nn(act, glu_ref[...])
-        mask = wide(valid(base // SUB, CHUNK // SUB, limit_ref), feats)
+        kept["glu", c] = nn(act, glu_ref[...])
+
+    def gated(c):
+        at = pl.ds(c * CHUNK, CHUNK)
+        glu = kept.pop(("glu", c))
         value = glu[:, :feats]
         gate = jax.nn.sigmoid(glu[:, feats:])
-        branch = mask * gate
+        branch = wide(valid(c * CHUNK // SUB, CHUNK // SUB, limit_ref), feats) * gate
         branch_ref[at, :] = branch * value
         d_value = branch * cot_ref[at, :].astype(F32)
         dglu_ref[at, :feats] = d_value.astype(BF16)
         dglu_ref[at, feats:] = (d_value * value * (1.0 - gate)).astype(BF16)
-        return carry
-
-    repeat(0, rows // CHUNK, chunk, 0)
+
+    count = rows // CHUNK
+    for k in range(count + 2):
+        for lag, stage in enumerate((mixed, activate, gated)):
+            if 0 <= k - lag < count:
+                stage(k - lag)
     width = 256
 
     def tile(c, carry):
@@ -511,23 +528,22 @@
     spread_pairs(acc_ref, me, own, channels, orders, grads)
 
 
-def out_kernel(x_hbm, branch_ref, out_ref, x_ref, sems):
-    segs, steps, _, _ = x_ref.shape
-    size = 16
-    cut = steps // 4
-    places = [pl.ds(k * cut, cut) for k in range(4)]
-    copies = start_copies([x_hbm.at[:, p] for p in places], [x_ref.at[:, p] for p in places], sems)
-
-    def chunk(c, carry):
-        first = c * size
-        rows = branch_ref[pl.ds(pl.multiple_of(first * SUB, size * SUB), size * SUB), :]
-        at = pl.ds(first, size)
-        out_ref[:, at] = (x_ref[:, at].astype(F32) + rows_out(rows, x_ref)).astype(BF16)
-        return carry
-
-    for k in range(4):
-        copies[k].wait()
-        repeat(k * cut // size, (k + 1) * cut // size, chunk, 0)
+def send_steps(rows_of, out_hbm, out_ref, sems):
+    steps = out_ref.shape[1]
+    count = sems.shape[0]
+    cut = steps // count
+    copies = []
+    for k in range(count):
+        at = pl.ds(k * cut, cut)
+        out_ref[:, at] = rows_out(rows_of(pl.ds(k * cut * SUB, cut * SUB)), out_ref).astype(out_ref.dtype)
+        copies.append(pltpu.make_async_copy(out_ref.at[:, at], out_hbm.at[:, at], sems.at[k]))
+        copies[-1].start()
+    for c in copies:
+        c.wait()
+
+
+def out_kernel(x_ref, branch_ref, out_hbm, out_ref, sems):
+    send_steps(lambda at: x_ref[at, :].astype(F32) + branch_ref[at, :], out_hbm, out_ref, sems)
 
 
 def normed_kernel(dproj_ref, win_ref, dpre_ref, unit_ref, vec_ref, channel_ref, skip_ref, dnorm_ref, sums_ref):
@@ -556,29 +572,18 @@
     sums_ref[5:8, :] = jnp.zeros((3, feats), F32)
 
 
-def tokens_kernel(cot_hbm, dnorm_ref, unit_ref, inv_ref, vec_ref, out_ref, cot_ref, sems):
-    rows, feats = dnorm_ref.shape
+def tokens_kernel(cot_ref, dnorm_ref, unit_ref, inv_ref, vec_ref, out_hbm, out_ref, sems):
+    feats = dnorm_ref.shape[1]
     gain = vec_ref[0:1, :]
-    size = 128
-    steps = size // SUB
-    cut = cot_ref.shape[1] // 4
-    places = [pl.ds(k * cut, cut) for k in range(4)]
-    copies = start_copies([cot_hbm.at[:, p] for p in places], [cot_ref.at[:, p] for p in places], sems)
-
-    def chunk(c, carry):
-        at = pl.ds(c * size, size)
+
+    def rows_of(at):
         unit = unit_ref[at, :]
         d_unit = dnorm_ref[at, :] * gain
         first = jnp.mean(d_unit, axis=1, keepdims=True)
         second = jnp.mean(d_unit * unit, axis=1, keepdims=True)
-        rows = wide(inv_ref[at, :], feats) * (d_unit - first - unit * second)
-        step_at = pl.ds(c * steps, steps)
-        out_ref[:, step_at] = cot_ref[:, step_at].astype(F32) + rows_out(rows, cot_ref)
-        return carry
-
-    for k in range(4):
-        copies[k].wait()
-        repeat(k * cut // steps, (k + 1) * cut // steps, chunk, 0)
+        return cot_ref[at, :].astype(F32) + wide(inv_ref[at, :], feats) * (d_unit - first - unit * second)
+
+    send_steps(rows_of, out_hbm, out_ref, sems)
 
 
 def join_pairs(parts, flat_ref, out_ref):
@@ -776,14 +781,15 @@
         "prep",
     )
     b_own = jnp.concatenate([input_weight.transpose(1, 2, 0), small_own], axis=0)
-    low, unit, inv = call(
+    low, unit, inv, x_rows = call(
         norm_kernel,
-        [((rows, feats), BF16), ((rows, feats), F32), ((rows, 128), F32)],
+        [((rows, feats), BF16), ((rows, feats), F32), ((rows, 128), F32), ((rows, feats), BF16)],
         [x4, vec],
-        [],
+        [held(x4), pltpu.SemaphoreType.DMA((4,))],
         12,
         rows * feats * 20,
         "norm",
+        fetched=(0,),
     )
     (limit,) = call(
         functools.partial(limit_kernel, group, rows // SUB),
@@ -925,22 +931,22 @@
     (grad4,) = call(
         tokens_kernel,
         [(cot4.shape, F32)],
-        [cot4, tie(d_normed, both, chain.sent[-1]), unit, inv, vec],
-        [held(cot4), pltpu.SemaphoreType.DMA((4,))],
+        [cot, tie(d_normed, both, chain.sent[-1]), unit, inv, vec],
+        [pltpu.VMEM(cot4.shape, F32), pltpu.SemaphoreType.DMA((8,))],
         12,
         full,
         "tokens",
-        fetched=(0,),
+        sent=True,
     )
     (out4,) = call(
         out_kernel,
         [(x4.shape, BF16)],
-        [x4, tie(branch, both, chain.sent[-1])],
-        [held(x4), pltpu.SemaphoreType.DMA((4,))],
+        [x_rows, tie(branch, both, chain.sent[-1])],
+        [held(x4), pltpu.SemaphoreType.DMA((8,))],
         8,
         MIB,
         "out",
-        fetched=(0,),
+        sent=True,
     )
     chain.take()
     chain.held = chain.held + exchange(chain.held, state_bits[0])
@@ -994,7 +1000,7 @@
     near_masks = [[0], rest]
     far = [f for p, o in zip(submasks(all_groups[0]), far_own) for f in (o, exchange(near[1], p))]
     far_masks = [[m ^ p for m in ms] for p in submasks(all_groups[0]) for ms in near_masks]
-    grad_glu = place_blocks(tie(near, last), near_masks, parts, (feats, 2 * feats))
+    grad_glu = place_blocks(near, near_masks, parts, (feats, 2 * feats))
     grad_glu = place_blocks(tie(far, grad_in), far_masks, parts, (feats, 2 * feats), grad_glu)
     return (
         out4.reshape(tokens.shape),

time: 73.5 us -> 70.7 us (0.962)
  waiting for transfers between devices: 19.9 us -> 17.3 us
  Pallas kernels: 24.2 us -> 23 us
  starting transfers between devices: 23.2 us -> 24.4 us
    ppermute x28, waiting for transfers between devices: 19.9 us -> 17.3 us  [exchange(): lax.ppermute(x, ('seq', 'state'), [(i, i ^ mask) for i in range(count)])]
    pallas_call x15, Pallas kernels: 22.2 us -> 21 us  [call(): pl.pallas_call(body, out_shape=[jax.ShapeDtypeStruct(s, d) for s, d in ou...]
    ppermute x28, starting transfers between devices: 23.2 us -> 24.4 us  [exchange(): lax.ppermute(x, ('seq', 'state'), [(i, i ^ mask) for i in range(count)])]
    unnamed x12 -> x10, local copies, waits for them, and re-layouts: 1.9 us -> 1.89 us
where the time goes in v6:
time: 70.7 us; the launch traced here: 70.5 us
  starting transfers between devices  24.4 us (35%)
  Pallas kernels  23 us (33%)
  waiting for transfers between devices  17.3 us (24%)
  local copies, waits for them, and re-layouts  2.8 us (4%)
  other arithmetic  1.91 us (3%)
  between operations  1.19 us (2%)
    ppermute x28, starting transfers between devices, exchange(): lax.ppermute(x, ('seq', 'state'), [(i, i ^ mask) for i in range(count)])  24.4 us
    pallas_call x15, Pallas kernels, call(): pl.pallas_call(body, out_shape=[jax.ShapeDtypeStruct(s, d) for s, d in ou...  21 us
    ppermute x28, waiting for transfers between devices, exchange(): lax.ppermute(x, ('seq', 'state'), [(i, i ^ mask) for i in range(count)])  17.3 us
    pallas_call x2, Pallas kernels, place_blocks(): pl.pallas_call(functools.partial(place_kernel, masks, parts), out_shape=j...  2.03 us
    unnamed x10, local copies, waits for them, and re-layouts  1.89 us
  transfers between devices with their start and end apart: 28, of which 15 were waited for; matrix products, arithmetic and copies ran while one was open for 1% of the time, Pallas kernels for 24%

profile of v6, /device:TPU:0, one launch (start us, length us, event | category | flops | bytes accessed | tf_op | source)
XLA Modules:
  0.0 70.5 jit_solution(15997074619615394729)
XLA Ops:
  0.7 0.8 %concatenate.57 = f32[1728]{0:T(1024)S(1)} concatenate(f32[512]{0:T(512)} %param.13, f32[512]{0:T(512)} %param.14, f32[512]{0:T(512)} %param.20, f32[64]{0:T(128)} %param.17, f32[64]{0:T(128)} %param.18, f32[64]{0:T(128)} %param.19), dimensions={0} | concatenate | bytes 13824 | tf_op jit(solution)/shard_map/concatenate | solution.py:772
  1.5 0.1 prep.1
  1.7 1.1 %pad_maximum_fusion.5.refs_0_ = bf16[72,2,512]{2,1,0:T(2,128)(2,1)S(1)} fusion(bf16[8,2,512]{2,1,0:T(2,128)(2,1)S(1)} %get-tuple-element.84, bf16[64,2,512]{2,1,0:T(2,128)(2,1)} %bitcast.58), kind=kLoop, calls=%fused_computation.20 | loop fusion | flops 73728 | bytes 294912 | tf_op jit(solution)/shard_map/concatenate | solution.py:783
  2.8 3.0 %collective-permute-start.1 = (bf16[72,2,512]{2,1,0:T(2,128)(2,1)S(1)}, bf16[72,2,512]{2,1,0:T(2,128)(2,1)S(1)}, u32[]{:S(2)}, u32[]{:S(2)}) collective-permute-start(bf16[72,2,512]{2,1,0:T(2,128)(2,1)S(1)} %pad_maximum_fusion.5.refs_0_), channel_id=1, source_target_pairs={{0,2},{1,3},{2,0},{3,1},{4,6},{5,7},{6,4},{7,5},{8,10},{9,11},{10,... | collective-permute-start | bytes 442376 | tf_op jit(solution)/shard_map/ppermute | solution.py:660
  5.8 1.2 %copy-done = bf16[512,2,512]{2,1,0:T(2,128)(2,1)S(1)} copy-done((bf16[512,2,512]{2,1,0:T(2,128)(2,1)S(1)}, bf16[512,2,512]{2,1,0:T(2,128)(2,1)}, u32[]{:S(2)}) %copy-start) | copy-done | bytes 1048600
  7.0 1.8 %norm.1 = (bf16[1024,512]{1,0:T(8,128)(2,1)S(1)}, f32[1024,512]{1,0:T(8,128)S(1)}, f32[1024,128]{1,0:T(8,128)S(1)}, bf16[1024,512]{1,0:T(8,128)(2,1)S(1)}) custom-call(bf16[4,128,2,512]{3,2,1,0:T(2,128)(2,1)S(1)} %bitcast.47, f32[8,512]{1,0:T(8,128)S(1)} %get-tuple-element.80.vec_ref.refs_8_.refs_3_), custom_call_target="tpu_custom_call" | custom-call | flops 10485760 | bytes 4194304 | tf_op jit(solution)/shard_map/norm/pallas_call | solution.py:67
  8.8 0.6 copy-done.4
  9.5 0.6 limit.1.limit_ref.refs_7_
  10.0 0.6 collective-permute-start.2
  10.6 0.7 %collective-permute-start.6 = (bf16[64,2,512]{2,1,0:T(2,128)(2,1)}, bf16[64,2,512]{2,1,0:T(2,128)(2,1)S(1)}, u32[]{:S(2)}, u32[]{:S(2)}) collective-permute-start(bf16[64,2,512]{2,1,0:T(2,128)(2,1)} %refs_0_), channel_id=1, source_target_pairs={{0,2},{1,3},{2,0},{3,1},{4,6},{5,7},{6,4},{7,5},{8,10},{9,11},{10,... | collective-permute-start | bytes 393224 | tf_op jit(solution)/shard_map/ppermute | solution.py:660
  11.4 0.3 collective-permute-done.2.refs_3_
  11.6 1.6 %project.1 = (f32[1024,512]{1,0:T(8,128)S(1)}, f32[8,512]{1,0:T(8,128)S(1)}, bf16[512,512]{1,0:T(8,128)(2,1)S(1)}, f32[8,512]{1,0:T(8,128)S(1)}) custom-call(bf16[1024,512]{1,0:T(8,128)(2,1)S(1)} %get-tuple-element.82.low_ref.refs_6_, s32[8,128]{1,0:T(8,128)S(1)} %limit.1.limit_ref.refs_7_, bf16[72,2,512]{2,1,0:T(2,128)(2,1)S(1)} %pad_maximum_fusion.5.refs_0_, ...), custom_call_target="tpu_custom_call" | custom-call | flops 536870912 | bytes 4194304 | tf_op jit(solution)/shard_map/project/pallas_call | solution.py:67
  13.2 1.2 %collective-permute-start.3 = (f32[1,8,512]{2,1,0:T(8,128)S(1)}, f32[1,8,512]{2,1,0:T(8,128)S(1)}, u32[]{:S(2)}, u32[]{:S(2)}) collective-permute-start(f32[1,8,512]{2,1,0:T(8,128)S(1)} %bitcast.53), channel_id=1, source_target_pairs={{0,2},{1,3},{2,0},{3,1},{4,6},{5,7},{6,4},{7,5},{8,10},{9,11},{10,... | collective-permute-start | bytes 49160 | tf_op jit(solution)/shard_map/ppermute | solution.py:660
  14.4 1.9 %collective-permute-done.6.refs_2_ = bf16[64,2,512]{2,1,0:T(2,128)(2,1)S(1)} collective-permute-done((bf16[64,2,512]{2,1,0:T(2,128)(2,1)}, bf16[64,2,512]{2,1,0:T(2,128)(2,1)S(1)}, u32[]{:S(2)}, u32[]{:S(2)}) %collective-permute-start.6) | collective-permute-done | bytes 131104 | tf_op jit(solution)/shard_map/ppermute | solution.py:660
  16.3 0.7 %collective-permute-done.3 = f32[1,8,512]{2,1,0:T(8,128)S(1)} collective-permute-done((f32[1,8,512]{2,1,0:T(8,128)S(1)}, f32[1,8,512]{2,1,0:T(8,128)S(1)}, u32[]{:S(2)}, u32[]{:S(2)}) %collective-permute-start.3) | collective-permute-done | bytes 16416 | tf_op jit(solution)/shard_map/ppermute | solution.py:660
  17.1 0.3 cotangent.1.refs_6_.cot_ref
  17.4 0.3 collective-permute-done.7.refs_3_
  17.7 0.4 weights.1.refs_4_.cw_ref
  18.0 0.2 collective-permute-done.4
  18.3 5.1 %mix.1 = (f32[1032,512]{1,0:T(8,128)S(1)}, bf16[1024,512]{1,0:T(8,128)(2,1)S(1)}, f32[1024,512]{1,0:T(8,128)S(1)}, bf16[1024,1024]{1,0:T(8,128)(2,1)S(1)}, f32[1...) custom-call(f32[1024,512]{1,0:T(8,128)S(1)} %get-tuple-element.86.re, ...), custom_call_target="tpu_custom_call" | custom-call | flops 2684354560 | bytes 4194304 | tf_op jit(solution)/shard_map/mix/pallas_call | solution.py:67
  23.4 0.3 collective-permute-start.8
  23.7 2.1 %back.1 = (f32[1024,512]{1,0:T(8,128)S(1)}, bf16[1024,512]{1,0:T(8,128)(2,1)S(1)}, f32[8,512]{1,0:T(8,128)S(1)}, bf16[4,64,512]{2,1,0:T(8,128)(2,1)S(1)}, f32[1,...) custom-call(bf16[1024,1024]{1,0:T(8,128)(2,1)S(1)} %get-tuple-element.97, ...), custom_call_target="tpu_custom_call" | custom-call | flops 1610612736 | bytes 4194304 | tf_op jit(solution)/shard_map/back/pallas_call | solution.py:67
  25.7 0.4 collective-permute-start.9
  26.1 1.2 %starts.1 = (f32[1024,512]{1,0:T(8,128)S(1)}, f32[8,512]{1,0:T(8,128)S(1)}) custom-call(bf16[1024,512]{1,0:T(8,128)(2,1)S(1)} %get-tuple-element.101.dmix_ref, bf16[512,512]{1,0:T(8,128)(2,1)S(1)} %weights.1.refs_4_.cw_ref, f32[8,512]{1,0:T(8,128)S(1)} %get-tuple-element.88.refs_2_.cst_ref), custom_call_target="tpu_custom_call" | custom-call | flops 536870912 | bytes 4194304 | tf_op jit(solution)/shard_map/starts/pallas_call | solution.py:67
  27.3 0.0 collective-permute-done.9
  27.3 1.3 %collective-permute-start.13 = (f32[1,8,512]{2,1,0:T(8,128)S(1)}, f32[1,8,512]{2,1,0:T(8,128)S(1)}, u32[]{:S(2)}, u32[]{:S(2)}) collective-permute-start(f32[1,8,512]{2,1,0:T(8,128)S(1)} %bitcast.50), channel_id=1, source_target_pairs={{0,2},{1,3},{2,0},{3,1},{4,6},{5,7},{6,4},{7,5},{8,10},{9,11},{10,... | collective-permute-start | bytes 49160 | tf_op jit(solution)/shard_map/ppermute | solution.py:660
  28.6 0.1 convert_add_fusion.3
  28.7 0.2 convert_add_fusion.2
  28.9 0.9 %collective-permute-start.10 = (bf16[1,64,1536]{2,1,0:T(8,128)(2,1)S(1)}, bf16[1,64,1536]{2,1,0:T(8,128)(2,1)S(1)}, u32[]{:S(2)}, u32[]{:S(2)}) collective-permute-start(bf16[1,64,1536]{2,1,0:T(8,128)(2,1)S(1)} %pad_maximum_fusion.2), channel_id=1, source_target_pairs={{0,2},{1,3},{2,0},{3,1},{4,6},{5,7},{6,4},{7,5},{8,10},{9,11},{10,... | collective-permute-start | bytes 589832 | tf_op jit(solution)/shard_map/ppermute | solution.py:660
  29.8 1.6 %collective-permute-start.11 = (bf16[1,64,1536]{2,1,0:T(8,128)(2,1)S(1)}, bf16[1,64,1536]{2,1,0:T(8,128)(2,1)S(1)}, u32[]{:S(2)}, u32[]{:S(2)}) collective-permute-start(bf16[1,64,1536]{2,1,0:T(8,128)(2,1)S(1)} %pad_maximum_fusion.3), channel_id=1, source_target_pairs={{0,4},{1,5},{2,6},{3,7},{4,0},{5,1},{6,2},{7,3},{8,12},{9,13},{10,... | collective-permute-start | bytes 589832 | tf_op jit(solution)/shard_map/ppermute | solution.py:660
  31.4 0.1 collective-permute-start.14
  31.5 1.9 %collective-permute-start.12 = (bf16[1,64,1536]{2,1,0:T(8,128)(2,1)S(1)}, bf16[1,64,1536]{2,1,0:T(8,128)(2,1)S(1)}, u32[]{:S(2)}, u32[]{:S(2)}) collective-permute-start(bf16[1,64,1536]{2,1,0:T(8,128)(2,1)S(1)} %pad_maximum_fusion.4), channel_id=1, source_target_pairs={{0,6},{1,7},{2,4},{3,5},{4,2},{5,3},{6,0},{7,1},{8,14},{9,15},{10,... | collective-permute-start | bytes 589832 | tf_op jit(solution)/shard_map/ppermute | solution.py:660
  33.4 1.9 %adjoint.1 = (bf16[1024,512]{1,0:T(8,128)(2,1)S(1)}, f32[8,768]{1,0:T(8,128)S(1)}, bf16[2,128,512]{2,1,0:T(8,128)(2,1)S(1)}, f32[1,128,512]{2,1,0:T(8,128)S(1)}, f32[1,128,512]{2,1,0:T(8,128)S(1)}) custom-call(f32[1024,512]{1,0:T(8,128)S(1)} %get-tuple-element.113.refs_0_, f32[8,512]{1,0:T(8,128)S(1)} %get-tuple-element.114.refs_1_, ...), custom_call_target="tpu_custom_call" | custom-call | flops 1073741824 | bytes 4194304 | tf_op jit(solution)/shard_map/adjoint/pallas_call | solution.py:67
  35.4 0.3 collective-permute-start.15
  35.6 0.8 %normed.1 = (f32[1024,512]{1,0:T(8,128)S(1)}, f32[8,512]{1,0:T(8,128)S(1)}) custom-call(bf16[1024,512]{1,0:T(8,128)(2,1)S(1)} %get-tuple-element.118.dproj_ref, bf16[512,512]{1,0:T(8,128)(2,1)S(1)} %get-tuple-element.119.win_ref, f32[1024,512]{1,0:T(8,128)S(1)} %get-tuple-element.120.dpre_ref, f32[1024,512]{1,0:T(8,128)S(1)} %get-tuple-element.92.refs_5_.refs_2_.unit_ref, ...), custom_call_target="tpu_custom_call" | custom-call | flops 536870912 | bytes 4194304 | tf_op jit(solution)/shard_map/normed/pallas_call | solution.py:67
  36.5 0.5 collective-permute-done.15
  37.0 0.9 %collective-permute-start.16 = (bf16[144,512]{1,0:T(8,128)(2,1)S(1)}, bf16[144,512]{1,0:T(8,128)(2,1)S(1)}, u32[]{:S(2)}, u32[]{:S(2)}) collective-permute-start(bf16[144,512]{1,0:T(8,128)(2,1)S(1)} %pad_maximum_fusion.6), channel_id=1, source_target_pairs={{0,2},{1,3},{2,0},{3,1},{4,6},{5,7},{6,4},{7,5},{8,10},{9,11},{10,... | collective-permute-start | bytes 442376 | tf_op jit(solution)/shard_map/ppermute | solution.py:660
  37.9 1.7 %collective-permute-done.11 = bf16[1,64,1536]{2,1,0:T(8,128)(2,1)S(1)} collective-permute-done((bf16[1,64,1536]{2,1,0:T(8,128)(2,1)S(1)}, bf16[1,64,1536]{2,1,0:T(8,128)(2,1)S(1)}, u32[]{:S(2)}, u32[]{:S(2)}) %collective-permute-start.11) | collective-permute-done | bytes 196640 | tf_op jit(solution)/shard_map/ppermute | solution.py:660
  39.6 1.9 %collective-permute-done.12 = bf16[1,64,1536]{2,1,0:T(8,128)(2,1)S(1)} collective-permute-done((bf16[1,64,1536]{2,1,0:T(8,128)(2,1)S(1)}, bf16[1,64,1536]{2,1,0:T(8,128)(2,1)S(1)}, u32[]{:S(2)}, u32[]{:S(2)}) %collective-permute-start.12) | collective-permute-done | bytes 196640 | tf_op jit(solution)/shard_map/ppermute | solution.py:660
  41.5 0.1 reduce-precision_convert_fusion.2
  41.6 3.6 %collective-permute-start.19 = (bf16[64,1536]{1,0:T(8,128)(2,1)S(1)}, bf16[64,1536]{1,0:T(8,128)(2,1)S(1)}, u32[]{:S(2)}, u32[]{:S(2)}) collective-permute-start(bf16[64,1536]{1,0:T(8,128)(2,1)S(1)} %reduce-precision_convert_fusion.2), channel_id=1, source_target_pairs={{0,24},{1,25},{2,26},{3,27},{4,28},{5,29},{6,30},{7,31},{8,16},{9,... | collective-permute-start | bytes 589832 | tf_op jit(solution)/shard_map/ppermute | solution.py:660
  45.3 1.7 %out.1 = bf16[4,128,2,512]{3,2,1,0:T(2,128)(2,1)} custom-call(bf16[1024,512]{1,0:T(8,128)(2,1)S(1)} %get-tuple-element.81.x_ref, f32[1024,512]{1,0:T(8,128)S(1)} %get-tuple-element.127.branch_ref), custom_call_target="tpu_custom_call" | custom-call | flops 1048576 | bytes 4194304 | tf_op jit(solution)/shard_map/out/pallas_call | solution.py:67
  47.0 1.8 %tokens.1 = f32[4,128,2,512]{3,2,1,0:T(2,128)} custom-call(bf16[1024,512]{1,0:T(8,128)(2,1)S(1)} %cotangent.1.refs_6_.cot_ref, f32[1024,512]{1,0:T(8,128)S(1)} %get-tuple-element.129.dnorm_ref, f32[1024,512]{1,0:T(8,128)S(1)} %get-tuple-element.92.refs_5_.refs_2_.unit_ref, f32[1024,128]{1,0:T(8,128)S(1)} %get-tuple-element.130.inv_ref, ...), custom_call_target="tpu_custom_call" | custom-call | flops 536870912 | bytes 4194304 | tf_op jit(solution)/shard_map/tokens/pallas_call | solution.py:67
  48.9 0.1 collective-permute-start.17
  48.9 0.1 fusion.3
  49.0 1.1 %collective-permute-done.17 = f32[8,512]{1,0:T(8,128)S(1)} collective-permute-done((f32[8,512]{1,0:T(8,128)S(1)}, f32[8,512]{1,0:T(8,128)S(1)}, u32[]{:S(2)}, u32[]{:S(2)}) %collective-permute-start.17) | collective-permute-done | bytes 16416 | tf_op jit(solution)/shard_map/ppermute | solution.py:660
  50.1 0.7 collective-permute-start.18
  50.9 2.0 %collective-permute-start.21 = (bf16[64,1536]{1,0:T(8,128)(2,1)S(1)}, bf16[64,1536]{1,0:T(8,128)(2,1)S(1)}, u32[]{:S(2)}, u32[]{:S(2)}) collective-permute-start(bf16[64,1536]{1,0:T(8,128)(2,1)S(1)} %reduce-precision_convert_fusion.1), channel_id=1, source_target_pairs={{0,8},{1,9},{2,10},{3,11},{4,12},{5,13},{6,14},{7,15},{8,0},{9,1},... | collective-permute-start | bytes 589832 | tf_op jit(solution)/shard_map/ppermute | solution.py:660
  52.9 3.3 %collective-permute-done.18 = bf16[144,512]{1,0:T(8,128)(2,1)S(1)} collective-permute-done((bf16[144,512]{1,0:T(8,128)(2,1)S(1)}, bf16[144,512]{1,0:T(8,128)(2,1)S(1)}, u32[]{:S(2)}, u32[]{:S(2)}) %collective-permute-start.18) | collective-permute-done | bytes 147488 | tf_op jit(solution)/shard_map/ppermute | solution.py:660
  56.2 0.3 collective-permute-start.20
  56.5 1.1 %collective-permute-done.21 = bf16[64,1536]{1,0:T(8,128)(2,1)S(1)} collective-permute-done((bf16[64,1536]{1,0:T(8,128)(2,1)S(1)}, bf16[64,1536]{1,0:T(8,128)(2,1)S(1)}, u32[]{:S(2)}, u32[]{:S(2)}) %collective-permute-start.21) | collective-permute-done | bytes 196640 | tf_op jit(solution)/shard_map/ppermute | solution.py:660
  57.7 1.5 %collective-permute-start.23 = (bf16[64,1536]{1,0:T(8,128)(2,1)S(1)}, bf16[64,1536]{1,0:T(8,128)(2,1)S(1)}, u32[]{:S(2)}, u32[]{:S(2)}) collective-permute-start(bf16[64,1536]{1,0:T(8,128)(2,1)S(1)} %reduce-precision_convert_fusion), channel_id=1, source_target_pairs={{0,4},{1,5},{2,6},{3,7},{4,0},{5,1},{6,2},{7,3},{8,12},{9,13},{10,... | collective-permute-start | bytes 589832 | tf_op jit(solution)/shard_map/ppermute | solution.py:660
  59.2 1.0 %collective-permute-start.25 = (bf16[64,1024]{1,0:T(8,128)(2,1)S(1)}, bf16[64,1024]{1,0:T(8,128)(2,1)S(1)}, u32[]{:S(2)}, u32[]{:S(2)}) collective-permute-start(bf16[64,1024]{1,0:T(8,128)(2,1)S(1)} %get-tuple-element.159), channel_id=1, source_target_pairs={{0,2},{1,3},{2,0},{3,1},{4,6},{5,7},{6,4},{7,5},{8,10},{9,11},{10,... | collective-permute-start | bytes 393224 | tf_op jit(solution)/shard_map/ppermute | solution.py:660
  60.2 1.2 %collective-permute-start.26 = (bf16[64,1024]{1,0:T(8,128)(2,1)S(1)}, bf16[64,1024]{1,0:T(8,128)(2,1)S(1)}, u32[]{:S(2)}, u32[]{:S(2)}) collective-permute-start(bf16[64,1024]{1,0:T(8,128)(2,1)S(1)} %get-tuple-element.159), channel_id=1, source_target_pairs={{0,6},{1,7},{2,4},{3,5},{4,2},{5,3},{6,0},{7,1},{8,14},{9,15},{10,... | collective-permute-start | bytes 393224 | tf_op jit(solution)/shard_map/ppermute | solution.py:660
  61.3 2.0 %collective-permute-done.20 = bf16[144,512]{1,0:T(8,128)(2,1)S(1)} collective-permute-done((bf16[144,512]{1,0:T(8,128)(2,1)S(1)}, bf16[144,512]{1,0:T(8,128)(2,1)S(1)}, u32[]{:S(2)}, u32[]{:S(2)}) %collective-permute-start.20) | collective-permute-done | bytes 147488 | tf_op jit(solution)/shard_map/ppermute | solution.py:660
  63.3 0.9 %collective-permute-start.22 = (bf16[144,512]{1,0:T(8,128)(2,1)S(1)}, bf16[144,512]{1,0:T(8,128)(2,1)S(1)}, u32[]{:S(2)}, u32[]{:S(2)}) collective-permute-start(bf16[144,512]{1,0:T(8,128)(2,1)S(1)} %pad_maximum_fusion.9), channel_id=1, source_target_pairs={{0,8},{1,9},{2,10},{3,11},{4,12},{5,13},{6,14},{7,15},{8,0},{9,1},... | collective-permute-start | bytes 442376 | tf_op jit(solution)/shard_map/ppermute | solution.py:660
  64.3 0.7 collective-permute-done.23
  65.0 0.8 %halves.1 = f32[64,2,512]{2,1,0:T(2,128)} custom-call(bf16[64,512]{1,0:T(8,128)(2,1)S(1)} %slice.118.mine_ref, bf16[64,512]{1,0:T(8,128)(2,1)S(1)} %slice.119.other_ref), custom_call_target="tpu_custom_call" | custom-call | flops 1048576 | bytes 4194304 | tf_op jit(solution)/shard_map/halves/pallas_call | solution.py:67
  65.8 0.6 collective-permute-done.26
  66.4 0.1 collective-permute-start.27
  66.5 1.0 %place.2.refs_2_ = f32[512,1024]{1,0:T(8,128)} custom-call(bf16[1,64,1024]{2,1,0:T(8,128)(2,1)S(1)} %get-tuple-element.160.refs_0_, bf16[3,64,1024]{2,1,0:T(8,128)(2,1)S(1)} %pad_maximum_fusion.1.refs_1_), custom_call_target="tpu_custom_call" | custom-call | flops 1048576 | bytes 2097152 | tf_op jit(solution)/shard_map/place/pallas_call | solution.py:645
  67.5 1.0 %collective-permute-done.22 = bf16[144,512]{1,0:T(8,128)(2,1)S(1)} collective-permute-done((bf16[144,512]{1,0:T(8,128)(2,1)S(1)}, bf16[144,512]{1,0:T(8,128)(2,1)S(1)}, u32[]{:S(2)}, u32[]{:S(2)}) %collective-permute-start.22) | collective-permute-done | bytes 147488 | tf_op jit(solution)/shard_map/ppermute | solution.py:660
  68.6 0.8 %finish.1 = (f32[64,2,512]{2,1,0:T(2,128)}, f32[1,512]{1,0:T(1,128)}, f32[1,512]{1,0:T(1,128)}, f32[1,512]{1,0:T(1,128)}, f32[1,64]{1,0:T(1,128)}, /*index=5*/f32[1,64]{1,0:T(1,128)}, f32[1,64]{1,0:T(1,128)}) custom-call(f32[128,512]{1,0:T(8,128)S(1)} %convert_add_fusion.1.total_ref, f32[8,512]{1,0:T(8,128)S(1)} %add_add_fusion.sums_ref, ...), custom_call_target="tpu_custom_call" | custom-call | flops 1048576 | bytes 4194304 | tf_op jit(solution)/shard_map/finish/pallas_call | solution.py:67
  69.4 1.0 %place.3 = f32[512,1024]{1,0:T(8,128)} custom-call(bf16[1,64,1024]{2,1,0:T(8,128)(2,1)S(1)} %collective-permute-done.24.refs_0_, bf16[3,64,1024]{2,1,0:T(8,128)(2,1)S(1)} %collective-permute-done.27.refs_1_, f32[512,1024]{1,0:T(8,128)} %place.2.refs_2_), custom_call_target="tpu_custom_call", output_to_operand_aliasing={{}: (2, {})} | custom-call | flops 1048576 | bytes 2097152 | tf_op jit(solution)/shard_map/place/pallas_call | solution.py:645
  (56 shorter events, 0.6 us)
Async XLA Ops:
  0.6 13.8 %copy-start.3 = (bf16[64,2,512]{2,1,0:T(2,128)(2,1)S(1)}, bf16[64,2,512]{2,1,0:T(2,128)(2,1)}, u32[]{:S(2)}) copy-start(bf16[64,2,512]{2,1,0:T(2,128)(2,1)} %refs_0_) | copy-start | bytes 393220
  2.8 7.3 %collective-permute-start.1 = (bf16[72,2,512]{2,1,0:T(2,128)(2,1)S(1)}, bf16[72,2,512]{2,1,0:T(2,128)(2,1)S(1)}, u32[]{:S(2)}, u32[]{:S(2)}) collective-permute-start(bf16[72,2,512]{2,1,0:T(2,128)(2,1)S(1)} %pad_maximum_fusion.5.refs_0_), channel_id=1, source_target_pairs={{0,2},{1,3},{2,0},{3,1},{4,6},{5,7},{6,4},{7,5},{8,10},{9,11},{10,... | collective-permute-start | bytes 442376 | tf_op jit(solution)/shard_map/ppermute | solution.py:660
  5.8 5.6 %collective-permute-start = (bf16[72,2,512]{2,1,0:T(2,128)(2,1)S(1)}, bf16[72,2,512]{2,1,0:T(2,128)(2,1)S(1)}, u32[]{:S(2)}, u32[]{:S(2)}) collective-permute-start(bf16[72,2,512]{2,1,0:T(2,128)(2,1)S(1)} %pad_maximum_fusion.5.refs_0_), channel_id=1, source_target_pairs={{0,1},{1,0},{2,3},{3,2},{4,5},{5,4},{6,7},{7,6},{8,9},{9,8},{10,11... | collective-permute-start | bytes 442376 | tf_op jit(solution)/shard_map/ppermute | solution.py:660
  5.8 1.2 %copy-start = (bf16[512,2,512]{2,1,0:T(2,128)(2,1)S(1)}, bf16[512,2,512]{2,1,0:T(2,128)(2,1)}, u32[]{:S(2)}) copy-start(bf16[512,2,512]{2,1,0:T(2,128)(2,1)} %param.12) | copy-start | bytes 3145732
  7.0 10.1 %copy-start.1 = (bf16[512,2,512]{2,1,0:T(2,128)(2,1)S(1)}, bf16[512,2,512]{2,1,0:T(2,128)(2,1)}, u32[]{:S(2)}) copy-start(bf16[512,2,512]{2,1,0:T(2,128)(2,1)} %param.23) | copy-start | bytes 3145732
  8.8 0.7 copy-start.4
  10.0 1.6 %collective-permute-start.2 = (bf16[72,2,512]{2,1,0:T(2,128)(2,1)S(1)}, bf16[72,2,512]{2,1,0:T(2,128)(2,1)S(1)}, u32[]{:S(2)}, u32[]{:S(2)}) collective-permute-start(bf16[72,2,512]{2,1,0:T(2,128)(2,1)S(1)} %collective-permute-done.1.refs_2_), channel_id=1, source_target_pairs={{0,1},{1,0},{2,3},{3,2},{4,5},{5,4},{6,7},{7,6},{8,9},{9,8},{10,11... | collective-permute-start | bytes 442376 | tf_op jit(solution)/shard_map/ppermute | solution.py:660
  10.6 5.7 %collective-permute-start.6 = (bf16[64,2,512]{2,1,0:T(2,128)(2,1)}, bf16[64,2,512]{2,1,0:T(2,128)(2,1)S(1)}, u32[]{:S(2)}, u32[]{:S(2)}) collective-permute-start(bf16[64,2,512]{2,1,0:T(2,128)(2,1)} %refs_0_), channel_id=1, source_target_pairs={{0,2},{1,3},{2,0},{3,1},{4,6},{5,7},{6,4},{7,5},{8,10},{9,11},{10,... | collective-permute-start | bytes 393224 | tf_op jit(solution)/shard_map/ppermute | solution.py:660
  13.2 5.1 %copy-start.2 = (bf16[512,1024]{1,0:T(8,128)(2,1)S(1)}, bf16[512,1024]{1,0:T(8,128)(2,1)}, u32[]{:S(2)}) copy-start(bf16[512,1024]{1,0:T(8,128)(2,1)} %refs_4_.1) | copy-start | bytes 3145732
  13.2 3.8 %collective-permute-start.3 = (f32[1,8,512]{2,1,0:T(8,128)S(1)}, f32[1,8,512]{2,1,0:T(8,128)S(1)}, u32[]{:S(2)}, u32[]{:S(2)}) collective-permute-start(f32[1,8,512]{2,1,0:T(8,128)S(1)} %bitcast.53), channel_id=1, source_target_pairs={{0,2},{1,3},{2,0},{3,1},{4,6},{5,7},{6,4},{7,5},{8,10},{9,11},{10,... | collective-permute-start | bytes 49160 | tf_op jit(solution)/shard_map/ppermute | solution.py:660
  14.4 3.0 %collective-permute-start.5 = (bf16[64,2,512]{2,1,0:T(2,128)(2,1)S(1)}, bf16[64,2,512]{2,1,0:T(2,128)(2,1)S(1)}, u32[]{:S(2)}, u32[]{:S(2)}) collective-permute-start(bf16[64,2,512]{2,1,0:T(2,128)(2,1)S(1)} %copy-done.3), channel_id=1, source_target_pairs={{0,1},{1,0},{2,3},{3,2},{4,5},{5,4},{6,7},{7,6},{8,9},{9,8},{10,11... | collective-permute-start | bytes 393224 | tf_op jit(solution)/shard_map/ppermute | solution.py:660
  16.3 1.3 %collective-permute-start.7 = (bf16[64,2,512]{2,1,0:T(2,128)(2,1)S(1)}, bf16[64,2,512]{2,1,0:T(2,128)(2,1)S(1)}, u32[]{:S(2)}, u32[]{:S(2)}) collective-permute-start(bf16[64,2,512]{2,1,0:T(2,128)(2,1)S(1)} %collective-permute-done.6.refs_2_), channel_id=1, source_target_pairs={{0,1},{1,0},{2,3},{3,2},{4,5},{5,4},{6,7},{7,6},{8,9},{9,8},{10,11... | collective-permute-start | bytes 393224 | tf_op jit(solution)/shard_map/ppermute | solution.py:660
  17.1 1.2 %collective-permute-start.4 = (f32[2,8,512]{2,1,0:T(8,128)S(1)}, f32[2,8,512]{2,1,0:T(8,128)S(1)}, u32[]{:S(2)}, u32[]{:S(2)}) collective-permute-start(f32[2,8,512]{2,1,0:T(8,128)S(1)} %get-tuple-element.170), channel_id=1, source_target_pairs={{0,1},{1,0},{2,3},{3,2},{4,5},{5,4},{6,7},{7,6},{8,9},{9,8},{10,11... | collective-permute-start | bytes 98312 | tf_op jit(solution)/shard_map/ppermute | solution.py:660
  23.4 3.9 %collective-permute-start.8 = (bf16[4,64,1024]{2,1,0:T(8,128)(2,1)S(1)}, bf16[4,64,1024]{2,1,0:T(8,128)(2,1)S(1)}, u32[]{:S(2)}, u32[]{:S(2)}) collective-permute-start(bf16[4,64,1024]{2,1,0:T(8,128)(2,1)S(1)} %get-tuple-element.96), channel_id=1, source_target_pairs={{0,1},{1,0},{2,3},{3,2},{4,5},{5,4},{6,7},{7,6},{8,9},{9,8},{10,11... | collective-permute-start | bytes 1572872 | tf_op jit(solution)/shard_map/ppermute | solution.py:660
  25.7 1.6 %collective-permute-start.9 = (bf16[4,64,512]{2,1,0:T(8,128)(2,1)S(1)}, bf16[4,64,512]{2,1,0:T(8,128)(2,1)S(1)}, u32[]{:S(2)}, u32[]{:S(2)}) collective-permute-start(bf16[4,64,512]{2,1,0:T(8,128)(2,1)S(1)} %get-tuple-element.100), channel_id=1, source_target_pairs={{0,1},{1,0},{2,3},{3,2},{4,5},{5,4},{6,7},{7,6},{8,9},{9,8},{10,11... | collective-permute-start | bytes 786440 | tf_op jit(solution)/shard_map/ppermute | solution.py:660
  27.3 4.0 %collective-permute-start.13 = (f32[1,8,512]{2,1,0:T(8,128)S(1)}, f32[1,8,512]{2,1,0:T(8,128)S(1)}, u32[]{:S(2)}, u32[]{:S(2)}) collective-permute-start(f32[1,8,512]{2,1,0:T(8,128)S(1)} %bitcast.50), channel_id=1, source_target_pairs={{0,2},{1,3},{2,0},{3,1},{4,6},{5,7},{6,4},{7,5},{8,10},{9,11},{10,... | collective-permute-start | bytes 49160 | tf_op jit(solution)/shard_map/ppermute | solution.py:660
  28.9 9.0 %collective-permute-start.10 = (bf16[1,64,1536]{2,1,0:T(8,128)(2,1)S(1)}, bf16[1,64,1536]{2,1,0:T(8,128)(2,1)S(1)}, u32[]{:S(2)}, u32[]{:S(2)}) collective-permute-start(bf16[1,64,1536]{2,1,0:T(8,128)(2,1)S(1)} %pad_maximum_fusion.2), channel_id=1, source_target_pairs={{0,2},{1,3},{2,0},{3,1},{4,6},{5,7},{6,4},{7,5},{8,10},{9,11},{10,... | collective-permute-start | bytes 589832 | tf_op jit(solution)/shard_map/ppermute | solution.py:660
  29.8 9.8 %collective-permute-start.11 = (bf16[1,64,1536]{2,1,0:T(8,128)(2,1)S(1)}, bf16[1,64,1536]{2,1,0:T(8,128)(2,1)S(1)}, u32[]{:S(2)}, u32[]{:S(2)}) collective-permute-start(bf16[1,64,1536]{2,1,0:T(8,128)(2,1)S(1)} %pad_maximum_fusion.3), channel_id=1, source_target_pairs={{0,4},{1,5},{2,6},{3,7},{4,0},{5,1},{6,2},{7,3},{8,12},{9,13},{10,... | collective-permute-start | bytes 589832 | tf_op jit(solution)/shard_map/ppermute | solution.py:660
  31.4 2.0 %collective-permute-start.14 = (f32[2,8,512]{2,1,0:T(8,128)S(1)}, f32[2,8,512]{2,1,0:T(8,128)S(1)}, u32[]{:S(2)}, u32[]{:S(2)}) collective-permute-start(f32[2,8,512]{2,1,0:T(8,128)S(1)} %get-tuple-element.168), channel_id=1, source_target_pairs={{0,1},{1,0},{2,3},{3,2},{4,5},{5,4},{6,7},{7,6},{8,9},{9,8},{10,11... | collective-permute-start | bytes 98312 | tf_op jit(solution)/shard_map/ppermute | solution.py:660
  31.5 10.1 %collective-permute-start.12 = (bf16[1,64,1536]{2,1,0:T(8,128)(2,1)S(1)}, bf16[1,64,1536]{2,1,0:T(8,128)(2,1)S(1)}, u32[]{:S(2)}, u32[]{:S(2)}) collective-permute-start(bf16[1,64,1536]{2,1,0:T(8,128)(2,1)S(1)} %pad_maximum_fusion.4), channel_id=1, source_target_pairs={{0,6},{1,7},{2,4},{3,5},{4,2},{5,3},{6,0},{7,1},{8,14},{9,15},{10,... | collective-permute-start | bytes 589832 | tf_op jit(solution)/shard_map/ppermute | solution.py:660
  35.4 1.6 %collective-permute-start.15 = (bf16[2,128,512]{2,1,0:T(8,128)(2,1)S(1)}, bf16[2,128,512]{2,1,0:T(8,128)(2,1)S(1)}, u32[]{:S(2)}, u32[]{:S(2)}) collective-permute-start(bf16[2,128,512]{2,1,0:T(8,128)(2,1)S(1)} %get-tuple-element.117), channel_id=1, source_target_pairs={{0,1},{1,0},{2,3},{3,2},{4,5},{5,4},{6,7},{7,6},{8,9},{9,8},{10,11... | collective-permute-start | bytes 786440 | tf_op jit(solution)/shard_map/ppermute | solution.py:660
  37.0 11.8 %collective-permute-start.16 = (bf16[144,512]{1,0:T(8,128)(2,1)S(1)}, bf16[144,512]{1,0:T(8,128)(2,1)S(1)}, u32[]{:S(2)}, u32[]{:S(2)}) collective-permute-start(bf16[144,512]{1,0:T(8,128)(2,1)S(1)} %pad_maximum_fusion.6), channel_id=1, source_target_pairs={{0,2},{1,3},{2,0},{3,1},{4,6},{5,7},{6,4},{7,5},{8,10},{9,11},{10,... | collective-permute-start | bytes 442376 | tf_op jit(solution)/shard_map/ppermute | solution.py:660
  41.6 9.2 %collective-permute-start.19 = (bf16[64,1536]{1,0:T(8,128)(2,1)S(1)}, bf16[64,1536]{1,0:T(8,128)(2,1)S(1)}, u32[]{:S(2)}, u32[]{:S(2)}) collective-permute-start(bf16[64,1536]{1,0:T(8,128)(2,1)S(1)} %reduce-precision_convert_fusion.2), channel_id=1, source_target_pairs={{0,24},{1,25},{2,26},{3,27},{4,28},{5,29},{6,30},{7,31},{8,16},{9,... | collective-permute-start | bytes 589832 | tf_op jit(solution)/shard_map/ppermute | solution.py:660
  48.9 1.2 %collective-permute-start.17 = (f32[8,512]{1,0:T(8,128)S(1)}, f32[8,512]{1,0:T(8,128)S(1)}, u32[]{:S(2)}, u32[]{:S(2)}) collective-permute-start(f32[8,512]{1,0:T(8,128)S(1)} %add_add_fusion.3), channel_id=1, source_target_pairs={{0,1},{1,0},{2,3},{3,2},{4,5},{5,4},{6,7},{7,6},{8,9},{9,8},{10,11... | collective-permute-start | bytes 49160 | tf_op jit(solution)/shard_map/ppermute | solution.py:660
  50.1 6.0 %collective-permute-start.18 = (bf16[144,512]{1,0:T(8,128)(2,1)S(1)}, bf16[144,512]{1,0:T(8,128)(2,1)S(1)}, u32[]{:S(2)}, u32[]{:S(2)}) collective-permute-start(bf16[144,512]{1,0:T(8,128)(2,1)S(1)} %pad_maximum_fusion.7), channel_id=1, source_target_pairs={{0,4},{1,5},{2,6},{3,7},{4,0},{5,1},{6,2},{7,3},{8,12},{9,13},{10,... | collective-permute-start | bytes 442376 | tf_op jit(solution)/shard_map/ppermute | solution.py:660
  50.9 6.8 %collective-permute-start.21 = (bf16[64,1536]{1,0:T(8,128)(2,1)S(1)}, bf16[64,1536]{1,0:T(8,128)(2,1)S(1)}, u32[]{:S(2)}, u32[]{:S(2)}) collective-permute-start(bf16[64,1536]{1,0:T(8,128)(2,1)S(1)} %reduce-precision_convert_fusion.1), channel_id=1, source_target_pairs={{0,8},{1,9},{2,10},{3,11},{4,12},{5,13},{6,14},{7,15},{8,0},{9,1},... | collective-permute-start | bytes 589832 | tf_op jit(solution)/shard_map/ppermute | solution.py:660
  56.2 7.1 %collective-permute-start.20 = (bf16[144,512]{1,0:T(8,128)(2,1)S(1)}, bf16[144,512]{1,0:T(8,128)(2,1)S(1)}, u32[]{:S(2)}, u32[]{:S(2)}) collective-permute-start(bf16[144,512]{1,0:T(8,128)(2,1)S(1)} %pad_maximum_fusion.8), channel_id=1, source_target_pairs={{0,24},{1,25},{2,26},{3,27},{4,28},{5,29},{6,30},{7,31},{8,16},{9,... | collective-permute-start | bytes 442376 | tf_op jit(solution)/shard_map/ppermute | solution.py:660
  57.7 7.3 %collective-permute-start.23 = (bf16[64,1536]{1,0:T(8,128)(2,1)S(1)}, bf16[64,1536]{1,0:T(8,128)(2,1)S(1)}, u32[]{:S(2)}, u32[]{:S(2)}) collective-permute-start(bf16[64,1536]{1,0:T(8,128)(2,1)S(1)} %reduce-precision_convert_fusion), channel_id=1, source_target_pairs={{0,4},{1,5},{2,6},{3,7},{4,0},{5,1},{6,2},{7,3},{8,12},{9,13},{10,... | collective-permute-start | bytes 589832 | tf_op jit(solution)/shard_map/ppermute | solution.py:660
  59.2 6.6 %collective-permute-start.25 = (bf16[64,1024]{1,0:T(8,128)(2,1)S(1)}, bf16[64,1024]{1,0:T(8,128)(2,1)S(1)}, u32[]{:S(2)}, u32[]{:S(2)}) collective-permute-start(bf16[64,1024]{1,0:T(8,128)(2,1)S(1)} %get-tuple-element.159), channel_id=1, source_target_pairs={{0,2},{1,3},{2,0},{3,1},{4,6},{5,7},{6,4},{7,5},{8,10},{9,11},{10,... | collective-permute-start | bytes 393224 | tf_op jit(solution)/shard_map/ppermute | solution.py:660
  60.2 6.2 %collective-permute-start.26 = (bf16[64,1024]{1,0:T(8,128)(2,1)S(1)}, bf16[64,1024]{1,0:T(8,128)(2,1)S(1)}, u32[]{:S(2)}, u32[]{:S(2)}) collective-permute-start(bf16[64,1024]{1,0:T(8,128)(2,1)S(1)} %get-tuple-element.159), channel_id=1, source_target_pairs={{0,6},{1,7},{2,4},{3,5},{4,2},{5,3},{6,0},{7,1},{8,14},{9,15},{10,... | collective-permute-start | bytes 393224 | tf_op jit(solution)/shard_map/ppermute | solution.py:660
  61.3 3.7 %collective-permute-start.24 = (bf16[1,64,1024]{2,1,0:T(8,128)(2,1)S(1)}, bf16[1,64,1024]{2,1,0:T(8,128)(2,1)S(1)}, u32[]{:S(2)}, u32[]{:S(2)}) collective-permute-start(bf16[1,64,1024]{2,1,0:T(8,128)(2,1)S(1)} %get-tuple-element.160.refs_0_), channel_id=1, source_target_pairs={{0,1},{1,0},{2,3},{3,2},{4,5},{5,4},{6,7},{7,6},{8,9},{9,8},{10,11... | collective-permute-start | bytes 393224 | tf_op jit(solution)/shard_map/ppermute | solution.py:660
  63.3 5.2 %collective-permute-start.22 = (bf16[144,512]{1,0:T(8,128)(2,1)S(1)}, bf16[144,512]{1,0:T(8,128)(2,1)S(1)}, u32[]{:S(2)}, u32[]{:S(2)}) collective-permute-start(bf16[144,512]{1,0:T(8,128)(2,1)S(1)} %pad_maximum_fusion.9), channel_id=1, source_target_pairs={{0,8},{1,9},{2,10},{3,11},{4,12},{5,13},{6,14},{7,15},{8,0},{9,1},... | collective-permute-start | bytes 442376 | tf_op jit(solution)/shard_map/ppermute | solution.py:660
  66.4 3.0 %collective-permute-start.27 = (bf16[3,64,1024]{2,1,0:T(8,128)(2,1)S(1)}, bf16[3,64,1024]{2,1,0:T(8,128)(2,1)S(1)}, u32[]{:S(2)}, u32[]{:S(2)}) collective-permute-start(bf16[3,64,1024]{2,1,0:T(8,128)(2,1)S(1)} %pad_maximum_fusion.1.refs_1_), channel_id=1, source_target_pairs={{0,1},{1,0},{2,3},{3,2},{4,5},{5,4},{6,7},{7,6},{8,9},{9,8},{10,11... | collective-permute-start | bytes 1179656 | tf_op jit(solution)/shard_map/ppermute | solution.py:660

commit v7 on v6

--- a/solution.py
+++ b/solution.py
@@ -602,7 +602,7 @@
     join_pairs([jnp.where(first, a, b), jnp.where(first, b, a)], flat_ref, out_ref)
 
 
-def finish_kernel(total_ref, sums_ref, vec_ref, in_ref, gain_ref, bias_ref, skip_ref, rate_ref, angle_ref, level_ref, flat_ref):
+def finish(total_ref, sums_ref, vec_ref, in_ref, gain_ref, bias_ref, skip_ref, rate_ref, angle_ref, level_ref, flat_ref):
     own, _, feats = in_ref.shape
     join_pairs([total_ref[:own, :], total_ref[own:, :]], flat_ref, in_ref)
     sums = sums_ref[...]
@@ -620,8 +620,7 @@
     level_ref[...] = pick(sums[1:2, :channels])
 
 
-def place_kernel(masks, parts, *refs):
-    arrays, out_ref, wide_ref, sems = refs[: len(masks)], refs[-3], refs[-2], refs[-1]
+def start_placing(masks, parts, arrays, out_ref, wide_ref, sems):
     place = lax.axis_index("state") + parts * (lax.axis_index("seq") & 1)
     size = arrays[0].shape[1]
     copies = []
@@ -632,27 +631,61 @@
             at = pl.ds(pl.multiple_of((place ^ m) * size, size), size)
             copies.append(pltpu.make_async_copy(wide_ref.at[n], out_ref.at[at, :], sems.at[n]))
             copies[-1].start()
-    for c in copies:
+    return copies
+
+
+def place_kernel(masks, parts, *refs):
+    for c in start_placing(masks, parts, refs[: len(masks)], *refs[-3:]):
         c.wait()
 
 
-def place_blocks(arrays, masks, parts, shape, out=None):
+def place_blocks(arrays, masks, parts, shape):
     count = sum(len(m) for m in masks)
     _, size, width = arrays[0].shape
-    ins = list(arrays) + ([] if out is None else [out])
-    specs = [pl.BlockSpec(memory_space=pltpu.VMEM)] * len(arrays)
-    specs += [pl.BlockSpec(memory_space=pl.ANY)] * (len(ins) - len(arrays))
     return pl.pallas_call(
         functools.partial(place_kernel, masks, parts),
         out_shape=jax.ShapeDtypeStruct(shape, F32),
-        in_specs=specs,
+        in_specs=[pl.BlockSpec(memory_space=pltpu.VMEM)] * len(arrays),
         out_specs=pl.BlockSpec(memory_space=pl.ANY),
         scratch_shapes=[pltpu.VMEM((count, size, width), F32), pltpu.SemaphoreType.DMA((count,))],
-        input_output_aliases={} if out is None else {len(arrays): 0},
         compiler_params=pltpu.CompilerParams(vmem_limit_bytes=8 * MIB),
         cost_estimate=pl.CostEstimate(flops=MIB, bytes_accessed=2 * MIB, transcendentals=0),
         name="place",
-    )(*ins)
+    )(*arrays)
+
+
+def last_kernel(masks, parts, *refs):
+    n = len(masks)
+    out_ref, in_ref = refs[n + 4 : n + 6]
+    wide_ref, sems, flat_ref = refs[-3:]
+    copies = start_placing(masks, parts, refs[:n], out_ref, wide_ref, sems)
+    finish(*refs[n : n + 3], in_ref, *refs[n + 6 : n + 12], flat_ref)
+    for c in copies:
+        c.wait()
+
+
+def last_step(arrays, masks, parts, glu, total, sums, vec, own):
+    count = sum(len(m) for m in masks)
+    _, size, width = arrays[0].shape
+    feats = vec.shape[1]
+    shapes = [glu.shape, (own, 2, feats)] + [(1, feats)] * 3 + [(1, own)] * 3
+    spaces = [pl.ANY] + [pltpu.VMEM] * 7
+    n = len(arrays) + 3
+    return pl.pallas_call(
+        functools.partial(last_kernel, masks, parts),
+        out_shape=[jax.ShapeDtypeStruct(s, F32) for s in shapes],
+        in_specs=[pl.BlockSpec(memory_space=pltpu.VMEM)] * n + [pl.BlockSpec(memory_space=pl.ANY)],
+        out_specs=[pl.BlockSpec(memory_space=s) for s in spaces],
+        scratch_shapes=[
+            pltpu.VMEM((count, size, width), F32),
+            pltpu.SemaphoreType.DMA((count,)),
+            pltpu.VMEM((feats // 128, 2 * own, 128), F32),
+        ],
+        input_output_aliases={n: 0},
+        compiler_params=pltpu.CompilerParams(vmem_limit_bytes=8 * MIB),
+        cost_estimate=pl.CostEstimate(flops=MIB, bytes_accessed=2 * MIB, transcendentals=0),
+        name="last",
+    )(*arrays, total, sums, vec, glu)
 
 
 def exchange(x, mask):
@@ -886,7 +919,6 @@
         2 * full,
         "adjoint",
     )
-    in_parts = halve(in_parts, state_groups[0])
     d_normed, sums = call(
         normed_kernel,
         [((rows, feats), F32), ((SUB, feats), F32)],
@@ -898,7 +930,7 @@
     )
     class chain:
         parts, total, held = in_parts, None, sums
-        masks = state_bits[1:] + seq_masks[:1] + seq_masks[:0:-1]
+        masks = state_bits + seq_masks[:1] + seq_masks[:0:-1]
         sent = []
 
         def send(after=()):
@@ -909,8 +941,8 @@
                 chain.low = rounded(chain.parts[0][0]).astype(BF16)
             chain.sent.append(tie(jnp.concatenate([chain.low] + chain.two, axis=0), after))
 
-        def take():
-            got = exchange(chain.sent[-1], chain.masks[len(chain.sent) - 1])
+        def take(after=()):
+            got = tie(exchange(chain.sent[-1], chain.masks[len(chain.sent) - 1]), after)
             chain.got, rest, off = got, [], 0
             if len(chain.parts) > 1:
                 for p in chain.parts[1:]:
@@ -924,6 +956,18 @@
             chain.held = sum_of(chain.two) + sum_of([got[off : off + SUB], got[off + SUB :]])
 
     chain.send()
+    (out4,) = call(
+        out_kernel,
+        [(x4.shape, BF16)],
+        [x_rows, tie(branch, chain.sent[-1])],
+        [held(x4), pltpu.SemaphoreType.DMA((8,))],
+        8,
+        4096 * MIB,
+        "out",
+        sent=True,
+    )
+    chain.take(out4)
+    chain.send()
     for g in all_groups[1:]:
         got = swap(both, g)
         both = add_up(both, tie(got, chain.sent[-1]))
@@ -934,22 +978,11 @@
         [cot, tie(d_normed, both, chain.sent[-1]), unit, inv, vec],
         [pltpu.VMEM(cot4.shape, F32), pltpu.SemaphoreType.DMA((8,))],
         12,
-        full,
+        4096 * MIB,
         "tokens",
         sent=True,
     )
-    (out4,) = call(
-        out_kernel,
-        [(x4.shape, BF16)],
-        [x_rows, tie(branch, both, chain.sent[-1])],
-        [held(x4), pltpu.SemaphoreType.DMA((8,))],
-        8,
-        MIB,
-        "out",
-        sent=True,
-    )
     chain.take()
-    chain.held = chain.held + exchange(chain.held, state_bits[0])
     chain.send()
     glu_masks = seq_masks[:0:-1]
     for n, m in enumerate(glu_masks):
@@ -958,23 +991,13 @@
         if n:
             chain.take()
             chain.send(mine)
-        got = tie(got, chain.sent[-1], grad4, out4)
+        got = tie(got, chain.sent[-1], grad4)
         both = mine.astype(F32) + got.astype(F32)
     both = rounded(both).astype(BF16)
     while len(chain.sent) < len(chain.masks):
         chain.take()
         chain.send(both)
     chain.take()
-    last = chain.got
-    grad_in, grad_gain, grad_bias, grad_skip, grad_rate, grad_angle, grad_level = call(
-        finish_kernel,
-        [((own, 2, feats), F32)] + [((1, feats), F32)] * 3 + [((1, own), F32)] * 3,
-        [chain.parts[0][0], chain.held, vec],
-        [flat],
-        8,
-        MIB,
-        "finish",
-    )
     blocks = {0: both[:, : 2 * feats]}
     for g in reversed(all_groups[1:]):
         for m in list(blocks):
@@ -997,11 +1020,14 @@
     )
     rest = [m for m in blocks if m]
     near = [blocks[0][None], jnp.stack(tie([blocks[m] for m in rest], grad_out, chain.sent[-1]))]
-    near_masks = [[0], rest]
-    far = [f for p, o in zip(submasks(all_groups[0]), far_own) for f in (o, exchange(near[1], p))]
-    far_masks = [[m ^ p for m in ms] for p in submasks(all_groups[0]) for ms in near_masks]
-    grad_glu = place_blocks(near, near_masks, parts, (feats, 2 * feats))
-    grad_glu = place_blocks(tie(far, grad_in), far_masks, parts, (feats, 2 * feats), grad_glu)
+    outer = submasks(all_groups[0])
+    far = [exchange(near[1], p) for p in outer]
+    first_masks = [[0], rest] + [[p] for p in outer]
+    far_masks = [[m ^ p for m in rest] for p in outer]
+    grad_glu = place_blocks(near + far_own, first_masks, parts, (feats, 2 * feats))
+    grad_glu, grad_in, grad_gain, grad_bias, grad_skip, grad_rate, grad_angle, grad_level = last_step(
+        far, far_masks, parts, grad_glu, chain.parts[0][0], chain.held, vec, own
+    )
     return (
         out4.reshape(tokens.shape),
         grad4.reshape(tokens.shape),

time: 70.7 us -> 70.7 us (level)
  waiting for transfers between devices: 17.3 us -> 11.4 us
  starting transfers between devices: 24.4 us -> 30.2 us
    ppermute x28 -> x27, waiting for transfers between devices: 17.3 us -> 11.4 us  [exchange(): lax.ppermute(x, ('seq', 'state'), [(i, i ^ mask) for i in range(count)])]
    ppermute x28 -> x27, starting transfers between devices: 24.4 us -> 30.2 us  [exchange(): lax.ppermute(x, ('seq', 'state'), [(i, i ^ mask) for i in range(count)])]
    pallas_call x0 -> x1, Pallas kernels: none -> 1.65 us  [last_step(): pl.pallas_call(functools.partial(last_kernel, masks, parts), out_shape=[j...]
    pallas_call x2 -> x1, Pallas kernels: 2.03 us -> 1.11 us  [place_blocks(): pl.pallas_call(functools.partial(place_kernel, masks, parts), out_shape=j...]
    pallas_call x15 -> x14, Pallas kernels: 21 us -> 20.3 us  [call(): pl.pallas_call(body, out_shape=[jax.ShapeDtypeStruct(s, d) for s, d in ou...]
  transfers between devices with their start and end apart: 28 -> 27, of which waited for: 15 -> 13; matrix products, arithmetic and copies ran while one was open for 1% -> 1% of each run, Pallas kernels for 24% -> 23%
where the time goes in v7:
time: 70.7 us; the launch traced here: 70.5 us
  starting transfers between devices  30.2 us (43%)
  Pallas kernels  23 us (33%)
  waiting for transfers between devices  11.4 us (16%)
  local copies, waits for them, and re-layouts  2.8 us (4%)
  other arithmetic  1.94 us (3%)
  between operations  1.23 us (2%)
    ppermute x27, starting transfers between devices, exchange(): lax.ppermute(x, ('seq', 'state'), [(i, i ^ mask) for i in range(count)])  30.2 us
    pallas_call x14, Pallas kernels, call(): pl.pallas_call(body, out_shape=[jax.ShapeDtypeStruct(s, d) for s, d in ou...  20.3 us
    ppermute x27, waiting for transfers between devices, exchange(): lax.ppermute(x, ('seq', 'state'), [(i, i ^ mask) for i in range(count)])  11.4 us
    unnamed x10, local copies, waits for them, and re-layouts  1.89 us
    pallas_call x1, Pallas kernels, last_step(): pl.pallas_call(functools.partial(last_kernel, masks, parts), out_shape=[j...  1.65 us
  transfers between devices with their start and end apart: 27, of which 13 were waited for; matrix products, arithmetic and copies ran while one was open for 1% of the time, Pallas kernels for 23%

profile of v7, /device:TPU:0, one launch (start us, length us, event | category | flops | bytes accessed | tf_op | source)
XLA Modules:
  0.0 70.5 jit_solution(766064918256199275)
XLA Ops:
  0.6 0.0 copy-start.3
  0.7 0.8 %concatenate.60 = f32[1728]{0:T(1024)S(1)} concatenate(f32[512]{0:T(512)} %param.13, f32[512]{0:T(512)} %param.14, f32[512]{0:T(512)} %param.20, f32[64]{0:T(128)} %param.17, f32[64]{0:T(128)} %param.18, f32[64]{0:T(128)} %param.19), dimensions={0} | concatenate | bytes 13824 | tf_op jit(solution)/shard_map/concatenate | solution.py:805
  1.5 0.1 prep.1
  1.7 1.1 %pad_maximum_fusion.6.refs_0_ = bf16[72,2,512]{2,1,0:T(2,128)(2,1)S(1)} fusion(bf16[8,2,512]{2,1,0:T(2,128)(2,1)S(1)} %get-tuple-element.84, bf16[64,2,512]{2,1,0:T(2,128)(2,1)} %bitcast.64), kind=kLoop, calls=%fused_computation.23 | loop fusion | flops 73728 | bytes 294912 | tf_op jit(solution)/shard_map/concatenate | solution.py:816
  2.8 3.0 %collective-permute-start.1 = (bf16[72,2,512]{2,1,0:T(2,128)(2,1)S(1)}, bf16[72,2,512]{2,1,0:T(2,128)(2,1)S(1)}, u32[]{:S(2)}, u32[]{:S(2)}) collective-permute-start(bf16[72,2,512]{2,1,0:T(2,128)(2,1)S(1)} %pad_maximum_fusion.6.refs_0_), channel_id=1, source_target_pairs={{0,2},{1,3},{2,0},{3,1},{4,6},{5,7},{6,4},{7,5},{8,10},{9,11},{10,... | collective-permute-start | bytes 442376 | tf_op jit(solution)/shard_map/ppermute | solution.py:693
  5.8 0.0 collective-permute-start
  5.8 1.2 %copy-done = bf16[512,2,512]{2,1,0:T(2,128)(2,1)S(1)} copy-done((bf16[512,2,512]{2,1,0:T(2,128)(2,1)S(1)}, bf16[512,2,512]{2,1,0:T(2,128)(2,1)}, u32[]{:S(2)}) %copy-start) | copy-done | bytes 1048600
  7.0 1.8 %norm.1 = (bf16[1024,512]{1,0:T(8,128)(2,1)S(1)}, f32[1024,512]{1,0:T(8,128)S(1)}, f32[1024,128]{1,0:T(8,128)S(1)}, bf16[1024,512]{1,0:T(8,128)(2,1)S(1)}) custom-call(bf16[4,128,2,512]{3,2,1,0:T(2,128)(2,1)S(1)} %bitcast.54, f32[8,512]{1,0:T(8,128)S(1)} %get-tuple-element.80.vec_ref.refs_8_.refs_3_), custom_call_target="tpu_custom_call" | custom-call | flops 10485760 | bytes 4194304 | tf_op jit(solution)/shard_map/norm/pallas_call | solution.py:67
  8.8 0.0 copy-start.4
  8.8 0.6 copy-done.4
  9.5 0.6 limit.1.limit_ref.refs_7_
  10.0 0.6 collective-permute-start.2
  10.6 0.7 %collective-permute-start.6 = (bf16[64,2,512]{2,1,0:T(2,128)(2,1)}, bf16[64,2,512]{2,1,0:T(2,128)(2,1)S(1)}, u32[]{:S(2)}, u32[]{:S(2)}) collective-permute-start(bf16[64,2,512]{2,1,0:T(2,128)(2,1)} %refs_0_), channel_id=1, source_target_pairs={{0,2},{1,3},{2,0},{3,1},{4,6},{5,7},{6,4},{7,5},{8,10},{9,11},{10,... | collective-permute-start | bytes 393224 | tf_op jit(solution)/shard_map/ppermute | solution.py:693
  11.4 0.3 collective-permute-done.2.refs_3_
  11.6 1.6 %project.1 = (f32[1024,512]{1,0:T(8,128)S(1)}, f32[8,512]{1,0:T(8,128)S(1)}, bf16[512,512]{1,0:T(8,128)(2,1)S(1)}, f32[8,512]{1,0:T(8,128)S(1)}) custom-call(bf16[1024,512]{1,0:T(8,128)(2,1)S(1)} %get-tuple-element.82.low_ref.refs_6_, s32[8,128]{1,0:T(8,128)S(1)} %limit.1.limit_ref.refs_7_, bf16[72,2,512]{2,1,0:T(2,128)(2,1)S(1)} %pad_maximum_fusion.6.refs_0_, ...), custom_call_target="tpu_custom_call" | custom-call | flops 536870912 | bytes 4194304 | tf_op jit(solution)/shard_map/project/pallas_call | solution.py:67
  13.2 0.0 copy-start.2
  13.2 1.2 %collective-permute-start.3 = (f32[1,8,512]{2,1,0:T(8,128)S(1)}, f32[1,8,512]{2,1,0:T(8,128)S(1)}, u32[]{:S(2)}, u32[]{:S(2)}) collective-permute-start(f32[1,8,512]{2,1,0:T(8,128)S(1)} %bitcast.61), channel_id=1, source_target_pairs={{0,2},{1,3},{2,0},{3,1},{4,6},{5,7},{6,4},{7,5},{8,10},{9,11},{10,... | collective-permute-start | bytes 49160 | tf_op jit(solution)/shard_map/ppermute | solution.py:693
  14.4 1.9 %collective-permute-done.6.refs_2_ = bf16[64,2,512]{2,1,0:T(2,128)(2,1)S(1)} collective-permute-done((bf16[64,2,512]{2,1,0:T(2,128)(2,1)}, bf16[64,2,512]{2,1,0:T(2,128)(2,1)S(1)}, u32[]{:S(2)}, u32[]{:S(2)}) %collective-permute-start.6) | collective-permute-done | bytes 131104 | tf_op jit(solution)/shard_map/ppermute | solution.py:693
  16.3 0.7 %collective-permute-done.3 = f32[1,8,512]{2,1,0:T(8,128)S(1)} collective-permute-done((f32[1,8,512]{2,1,0:T(8,128)S(1)}, f32[1,8,512]{2,1,0:T(8,128)S(1)}, u32[]{:S(2)}, u32[]{:S(2)}) %collective-permute-start.3) | collective-permute-done | bytes 16416 | tf_op jit(solution)/shard_map/ppermute | solution.py:693
  17.1 0.3 cotangent.1.refs_6_.cot_ref
  17.4 0.3 collective-permute-done.7.refs_3_
  17.7 0.4 weights.1.refs_4_.cw_ref
  18.0 0.2 collective-permute-done.4
  18.3 5.1 %mix.1 = (f32[1032,512]{1,0:T(8,128)S(1)}, bf16[1024,512]{1,0:T(8,128)(2,1)S(1)}, f32[1024,512]{1,0:T(8,128)S(1)}, bf16[1024,1024]{1,0:T(8,128)(2,1)S(1)}, f32[1...) custom-call(f32[1024,512]{1,0:T(8,128)S(1)} %get-tuple-element.86.re, ...), custom_call_target="tpu_custom_call" | custom-call | flops 2684354560 | bytes 4194304 | tf_op jit(solution)/shard_map/mix/pallas_call | solution.py:67
  23.4 0.2 collective-permute-start.8
  23.6 2.1 %back.1 = (f32[1024,512]{1,0:T(8,128)S(1)}, bf16[1024,512]{1,0:T(8,128)(2,1)S(1)}, f32[8,512]{1,0:T(8,128)S(1)}, bf16[4,64,512]{2,1,0:T(8,128)(2,1)S(1)}, f32[1,...) custom-call(bf16[1024,1024]{1,0:T(8,128)(2,1)S(1)} %get-tuple-element.95, ...), custom_call_target="tpu_custom_call" | custom-call | flops 1610612736 | bytes 4194304 | tf_op jit(solution)/shard_map/back/pallas_call | solution.py:67
  25.7 0.4 collective-permute-start.9
  26.1 1.2 %starts.1 = (f32[1024,512]{1,0:T(8,128)S(1)}, f32[8,512]{1,0:T(8,128)S(1)}) custom-call(bf16[1024,512]{1,0:T(8,128)(2,1)S(1)} %get-tuple-element.98.dmix_ref, bf16[512,512]{1,0:T(8,128)(2,1)S(1)} %weights.1.refs_4_.cw_ref, f32[8,512]{1,0:T(8,128)S(1)} %get-tuple-element.88.refs_2_.cst_ref), custom_call_target="tpu_custom_call" | custom-call | flops 536870912 | bytes 4194304 | tf_op jit(solution)/shard_map/starts/pallas_call | solution.py:67
  27.4 1.2 %collective-permute-start.10 = (f32[1,8,512]{2,1,0:T(8,128)S(1)}, f32[1,8,512]{2,1,0:T(8,128)S(1)}, u32[]{:S(2)}, u32[]{:S(2)}) collective-permute-start(f32[1,8,512]{2,1,0:T(8,128)S(1)} %bitcast.58), channel_id=1, source_target_pairs={{0,2},{1,3},{2,0},{3,1},{4,6},{5,7},{6,4},{7,5},{8,10},{9,11},{10,... | collective-permute-start | bytes 49160 | tf_op jit(solution)/shard_map/ppermute | solution.py:693
  28.6 0.1 convert_add_fusion.5
  28.7 0.1 convert_add_fusion.4
  28.8 0.9 %collective-permute-start.12 = (bf16[1,64,1536]{2,1,0:T(8,128)(2,1)S(1)}, bf16[1,64,1536]{2,1,0:T(8,128)(2,1)S(1)}, u32[]{:S(2)}, u32[]{:S(2)}) collective-permute-start(bf16[1,64,1536]{2,1,0:T(8,128)(2,1)S(1)} %pad_maximum_fusion.3), channel_id=1, source_target_pairs={{0,2},{1,3},{2,0},{3,1},{4,6},{5,7},{6,4},{7,5},{8,10},{9,11},{10,... | collective-permute-start | bytes 589832 | tf_op jit(solution)/shard_map/ppermute | solution.py:693
  29.8 1.6 %collective-permute-start.13 = (bf16[1,64,1536]{2,1,0:T(8,128)(2,1)S(1)}, bf16[1,64,1536]{2,1,0:T(8,128)(2,1)S(1)}, u32[]{:S(2)}, u32[]{:S(2)}) collective-permute-start(bf16[1,64,1536]{2,1,0:T(8,128)(2,1)S(1)} %pad_maximum_fusion.4), channel_id=1, source_target_pairs={{0,4},{1,5},{2,6},{3,7},{4,0},{5,1},{6,2},{7,3},{8,12},{9,13},{10,... | collective-permute-start | bytes 589832 | tf_op jit(solution)/shard_map/ppermute | solution.py:693
  31.4 0.1 collective-permute-start.11
  31.5 2.0 %collective-permute-start.14 = (bf16[1,64,1536]{2,1,0:T(8,128)(2,1)S(1)}, bf16[1,64,1536]{2,1,0:T(8,128)(2,1)S(1)}, u32[]{:S(2)}, u32[]{:S(2)}) collective-permute-start(bf16[1,64,1536]{2,1,0:T(8,128)(2,1)S(1)} %pad_maximum_fusion.5), channel_id=1, source_target_pairs={{0,6},{1,7},{2,4},{3,5},{4,2},{5,3},{6,0},{7,1},{8,14},{9,15},{10,... | collective-permute-start | bytes 589832 | tf_op jit(solution)/shard_map/ppermute | solution.py:693
  33.5 1.9 %adjoint.1 = (bf16[1024,512]{1,0:T(8,128)(2,1)S(1)}, f32[8,768]{1,0:T(8,128)S(1)}, bf16[2,128,512]{2,1,0:T(8,128)(2,1)S(1)}, f32[1,128,512]{2,1,0:T(8,128)S(1)}, f32[1,128,512]{2,1,0:T(8,128)S(1)}) custom-call(f32[1024,512]{1,0:T(8,128)S(1)} %get-tuple-element.107.refs_0_, f32[8,512]{1,0:T(8,128)S(1)} %get-tuple-element.108.refs_1_, ...), custom_call_target="tpu_custom_call" | custom-call | flops 1073741824 | bytes 4194304 | tf_op jit(solution)/shard_map/adjoint/pallas_call | solution.py:67
  35.4 0.9 %normed.1 = (f32[1024,512]{1,0:T(8,128)S(1)}, f32[8,512]{1,0:T(8,128)S(1)}) custom-call(bf16[1024,512]{1,0:T(8,128)(2,1)S(1)} %get-tuple-element.111.dproj_ref, bf16[512,512]{1,0:T(8,128)(2,1)S(1)} %get-tuple-element.112.win_ref, f32[1024,512]{1,0:T(8,128)S(1)} %get-tuple-element.113.dpre_ref, f32[1024,512]{1,0:T(8,128)S(1)} %get-tuple-element.92.refs_5_.refs_2_.unit_ref, ...), custom_call_target="tpu_custom_call" | custom-call | flops 536870912 | bytes 4194304 | tf_op jit(solution)/shard_map/normed/pallas_call | solution.py:67
  36.3 0.3 collective-permute-start.15
  36.6 1.7 %out.1 = bf16[4,128,2,512]{3,2,1,0:T(2,128)(2,1)} custom-call(bf16[1024,512]{1,0:T(8,128)(2,1)S(1)} %get-tuple-element.81.x_ref, f32[1024,512]{1,0:T(8,128)S(1)} %get-tuple-element.117.branch_ref), custom_call_target="tpu_custom_call" | custom-call | flops 4294967296 | bytes 4194304 | tf_op jit(solution)/shard_map/out/pallas_call | solution.py:67
  38.4 0.9 %collective-permute-start.17 = (bf16[144,512]{1,0:T(8,128)(2,1)S(1)}, bf16[144,512]{1,0:T(8,128)(2,1)S(1)}, u32[]{:S(2)}, u32[]{:S(2)}) collective-permute-start(bf16[144,512]{1,0:T(8,128)(2,1)S(1)} %pad_maximum_fusion.7), channel_id=1, source_target_pairs={{0,2},{1,3},{2,0},{3,1},{4,6},{5,7},{6,4},{7,5},{8,10},{9,11},{10,... | collective-permute-start | bytes 442376 | tf_op jit(solution)/shard_map/ppermute | solution.py:693
  39.3 0.3 collective-permute-done.13
  39.6 1.3 %collective-permute-done.14 = bf16[1,64,1536]{2,1,0:T(8,128)(2,1)S(1)} collective-permute-done((bf16[1,64,1536]{2,1,0:T(8,128)(2,1)S(1)}, bf16[1,64,1536]{2,1,0:T(8,128)(2,1)S(1)}, u32[]{:S(2)}, u32[]{:S(2)}) %collective-permute-start.14) | collective-permute-done | bytes 196640 | tf_op jit(solution)/shard_map/ppermute | solution.py:693
  40.9 0.1 reduce-precision_convert_fusion.2
  41.0 3.6 %collective-permute-start.16 = (bf16[64,1536]{1,0:T(8,128)(2,1)S(1)}, bf16[64,1536]{1,0:T(8,128)(2,1)S(1)}, u32[]{:S(2)}, u32[]{:S(2)}) collective-permute-start(bf16[64,1536]{1,0:T(8,128)(2,1)S(1)} %reduce-precision_convert_fusion.2), channel_id=1, source_target_pairs={{0,24},{1,25},{2,26},{3,27},{4,28},{5,29},{6,30},{7,31},{8,16},{9,... | collective-permute-start | bytes 589832 | tf_op jit(solution)/shard_map/ppermute | solution.py:693
  44.6 1.8 %tokens.1 = f32[4,128,2,512]{3,2,1,0:T(2,128)} custom-call(bf16[1024,512]{1,0:T(8,128)(2,1)S(1)} %cotangent.1.refs_6_.cot_ref, f32[1024,512]{1,0:T(8,128)S(1)} %get-tuple-element.130.dnorm_ref, f32[1024,512]{1,0:T(8,128)S(1)} %get-tuple-element.92.refs_5_.refs_2_.unit_ref, f32[1024,128]{1,0:T(8,128)S(1)} %get-tuple-element.131.inv_ref, ...), custom_call_target="tpu_custom_call" | custom-call | flops 4294967296 | bytes 4194304 | tf_op jit(solution)/shard_map/tokens/pallas_call | solution.py:67
  46.4 0.1 fusion.4
  46.5 1.3 %collective-permute-start.19 = (bf16[144,512]{1,0:T(8,128)(2,1)S(1)}, bf16[144,512]{1,0:T(8,128)(2,1)S(1)}, u32[]{:S(2)}, u32[]{:S(2)}) collective-permute-start(bf16[144,512]{1,0:T(8,128)(2,1)S(1)} %pad_maximum_fusion.8), channel_id=1, source_target_pairs={{0,4},{1,5},{2,6},{3,7},{4,0},{5,1},{6,2},{7,3},{8,12},{9,13},{10,... | collective-permute-start | bytes 442376 | tf_op jit(solution)/shard_map/ppermute | solution.py:693
  47.8 1.0 %collective-permute-done.16 = bf16[64,1536]{1,0:T(8,128)(2,1)S(1)} collective-permute-done((bf16[64,1536]{1,0:T(8,128)(2,1)S(1)}, bf16[64,1536]{1,0:T(8,128)(2,1)S(1)}, u32[]{:S(2)}, u32[]{:S(2)}) %collective-permute-start.16) | collective-permute-done | bytes 196640 | tf_op jit(solution)/shard_map/ppermute | solution.py:693
  48.9 0.1 reduce-precision_convert_fusion.1
  48.9 3.9 %collective-permute-start.18 = (bf16[64,1536]{1,0:T(8,128)(2,1)S(1)}, bf16[64,1536]{1,0:T(8,128)(2,1)S(1)}, u32[]{:S(2)}, u32[]{:S(2)}) collective-permute-start(bf16[64,1536]{1,0:T(8,128)(2,1)S(1)} %reduce-precision_convert_fusion.1), channel_id=1, source_target_pairs={{0,8},{1,9},{2,10},{3,11},{4,12},{5,13},{6,14},{7,15},{8,0},{9,1},... | collective-permute-start | bytes 589832 | tf_op jit(solution)/shard_map/ppermute | solution.py:693
  52.9 2.5 %collective-permute-start.24 = (bf16[144,512]{1,0:T(8,128)(2,1)S(1)}, bf16[144,512]{1,0:T(8,128)(2,1)S(1)}, u32[]{:S(2)}, u32[]{:S(2)}) collective-permute-start(bf16[144,512]{1,0:T(8,128)(2,1)S(1)} %pad_maximum_fusion.9), channel_id=1, source_target_pairs={{0,24},{1,25},{2,26},{3,27},{4,28},{5,29},{6,30},{7,31},{8,16},{9,... | collective-permute-start | bytes 442376 | tf_op jit(solution)/shard_map/ppermute | solution.py:693
  55.4 2.9 %collective-permute-done.18 = bf16[64,1536]{1,0:T(8,128)(2,1)S(1)} collective-permute-done((bf16[64,1536]{1,0:T(8,128)(2,1)S(1)}, bf16[64,1536]{1,0:T(8,128)(2,1)S(1)}, u32[]{:S(2)}, u32[]{:S(2)}) %collective-permute-start.18) | collective-permute-done | bytes 196640 | tf_op jit(solution)/shard_map/ppermute | solution.py:693
  58.4 1.4 %collective-permute-start.21 = (bf16[64,1536]{1,0:T(8,128)(2,1)S(1)}, bf16[64,1536]{1,0:T(8,128)(2,1)S(1)}, u32[]{:S(2)}, u32[]{:S(2)}) collective-permute-start(bf16[64,1536]{1,0:T(8,128)(2,1)S(1)} %reduce-precision_convert_fusion), channel_id=1, source_target_pairs={{0,4},{1,5},{2,6},{3,7},{4,0},{5,1},{6,2},{7,3},{8,12},{9,13},{10,... | collective-permute-start | bytes 589832 | tf_op jit(solution)/shard_map/ppermute | solution.py:693
  59.9 1.0 %collective-permute-start.22 = (bf16[64,1024]{1,0:T(8,128)(2,1)S(1)}, bf16[64,1024]{1,0:T(8,128)(2,1)S(1)}, u32[]{:S(2)}, u32[]{:S(2)}) collective-permute-start(bf16[64,1024]{1,0:T(8,128)(2,1)S(1)} %get-tuple-element.162), channel_id=1, source_target_pairs={{0,6},{1,7},{2,4},{3,5},{4,2},{5,3},{6,0},{7,1},{8,14},{9,15},{10,... | collective-permute-start | bytes 393224 | tf_op jit(solution)/shard_map/ppermute | solution.py:693
  60.9 1.2 %collective-permute-start.20 = (bf16[64,1024]{1,0:T(8,128)(2,1)S(1)}, bf16[64,1024]{1,0:T(8,128)(2,1)S(1)}, u32[]{:S(2)}, u32[]{:S(2)}) collective-permute-start(bf16[64,1024]{1,0:T(8,128)(2,1)S(1)} %get-tuple-element.162), channel_id=1, source_target_pairs={{0,2},{1,3},{2,0},{3,1},{4,6},{5,7},{6,4},{7,5},{8,10},{9,11},{10,... | collective-permute-start | bytes 393224 | tf_op jit(solution)/shard_map/ppermute | solution.py:693
  62.1 2.0 %collective-permute-start.26 = (bf16[144,512]{1,0:T(8,128)(2,1)S(1)}, bf16[144,512]{1,0:T(8,128)(2,1)S(1)}, u32[]{:S(2)}, u32[]{:S(2)}) collective-permute-start(bf16[144,512]{1,0:T(8,128)(2,1)S(1)} %pad_maximum_fusion.10), channel_id=1, source_target_pairs={{0,8},{1,9},{2,10},{3,11},{4,12},{5,13},{6,14},{7,15},{8,0},{9,1},... | collective-permute-start | bytes 442376 | tf_op jit(solution)/shard_map/ppermute | solution.py:693
  64.2 0.3 collective-permute-done.21
  64.5 0.8 %halves.1 = f32[64,2,512]{2,1,0:T(2,128)} custom-call(bf16[64,512]{1,0:T(8,128)(2,1)S(1)} %slice.120.mine_ref, bf16[64,512]{1,0:T(8,128)(2,1)S(1)} %slice.121.other_ref), custom_call_target="tpu_custom_call" | custom-call | flops 1048576 | bytes 4194304 | tf_op jit(solution)/shard_map/halves/pallas_call | solution.py:67
  65.3 0.5 collective-permute-done.22
  65.8 0.6 collective-permute-done.20
  66.5 0.1 collective-permute-start.25
  66.6 1.1 %place.1.refs_4_ = f32[512,1024]{1,0:T(8,128)} custom-call(bf16[1,64,1024]{2,1,0:T(8,128)(2,1)S(1)} %get-tuple-element.161.refs_0_, bf16[3,64,1024]{2,1,0:T(8,128)(2,1)S(1)} %pad_maximum_fusion.1.refs_1_, bf16[1,64,1024]{2,1,0:T(8,128)(2,1)S(1)} %collective-permute-done.23.refs_2_), custom_call_target="tpu_custom_call" | custom-call | flops 1048576 | bytes 2097152 | tf_op jit(solution)/shard_map/place/pallas_call | solution.py:645
  67.7 1.0 %collective-permute-done.26 = bf16[144,512]{1,0:T(8,128)(2,1)S(1)} collective-permute-done((bf16[144,512]{1,0:T(8,128)(2,1)S(1)}, bf16[144,512]{1,0:T(8,128)(2,1)S(1)}, u32[]{:S(2)}, u32[]{:S(2)}) %collective-permute-start.26) | collective-permute-done | bytes 147488 | tf_op jit(solution)/shard_map/ppermute | solution.py:693
  68.7 1.6 %last.1 = (f32[512,1024]{1,0:T(8,128)}, f32[64,2,512]{2,1,0:T(2,128)}, f32[1,512]{1,0:T(1,128)}, f32[1,512]{1,0:T(1,128)}, f32[1,512]{1,0:T(1,128)}, /*index=5*/...) custom-call(bf16[3,64,1024]{2,1,0:T(8,128)(2,1)S(1)} %collective-permute-done.25.refs_0_, ...), custom_call_target="tpu_custom_call", output_to_operand_aliasing={{0}: (4, {})} | custom-call | flops 1048576 | bytes 2097152 | tf_op jit(solution)/shard_map/last/pallas_call | solution.py:674
  (54 shorter events, 0.5 us)
Async XLA Ops:
  0.6 13.8 %copy-start.3 = (bf16[64,2,512]{2,1,0:T(2,128)(2,1)S(1)}, bf16[64,2,512]{2,1,0:T(2,128)(2,1)}, u32[]{:S(2)}) copy-start(bf16[64,2,512]{2,1,0:T(2,128)(2,1)} %refs_0_) | copy-start | bytes 393220
  2.8 7.3 %collective-permute-start.1 = (bf16[72,2,512]{2,1,0:T(2,128)(2,1)S(1)}, bf16[72,2,512]{2,1,0:T(2,128)(2,1)S(1)}, u32[]{:S(2)}, u32[]{:S(2)}) collective-permute-start(bf16[72,2,512]{2,1,0:T(2,128)(2,1)S(1)} %pad_maximum_fusion.6.refs_0_), channel_id=1, source_target_pairs={{0,2},{1,3},{2,0},{3,1},{4,6},{5,7},{6,4},{7,5},{8,10},{9,11},{10,... | collective-permute-start | bytes 442376 | tf_op jit(solution)/shard_map/ppermute | solution.py:693
  5.8 5.6 %collective-permute-start = (bf16[72,2,512]{2,1,0:T(2,128)(2,1)S(1)}, bf16[72,2,512]{2,1,0:T(2,128)(2,1)S(1)}, u32[]{:S(2)}, u32[]{:S(2)}) collective-permute-start(bf16[72,2,512]{2,1,0:T(2,128)(2,1)S(1)} %pad_maximum_fusion.6.refs_0_), channel_id=1, source_target_pairs={{0,1},{1,0},{2,3},{3,2},{4,5},{5,4},{6,7},{7,6},{8,9},{9,8},{10,11... | collective-permute-start | bytes 442376 | tf_op jit(solution)/shard_map/ppermute | solution.py:693
  5.8 1.2 %copy-start = (bf16[512,2,512]{2,1,0:T(2,128)(2,1)S(1)}, bf16[512,2,512]{2,1,0:T(2,128)(2,1)}, u32[]{:S(2)}) copy-start(bf16[512,2,512]{2,1,0:T(2,128)(2,1)} %param.12) | copy-start | bytes 3145732
  7.0 10.1 %copy-start.1 = (bf16[512,2,512]{2,1,0:T(2,128)(2,1)S(1)}, bf16[512,2,512]{2,1,0:T(2,128)(2,1)}, u32[]{:S(2)}) copy-start(bf16[512,2,512]{2,1,0:T(2,128)(2,1)} %param.23) | copy-start | bytes 3145732
  8.8 0.7 copy-start.4
  10.0 1.6 %collective-permute-start.2 = (bf16[72,2,512]{2,1,0:T(2,128)(2,1)S(1)}, bf16[72,2,512]{2,1,0:T(2,128)(2,1)S(1)}, u32[]{:S(2)}, u32[]{:S(2)}) collective-permute-start(bf16[72,2,512]{2,1,0:T(2,128)(2,1)S(1)} %collective-permute-done.1.refs_2_), channel_id=1, source_target_pairs={{0,1},{1,0},{2,3},{3,2},{4,5},{5,4},{6,7},{7,6},{8,9},{9,8},{10,11... | collective-permute-start | bytes 442376 | tf_op jit(solution)/shard_map/ppermute | solution.py:693
  10.6 5.7 %collective-permute-start.6 = (bf16[64,2,512]{2,1,0:T(2,128)(2,1)}, bf16[64,2,512]{2,1,0:T(2,128)(2,1)S(1)}, u32[]{:S(2)}, u32[]{:S(2)}) collective-permute-start(bf16[64,2,512]{2,1,0:T(2,128)(2,1)} %refs_0_), channel_id=1, source_target_pairs={{0,2},{1,3},{2,0},{3,1},{4,6},{5,7},{6,4},{7,5},{8,10},{9,11},{10,... | collective-permute-start | bytes 393224 | tf_op jit(solution)/shard_map/ppermute | solution.py:693
  13.2 5.1 %copy-start.2 = (bf16[512,1024]{1,0:T(8,128)(2,1)S(1)}, bf16[512,1024]{1,0:T(8,128)(2,1)}, u32[]{:S(2)}) copy-start(bf16[512,1024]{1,0:T(8,128)(2,1)} %refs_4_.1) | copy-start | bytes 3145732
  13.2 3.8 %collective-permute-start.3 = (f32[1,8,512]{2,1,0:T(8,128)S(1)}, f32[1,8,512]{2,1,0:T(8,128)S(1)}, u32[]{:S(2)}, u32[]{:S(2)}) collective-permute-start(f32[1,8,512]{2,1,0:T(8,128)S(1)} %bitcast.61), channel_id=1, source_target_pairs={{0,2},{1,3},{2,0},{3,1},{4,6},{5,7},{6,4},{7,5},{8,10},{9,11},{10,... | collective-permute-start | bytes 49160 | tf_op jit(solution)/shard_map/ppermute | solution.py:693
  14.4 3.0 %collective-permute-start.5 = (bf16[64,2,512]{2,1,0:T(2,128)(2,1)S(1)}, bf16[64,2,512]{2,1,0:T(2,128)(2,1)S(1)}, u32[]{:S(2)}, u32[]{:S(2)}) collective-permute-start(bf16[64,2,512]{2,1,0:T(2,128)(2,1)S(1)} %copy-done.3), channel_id=1, source_target_pairs={{0,1},{1,0},{2,3},{3,2},{4,5},{5,4},{6,7},{7,6},{8,9},{9,8},{10,11... | collective-permute-start | bytes 393224 | tf_op jit(solution)/shard_map/ppermute | solution.py:693
  16.3 1.3 %collective-permute-start.7 = (bf16[64,2,512]{2,1,0:T(2,128)(2,1)S(1)}, bf16[64,2,512]{2,1,0:T(2,128)(2,1)S(1)}, u32[]{:S(2)}, u32[]{:S(2)}) collective-permute-start(bf16[64,2,512]{2,1,0:T(2,128)(2,1)S(1)} %collective-permute-done.6.refs_2_), channel_id=1, source_target_pairs={{0,1},{1,0},{2,3},{3,2},{4,5},{5,4},{6,7},{7,6},{8,9},{9,8},{10,11... | collective-permute-start | bytes 393224 | tf_op jit(solution)/shard_map/ppermute | solution.py:693
  17.1 1.2 %collective-permute-start.4 = (f32[2,8,512]{2,1,0:T(8,128)S(1)}, f32[2,8,512]{2,1,0:T(8,128)S(1)}, u32[]{:S(2)}, u32[]{:S(2)}) collective-permute-start(f32[2,8,512]{2,1,0:T(8,128)S(1)} %get-tuple-element.172), channel_id=1, source_target_pairs={{0,1},{1,0},{2,3},{3,2},{4,5},{5,4},{6,7},{7,6},{8,9},{9,8},{10,11... | collective-permute-start | bytes 98312 | tf_op jit(solution)/shard_map/ppermute | solution.py:693
  23.4 3.9 %collective-permute-start.8 = (bf16[4,64,1024]{2,1,0:T(8,128)(2,1)S(1)}, bf16[4,64,1024]{2,1,0:T(8,128)(2,1)S(1)}, u32[]{:S(2)}, u32[]{:S(2)}) collective-permute-start(bf16[4,64,1024]{2,1,0:T(8,128)(2,1)S(1)} %get-tuple-element.101), channel_id=1, source_target_pairs={{0,1},{1,0},{2,3},{3,2},{4,5},{5,4},{6,7},{7,6},{8,9},{9,8},{10,11... | collective-permute-start | bytes 1572872 | tf_op jit(solution)/shard_map/ppermute | solution.py:693
  25.7 1.6 %collective-permute-start.9 = (bf16[4,64,512]{2,1,0:T(8,128)(2,1)S(1)}, bf16[4,64,512]{2,1,0:T(8,128)(2,1)S(1)}, u32[]{:S(2)}, u32[]{:S(2)}) collective-permute-start(bf16[4,64,512]{2,1,0:T(8,128)(2,1)S(1)} %get-tuple-element.102), channel_id=1, source_target_pairs={{0,1},{1,0},{2,3},{3,2},{4,5},{5,4},{6,7},{7,6},{8,9},{9,8},{10,11... | collective-permute-start | bytes 786440 | tf_op jit(solution)/shard_map/ppermute | solution.py:693
  27.4 4.0 %collective-permute-start.10 = (f32[1,8,512]{2,1,0:T(8,128)S(1)}, f32[1,8,512]{2,1,0:T(8,128)S(1)}, u32[]{:S(2)}, u32[]{:S(2)}) collective-permute-start(f32[1,8,512]{2,1,0:T(8,128)S(1)} %bitcast.58), channel_id=1, source_target_pairs={{0,2},{1,3},{2,0},{3,1},{4,6},{5,7},{6,4},{7,5},{8,10},{9,11},{10,... | collective-permute-start | bytes 49160 | tf_op jit(solution)/shard_map/ppermute | solution.py:693
  28.8 10.5 %collective-permute-start.12 = (bf16[1,64,1536]{2,1,0:T(8,128)(2,1)S(1)}, bf16[1,64,1536]{2,1,0:T(8,128)(2,1)S(1)}, u32[]{:S(2)}, u32[]{:S(2)}) collective-permute-start(bf16[1,64,1536]{2,1,0:T(8,128)(2,1)S(1)} %pad_maximum_fusion.3), channel_id=1, source_target_pairs={{0,2},{1,3},{2,0},{3,1},{4,6},{5,7},{6,4},{7,5},{8,10},{9,11},{10,... | collective-permute-start | bytes 589832 | tf_op jit(solution)/shard_map/ppermute | solution.py:693
  29.8 9.8 %collective-permute-start.13 = (bf16[1,64,1536]{2,1,0:T(8,128)(2,1)S(1)}, bf16[1,64,1536]{2,1,0:T(8,128)(2,1)S(1)}, u32[]{:S(2)}, u32[]{:S(2)}) collective-permute-start(bf16[1,64,1536]{2,1,0:T(8,128)(2,1)S(1)} %pad_maximum_fusion.4), channel_id=1, source_target_pairs={{0,4},{1,5},{2,6},{3,7},{4,0},{5,1},{6,2},{7,3},{8,12},{9,13},{10,... | collective-permute-start | bytes 589832 | tf_op jit(solution)/shard_map/ppermute | solution.py:693
  31.4 2.1 %collective-permute-start.11 = (f32[2,8,512]{2,1,0:T(8,128)S(1)}, f32[2,8,512]{2,1,0:T(8,128)S(1)}, u32[]{:S(2)}, u32[]{:S(2)}) collective-permute-start(f32[2,8,512]{2,1,0:T(8,128)S(1)} %get-tuple-element.170), channel_id=1, source_target_pairs={{0,1},{1,0},{2,3},{3,2},{4,5},{5,4},{6,7},{7,6},{8,9},{9,8},{10,11... | collective-permute-start | bytes 98312 | tf_op jit(solution)/shard_map/ppermute | solution.py:693
  31.5 9.4 %collective-permute-start.14 = (bf16[1,64,1536]{2,1,0:T(8,128)(2,1)S(1)}, bf16[1,64,1536]{2,1,0:T(8,128)(2,1)S(1)}, u32[]{:S(2)}, u32[]{:S(2)}) collective-permute-start(bf16[1,64,1536]{2,1,0:T(8,128)(2,1)S(1)} %pad_maximum_fusion.5), channel_id=1, source_target_pairs={{0,6},{1,7},{2,4},{3,5},{4,2},{5,3},{6,0},{7,1},{8,14},{9,15},{10,... | collective-permute-start | bytes 589832 | tf_op jit(solution)/shard_map/ppermute | solution.py:693
  36.3 2.0 %collective-permute-start.15 = (bf16[272,512]{1,0:T(8,128)(2,1)S(1)}, bf16[272,512]{1,0:T(8,128)(2,1)S(1)}, u32[]{:S(2)}, u32[]{:S(2)}) collective-permute-start(bf16[272,512]{1,0:T(8,128)(2,1)S(1)} %pad_maximum_fusion.2), channel_id=1, source_target_pairs={{0,1},{1,0},{2,3},{3,2},{4,5},{5,4},{6,7},{7,6},{8,9},{9,8},{10,11... | collective-permute-start | bytes 835592 | tf_op jit(solution)/shard_map/ppermute | solution.py:693
  38.4 8.0 %collective-permute-start.17 = (bf16[144,512]{1,0:T(8,128)(2,1)S(1)}, bf16[144,512]{1,0:T(8,128)(2,1)S(1)}, u32[]{:S(2)}, u32[]{:S(2)}) collective-permute-start(bf16[144,512]{1,0:T(8,128)(2,1)S(1)} %pad_maximum_fusion.7), channel_id=1, source_target_pairs={{0,2},{1,3},{2,0},{3,1},{4,6},{5,7},{6,4},{7,5},{8,10},{9,11},{10,... | collective-permute-start | bytes 442376 | tf_op jit(solution)/shard_map/ppermute | solution.py:693
  41.0 7.9 %collective-permute-start.16 = (bf16[64,1536]{1,0:T(8,128)(2,1)S(1)}, bf16[64,1536]{1,0:T(8,128)(2,1)S(1)}, u32[]{:S(2)}, u32[]{:S(2)}) collective-permute-start(bf16[64,1536]{1,0:T(8,128)(2,1)S(1)} %reduce-precision_convert_fusion.2), channel_id=1, source_target_pairs={{0,24},{1,25},{2,26},{3,27},{4,28},{5,29},{6,30},{7,31},{8,16},{9,... | collective-permute-start | bytes 589832 | tf_op jit(solution)/shard_map/ppermute | solution.py:693
  46.5 6.3 %collective-permute-start.19 = (bf16[144,512]{1,0:T(8,128)(2,1)S(1)}, bf16[144,512]{1,0:T(8,128)(2,1)S(1)}, u32[]{:S(2)}, u32[]{:S(2)}) collective-permute-start(bf16[144,512]{1,0:T(8,128)(2,1)S(1)} %pad_maximum_fusion.8), channel_id=1, source_target_pairs={{0,4},{1,5},{2,6},{3,7},{4,0},{5,1},{6,2},{7,3},{8,12},{9,13},{10,... | collective-permute-start | bytes 442376 | tf_op jit(solution)/shard_map/ppermute | solution.py:693
  48.9 9.4 %collective-permute-start.18 = (bf16[64,1536]{1,0:T(8,128)(2,1)S(1)}, bf16[64,1536]{1,0:T(8,128)(2,1)S(1)}, u32[]{:S(2)}, u32[]{:S(2)}) collective-permute-start(bf16[64,1536]{1,0:T(8,128)(2,1)S(1)} %reduce-precision_convert_fusion.1), channel_id=1, source_target_pairs={{0,8},{1,9},{2,10},{3,11},{4,12},{5,13},{6,14},{7,15},{8,0},{9,1},... | collective-permute-start | bytes 589832 | tf_op jit(solution)/shard_map/ppermute | solution.py:693
  52.9 9.2 %collective-permute-start.24 = (bf16[144,512]{1,0:T(8,128)(2,1)S(1)}, bf16[144,512]{1,0:T(8,128)(2,1)S(1)}, u32[]{:S(2)}, u32[]{:S(2)}) collective-permute-start(bf16[144,512]{1,0:T(8,128)(2,1)S(1)} %pad_maximum_fusion.9), channel_id=1, source_target_pairs={{0,24},{1,25},{2,26},{3,27},{4,28},{5,29},{6,30},{7,31},{8,16},{9,... | collective-permute-start | bytes 442376 | tf_op jit(solution)/shard_map/ppermute | solution.py:693
  58.4 6.1 %collective-permute-start.21 = (bf16[64,1536]{1,0:T(8,128)(2,1)S(1)}, bf16[64,1536]{1,0:T(8,128)(2,1)S(1)}, u32[]{:S(2)}, u32[]{:S(2)}) collective-permute-start(bf16[64,1536]{1,0:T(8,128)(2,1)S(1)} %reduce-precision_convert_fusion), channel_id=1, source_target_pairs={{0,4},{1,5},{2,6},{3,7},{4,0},{5,1},{6,2},{7,3},{8,12},{9,13},{10,... | collective-permute-start | bytes 589832 | tf_op jit(solution)/shard_map/ppermute | solution.py:693
  59.9 5.9 %collective-permute-start.22 = (bf16[64,1024]{1,0:T(8,128)(2,1)S(1)}, bf16[64,1024]{1,0:T(8,128)(2,1)S(1)}, u32[]{:S(2)}, u32[]{:S(2)}) collective-permute-start(bf16[64,1024]{1,0:T(8,128)(2,1)S(1)} %get-tuple-element.162), channel_id=1, source_target_pairs={{0,6},{1,7},{2,4},{3,5},{4,2},{5,3},{6,0},{7,1},{8,14},{9,15},{10,... | collective-permute-start | bytes 393224 | tf_op jit(solution)/shard_map/ppermute | solution.py:693
  60.9 5.6 %collective-permute-start.20 = (bf16[64,1024]{1,0:T(8,128)(2,1)S(1)}, bf16[64,1024]{1,0:T(8,128)(2,1)S(1)}, u32[]{:S(2)}, u32[]{:S(2)}) collective-permute-start(bf16[64,1024]{1,0:T(8,128)(2,1)S(1)} %get-tuple-element.162), channel_id=1, source_target_pairs={{0,2},{1,3},{2,0},{3,1},{4,6},{5,7},{6,4},{7,5},{8,10},{9,11},{10,... | collective-permute-start | bytes 393224 | tf_op jit(solution)/shard_map/ppermute | solution.py:693
  62.1 2.4 %collective-permute-start.23 = (bf16[1,64,1024]{2,1,0:T(8,128)(2,1)S(1)}, bf16[1,64,1024]{2,1,0:T(8,128)(2,1)S(1)}, u32[]{:S(2)}, u32[]{:S(2)}) collective-permute-start(bf16[1,64,1024]{2,1,0:T(8,128)(2,1)S(1)} %get-tuple-element.161.refs_0_), channel_id=1, source_target_pairs={{0,1},{1,0},{2,3},{3,2},{4,5},{5,4},{6,7},{7,6},{8,9},{9,8},{10,11... | collective-permute-start | bytes 393224 | tf_op jit(solution)/shard_map/ppermute | solution.py:693
  62.1 6.5 %collective-permute-start.26 = (bf16[144,512]{1,0:T(8,128)(2,1)S(1)}, bf16[144,512]{1,0:T(8,128)(2,1)S(1)}, u32[]{:S(2)}, u32[]{:S(2)}) collective-permute-start(bf16[144,512]{1,0:T(8,128)(2,1)S(1)} %pad_maximum_fusion.10), channel_id=1, source_target_pairs={{0,8},{1,9},{2,10},{3,11},{4,12},{5,13},{6,14},{7,15},{8,0},{9,1},... | collective-permute-start | bytes 442376 | tf_op jit(solution)/shard_map/ppermute | solution.py:693
  66.5 2.2 %collective-permute-start.25 = (bf16[3,64,1024]{2,1,0:T(8,128)(2,1)S(1)}, bf16[3,64,1024]{2,1,0:T(8,128)(2,1)S(1)}, u32[]{:S(2)}, u32[]{:S(2)}) collective-permute-start(bf16[3,64,1024]{2,1,0:T(8,128)(2,1)S(1)} %pad_maximum_fusion.1.refs_1_), channel_id=1, source_target_pairs={{0,1},{1,0},{2,3},{3,2},{4,5},{5,4},{6,7},{7,6},{8,9},{9,8},{10,11... | collective-permute-start | bytes 1179656 | tf_op jit(solution)/shard_map/ppermute | solution.py:693

commit v8 on v7

--- a/solution.py
+++ b/solution.py
@@ -930,7 +930,7 @@
     )
     class chain:
         parts, total, held = in_parts, None, sums
-        masks = state_bits + seq_masks[:1] + seq_masks[:0:-1]
+        masks = state_bits + seq_masks
         sent = []
 
         def send(after=()):
@@ -984,7 +984,7 @@
     )
     chain.take()
     chain.send()
-    glu_masks = seq_masks[:0:-1]
+    glu_masks = seq_masks[1:]
     for n, m in enumerate(glu_masks):
         mine = rounded(both).astype(BF16)
         got = exchange(mine, m)

time: 70.7 us -> 70.1 us (level)
  starting transfers between devices: 30.2 us -> 27.5 us
  waiting for transfers between devices: 11.4 us -> 13.4 us
    ppermute x27, starting transfers between devices: 30.2 us -> 27.5 us  [exchange(): lax.ppermute(x, ('seq', 'state'), [(i, i ^ mask) for i in range(count)])]
    ppermute x27, waiting for transfers between devices: 11.4 us -> 13.4 us  [exchange(): lax.ppermute(x, ('seq', 'state'), [(i, i ^ mask) for i in range(count)])]
  transfers between devices with their start and end apart: 27 -> 27, of which waited for: 13 -> 12; matrix products, arithmetic and copies ran while one was open for 1% -> 1% of each run, Pallas kernels for 23% -> 23%
where the time goes in v8:
time: 70.1 us; the launch traced here: 69.8 us
  starting transfers between devices  27.5 us (39%)
  Pallas kernels  23 us (33%)
  waiting for transfers between devices  13.4 us (19%)
  local copies, waits for them, and re-layouts  2.8 us (4%)
  other arithmetic  1.94 us (3%)
  between operations  1.23 us (2%)
    ppermute x27, starting transfers between devices, exchange(): lax.ppermute(x, ('seq', 'state'), [(i, i ^ mask) for i in range(count)])  27.5 us
    pallas_call x14, Pallas kernels, call(): pl.pallas_call(body, out_shape=[jax.ShapeDtypeStruct(s, d) for s, d in ou...  20.3 us
    ppermute x27, waiting for transfers between devices, exchange(): lax.ppermute(x, ('seq', 'state'), [(i, i ^ mask) for i in range(count)])  13.4 us
    unnamed x10, local copies, waits for them, and re-layouts  1.89 us
    pallas_call x1, Pallas kernels, last_step(): pl.pallas_call(functools.partial(last_kernel, masks, parts), out_shape=[j...  1.65 us
  transfers between devices with their start and end apart: 27, of which 12 were waited for; matrix products, arithmetic and copies ran while one was open for 1% of the time, Pallas kernels for 23%

profile of v8, /device:TPU:0, one launch (start us, length us, event | category | flops | bytes accessed | tf_op | source)
XLA Modules:
  0.0 69.8 jit_solution(15906343580039842910)
XLA Ops:
  0.6 0.0 copy-start.3
  0.7 0.8 %concatenate.60 = f32[1728]{0:T(1024)S(1)} concatenate(f32[512]{0:T(512)} %param.13, f32[512]{0:T(512)} %param.14, f32[512]{0:T(512)} %param.20, f32[64]{0:T(128)} %param.17, f32[64]{0:T(128)} %param.18, f32[64]{0:T(128)} %param.19), dimensions={0} | concatenate | bytes 13824 | tf_op jit(solution)/shard_map/concatenate | solution.py:805
  1.5 0.1 prep.1
  1.7 1.1 %pad_maximum_fusion.6.refs_0_ = bf16[72,2,512]{2,1,0:T(2,128)(2,1)S(1)} fusion(bf16[8,2,512]{2,1,0:T(2,128)(2,1)S(1)} %get-tuple-element.84, bf16[64,2,512]{2,1,0:T(2,128)(2,1)} %bitcast.64), kind=kLoop, calls=%fused_computation.23 | loop fusion | flops 73728 | bytes 294912 | tf_op jit(solution)/shard_map/concatenate | solution.py:816
  2.8 3.0 %collective-permute-start.1 = (bf16[72,2,512]{2,1,0:T(2,128)(2,1)S(1)}, bf16[72,2,512]{2,1,0:T(2,128)(2,1)S(1)}, u32[]{:S(2)}, u32[]{:S(2)}) collective-permute-start(bf16[72,2,512]{2,1,0:T(2,128)(2,1)S(1)} %pad_maximum_fusion.6.refs_0_), channel_id=1, source_target_pairs={{0,2},{1,3},{2,0},{3,1},{4,6},{5,7},{6,4},{7,5},{8,10},{9,11},{10,... | collective-permute-start | bytes 442376 | tf_op jit(solution)/shard_map/ppermute | solution.py:693
  5.8 0.0 collective-permute-start
  5.8 1.2 %copy-done = bf16[512,2,512]{2,1,0:T(2,128)(2,1)S(1)} copy-done((bf16[512,2,512]{2,1,0:T(2,128)(2,1)S(1)}, bf16[512,2,512]{2,1,0:T(2,128)(2,1)}, u32[]{:S(2)}) %copy-start) | copy-done | bytes 1048600
  7.0 1.8 %norm.1 = (bf16[1024,512]{1,0:T(8,128)(2,1)S(1)}, f32[1024,512]{1,0:T(8,128)S(1)}, f32[1024,128]{1,0:T(8,128)S(1)}, bf16[1024,512]{1,0:T(8,128)(2,1)S(1)}) custom-call(bf16[4,128,2,512]{3,2,1,0:T(2,128)(2,1)S(1)} %bitcast.54, f32[8,512]{1,0:T(8,128)S(1)} %get-tuple-element.80.vec_ref.refs_8_.refs_3_), custom_call_target="tpu_custom_call" | custom-call | flops 10485760 | bytes 4194304 | tf_op jit(solution)/shard_map/norm/pallas_call | solution.py:67
  8.8 0.0 copy-start.4
  8.8 0.6 copy-done.4
  9.5 0.6 limit.1.limit_ref.refs_7_
  10.0 0.6 collective-permute-start.2
  10.6 0.7 %collective-permute-start.6 = (bf16[64,2,512]{2,1,0:T(2,128)(2,1)}, bf16[64,2,512]{2,1,0:T(2,128)(2,1)S(1)}, u32[]{:S(2)}, u32[]{:S(2)}) collective-permute-start(bf16[64,2,512]{2,1,0:T(2,128)(2,1)} %refs_0_), channel_id=1, source_target_pairs={{0,2},{1,3},{2,0},{3,1},{4,6},{5,7},{6,4},{7,5},{8,10},{9,11},{10,... | collective-permute-start | bytes 393224 | tf_op jit(solution)/shard_map/ppermute | solution.py:693
  11.4 0.3 collective-permute-done.2.refs_3_
  11.6 1.6 %project.1 = (f32[1024,512]{1,0:T(8,128)S(1)}, f32[8,512]{1,0:T(8,128)S(1)}, bf16[512,512]{1,0:T(8,128)(2,1)S(1)}, f32[8,512]{1,0:T(8,128)S(1)}) custom-call(bf16[1024,512]{1,0:T(8,128)(2,1)S(1)} %get-tuple-element.82.low_ref.refs_6_, s32[8,128]{1,0:T(8,128)S(1)} %limit.1.limit_ref.refs_7_, bf16[72,2,512]{2,1,0:T(2,128)(2,1)S(1)} %pad_maximum_fusion.6.refs_0_, ...), custom_call_target="tpu_custom_call" | custom-call | flops 536870912 | bytes 4194304 | tf_op jit(solution)/shard_map/project/pallas_call | solution.py:67
  13.2 0.0 copy-start.2
  13.2 1.2 %collective-permute-start.3 = (f32[1,8,512]{2,1,0:T(8,128)S(1)}, f32[1,8,512]{2,1,0:T(8,128)S(1)}, u32[]{:S(2)}, u32[]{:S(2)}) collective-permute-start(f32[1,8,512]{2,1,0:T(8,128)S(1)} %bitcast.61), channel_id=1, source_target_pairs={{0,2},{1,3},{2,0},{3,1},{4,6},{5,7},{6,4},{7,5},{8,10},{9,11},{10,... | collective-permute-start | bytes 49160 | tf_op jit(solution)/shard_map/ppermute | solution.py:693
  14.4 0.0 collective-permute-start.5
  14.4 1.9 %collective-permute-done.6.refs_2_ = bf16[64,2,512]{2,1,0:T(2,128)(2,1)S(1)} collective-permute-done((bf16[64,2,512]{2,1,0:T(2,128)(2,1)}, bf16[64,2,512]{2,1,0:T(2,128)(2,1)S(1)}, u32[]{:S(2)}, u32[]{:S(2)}) %collective-permute-start.6) | collective-permute-done | bytes 131104 | tf_op jit(solution)/shard_map/ppermute | solution.py:693
  16.3 0.7 %collective-permute-done.3 = f32[1,8,512]{2,1,0:T(8,128)S(1)} collective-permute-done((f32[1,8,512]{2,1,0:T(8,128)S(1)}, f32[1,8,512]{2,1,0:T(8,128)S(1)}, u32[]{:S(2)}, u32[]{:S(2)}) %collective-permute-start.3) | collective-permute-done | bytes 16416 | tf_op jit(solution)/shard_map/ppermute | solution.py:693
  17.1 0.0 collective-permute-start.4
  17.1 0.3 cotangent.1.refs_6_.cot_ref
  17.4 0.3 collective-permute-done.7.refs_3_
  17.7 0.4 weights.1.refs_4_.cw_ref
  18.0 0.2 collective-permute-done.4
  18.3 5.1 %mix.1 = (f32[1032,512]{1,0:T(8,128)S(1)}, bf16[1024,512]{1,0:T(8,128)(2,1)S(1)}, f32[1024,512]{1,0:T(8,128)S(1)}, bf16[1024,1024]{1,0:T(8,128)(2,1)S(1)}, f32[1...) custom-call(f32[1024,512]{1,0:T(8,128)S(1)} %get-tuple-element.86.re, ...), custom_call_target="tpu_custom_call" | custom-call | flops 2684354560 | bytes 4194304 | tf_op jit(solution)/shard_map/mix/pallas_call | solution.py:67
  23.4 0.2 collective-permute-start.8
  23.6 2.1 %back.1 = (f32[1024,512]{1,0:T(8,128)S(1)}, bf16[1024,512]{1,0:T(8,128)(2,1)S(1)}, f32[8,512]{1,0:T(8,128)S(1)}, bf16[4,64,512]{2,1,0:T(8,128)(2,1)S(1)}, f32[1,...) custom-call(bf16[1024,1024]{1,0:T(8,128)(2,1)S(1)} %get-tuple-element.95, ...), custom_call_target="tpu_custom_call" | custom-call | flops 1610612736 | bytes 4194304 | tf_op jit(solution)/shard_map/back/pallas_call | solution.py:67
  25.7 0.4 collective-permute-start.9
  26.1 1.2 %starts.1 = (f32[1024,512]{1,0:T(8,128)S(1)}, f32[8,512]{1,0:T(8,128)S(1)}) custom-call(bf16[1024,512]{1,0:T(8,128)(2,1)S(1)} %get-tuple-element.98.dmix_ref, bf16[512,512]{1,0:T(8,128)(2,1)S(1)} %weights.1.refs_4_.cw_ref, f32[8,512]{1,0:T(8,128)S(1)} %get-tuple-element.88.refs_2_.cst_ref), custom_call_target="tpu_custom_call" | custom-call | flops 536870912 | bytes 4194304 | tf_op jit(solution)/shard_map/starts/pallas_call | solution.py:67
  27.4 1.2 %collective-permute-start.10 = (f32[1,8,512]{2,1,0:T(8,128)S(1)}, f32[1,8,512]{2,1,0:T(8,128)S(1)}, u32[]{:S(2)}, u32[]{:S(2)}) collective-permute-start(f32[1,8,512]{2,1,0:T(8,128)S(1)} %bitcast.58), channel_id=1, source_target_pairs={{0,2},{1,3},{2,0},{3,1},{4,6},{5,7},{6,4},{7,5},{8,10},{9,11},{10,... | collective-permute-start | bytes 49160 | tf_op jit(solution)/shard_map/ppermute | solution.py:693
  28.6 0.1 convert_add_fusion.5
  28.7 0.1 convert_add_fusion.4
  28.8 0.9 %collective-permute-start.12 = (bf16[1,64,1536]{2,1,0:T(8,128)(2,1)S(1)}, bf16[1,64,1536]{2,1,0:T(8,128)(2,1)S(1)}, u32[]{:S(2)}, u32[]{:S(2)}) collective-permute-start(bf16[1,64,1536]{2,1,0:T(8,128)(2,1)S(1)} %pad_maximum_fusion.3), channel_id=1, source_target_pairs={{0,2},{1,3},{2,0},{3,1},{4,6},{5,7},{6,4},{7,5},{8,10},{9,11},{10,... | collective-permute-start | bytes 589832 | tf_op jit(solution)/shard_map/ppermute | solution.py:693
  29.8 1.6 %collective-permute-start.13 = (bf16[1,64,1536]{2,1,0:T(8,128)(2,1)S(1)}, bf16[1,64,1536]{2,1,0:T(8,128)(2,1)S(1)}, u32[]{:S(2)}, u32[]{:S(2)}) collective-permute-start(bf16[1,64,1536]{2,1,0:T(8,128)(2,1)S(1)} %pad_maximum_fusion.4), channel_id=1, source_target_pairs={{0,4},{1,5},{2,6},{3,7},{4,0},{5,1},{6,2},{7,3},{8,12},{9,13},{10,... | collective-permute-start | bytes 589832 | tf_op jit(solution)/shard_map/ppermute | solution.py:693
  31.4 0.1 collective-permute-start.11
  31.5 2.0 %collective-permute-start.14 = (bf16[1,64,1536]{2,1,0:T(8,128)(2,1)S(1)}, bf16[1,64,1536]{2,1,0:T(8,128)(2,1)S(1)}, u32[]{:S(2)}, u32[]{:S(2)}) collective-permute-start(bf16[1,64,1536]{2,1,0:T(8,128)(2,1)S(1)} %pad_maximum_fusion.5), channel_id=1, source_target_pairs={{0,6},{1,7},{2,4},{3,5},{4,2},{5,3},{6,0},{7,1},{8,14},{9,15},{10,... | collective-permute-start | bytes 589832 | tf_op jit(solution)/shard_map/ppermute | solution.py:693
  33.5 1.9 %adjoint.1 = (bf16[1024,512]{1,0:T(8,128)(2,1)S(1)}, f32[8,768]{1,0:T(8,128)S(1)}, bf16[2,128,512]{2,1,0:T(8,128)(2,1)S(1)}, f32[1,128,512]{2,1,0:T(8,128)S(1)}, f32[1,128,512]{2,1,0:T(8,128)S(1)}) custom-call(f32[1024,512]{1,0:T(8,128)S(1)} %get-tuple-element.107.refs_0_, f32[8,512]{1,0:T(8,128)S(1)} %get-tuple-element.108.refs_1_, ...), custom_call_target="tpu_custom_call" | custom-call | flops 1073741824 | bytes 4194304 | tf_op jit(solution)/shard_map/adjoint/pallas_call | solution.py:67
  35.4 0.9 %normed.1 = (f32[1024,512]{1,0:T(8,128)S(1)}, f32[8,512]{1,0:T(8,128)S(1)}) custom-call(bf16[1024,512]{1,0:T(8,128)(2,1)S(1)} %get-tuple-element.111.dproj_ref, bf16[512,512]{1,0:T(8,128)(2,1)S(1)} %get-tuple-element.112.win_ref, f32[1024,512]{1,0:T(8,128)S(1)} %get-tuple-element.113.dpre_ref, f32[1024,512]{1,0:T(8,128)S(1)} %get-tuple-element.92.refs_5_.refs_2_.unit_ref, ...), custom_call_target="tpu_custom_call" | custom-call | flops 536870912 | bytes 4194304 | tf_op jit(solution)/shard_map/normed/pallas_call | solution.py:67
  36.3 0.3 collective-permute-start.15
  36.6 1.7 %out.1 = bf16[4,128,2,512]{3,2,1,0:T(2,128)(2,1)} custom-call(bf16[1024,512]{1,0:T(8,128)(2,1)S(1)} %get-tuple-element.81.x_ref, f32[1024,512]{1,0:T(8,128)S(1)} %get-tuple-element.117.branch_ref), custom_call_target="tpu_custom_call" | custom-call | flops 4294967296 | bytes 4194304 | tf_op jit(solution)/shard_map/out/pallas_call | solution.py:67
  38.4 0.9 %collective-permute-start.17 = (bf16[144,512]{1,0:T(8,128)(2,1)S(1)}, bf16[144,512]{1,0:T(8,128)(2,1)S(1)}, u32[]{:S(2)}, u32[]{:S(2)}) collective-permute-start(bf16[144,512]{1,0:T(8,128)(2,1)S(1)} %pad_maximum_fusion.7), channel_id=1, source_target_pairs={{0,2},{1,3},{2,0},{3,1},{4,6},{5,7},{6,4},{7,5},{8,10},{9,11},{10,... | collective-permute-start | bytes 442376 | tf_op jit(solution)/shard_map/ppermute | solution.py:693
  39.3 0.3 collective-permute-done.13
  39.6 1.3 %collective-permute-done.14 = bf16[1,64,1536]{2,1,0:T(8,128)(2,1)S(1)} collective-permute-done((bf16[1,64,1536]{2,1,0:T(8,128)(2,1)S(1)}, bf16[1,64,1536]{2,1,0:T(8,128)(2,1)S(1)}, u32[]{:S(2)}, u32[]{:S(2)}) %collective-permute-start.14) | collective-permute-done | bytes 196640 | tf_op jit(solution)/shard_map/ppermute | solution.py:693
  40.9 0.1 reduce-precision_convert_fusion.2
  41.0 1.6 %collective-permute-start.16 = (bf16[64,1536]{1,0:T(8,128)(2,1)S(1)}, bf16[64,1536]{1,0:T(8,128)(2,1)S(1)}, u32[]{:S(2)}, u32[]{:S(2)}) collective-permute-start(bf16[64,1536]{1,0:T(8,128)(2,1)S(1)} %reduce-precision_convert_fusion.2), channel_id=1, source_target_pairs={{0,8},{1,9},{2,10},{3,11},{4,12},{5,13},{6,14},{7,15},{8,0},{9,1},... | collective-permute-start | bytes 589832 | tf_op jit(solution)/shard_map/ppermute | solution.py:693
  42.6 1.8 %tokens.1 = f32[4,128,2,512]{3,2,1,0:T(2,128)} custom-call(bf16[1024,512]{1,0:T(8,128)(2,1)S(1)} %cotangent.1.refs_6_.cot_ref, f32[1024,512]{1,0:T(8,128)S(1)} %get-tuple-element.130.dnorm_ref, f32[1024,512]{1,0:T(8,128)S(1)} %get-tuple-element.92.refs_5_.refs_2_.unit_ref, f32[1024,128]{1,0:T(8,128)S(1)} %get-tuple-element.131.inv_ref, ...), custom_call_target="tpu_custom_call" | custom-call | flops 4294967296 | bytes 4194304 | tf_op jit(solution)/shard_map/tokens/pallas_call | solution.py:67
  44.4 0.1 collective-permute-done.17
  44.6 1.2 %collective-permute-start.19 = (bf16[144,512]{1,0:T(8,128)(2,1)S(1)}, bf16[144,512]{1,0:T(8,128)(2,1)S(1)}, u32[]{:S(2)}, u32[]{:S(2)}) collective-permute-start(bf16[144,512]{1,0:T(8,128)(2,1)S(1)} %pad_maximum_fusion.8), channel_id=1, source_target_pairs={{0,4},{1,5},{2,6},{3,7},{4,0},{5,1},{6,2},{7,3},{8,12},{9,13},{10,... | collective-permute-start | bytes 442376 | tf_op jit(solution)/shard_map/ppermute | solution.py:693
  45.8 1.1 %collective-permute-done.16 = bf16[64,1536]{1,0:T(8,128)(2,1)S(1)} collective-permute-done((bf16[64,1536]{1,0:T(8,128)(2,1)S(1)}, bf16[64,1536]{1,0:T(8,128)(2,1)S(1)}, u32[]{:S(2)}, u32[]{:S(2)}) %collective-permute-start.16) | collective-permute-done | bytes 196640 | tf_op jit(solution)/shard_map/ppermute | solution.py:693
  46.9 0.1 reduce-precision_convert_fusion.1
  47.0 3.6 %collective-permute-start.18 = (bf16[64,1536]{1,0:T(8,128)(2,1)S(1)}, bf16[64,1536]{1,0:T(8,128)(2,1)S(1)}, u32[]{:S(2)}, u32[]{:S(2)}) collective-permute-start(bf16[64,1536]{1,0:T(8,128)(2,1)S(1)} %reduce-precision_convert_fusion.1), channel_id=1, source_target_pairs={{0,24},{1,25},{2,26},{3,27},{4,28},{5,29},{6,30},{7,31},{8,16},{9,... | collective-permute-start | bytes 589832 | tf_op jit(solution)/shard_map/ppermute | solution.py:693
  50.7 0.9 %collective-permute-start.24 = (bf16[144,512]{1,0:T(8,128)(2,1)S(1)}, bf16[144,512]{1,0:T(8,128)(2,1)S(1)}, u32[]{:S(2)}, u32[]{:S(2)}) collective-permute-start(bf16[144,512]{1,0:T(8,128)(2,1)S(1)} %pad_maximum_fusion.9), channel_id=1, source_target_pairs={{0,8},{1,9},{2,10},{3,11},{4,12},{5,13},{6,14},{7,15},{8,0},{9,1},... | collective-permute-start | bytes 442376 | tf_op jit(solution)/shard_map/ppermute | solution.py:693
  51.6 4.4 %collective-permute-done.18 = bf16[64,1536]{1,0:T(8,128)(2,1)S(1)} collective-permute-done((bf16[64,1536]{1,0:T(8,128)(2,1)S(1)}, bf16[64,1536]{1,0:T(8,128)(2,1)S(1)}, u32[]{:S(2)}, u32[]{:S(2)}) %collective-permute-start.18) | collective-permute-done | bytes 196640 | tf_op jit(solution)/shard_map/ppermute | solution.py:693
  56.0 1.5 %collective-permute-start.21 = (bf16[64,1536]{1,0:T(8,128)(2,1)S(1)}, bf16[64,1536]{1,0:T(8,128)(2,1)S(1)}, u32[]{:S(2)}, u32[]{:S(2)}) collective-permute-start(bf16[64,1536]{1,0:T(8,128)(2,1)S(1)} %reduce-precision_convert_fusion), channel_id=1, source_target_pairs={{0,4},{1,5},{2,6},{3,7},{4,0},{5,1},{6,2},{7,3},{8,12},{9,13},{10,... | collective-permute-start | bytes 589832 | tf_op jit(solution)/shard_map/ppermute | solution.py:693
  57.5 1.4 %collective-permute-start.22 = (bf16[64,1024]{1,0:T(8,128)(2,1)S(1)}, bf16[64,1024]{1,0:T(8,128)(2,1)S(1)}, u32[]{:S(2)}, u32[]{:S(2)}) collective-permute-start(bf16[64,1024]{1,0:T(8,128)(2,1)S(1)} %get-tuple-element.162), channel_id=1, source_target_pairs={{0,6},{1,7},{2,4},{3,5},{4,2},{5,3},{6,0},{7,1},{8,14},{9,15},{10,... | collective-permute-start | bytes 393224 | tf_op jit(solution)/shard_map/ppermute | solution.py:693
  58.9 0.7 %collective-permute-start.20 = (bf16[64,1024]{1,0:T(8,128)(2,1)S(1)}, bf16[64,1024]{1,0:T(8,128)(2,1)S(1)}, u32[]{:S(2)}, u32[]{:S(2)}) collective-permute-start(bf16[64,1024]{1,0:T(8,128)(2,1)S(1)} %get-tuple-element.162), channel_id=1, source_target_pairs={{0,2},{1,3},{2,0},{3,1},{4,6},{5,7},{6,4},{7,5},{8,10},{9,11},{10,... | collective-permute-start | bytes 393224 | tf_op jit(solution)/shard_map/ppermute | solution.py:693
  59.7 3.3 %collective-permute-start.26 = (bf16[144,512]{1,0:T(8,128)(2,1)S(1)}, bf16[144,512]{1,0:T(8,128)(2,1)S(1)}, u32[]{:S(2)}, u32[]{:S(2)}) collective-permute-start(bf16[144,512]{1,0:T(8,128)(2,1)S(1)} %pad_maximum_fusion.10), channel_id=1, source_target_pairs={{0,24},{1,25},{2,26},{3,27},{4,28},{5,29},{6,30},{7,31},{8,16},{9,... | collective-permute-start | bytes 442376 | tf_op jit(solution)/shard_map/ppermute | solution.py:693
  63.1 0.8 %halves.1 = f32[64,2,512]{2,1,0:T(2,128)} custom-call(bf16[64,512]{1,0:T(8,128)(2,1)S(1)} %slice.120.mine_ref, bf16[64,512]{1,0:T(8,128)(2,1)S(1)} %slice.121.other_ref), custom_call_target="tpu_custom_call" | custom-call | flops 1048576 | bytes 4194304 | tf_op jit(solution)/shard_map/halves/pallas_call | solution.py:67
  63.9 0.2 collective-permute-done.20
  64.1 0.1 collective-permute-start.25
  64.2 1.1 %place.1.refs_4_ = f32[512,1024]{1,0:T(8,128)} custom-call(bf16[1,64,1024]{2,1,0:T(8,128)(2,1)S(1)} %get-tuple-element.161.refs_0_, bf16[3,64,1024]{2,1,0:T(8,128)(2,1)S(1)} %pad_maximum_fusion.1.refs_1_, bf16[1,64,1024]{2,1,0:T(8,128)(2,1)S(1)} %collective-permute-done.23.refs_2_), custom_call_target="tpu_custom_call" | custom-call | flops 1048576 | bytes 2097152 | tf_op jit(solution)/shard_map/place/pallas_call | solution.py:645
  65.3 2.6 %collective-permute-done.26 = bf16[144,512]{1,0:T(8,128)(2,1)S(1)} collective-permute-done((bf16[144,512]{1,0:T(8,128)(2,1)S(1)}, bf16[144,512]{1,0:T(8,128)(2,1)S(1)}, u32[]{:S(2)}, u32[]{:S(2)}) %collective-permute-start.26) | collective-permute-done | bytes 147488 | tf_op jit(solution)/shard_map/ppermute | solution.py:693
  68.0 1.6 %last.1 = (f32[512,1024]{1,0:T(8,128)}, f32[64,2,512]{2,1,0:T(2,128)}, f32[1,512]{1,0:T(1,128)}, f32[1,512]{1,0:T(1,128)}, f32[1,512]{1,0:T(1,128)}, /*index=5*/...) custom-call(bf16[3,64,1024]{2,1,0:T(8,128)(2,1)S(1)} %collective-permute-done.25.refs_0_, ...), custom_call_target="tpu_custom_call", output_to_operand_aliasing={{0}: (4, {})} | custom-call | flops 1048576 | bytes 2097152 | tf_op jit(solution)/shard_map/last/pallas_call | solution.py:674
  (54 shorter events, 0.6 us)
Async XLA Ops:
  0.6 13.8 %copy-start.3 = (bf16[64,2,512]{2,1,0:T(2,128)(2,1)S(1)}, bf16[64,2,512]{2,1,0:T(2,128)(2,1)}, u32[]{:S(2)}) copy-start(bf16[64,2,512]{2,1,0:T(2,128)(2,1)} %refs_0_) | copy-start | bytes 393220
  2.8 7.3 %collective-permute-start.1 = (bf16[72,2,512]{2,1,0:T(2,128)(2,1)S(1)}, bf16[72,2,512]{2,1,0:T(2,128)(2,1)S(1)}, u32[]{:S(2)}, u32[]{:S(2)}) collective-permute-start(bf16[72,2,512]{2,1,0:T(2,128)(2,1)S(1)} %pad_maximum_fusion.6.refs_0_), channel_id=1, source_target_pairs={{0,2},{1,3},{2,0},{3,1},{4,6},{5,7},{6,4},{7,5},{8,10},{9,11},{10,... | collective-permute-start | bytes 442376 | tf_op jit(solution)/shard_map/ppermute | solution.py:693
  5.8 5.6 %collective-permute-start = (bf16[72,2,512]{2,1,0:T(2,128)(2,1)S(1)}, bf16[72,2,512]{2,1,0:T(2,128)(2,1)S(1)}, u32[]{:S(2)}, u32[]{:S(2)}) collective-permute-start(bf16[72,2,512]{2,1,0:T(2,128)(2,1)S(1)} %pad_maximum_fusion.6.refs_0_), channel_id=1, source_target_pairs={{0,1},{1,0},{2,3},{3,2},{4,5},{5,4},{6,7},{7,6},{8,9},{9,8},{10,11... | collective-permute-start | bytes 442376 | tf_op jit(solution)/shard_map/ppermute | solution.py:693
  5.8 1.2 %copy-start = (bf16[512,2,512]{2,1,0:T(2,128)(2,1)S(1)}, bf16[512,2,512]{2,1,0:T(2,128)(2,1)}, u32[]{:S(2)}) copy-start(bf16[512,2,512]{2,1,0:T(2,128)(2,1)} %param.12) | copy-start | bytes 3145732
  7.0 10.1 %copy-start.1 = (bf16[512,2,512]{2,1,0:T(2,128)(2,1)S(1)}, bf16[512,2,512]{2,1,0:T(2,128)(2,1)}, u32[]{:S(2)}) copy-start(bf16[512,2,512]{2,1,0:T(2,128)(2,1)} %param.23) | copy-start | bytes 3145732
  8.8 0.7 copy-start.4
  10.0 1.6 %collective-permute-start.2 = (bf16[72,2,512]{2,1,0:T(2,128)(2,1)S(1)}, bf16[72,2,512]{2,1,0:T(2,128)(2,1)S(1)}, u32[]{:S(2)}, u32[]{:S(2)}) collective-permute-start(bf16[72,2,512]{2,1,0:T(2,128)(2,1)S(1)} %collective-permute-done.1.refs_2_), channel_id=1, source_target_pairs={{0,1},{1,0},{2,3},{3,2},{4,5},{5,4},{6,7},{7,6},{8,9},{9,8},{10,11... | collective-permute-start | bytes 442376 | tf_op jit(solution)/shard_map/ppermute | solution.py:693
  10.6 5.7 %collective-permute-start.6 = (bf16[64,2,512]{2,1,0:T(2,128)(2,1)}, bf16[64,2,512]{2,1,0:T(2,128)(2,1)S(1)}, u32[]{:S(2)}, u32[]{:S(2)}) collective-permute-start(bf16[64,2,512]{2,1,0:T(2,128)(2,1)} %refs_0_), channel_id=1, source_target_pairs={{0,2},{1,3},{2,0},{3,1},{4,6},{5,7},{6,4},{7,5},{8,10},{9,11},{10,... | collective-permute-start | bytes 393224 | tf_op jit(solution)/shard_map/ppermute | solution.py:693
  13.2 5.1 %copy-start.2 = (bf16[512,1024]{1,0:T(8,128)(2,1)S(1)}, bf16[512,1024]{1,0:T(8,128)(2,1)}, u32[]{:S(2)}) copy-start(bf16[512,1024]{1,0:T(8,128)(2,1)} %refs_4_.1) | copy-start | bytes 3145732
  13.2 3.8 %collective-permute-start.3 = (f32[1,8,512]{2,1,0:T(8,128)S(1)}, f32[1,8,512]{2,1,0:T(8,128)S(1)}, u32[]{:S(2)}, u32[]{:S(2)}) collective-permute-start(f32[1,8,512]{2,1,0:T(8,128)S(1)} %bitcast.61), channel_id=1, source_target_pairs={{0,2},{1,3},{2,0},{3,1},{4,6},{5,7},{6,4},{7,5},{8,10},{9,11},{10,... | collective-permute-start | bytes 49160 | tf_op jit(solution)/shard_map/ppermute | solution.py:693
  14.4 3.0 %collective-permute-start.5 = (bf16[64,2,512]{2,1,0:T(2,128)(2,1)S(1)}, bf16[64,2,512]{2,1,0:T(2,128)(2,1)S(1)}, u32[]{:S(2)}, u32[]{:S(2)}) collective-permute-start(bf16[64,2,512]{2,1,0:T(2,128)(2,1)S(1)} %copy-done.3), channel_id=1, source_target_pairs={{0,1},{1,0},{2,3},{3,2},{4,5},{5,4},{6,7},{7,6},{8,9},{9,8},{10,11... | collective-permute-start | bytes 393224 | tf_op jit(solution)/shard_map/ppermute | solution.py:693
  16.3 1.3 %collective-permute-start.7 = (bf16[64,2,512]{2,1,0:T(2,128)(2,1)S(1)}, bf16[64,2,512]{2,1,0:T(2,128)(2,1)S(1)}, u32[]{:S(2)}, u32[]{:S(2)}) collective-permute-start(bf16[64,2,512]{2,1,0:T(2,128)(2,1)S(1)} %collective-permute-done.6.refs_2_), channel_id=1, source_target_pairs={{0,1},{1,0},{2,3},{3,2},{4,5},{5,4},{6,7},{7,6},{8,9},{9,8},{10,11... | collective-permute-start | bytes 393224 | tf_op jit(solution)/shard_map/ppermute | solution.py:693
  17.1 1.2 %collective-permute-start.4 = (f32[2,8,512]{2,1,0:T(8,128)S(1)}, f32[2,8,512]{2,1,0:T(8,128)S(1)}, u32[]{:S(2)}, u32[]{:S(2)}) collective-permute-start(f32[2,8,512]{2,1,0:T(8,128)S(1)} %get-tuple-element.172), channel_id=1, source_target_pairs={{0,1},{1,0},{2,3},{3,2},{4,5},{5,4},{6,7},{7,6},{8,9},{9,8},{10,11... | collective-permute-start | bytes 98312 | tf_op jit(solution)/shard_map/ppermute | solution.py:693
  23.4 3.9 %collective-permute-start.8 = (bf16[4,64,1024]{2,1,0:T(8,128)(2,1)S(1)}, bf16[4,64,1024]{2,1,0:T(8,128)(2,1)S(1)}, u32[]{:S(2)}, u32[]{:S(2)}) collective-permute-start(bf16[4,64,1024]{2,1,0:T(8,128)(2,1)S(1)} %get-tuple-element.101), channel_id=1, source_target_pairs={{0,1},{1,0},{2,3},{3,2},{4,5},{5,4},{6,7},{7,6},{8,9},{9,8},{10,11... | collective-permute-start | bytes 1572872 | tf_op jit(solution)/shard_map/ppermute | solution.py:693
  25.7 1.6 %collective-permute-start.9 = (bf16[4,64,512]{2,1,0:T(8,128)(2,1)S(1)}, bf16[4,64,512]{2,1,0:T(8,128)(2,1)S(1)}, u32[]{:S(2)}, u32[]{:S(2)}) collective-permute-start(bf16[4,64,512]{2,1,0:T(8,128)(2,1)S(1)} %get-tuple-element.102), channel_id=1, source_target_pairs={{0,1},{1,0},{2,3},{3,2},{4,5},{5,4},{6,7},{7,6},{8,9},{9,8},{10,11... | collective-permute-start | bytes 786440 | tf_op jit(solution)/shard_map/ppermute | solution.py:693
  27.4 4.0 %collective-permute-start.10 = (f32[1,8,512]{2,1,0:T(8,128)S(1)}, f32[1,8,512]{2,1,0:T(8,128)S(1)}, u32[]{:S(2)}, u32[]{:S(2)}) collective-permute-start(f32[1,8,512]{2,1,0:T(8,128)S(1)} %bitcast.58), channel_id=1, source_target_pairs={{0,2},{1,3},{2,0},{3,1},{4,6},{5,7},{6,4},{7,5},{8,10},{9,11},{10,... | collective-permute-start | bytes 49160 | tf_op jit(solution)/shard_map/ppermute | solution.py:693
  28.8 10.5 %collective-permute-start.12 = (bf16[1,64,1536]{2,1,0:T(8,128)(2,1)S(1)}, bf16[1,64,1536]{2,1,0:T(8,128)(2,1)S(1)}, u32[]{:S(2)}, u32[]{:S(2)}) collective-permute-start(bf16[1,64,1536]{2,1,0:T(8,128)(2,1)S(1)} %pad_maximum_fusion.3), channel_id=1, source_target_pairs={{0,2},{1,3},{2,0},{3,1},{4,6},{5,7},{6,4},{7,5},{8,10},{9,11},{10,... | collective-permute-start | bytes 589832 | tf_op jit(solution)/shard_map/ppermute | solution.py:693
  29.8 9.8 %collective-permute-start.13 = (bf16[1,64,1536]{2,1,0:T(8,128)(2,1)S(1)}, bf16[1,64,1536]{2,1,0:T(8,128)(2,1)S(1)}, u32[]{:S(2)}, u32[]{:S(2)}) collective-permute-start(bf16[1,64,1536]{2,1,0:T(8,128)(2,1)S(1)} %pad_maximum_fusion.4), channel_id=1, source_target_pairs={{0,4},{1,5},{2,6},{3,7},{4,0},{5,1},{6,2},{7,3},{8,12},{9,13},{10,... | collective-permute-start | bytes 589832 | tf_op jit(solution)/shard_map/ppermute | solution.py:693
  31.4 2.1 %collective-permute-start.11 = (f32[2,8,512]{2,1,0:T(8,128)S(1)}, f32[2,8,512]{2,1,0:T(8,128)S(1)}, u32[]{:S(2)}, u32[]{:S(2)}) collective-permute-start(f32[2,8,512]{2,1,0:T(8,128)S(1)} %get-tuple-element.170), channel_id=1, source_target_pairs={{0,1},{1,0},{2,3},{3,2},{4,5},{5,4},{6,7},{7,6},{8,9},{9,8},{10,11... | collective-permute-start | bytes 98312 | tf_op jit(solution)/shard_map/ppermute | solution.py:693
  31.5 9.4 %collective-permute-start.14 = (bf16[1,64,1536]{2,1,0:T(8,128)(2,1)S(1)}, bf16[1,64,1536]{2,1,0:T(8,128)(2,1)S(1)}, u32[]{:S(2)}, u32[]{:S(2)}) collective-permute-start(bf16[1,64,1536]{2,1,0:T(8,128)(2,1)S(1)} %pad_maximum_fusion.5), channel_id=1, source_target_pairs={{0,6},{1,7},{2,4},{3,5},{4,2},{5,3},{6,0},{7,1},{8,14},{9,15},{10,... | collective-permute-start | bytes 589832 | tf_op jit(solution)/shard_map/ppermute | solution.py:693
  36.3 2.0 %collective-permute-start.15 = (bf16[272,512]{1,0:T(8,128)(2,1)S(1)}, bf16[272,512]{1,0:T(8,128)(2,1)S(1)}, u32[]{:S(2)}, u32[]{:S(2)}) collective-permute-start(bf16[272,512]{1,0:T(8,128)(2,1)S(1)} %pad_maximum_fusion.2), channel_id=1, source_target_pairs={{0,1},{1,0},{2,3},{3,2},{4,5},{5,4},{6,7},{7,6},{8,9},{9,8},{10,11... | collective-permute-start | bytes 835592 | tf_op jit(solution)/shard_map/ppermute | solution.py:693
  38.4 6.1 %collective-permute-start.17 = (bf16[144,512]{1,0:T(8,128)(2,1)S(1)}, bf16[144,512]{1,0:T(8,128)(2,1)S(1)}, u32[]{:S(2)}, u32[]{:S(2)}) collective-permute-start(bf16[144,512]{1,0:T(8,128)(2,1)S(1)} %pad_maximum_fusion.7), channel_id=1, source_target_pairs={{0,2},{1,3},{2,0},{3,1},{4,6},{5,7},{6,4},{7,5},{8,10},{9,11},{10,... | collective-permute-start | bytes 442376 | tf_op jit(solution)/shard_map/ppermute | solution.py:693
  41.0 6.0 %collective-permute-start.16 = (bf16[64,1536]{1,0:T(8,128)(2,1)S(1)}, bf16[64,1536]{1,0:T(8,128)(2,1)S(1)}, u32[]{:S(2)}, u32[]{:S(2)}) collective-permute-start(bf16[64,1536]{1,0:T(8,128)(2,1)S(1)} %reduce-precision_convert_fusion.2), channel_id=1, source_target_pairs={{0,8},{1,9},{2,10},{3,11},{4,12},{5,13},{6,14},{7,15},{8,0},{9,1},... | collective-permute-start | bytes 589832 | tf_op jit(solution)/shard_map/ppermute | solution.py:693
  44.6 6.0 %collective-permute-start.19 = (bf16[144,512]{1,0:T(8,128)(2,1)S(1)}, bf16[144,512]{1,0:T(8,128)(2,1)S(1)}, u32[]{:S(2)}, u32[]{:S(2)}) collective-permute-start(bf16[144,512]{1,0:T(8,128)(2,1)S(1)} %pad_maximum_fusion.8), channel_id=1, source_target_pairs={{0,4},{1,5},{2,6},{3,7},{4,0},{5,1},{6,2},{7,3},{8,12},{9,13},{10,... | collective-permute-start | bytes 442376 | tf_op jit(solution)/shard_map/ppermute | solution.py:693
  47.0 8.9 %collective-permute-start.18 = (bf16[64,1536]{1,0:T(8,128)(2,1)S(1)}, bf16[64,1536]{1,0:T(8,128)(2,1)S(1)}, u32[]{:S(2)}, u32[]{:S(2)}) collective-permute-start(bf16[64,1536]{1,0:T(8,128)(2,1)S(1)} %reduce-precision_convert_fusion.1), channel_id=1, source_target_pairs={{0,24},{1,25},{2,26},{3,27},{4,28},{5,29},{6,30},{7,31},{8,16},{9,... | collective-permute-start | bytes 589832 | tf_op jit(solution)/shard_map/ppermute | solution.py:693
  50.7 8.9 %collective-permute-start.24 = (bf16[144,512]{1,0:T(8,128)(2,1)S(1)}, bf16[144,512]{1,0:T(8,128)(2,1)S(1)}, u32[]{:S(2)}, u32[]{:S(2)}) collective-permute-start(bf16[144,512]{1,0:T(8,128)(2,1)S(1)} %pad_maximum_fusion.9), channel_id=1, source_target_pairs={{0,8},{1,9},{2,10},{3,11},{4,12},{5,13},{6,14},{7,15},{8,0},{9,1},... | collective-permute-start | bytes 442376 | tf_op jit(solution)/shard_map/ppermute | solution.py:693
  56.0 7.1 %collective-permute-start.21 = (bf16[64,1536]{1,0:T(8,128)(2,1)S(1)}, bf16[64,1536]{1,0:T(8,128)(2,1)S(1)}, u32[]{:S(2)}, u32[]{:S(2)}) collective-permute-start(bf16[64,1536]{1,0:T(8,128)(2,1)S(1)} %reduce-precision_convert_fusion), channel_id=1, source_target_pairs={{0,4},{1,5},{2,6},{3,7},{4,0},{5,1},{6,2},{7,3},{8,12},{9,13},{10,... | collective-permute-start | bytes 589832 | tf_op jit(solution)/shard_map/ppermute | solution.py:693
  57.5 6.3 %collective-permute-start.22 = (bf16[64,1024]{1,0:T(8,128)(2,1)S(1)}, bf16[64,1024]{1,0:T(8,128)(2,1)S(1)}, u32[]{:S(2)}, u32[]{:S(2)}) collective-permute-start(bf16[64,1024]{1,0:T(8,128)(2,1)S(1)} %get-tuple-element.162), channel_id=1, source_target_pairs={{0,6},{1,7},{2,4},{3,5},{4,2},{5,3},{6,0},{7,1},{8,14},{9,15},{10,... | collective-permute-start | bytes 393224 | tf_op jit(solution)/shard_map/ppermute | solution.py:693
  58.9 5.1 %collective-permute-start.20 = (bf16[64,1024]{1,0:T(8,128)(2,1)S(1)}, bf16[64,1024]{1,0:T(8,128)(2,1)S(1)}, u32[]{:S(2)}, u32[]{:S(2)}) collective-permute-start(bf16[64,1024]{1,0:T(8,128)(2,1)S(1)} %get-tuple-element.162), channel_id=1, source_target_pairs={{0,2},{1,3},{2,0},{3,1},{4,6},{5,7},{6,4},{7,5},{8,10},{9,11},{10,... | collective-permute-start | bytes 393224 | tf_op jit(solution)/shard_map/ppermute | solution.py:693
  59.6 3.4 %collective-permute-start.23 = (bf16[1,64,1024]{2,1,0:T(8,128)(2,1)S(1)}, bf16[1,64,1024]{2,1,0:T(8,128)(2,1)S(1)}, u32[]{:S(2)}, u32[]{:S(2)}) collective-permute-start(bf16[1,64,1024]{2,1,0:T(8,128)(2,1)S(1)} %get-tuple-element.161.refs_0_), channel_id=1, source_target_pairs={{0,1},{1,0},{2,3},{3,2},{4,5},{5,4},{6,7},{7,6},{8,9},{9,8},{10,11... | collective-permute-start | bytes 393224 | tf_op jit(solution)/shard_map/ppermute | solution.py:693
  59.7 8.2 %collective-permute-start.26 = (bf16[144,512]{1,0:T(8,128)(2,1)S(1)}, bf16[144,512]{1,0:T(8,128)(2,1)S(1)}, u32[]{:S(2)}, u32[]{:S(2)}) collective-permute-start(bf16[144,512]{1,0:T(8,128)(2,1)S(1)} %pad_maximum_fusion.10), channel_id=1, source_target_pairs={{0,24},{1,25},{2,26},{3,27},{4,28},{5,29},{6,30},{7,31},{8,16},{9,... | collective-permute-start | bytes 442376 | tf_op jit(solution)/shard_map/ppermute | solution.py:693
  64.1 3.9 %collective-permute-start.25 = (bf16[3,64,1024]{2,1,0:T(8,128)(2,1)S(1)}, bf16[3,64,1024]{2,1,0:T(8,128)(2,1)S(1)}, u32[]{:S(2)}, u32[]{:S(2)}) collective-permute-start(bf16[3,64,1024]{2,1,0:T(8,128)(2,1)S(1)} %pad_maximum_fusion.1.refs_1_), channel_id=1, source_target_pairs={{0,1},{1,0},{2,3},{3,2},{4,5},{5,4},{6,7},{7,6},{8,9},{9,8},{10,11... | collective-permute-start | bytes 1179656 | tf_op jit(solution)/shard_map/ppermute | solution.py:693

commit v9 on v8

--- a/solution.py
+++ b/solution.py
@@ -1012,7 +1012,7 @@
     (grad_out,) = call(
         halves_kernel,
         [((own, 2, feats), F32)],
-        [both[:, 2 * feats :], tie(other_half, far_own)],
+        [both[:, 2 * feats :], other_half],
         [flat],
         8,
         MIB,

time: 70.1 us -> 70 us (level)
  no operation moved by 1% of the time
where the time goes in v9:
time: 70 us; the launch traced here: 69.8 us
  starting transfers between devices  27.7 us (40%)
  Pallas kernels  23 us (33%)
  waiting for transfers between devices  13.1 us (19%)
  local copies, waits for them, and re-layouts  2.8 us (4%)
  other arithmetic  1.94 us (3%)
  between operations  1.24 us (2%)
    ppermute x27, starting transfers between devices, exchange(): lax.ppermute(x, ('seq', 'state'), [(i, i ^ mask) for i in range(count)])  27.7 us
    pallas_call x14, Pallas kernels, call(): pl.pallas_call(body, out_shape=[jax.ShapeDtypeStruct(s, d) for s, d in ou...  20.3 us
    ppermute x27, waiting for transfers between devices, exchange(): lax.ppermute(x, ('seq', 'state'), [(i, i ^ mask) for i in range(count)])  13.1 us
    unnamed x10, local copies, waits for them, and re-layouts  1.89 us
    pallas_call x1, Pallas kernels, last_step(): pl.pallas_call(functools.partial(last_kernel, masks, parts), out_shape=[j...  1.65 us
  transfers between devices with their start and end apart: 27, of which 12 were waited for; matrix products, arithmetic and copies ran while one was open for 1% of the time, Pallas kernels for 23%

profile of v9, /device:TPU:0, one launch (start us, length us, event | category | flops | bytes accessed | tf_op | source)
XLA Modules:
  0.0 69.8 jit_solution(1952889973134512558)
XLA Ops:
  0.6 0.0 copy-start.3
  0.7 0.8 %concatenate.60 = f32[1728]{0:T(1024)S(1)} concatenate(f32[512]{0:T(512)} %param.13, f32[512]{0:T(512)} %param.14, f32[512]{0:T(512)} %param.20, f32[64]{0:T(128)} %param.17, f32[64]{0:T(128)} %param.18, f32[64]{0:T(128)} %param.19), dimensions={0} | concatenate | bytes 13824 | tf_op jit(solution)/shard_map/concatenate | solution.py:805
  1.5 0.1 prep.1
  1.7 1.1 %pad_maximum_fusion.6.refs_0_ = bf16[72,2,512]{2,1,0:T(2,128)(2,1)S(1)} fusion(bf16[8,2,512]{2,1,0:T(2,128)(2,1)S(1)} %get-tuple-element.83, bf16[64,2,512]{2,1,0:T(2,128)(2,1)} %bitcast.64), kind=kLoop, calls=%fused_computation.23 | loop fusion | flops 73728 | bytes 294912 | tf_op jit(solution)/shard_map/concatenate | solution.py:816
  2.8 3.0 %collective-permute-start.1 = (bf16[72,2,512]{2,1,0:T(2,128)(2,1)S(1)}, bf16[72,2,512]{2,1,0:T(2,128)(2,1)S(1)}, u32[]{:S(2)}, u32[]{:S(2)}) collective-permute-start(bf16[72,2,512]{2,1,0:T(2,128)(2,1)S(1)} %pad_maximum_fusion.6.refs_0_), channel_id=1, source_target_pairs={{0,2},{1,3},{2,0},{3,1},{4,6},{5,7},{6,4},{7,5},{8,10},{9,11},{10,... | collective-permute-start | bytes 442376 | tf_op jit(solution)/shard_map/ppermute | solution.py:693
  5.8 1.2 %copy-done = bf16[512,2,512]{2,1,0:T(2,128)(2,1)S(1)} copy-done((bf16[512,2,512]{2,1,0:T(2,128)(2,1)S(1)}, bf16[512,2,512]{2,1,0:T(2,128)(2,1)}, u32[]{:S(2)}) %copy-start) | copy-done | bytes 1048600
  7.0 1.8 %norm.1 = (bf16[1024,512]{1,0:T(8,128)(2,1)S(1)}, f32[1024,512]{1,0:T(8,128)S(1)}, f32[1024,128]{1,0:T(8,128)S(1)}, bf16[1024,512]{1,0:T(8,128)(2,1)S(1)}) custom-call(bf16[4,128,2,512]{3,2,1,0:T(2,128)(2,1)S(1)} %bitcast.54, f32[8,512]{1,0:T(8,128)S(1)} %get-tuple-element.79.vec_ref.refs_8_.refs_3_), custom_call_target="tpu_custom_call" | custom-call | flops 10485760 | bytes 4194304 | tf_op jit(solution)/shard_map/norm/pallas_call | solution.py:67
  8.8 0.0 copy-start.4
  8.8 0.6 copy-done.4
  9.5 0.6 limit.1.limit_ref.refs_7_
  10.0 0.0 collective-permute-done.1.refs_2_
  10.0 0.6 collective-permute-start.2
  10.6 0.7 %collective-permute-start.6 = (bf16[64,2,512]{2,1,0:T(2,128)(2,1)}, bf16[64,2,512]{2,1,0:T(2,128)(2,1)S(1)}, u32[]{:S(2)}, u32[]{:S(2)}) collective-permute-start(bf16[64,2,512]{2,1,0:T(2,128)(2,1)} %refs_0_), channel_id=1, source_target_pairs={{0,2},{1,3},{2,0},{3,1},{4,6},{5,7},{6,4},{7,5},{8,10},{9,11},{10,... | collective-permute-start | bytes 393224 | tf_op jit(solution)/shard_map/ppermute | solution.py:693
  11.4 0.0 collective-permute-done.refs_1_
  11.4 0.3 collective-permute-done.2.refs_3_
  11.6 1.6 %project.1 = (f32[1024,512]{1,0:T(8,128)S(1)}, f32[8,512]{1,0:T(8,128)S(1)}, bf16[512,512]{1,0:T(8,128)(2,1)S(1)}, f32[8,512]{1,0:T(8,128)S(1)}) custom-call(bf16[1024,512]{1,0:T(8,128)(2,1)S(1)} %get-tuple-element.81.low_ref.refs_6_, s32[8,128]{1,0:T(8,128)S(1)} %limit.1.limit_ref.refs_7_, bf16[72,2,512]{2,1,0:T(2,128)(2,1)S(1)} %pad_maximum_fusion.6.refs_0_, ...), custom_call_target="tpu_custom_call" | custom-call | flops 536870912 | bytes 4194304 | tf_op jit(solution)/shard_map/project/pallas_call | solution.py:67
  13.2 0.0 copy-start.2
  13.2 1.2 %collective-permute-start.3 = (f32[1,8,512]{2,1,0:T(8,128)S(1)}, f32[1,8,512]{2,1,0:T(8,128)S(1)}, u32[]{:S(2)}, u32[]{:S(2)}) collective-permute-start(f32[1,8,512]{2,1,0:T(8,128)S(1)} %bitcast.61), channel_id=1, source_target_pairs={{0,2},{1,3},{2,0},{3,1},{4,6},{5,7},{6,4},{7,5},{8,10},{9,11},{10,... | collective-permute-start | bytes 49160 | tf_op jit(solution)/shard_map/ppermute | solution.py:693
  14.4 1.9 %collective-permute-done.6.refs_2_ = bf16[64,2,512]{2,1,0:T(2,128)(2,1)S(1)} collective-permute-done((bf16[64,2,512]{2,1,0:T(2,128)(2,1)}, bf16[64,2,512]{2,1,0:T(2,128)(2,1)S(1)}, u32[]{:S(2)}, u32[]{:S(2)}) %collective-permute-start.6) | collective-permute-done | bytes 131104 | tf_op jit(solution)/shard_map/ppermute | solution.py:693
  16.3 0.0 collective-permute-start.7
  16.3 0.7 %collective-permute-done.3 = f32[1,8,512]{2,1,0:T(8,128)S(1)} collective-permute-done((f32[1,8,512]{2,1,0:T(8,128)S(1)}, f32[1,8,512]{2,1,0:T(8,128)S(1)}, u32[]{:S(2)}, u32[]{:S(2)}) %collective-permute-start.3) | collective-permute-done | bytes 16416 | tf_op jit(solution)/shard_map/ppermute | solution.py:693
  17.1 0.3 cotangent.1.refs_6_.cot_ref
  17.4 0.3 collective-permute-done.7.refs_3_
  17.7 0.4 weights.1.refs_4_.cw_ref
  18.0 0.2 collective-permute-done.4
  18.3 5.1 %mix.1 = (f32[1032,512]{1,0:T(8,128)S(1)}, bf16[1024,512]{1,0:T(8,128)(2,1)S(1)}, f32[1024,512]{1,0:T(8,128)S(1)}, bf16[1024,1024]{1,0:T(8,128)(2,1)S(1)}, f32[1...) custom-call(f32[1024,512]{1,0:T(8,128)S(1)} %get-tuple-element.85.re, ...), custom_call_target="tpu_custom_call" | custom-call | flops 2684354560 | bytes 4194304 | tf_op jit(solution)/shard_map/mix/pallas_call | solution.py:67
  23.4 0.2 collective-permute-start.8
  23.6 2.1 %back.1 = (f32[1024,512]{1,0:T(8,128)S(1)}, bf16[1024,512]{1,0:T(8,128)(2,1)S(1)}, f32[8,512]{1,0:T(8,128)S(1)}, bf16[4,64,512]{2,1,0:T(8,128)(2,1)S(1)}, f32[1,...) custom-call(bf16[1024,1024]{1,0:T(8,128)(2,1)S(1)} %get-tuple-element.94, ...), custom_call_target="tpu_custom_call" | custom-call | flops 1610612736 | bytes 4194304 | tf_op jit(solution)/shard_map/back/pallas_call | solution.py:67
  25.7 0.4 collective-permute-start.9
  26.1 1.2 %starts.1 = (f32[1024,512]{1,0:T(8,128)S(1)}, f32[8,512]{1,0:T(8,128)S(1)}) custom-call(bf16[1024,512]{1,0:T(8,128)(2,1)S(1)} %get-tuple-element.97.dmix_ref, bf16[512,512]{1,0:T(8,128)(2,1)S(1)} %weights.1.refs_4_.cw_ref, f32[8,512]{1,0:T(8,128)S(1)} %get-tuple-element.87.refs_2_.cst_ref), custom_call_target="tpu_custom_call" | custom-call | flops 536870912 | bytes 4194304 | tf_op jit(solution)/shard_map/starts/pallas_call | solution.py:67
  27.4 1.2 %collective-permute-start.10 = (f32[1,8,512]{2,1,0:T(8,128)S(1)}, f32[1,8,512]{2,1,0:T(8,128)S(1)}, u32[]{:S(2)}, u32[]{:S(2)}) collective-permute-start(f32[1,8,512]{2,1,0:T(8,128)S(1)} %bitcast.58), channel_id=1, source_target_pairs={{0,2},{1,3},{2,0},{3,1},{4,6},{5,7},{6,4},{7,5},{8,10},{9,11},{10,... | collective-permute-start | bytes 49160 | tf_op jit(solution)/shard_map/ppermute | solution.py:693
  28.6 0.1 convert_add_fusion.5
  28.7 0.1 convert_add_fusion.4
  28.8 0.9 %collective-permute-start.12 = (bf16[1,64,1536]{2,1,0:T(8,128)(2,1)S(1)}, bf16[1,64,1536]{2,1,0:T(8,128)(2,1)S(1)}, u32[]{:S(2)}, u32[]{:S(2)}) collective-permute-start(bf16[1,64,1536]{2,1,0:T(8,128)(2,1)S(1)} %pad_maximum_fusion.3), channel_id=1, source_target_pairs={{0,2},{1,3},{2,0},{3,1},{4,6},{5,7},{6,4},{7,5},{8,10},{9,11},{10,... | collective-permute-start | bytes 589832 | tf_op jit(solution)/shard_map/ppermute | solution.py:693
  29.8 1.6 %collective-permute-start.13 = (bf16[1,64,1536]{2,1,0:T(8,128)(2,1)S(1)}, bf16[1,64,1536]{2,1,0:T(8,128)(2,1)S(1)}, u32[]{:S(2)}, u32[]{:S(2)}) collective-permute-start(bf16[1,64,1536]{2,1,0:T(8,128)(2,1)S(1)} %pad_maximum_fusion.4), channel_id=1, source_target_pairs={{0,4},{1,5},{2,6},{3,7},{4,0},{5,1},{6,2},{7,3},{8,12},{9,13},{10,... | collective-permute-start | bytes 589832 | tf_op jit(solution)/shard_map/ppermute | solution.py:693
  31.4 0.1 collective-permute-start.11
  31.5 2.0 %collective-permute-start.14 = (bf16[1,64,1536]{2,1,0:T(8,128)(2,1)S(1)}, bf16[1,64,1536]{2,1,0:T(8,128)(2,1)S(1)}, u32[]{:S(2)}, u32[]{:S(2)}) collective-permute-start(bf16[1,64,1536]{2,1,0:T(8,128)(2,1)S(1)} %pad_maximum_fusion.5), channel_id=1, source_target_pairs={{0,6},{1,7},{2,4},{3,5},{4,2},{5,3},{6,0},{7,1},{8,14},{9,15},{10,... | collective-permute-start | bytes 589832 | tf_op jit(solution)/shard_map/ppermute | solution.py:693
  33.5 1.9 %adjoint.1 = (bf16[1024,512]{1,0:T(8,128)(2,1)S(1)}, f32[8,768]{1,0:T(8,128)S(1)}, bf16[2,128,512]{2,1,0:T(8,128)(2,1)S(1)}, f32[1,128,512]{2,1,0:T(8,128)S(1)}, f32[1,128,512]{2,1,0:T(8,128)S(1)}) custom-call(f32[1024,512]{1,0:T(8,128)S(1)} %get-tuple-element.106.refs_0_, f32[8,512]{1,0:T(8,128)S(1)} %get-tuple-element.107.refs_1_, ...), custom_call_target="tpu_custom_call" | custom-call | flops 1073741824 | bytes 4194304 | tf_op jit(solution)/shard_map/adjoint/pallas_call | solution.py:67
  35.4 0.9 %normed.1 = (f32[1024,512]{1,0:T(8,128)S(1)}, f32[8,512]{1,0:T(8,128)S(1)}) custom-call(bf16[1024,512]{1,0:T(8,128)(2,1)S(1)} %get-tuple-element.110.dproj_ref, bf16[512,512]{1,0:T(8,128)(2,1)S(1)} %get-tuple-element.111.win_ref, f32[1024,512]{1,0:T(8,128)S(1)} %get-tuple-element.112.dpre_ref, f32[1024,512]{1,0:T(8,128)S(1)} %get-tuple-element.91.refs_5_.refs_2_.unit_ref, ...), custom_call_target="tpu_custom_call" | custom-call | flops 536870912 | bytes 4194304 | tf_op jit(solution)/shard_map/normed/pallas_call | solution.py:67
  36.3 0.3 collective-permute-start.15
  36.6 1.7 %out.1 = bf16[4,128,2,512]{3,2,1,0:T(2,128)(2,1)} custom-call(bf16[1024,512]{1,0:T(8,128)(2,1)S(1)} %get-tuple-element.80.x_ref, f32[1024,512]{1,0:T(8,128)S(1)} %get-tuple-element.116.branch_ref), custom_call_target="tpu_custom_call" | custom-call | flops 4294967296 | bytes 4194304 | tf_op jit(solution)/shard_map/out/pallas_call | solution.py:67
  38.4 0.9 %collective-permute-start.17 = (bf16[144,512]{1,0:T(8,128)(2,1)S(1)}, bf16[144,512]{1,0:T(8,128)(2,1)S(1)}, u32[]{:S(2)}, u32[]{:S(2)}) collective-permute-start(bf16[144,512]{1,0:T(8,128)(2,1)S(1)} %pad_maximum_fusion.7), channel_id=1, source_target_pairs={{0,2},{1,3},{2,0},{3,1},{4,6},{5,7},{6,4},{7,5},{8,10},{9,11},{10,... | collective-permute-start | bytes 442376 | tf_op jit(solution)/shard_map/ppermute | solution.py:693
  39.3 0.3 collective-permute-done.13
  39.6 1.3 %collective-permute-done.14 = bf16[1,64,1536]{2,1,0:T(8,128)(2,1)S(1)} collective-permute-done((bf16[1,64,1536]{2,1,0:T(8,128)(2,1)S(1)}, bf16[1,64,1536]{2,1,0:T(8,128)(2,1)S(1)}, u32[]{:S(2)}, u32[]{:S(2)}) %collective-permute-start.14) | collective-permute-done | bytes 196640 | tf_op jit(solution)/shard_map/ppermute | solution.py:693
  40.9 0.1 reduce-precision_convert_fusion.2
  41.0 1.6 %collective-permute-start.16 = (bf16[64,1536]{1,0:T(8,128)(2,1)S(1)}, bf16[64,1536]{1,0:T(8,128)(2,1)S(1)}, u32[]{:S(2)}, u32[]{:S(2)}) collective-permute-start(bf16[64,1536]{1,0:T(8,128)(2,1)S(1)} %reduce-precision_convert_fusion.2), channel_id=1, source_target_pairs={{0,8},{1,9},{2,10},{3,11},{4,12},{5,13},{6,14},{7,15},{8,0},{9,1},... | collective-permute-start | bytes 589832 | tf_op jit(solution)/shard_map/ppermute | solution.py:693
  42.6 1.8 %tokens.1 = f32[4,128,2,512]{3,2,1,0:T(2,128)} custom-call(bf16[1024,512]{1,0:T(8,128)(2,1)S(1)} %cotangent.1.refs_6_.cot_ref, f32[1024,512]{1,0:T(8,128)S(1)} %get-tuple-element.129.dnorm_ref, f32[1024,512]{1,0:T(8,128)S(1)} %get-tuple-element.91.refs_5_.refs_2_.unit_ref, f32[1024,128]{1,0:T(8,128)S(1)} %get-tuple-element.130.inv_ref, ...), custom_call_target="tpu_custom_call" | custom-call | flops 4294967296 | bytes 4194304 | tf_op jit(solution)/shard_map/tokens/pallas_call | solution.py:67
  44.4 0.1 collective-permute-done.17
  44.6 1.2 %collective-permute-start.19 = (bf16[144,512]{1,0:T(8,128)(2,1)S(1)}, bf16[144,512]{1,0:T(8,128)(2,1)S(1)}, u32[]{:S(2)}, u32[]{:S(2)}) collective-permute-start(bf16[144,512]{1,0:T(8,128)(2,1)S(1)} %pad_maximum_fusion.8), channel_id=1, source_target_pairs={{0,4},{1,5},{2,6},{3,7},{4,0},{5,1},{6,2},{7,3},{8,12},{9,13},{10,... | collective-permute-start | bytes 442376 | tf_op jit(solution)/shard_map/ppermute | solution.py:693
  45.8 1.1 %collective-permute-done.16 = bf16[64,1536]{1,0:T(8,128)(2,1)S(1)} collective-permute-done((bf16[64,1536]{1,0:T(8,128)(2,1)S(1)}, bf16[64,1536]{1,0:T(8,128)(2,1)S(1)}, u32[]{:S(2)}, u32[]{:S(2)}) %collective-permute-start.16) | collective-permute-done | bytes 196640 | tf_op jit(solution)/shard_map/ppermute | solution.py:693
  46.9 0.1 reduce-precision_convert_fusion.1
  47.0 3.6 %collective-permute-start.18 = (bf16[64,1536]{1,0:T(8,128)(2,1)S(1)}, bf16[64,1536]{1,0:T(8,128)(2,1)S(1)}, u32[]{:S(2)}, u32[]{:S(2)}) collective-permute-start(bf16[64,1536]{1,0:T(8,128)(2,1)S(1)} %reduce-precision_convert_fusion.1), channel_id=1, source_target_pairs={{0,24},{1,25},{2,26},{3,27},{4,28},{5,29},{6,30},{7,31},{8,16},{9,... | collective-permute-start | bytes 589832 | tf_op jit(solution)/shard_map/ppermute | solution.py:693
  50.7 0.9 %collective-permute-start.23 = (bf16[144,512]{1,0:T(8,128)(2,1)S(1)}, bf16[144,512]{1,0:T(8,128)(2,1)S(1)}, u32[]{:S(2)}, u32[]{:S(2)}) collective-permute-start(bf16[144,512]{1,0:T(8,128)(2,1)S(1)} %pad_maximum_fusion.9), channel_id=1, source_target_pairs={{0,8},{1,9},{2,10},{3,11},{4,12},{5,13},{6,14},{7,15},{8,0},{9,1},... | collective-permute-start | bytes 442376 | tf_op jit(solution)/shard_map/ppermute | solution.py:693
  51.6 4.4 %collective-permute-done.18 = bf16[64,1536]{1,0:T(8,128)(2,1)S(1)} collective-permute-done((bf16[64,1536]{1,0:T(8,128)(2,1)S(1)}, bf16[64,1536]{1,0:T(8,128)(2,1)S(1)}, u32[]{:S(2)}, u32[]{:S(2)}) %collective-permute-start.18) | collective-permute-done | bytes 196640 | tf_op jit(solution)/shard_map/ppermute | solution.py:693
  56.0 1.5 %collective-permute-start.21 = (bf16[64,1536]{1,0:T(8,128)(2,1)S(1)}, bf16[64,1536]{1,0:T(8,128)(2,1)S(1)}, u32[]{:S(2)}, u32[]{:S(2)}) collective-permute-start(bf16[64,1536]{1,0:T(8,128)(2,1)S(1)} %reduce-precision_convert_fusion), channel_id=1, source_target_pairs={{0,4},{1,5},{2,6},{3,7},{4,0},{5,1},{6,2},{7,3},{8,12},{9,13},{10,... | collective-permute-start | bytes 589832 | tf_op jit(solution)/shard_map/ppermute | solution.py:693
  57.5 1.4 %collective-permute-start.22 = (bf16[64,1024]{1,0:T(8,128)(2,1)S(1)}, bf16[64,1024]{1,0:T(8,128)(2,1)S(1)}, u32[]{:S(2)}, u32[]{:S(2)}) collective-permute-start(bf16[64,1024]{1,0:T(8,128)(2,1)S(1)} %get-tuple-element.160), channel_id=1, source_target_pairs={{0,6},{1,7},{2,4},{3,5},{4,2},{5,3},{6,0},{7,1},{8,14},{9,15},{10,... | collective-permute-start | bytes 393224 | tf_op jit(solution)/shard_map/ppermute | solution.py:693
  58.9 0.7 %collective-permute-start.20 = (bf16[64,1024]{1,0:T(8,128)(2,1)S(1)}, bf16[64,1024]{1,0:T(8,128)(2,1)S(1)}, u32[]{:S(2)}, u32[]{:S(2)}) collective-permute-start(bf16[64,1024]{1,0:T(8,128)(2,1)S(1)} %get-tuple-element.160), channel_id=1, source_target_pairs={{0,2},{1,3},{2,0},{3,1},{4,6},{5,7},{6,4},{7,5},{8,10},{9,11},{10,... | collective-permute-start | bytes 393224 | tf_op jit(solution)/shard_map/ppermute | solution.py:693
  59.7 3.3 %collective-permute-start.25 = (bf16[144,512]{1,0:T(8,128)(2,1)S(1)}, bf16[144,512]{1,0:T(8,128)(2,1)S(1)}, u32[]{:S(2)}, u32[]{:S(2)}) collective-permute-start(bf16[144,512]{1,0:T(8,128)(2,1)S(1)} %pad_maximum_fusion.10), channel_id=1, source_target_pairs={{0,24},{1,25},{2,26},{3,27},{4,28},{5,29},{6,30},{7,31},{8,16},{9,... | collective-permute-start | bytes 442376 | tf_op jit(solution)/shard_map/ppermute | solution.py:693
  63.1 0.8 %halves.1 = f32[64,2,512]{2,1,0:T(2,128)} custom-call(bf16[64,512]{1,0:T(8,128)(2,1)S(1)} %slice.120.mine_ref, bf16[64,512]{1,0:T(8,128)(2,1)S(1)} %slice.121.other_ref), custom_call_target="tpu_custom_call" | custom-call | flops 1048576 | bytes 4194304 | tf_op jit(solution)/shard_map/halves/pallas_call | solution.py:67
  63.9 0.2 collective-permute-done.20
  64.1 0.4 collective-permute-start.24
  64.5 2.3 %collective-permute-done.25 = bf16[144,512]{1,0:T(8,128)(2,1)S(1)} collective-permute-done((bf16[144,512]{1,0:T(8,128)(2,1)S(1)}, bf16[144,512]{1,0:T(8,128)(2,1)S(1)}, u32[]{:S(2)}, u32[]{:S(2)}) %collective-permute-start.25) | collective-permute-done | bytes 147488 | tf_op jit(solution)/shard_map/ppermute | solution.py:693
  66.8 1.1 %place.1.refs_4_ = f32[512,1024]{1,0:T(8,128)} custom-call(bf16[1,64,1024]{2,1,0:T(8,128)(2,1)S(1)} %get-tuple-element.159.refs_0_, bf16[3,64,1024]{2,1,0:T(8,128)(2,1)S(1)} %pad_maximum_fusion.1.refs_1_, bf16[1,64,1024]{2,1,0:T(8,128)(2,1)S(1)} %collective-permute-done.26.refs_2_), custom_call_target="tpu_custom_call" | custom-call | flops 1048576 | bytes 2097152 | tf_op jit(solution)/shard_map/place/pallas_call | solution.py:645
  68.0 1.6 %last.1 = (f32[512,1024]{1,0:T(8,128)}, f32[64,2,512]{2,1,0:T(2,128)}, f32[1,512]{1,0:T(1,128)}, f32[1,512]{1,0:T(1,128)}, f32[1,512]{1,0:T(1,128)}, /*index=5*/...) custom-call(bf16[3,64,1024]{2,1,0:T(8,128)(2,1)S(1)} %collective-permute-done.24.refs_0_, ...), custom_call_target="tpu_custom_call", output_to_operand_aliasing={{0}: (4, {})} | custom-call | flops 1048576 | bytes 2097152 | tf_op jit(solution)/shard_map/last/pallas_call | solution.py:674
  (54 shorter events, 0.6 us)
Async XLA Ops:
  0.6 13.8 %copy-start.3 = (bf16[64,2,512]{2,1,0:T(2,128)(2,1)S(1)}, bf16[64,2,512]{2,1,0:T(2,128)(2,1)}, u32[]{:S(2)}) copy-start(bf16[64,2,512]{2,1,0:T(2,128)(2,1)} %refs_0_) | copy-start | bytes 393220
  2.8 7.3 %collective-permute-start.1 = (bf16[72,2,512]{2,1,0:T(2,128)(2,1)S(1)}, bf16[72,2,512]{2,1,0:T(2,128)(2,1)S(1)}, u32[]{:S(2)}, u32[]{:S(2)}) collective-permute-start(bf16[72,2,512]{2,1,0:T(2,128)(2,1)S(1)} %pad_maximum_fusion.6.refs_0_), channel_id=1, source_target_pairs={{0,2},{1,3},{2,0},{3,1},{4,6},{5,7},{6,4},{7,5},{8,10},{9,11},{10,... | collective-permute-start | bytes 442376 | tf_op jit(solution)/shard_map/ppermute | solution.py:693
  5.8 5.6 %collective-permute-start = (bf16[72,2,512]{2,1,0:T(2,128)(2,1)S(1)}, bf16[72,2,512]{2,1,0:T(2,128)(2,1)S(1)}, u32[]{:S(2)}, u32[]{:S(2)}) collective-permute-start(bf16[72,2,512]{2,1,0:T(2,128)(2,1)S(1)} %pad_maximum_fusion.6.refs_0_), channel_id=1, source_target_pairs={{0,1},{1,0},{2,3},{3,2},{4,5},{5,4},{6,7},{7,6},{8,9},{9,8},{10,11... | collective-permute-start | bytes 442376 | tf_op jit(solution)/shard_map/ppermute | solution.py:693
  5.8 1.2 %copy-start = (bf16[512,2,512]{2,1,0:T(2,128)(2,1)S(1)}, bf16[512,2,512]{2,1,0:T(2,128)(2,1)}, u32[]{:S(2)}) copy-start(bf16[512,2,512]{2,1,0:T(2,128)(2,1)} %param.12) | copy-start | bytes 3145732
  7.0 10.1 %copy-start.1 = (bf16[512,2,512]{2,1,0:T(2,128)(2,1)S(1)}, bf16[512,2,512]{2,1,0:T(2,128)(2,1)}, u32[]{:S(2)}) copy-start(bf16[512,2,512]{2,1,0:T(2,128)(2,1)} %param.23) | copy-start | bytes 3145732
  8.8 0.7 copy-start.4
  10.0 1.6 %collective-permute-start.2 = (bf16[72,2,512]{2,1,0:T(2,128)(2,1)S(1)}, bf16[72,2,512]{2,1,0:T(2,128)(2,1)S(1)}, u32[]{:S(2)}, u32[]{:S(2)}) collective-permute-start(bf16[72,2,512]{2,1,0:T(2,128)(2,1)S(1)} %collective-permute-done.1.refs_2_), channel_id=1, source_target_pairs={{0,1},{1,0},{2,3},{3,2},{4,5},{5,4},{6,7},{7,6},{8,9},{9,8},{10,11... | collective-permute-start | bytes 442376 | tf_op jit(solution)/shard_map/ppermute | solution.py:693
  10.6 5.7 %collective-permute-start.6 = (bf16[64,2,512]{2,1,0:T(2,128)(2,1)}, bf16[64,2,512]{2,1,0:T(2,128)(2,1)S(1)}, u32[]{:S(2)}, u32[]{:S(2)}) collective-permute-start(bf16[64,2,512]{2,1,0:T(2,128)(2,1)} %refs_0_), channel_id=1, source_target_pairs={{0,2},{1,3},{2,0},{3,1},{4,6},{5,7},{6,4},{7,5},{8,10},{9,11},{10,... | collective-permute-start | bytes 393224 | tf_op jit(solution)/shard_map/ppermute | solution.py:693
  13.2 5.1 %copy-start.2 = (bf16[512,1024]{1,0:T(8,128)(2,1)S(1)}, bf16[512,1024]{1,0:T(8,128)(2,1)}, u32[]{:S(2)}) copy-start(bf16[512,1024]{1,0:T(8,128)(2,1)} %refs_4_.1) | copy-start | bytes 3145732
  13.2 3.8 %collective-permute-start.3 = (f32[1,8,512]{2,1,0:T(8,128)S(1)}, f32[1,8,512]{2,1,0:T(8,128)S(1)}, u32[]{:S(2)}, u32[]{:S(2)}) collective-permute-start(f32[1,8,512]{2,1,0:T(8,128)S(1)} %bitcast.61), channel_id=1, source_target_pairs={{0,2},{1,3},{2,0},{3,1},{4,6},{5,7},{6,4},{7,5},{8,10},{9,11},{10,... | collective-permute-start | bytes 49160 | tf_op jit(solution)/shard_map/ppermute | solution.py:693
  14.4 3.0 %collective-permute-start.5 = (bf16[64,2,512]{2,1,0:T(2,128)(2,1)S(1)}, bf16[64,2,512]{2,1,0:T(2,128)(2,1)S(1)}, u32[]{:S(2)}, u32[]{:S(2)}) collective-permute-start(bf16[64,2,512]{2,1,0:T(2,128)(2,1)S(1)} %copy-done.3), channel_id=1, source_target_pairs={{0,1},{1,0},{2,3},{3,2},{4,5},{5,4},{6,7},{7,6},{8,9},{9,8},{10,11... | collective-permute-start | bytes 393224 | tf_op jit(solution)/shard_map/ppermute | solution.py:693
  16.3 1.3 %collective-permute-start.7 = (bf16[64,2,512]{2,1,0:T(2,128)(2,1)S(1)}, bf16[64,2,512]{2,1,0:T(2,128)(2,1)S(1)}, u32[]{:S(2)}, u32[]{:S(2)}) collective-permute-start(bf16[64,2,512]{2,1,0:T(2,128)(2,1)S(1)} %collective-permute-done.6.refs_2_), channel_id=1, source_target_pairs={{0,1},{1,0},{2,3},{3,2},{4,5},{5,4},{6,7},{7,6},{8,9},{9,8},{10,11... | collective-permute-start | bytes 393224 | tf_op jit(solution)/shard_map/ppermute | solution.py:693
  17.1 1.2 %collective-permute-start.4 = (f32[2,8,512]{2,1,0:T(8,128)S(1)}, f32[2,8,512]{2,1,0:T(8,128)S(1)}, u32[]{:S(2)}, u32[]{:S(2)}) collective-permute-start(f32[2,8,512]{2,1,0:T(8,128)S(1)} %get-tuple-element.170), channel_id=1, source_target_pairs={{0,1},{1,0},{2,3},{3,2},{4,5},{5,4},{6,7},{7,6},{8,9},{9,8},{10,11... | collective-permute-start | bytes 98312 | tf_op jit(solution)/shard_map/ppermute | solution.py:693
  23.4 3.9 %collective-permute-start.8 = (bf16[4,64,1024]{2,1,0:T(8,128)(2,1)S(1)}, bf16[4,64,1024]{2,1,0:T(8,128)(2,1)S(1)}, u32[]{:S(2)}, u32[]{:S(2)}) collective-permute-start(bf16[4,64,1024]{2,1,0:T(8,128)(2,1)S(1)} %get-tuple-element.100), channel_id=1, source_target_pairs={{0,1},{1,0},{2,3},{3,2},{4,5},{5,4},{6,7},{7,6},{8,9},{9,8},{10,11... | collective-permute-start | bytes 1572872 | tf_op jit(solution)/shard_map/ppermute | solution.py:693
  25.7 1.6 %collective-permute-start.9 = (bf16[4,64,512]{2,1,0:T(8,128)(2,1)S(1)}, bf16[4,64,512]{2,1,0:T(8,128)(2,1)S(1)}, u32[]{:S(2)}, u32[]{:S(2)}) collective-permute-start(bf16[4,64,512]{2,1,0:T(8,128)(2,1)S(1)} %get-tuple-element.101), channel_id=1, source_target_pairs={{0,1},{1,0},{2,3},{3,2},{4,5},{5,4},{6,7},{7,6},{8,9},{9,8},{10,11... | collective-permute-start | bytes 786440 | tf_op jit(solution)/shard_map/ppermute | solution.py:693
  27.4 4.0 %collective-permute-start.10 = (f32[1,8,512]{2,1,0:T(8,128)S(1)}, f32[1,8,512]{2,1,0:T(8,128)S(1)}, u32[]{:S(2)}, u32[]{:S(2)}) collective-permute-start(f32[1,8,512]{2,1,0:T(8,128)S(1)} %bitcast.58), channel_id=1, source_target_pairs={{0,2},{1,3},{2,0},{3,1},{4,6},{5,7},{6,4},{7,5},{8,10},{9,11},{10,... | collective-permute-start | bytes 49160 | tf_op jit(solution)/shard_map/ppermute | solution.py:693
  28.8 10.5 %collective-permute-start.12 = (bf16[1,64,1536]{2,1,0:T(8,128)(2,1)S(1)}, bf16[1,64,1536]{2,1,0:T(8,128)(2,1)S(1)}, u32[]{:S(2)}, u32[]{:S(2)}) collective-permute-start(bf16[1,64,1536]{2,1,0:T(8,128)(2,1)S(1)} %pad_maximum_fusion.3), channel_id=1, source_target_pairs={{0,2},{1,3},{2,0},{3,1},{4,6},{5,7},{6,4},{7,5},{8,10},{9,11},{10,... | collective-permute-start | bytes 589832 | tf_op jit(solution)/shard_map/ppermute | solution.py:693
  29.8 9.8 %collective-permute-start.13 = (bf16[1,64,1536]{2,1,0:T(8,128)(2,1)S(1)}, bf16[1,64,1536]{2,1,0:T(8,128)(2,1)S(1)}, u32[]{:S(2)}, u32[]{:S(2)}) collective-permute-start(bf16[1,64,1536]{2,1,0:T(8,128)(2,1)S(1)} %pad_maximum_fusion.4), channel_id=1, source_target_pairs={{0,4},{1,5},{2,6},{3,7},{4,0},{5,1},{6,2},{7,3},{8,12},{9,13},{10,... | collective-permute-start | bytes 589832 | tf_op jit(solution)/shard_map/ppermute | solution.py:693
  31.4 2.1 %collective-permute-start.11 = (f32[2,8,512]{2,1,0:T(8,128)S(1)}, f32[2,8,512]{2,1,0:T(8,128)S(1)}, u32[]{:S(2)}, u32[]{:S(2)}) collective-permute-start(f32[2,8,512]{2,1,0:T(8,128)S(1)} %get-tuple-element.168), channel_id=1, source_target_pairs={{0,1},{1,0},{2,3},{3,2},{4,5},{5,4},{6,7},{7,6},{8,9},{9,8},{10,11... | collective-permute-start | bytes 98312 | tf_op jit(solution)/shard_map/ppermute | solution.py:693
  31.5 9.4 %collective-permute-start.14 = (bf16[1,64,1536]{2,1,0:T(8,128)(2,1)S(1)}, bf16[1,64,1536]{2,1,0:T(8,128)(2,1)S(1)}, u32[]{:S(2)}, u32[]{:S(2)}) collective-permute-start(bf16[1,64,1536]{2,1,0:T(8,128)(2,1)S(1)} %pad_maximum_fusion.5), channel_id=1, source_target_pairs={{0,6},{1,7},{2,4},{3,5},{4,2},{5,3},{6,0},{7,1},{8,14},{9,15},{10,... | collective-permute-start | bytes 589832 | tf_op jit(solution)/shard_map/ppermute | solution.py:693
  36.3 2.0 %collective-permute-start.15 = (bf16[272,512]{1,0:T(8,128)(2,1)S(1)}, bf16[272,512]{1,0:T(8,128)(2,1)S(1)}, u32[]{:S(2)}, u32[]{:S(2)}) collective-permute-start(bf16[272,512]{1,0:T(8,128)(2,1)S(1)} %pad_maximum_fusion.2), channel_id=1, source_target_pairs={{0,1},{1,0},{2,3},{3,2},{4,5},{5,4},{6,7},{7,6},{8,9},{9,8},{10,11... | collective-permute-start | bytes 835592 | tf_op jit(solution)/shard_map/ppermute | solution.py:693
  38.4 6.1 %collective-permute-start.17 = (bf16[144,512]{1,0:T(8,128)(2,1)S(1)}, bf16[144,512]{1,0:T(8,128)(2,1)S(1)}, u32[]{:S(2)}, u32[]{:S(2)}) collective-permute-start(bf16[144,512]{1,0:T(8,128)(2,1)S(1)} %pad_maximum_fusion.7), channel_id=1, source_target_pairs={{0,2},{1,3},{2,0},{3,1},{4,6},{5,7},{6,4},{7,5},{8,10},{9,11},{10,... | collective-permute-start | bytes 442376 | tf_op jit(solution)/shard_map/ppermute | solution.py:693
  41.0 6.0 %collective-permute-start.16 = (bf16[64,1536]{1,0:T(8,128)(2,1)S(1)}, bf16[64,1536]{1,0:T(8,128)(2,1)S(1)}, u32[]{:S(2)}, u32[]{:S(2)}) collective-permute-start(bf16[64,1536]{1,0:T(8,128)(2,1)S(1)} %reduce-precision_convert_fusion.2), channel_id=1, source_target_pairs={{0,8},{1,9},{2,10},{3,11},{4,12},{5,13},{6,14},{7,15},{8,0},{9,1},... | collective-permute-start | bytes 589832 | tf_op jit(solution)/shard_map/ppermute | solution.py:693
  44.6 6.0 %collective-permute-start.19 = (bf16[144,512]{1,0:T(8,128)(2,1)S(1)}, bf16[144,512]{1,0:T(8,128)(2,1)S(1)}, u32[]{:S(2)}, u32[]{:S(2)}) collective-permute-start(bf16[144,512]{1,0:T(8,128)(2,1)S(1)} %pad_maximum_fusion.8), channel_id=1, source_target_pairs={{0,4},{1,5},{2,6},{3,7},{4,0},{5,1},{6,2},{7,3},{8,12},{9,13},{10,... | collective-permute-start | bytes 442376 | tf_op jit(solution)/shard_map/ppermute | solution.py:693
  47.0 8.9 %collective-permute-start.18 = (bf16[64,1536]{1,0:T(8,128)(2,1)S(1)}, bf16[64,1536]{1,0:T(8,128)(2,1)S(1)}, u32[]{:S(2)}, u32[]{:S(2)}) collective-permute-start(bf16[64,1536]{1,0:T(8,128)(2,1)S(1)} %reduce-precision_convert_fusion.1), channel_id=1, source_target_pairs={{0,24},{1,25},{2,26},{3,27},{4,28},{5,29},{6,30},{7,31},{8,16},{9,... | collective-permute-start | bytes 589832 | tf_op jit(solution)/shard_map/ppermute | solution.py:693
  50.7 8.9 %collective-permute-start.23 = (bf16[144,512]{1,0:T(8,128)(2,1)S(1)}, bf16[144,512]{1,0:T(8,128)(2,1)S(1)}, u32[]{:S(2)}, u32[]{:S(2)}) collective-permute-start(bf16[144,512]{1,0:T(8,128)(2,1)S(1)} %pad_maximum_fusion.9), channel_id=1, source_target_pairs={{0,8},{1,9},{2,10},{3,11},{4,12},{5,13},{6,14},{7,15},{8,0},{9,1},... | collective-permute-start | bytes 442376 | tf_op jit(solution)/shard_map/ppermute | solution.py:693
  56.0 7.1 %collective-permute-start.21 = (bf16[64,1536]{1,0:T(8,128)(2,1)S(1)}, bf16[64,1536]{1,0:T(8,128)(2,1)S(1)}, u32[]{:S(2)}, u32[]{:S(2)}) collective-permute-start(bf16[64,1536]{1,0:T(8,128)(2,1)S(1)} %reduce-precision_convert_fusion), channel_id=1, source_target_pairs={{0,4},{1,5},{2,6},{3,7},{4,0},{5,1},{6,2},{7,3},{8,12},{9,13},{10,... | collective-permute-start | bytes 589832 | tf_op jit(solution)/shard_map/ppermute | solution.py:693
  57.5 6.3 %collective-permute-start.22 = (bf16[64,1024]{1,0:T(8,128)(2,1)S(1)}, bf16[64,1024]{1,0:T(8,128)(2,1)S(1)}, u32[]{:S(2)}, u32[]{:S(2)}) collective-permute-start(bf16[64,1024]{1,0:T(8,128)(2,1)S(1)} %get-tuple-element.160), channel_id=1, source_target_pairs={{0,6},{1,7},{2,4},{3,5},{4,2},{5,3},{6,0},{7,1},{8,14},{9,15},{10,... | collective-permute-start | bytes 393224 | tf_op jit(solution)/shard_map/ppermute | solution.py:693
  58.9 5.1 %collective-permute-start.20 = (bf16[64,1024]{1,0:T(8,128)(2,1)S(1)}, bf16[64,1024]{1,0:T(8,128)(2,1)S(1)}, u32[]{:S(2)}, u32[]{:S(2)}) collective-permute-start(bf16[64,1024]{1,0:T(8,128)(2,1)S(1)} %get-tuple-element.160), channel_id=1, source_target_pairs={{0,2},{1,3},{2,0},{3,1},{4,6},{5,7},{6,4},{7,5},{8,10},{9,11},{10,... | collective-permute-start | bytes 393224 | tf_op jit(solution)/shard_map/ppermute | solution.py:693
  59.7 7.1 %collective-permute-start.25 = (bf16[144,512]{1,0:T(8,128)(2,1)S(1)}, bf16[144,512]{1,0:T(8,128)(2,1)S(1)}, u32[]{:S(2)}, u32[]{:S(2)}) collective-permute-start(bf16[144,512]{1,0:T(8,128)(2,1)S(1)} %pad_maximum_fusion.10), channel_id=1, source_target_pairs={{0,24},{1,25},{2,26},{3,27},{4,28},{5,29},{6,30},{7,31},{8,16},{9,... | collective-permute-start | bytes 442376 | tf_op jit(solution)/shard_map/ppermute | solution.py:693
  63.0 3.8 %collective-permute-start.26 = (bf16[1,64,1024]{2,1,0:T(8,128)(2,1)S(1)}, bf16[1,64,1024]{2,1,0:T(8,128)(2,1)S(1)}, u32[]{:S(2)}, u32[]{:S(2)}) collective-permute-start(bf16[1,64,1024]{2,1,0:T(8,128)(2,1)S(1)} %get-tuple-element.159.refs_0_), channel_id=1, source_target_pairs={{0,1},{1,0},{2,3},{3,2},{4,5},{5,4},{6,7},{7,6},{8,9},{9,8},{10,11... | collective-permute-start | bytes 393224 | tf_op jit(solution)/shard_map/ppermute | solution.py:693
  64.1 3.9 %collective-permute-start.24 = (bf16[3,64,1024]{2,1,0:T(8,128)(2,1)S(1)}, bf16[3,64,1024]{2,1,0:T(8,128)(2,1)S(1)}, u32[]{:S(2)}, u32[]{:S(2)}) collective-permute-start(bf16[3,64,1024]{2,1,0:T(8,128)(2,1)S(1)} %pad_maximum_fusion.1.refs_1_), channel_id=1, source_target_pairs={{0,1},{1,0},{2,3},{3,2},{4,5},{5,4},{6,7},{7,6},{8,9},{9,8},{10,11... | collective-permute-start | bytes 1179656 | tf_op jit(solution)/shard_map/ppermute | solution.py:693
